TPU v7x, 256 devices: a whole 4x4x8 slice. The times are simulated.
256 devices in a mesh: section: 2 (over core), tensor: 4 (over z_lo), dp: 32 (over z_hi, y, x).
Axes of the slice: x: 4, y: 4, z: 8 (z_hi: 2, z_lo: 4; z = z_hi * 4 + z_lo), core: 2. Of those that a mesh axis runs over, the one named last changes fastest.
Arguments:
- weights: bfloat16 [2, 4096, 4096], P('section', 'tensor'), may hold values from -0.09375 to 0.09375
- stash_in: bfloat16 [2, 4, 4096, 4096], P('section', None, 'dp', 'tensor'), may hold values from -0.079589844 to 0.079589844
- stash_grad: bfloat16 [2, 3, 4096, 4096], P('section', None, 'dp'), may hold values from -6 to 6
- head_grad: bfloat16 [4096, 4096], P('dp'), may hold values from -6 to 6
- pending: int32 [2], replicated, may hold values from 1 to 4, as said below
Outputs:
- input_grad: float32 [2, 4096, 4096], P('section', 'dp', 'tensor')
- weight_grad: float32 [2, 4096, 4096], P('section', 'tensor', 'dp')
Inputs may be any that keep to these rules, and one draw needn't show every extreme that they name: pending[s] counts the deferred tasks of segment s, which are its last pending[s] micro-batches; some segment has 4 of them.
All inputs are finite; a program needn't handle non-finite values.
Results may differ from a plain program's by a relative error of at most 0.0021.
Values may be sent and summed in bfloat16 or wider, within the bound.
No kernel may reach another device: no remote copies, remote signals or barrier semaphores. Data moves between devices by JAX's collectives and lax.ppermute only.
A program may use at most 128 MiB of HBM per device.

v0:
```python
import jax
import jax.numpy as jnp
from jax import lax
from jax.sharding import PartitionSpec as P


def shifted(value, axis, by):
    peers = lax.axis_size(axis)
    pairs = [(i, i + by) for i in range(peers) if 0 <= i + by < peers]
    return lax.ppermute(value, axis, pairs)


def contract_rows(left, right):
    return lax.dot_general(
        left, right, (((0,), (0,)), ((), ())), preferred_element_type=jnp.float32
    )


def local(weights, stash_in, stash_grad, head_grad, pending):
    segments = lax.axis_size("section")
    segment = lax.axis_index("section")
    weight = weights[0]
    local_width = weight.shape[0]
    micro_count = stash_in.shape[1]

    def backward_step(grad):
        return lax.dot_general(
            grad, weight, (((1,), (1,)), ((), ())), preferred_element_type=jnp.float32
        )

    is_last = segment == segments - 1

    def chain_turn(turn, grad):
        part_grad = backward_step(grad).astype(jnp.bfloat16)
        moved = shifted(part_grad, "section", -1)
        whole = lax.all_gather(moved, "tensor", axis=1, tiled=True)
        return jnp.where(is_last, head_grad, whole)

    grad = lax.fori_loop(0, segments - 1, chain_turn, head_grad)
    input_grad = backward_step(grad)[None]
    count = lax.dynamic_index_in_dim(pending, segment, 0, keepdims=False)
    micro = jnp.arange(micro_count, dtype=jnp.int32)
    keep = micro >= micro_count - count
    inputs = stash_in[0]
    masked = jnp.where(keep[:, None, None], inputs, jnp.zeros_like(inputs))
    x_rows = masked.reshape(-1, local_width)
    grads_all = jnp.concatenate([stash_grad[0], grad[None]], 0)
    g_rows = grads_all.reshape(-1, grads_all.shape[2])
    block = lax.psum_scatter(contract_rows(g_rows, x_rows), "dp", scatter_dimension=0, tiled=True).T
    weight_grad = block[None]
    return (input_grad, weight_grad)


def solution(mesh):
    return jax.shard_map(
        local,
        mesh=mesh,
        in_specs=(
            P("section", "tensor", None),
            P("section", None, "dp", "tensor"),
            P("section", None, "dp", None),
            P("dp", None),
            P(),
        ),
        out_specs=(P("section", "dp", "tensor"), P("section", "tensor", "dp")),
        check_vma=False,
    )
```

profile of v0, /device:TPU:64, one launch (start us, length us, event | category | flops | bytes accessed | tf_op | source)
XLA Modules:
  0.0 477.1 jit_solution(9395346068383908480)
XLA Ops:
  7.2 0.0 copy-start
  7.2 0.0 copy-start.3
  7.2 0.0 all-gather.2.cloned.1.call-start
  7.2 6.7 %fusion.10 = bf16[128,1024]{1,0:T(8,128)(2,1)S(1)} fusion(bf16[128,4096]{1,0:T(8,128)(2,1)} %param.8, bf16[1,1024,4096]{2,1,0:T(8,128)(2,1)} %param.5), kind=kOutput, calls=%fused_computation.9 | convolution fusion | flops 1073872896 | bytes 9699328 | tf_op jit(solution)/shard_map/while/body/eval_jaxpr/dot_general | solution.py:27
  13.9 1.3 collective-permute-start
  15.2 2.1 collective-permute-done
  17.3 0.0 copy-start.2
  17.3 0.7 copy-done.2
  18.0 0.0 all-gather.2.cloned.1.call-update
  18.1 0.0 reduce-scatter.2.cloned.1.call-start
  18.1 4.7 copy.7
  22.8 0.0 copy-done.3
  22.8 0.6 dynamic_slice.4
  24.0 28.4 %all-gather.2.cloned.1.call-done = bf16[128,4096]{1,0:T(8,128)(2,1)} async-done(((bf16[128,1024]{1,0:T(8,128)(2,1)}), bf16[128,4096]{1,0:T(8,128)(2,1)}) %all-gather.2.cloned.1.call-update) | async-done | bytes 1048592 | tf_op jit(solution)/shard_map/while/body/eval_jaxpr/all_gather | solution.py:36
  52.5 0.0 copy-done
  52.5 1.3 fusion.15
  53.8 0.7 copy.8
  54.5 9.9 %convolution_bitcast_fusion = f32[4096,1024]{1,0:T(8,128)} fusion(bf16[1,128,4096]{1,2,0:T(8,128)(2,1)S(1)} %copy.8, bf16[3,128,4096]{1,2,0:T(8,128)(2,1)} %bitcast.24, bf16[1,4,128,1024]{3,2,1,0:T(8,128)(2,1)} %param.6, pred[4]{0:T(512)(128)(4,1)S(1)} %iota_compare_fusion), kind=kOutput, calls=%fused_computation | convolution fusion | flops 4297588736 | bytes 22020100 | tf_op jit(solution)/shard_map/dot_general | solution.py:14
  64.4 0.0 copy-start.1
  64.4 0.0 reduce-scatter.2.cloned.1.call-update
  64.4 1.2 copy-done.1
  65.6 7.1 %fusion.7 = f32[1,128,1024]{2,1,0:T(8,128)} fusion(bf16[1,1024,4096]{2,1,0:T(8,128)(2,1)} %param.5, bf16[128,4096]{1,0:T(8,128)(2,1)S(1)} %copy-done, bf16[128,4096]{1,0:T(8,128)(2,1)S(1)} %copy-done.1, pred[]{:T(512)S(6)} %eq.3), kind=kOutput, calls=%fused_computation.8 | convolution fusion | flops 1074266112 | bytes 11010049 | tf_op jit(solution)/shard_map/dot_general | solution.py:27
  72.7 395.6 %reduce-scatter.2.cloned.1.call-done = f32[128,1024]{1,0:T(8,128)} async-done(((f32[4096,1024]{1,0:T(8,128)}), f32[128,1024]{1,0:T(8,128)}) %reduce-scatter.2.cloned.1.call-update) | async-done | bytes 524304 | tf_op jit(solution)/shard_map/reduce_scatter | solution.py:49
  468.2 2.0 copy.9
  (1 shorter events, 0.0 us)
Async XLA Ops:
  7.2 45.3 %copy-start = (bf16[128,4096]{1,0:T(8,128)(2,1)S(1)}, bf16[128,4096]{1,0:T(8,128)(2,1)}, u32[]{:S(2)}) copy-start(bf16[128,4096]{1,0:T(8,128)(2,1)} %param.8) | copy-start | bytes 3145732
  7.2 15.6 %copy-start.3 = (s32[2]{0:T(128)S(1)}, s32[2]{0:T(128)}, u32[]{:S(2)}) copy-start(s32[2]{0:T(128)} %param.9) | copy-start | bytes 28
  7.2 45.3 %all-gather.2.cloned.1.call-start = ((), (), s32[]{:S(2)}) async-start(), calls=%async_computation.1 | async-start | bytes 1310720 | tf_op jit(solution)/shard_map/while/body/eval_jaxpr/all_gather | solution.py:36
  13.9 3.4 collective-permute-start
  17.3 0.7 copy-start.2
  18.1 450.1 %reduce-scatter.2.cloned.1.call-start = ((), (), s32[]{:S(2)}) async-start(), calls=%async_computation.2 | async-start | bytes 17301504 | tf_op jit(solution)/shard_map/reduce_scatter | solution.py:49
  64.4 1.2 copy-start.1
Sparse Core Ops, SparseCore 0:
  18.2 34.2 all-gather.1
  64.5 403.6 reduce-scatter.1
where the time goes:
time: 477 us
  waiting for transfers between devices  426 us (89%)
  matrix products  23.6 us (5%)
  between operations  14.7 us (3%)
  local copies, waits for them, and re-layouts  9.84 us (2%)
    reduce_scatter x1, waiting for transfers between devices, local(): lax.psum_scatter(contract_rows(g_rows, x_rows), 'dp', scatter_dimension=0...  396 us
    all_gather x1, waiting for transfers between devices, chain_turn(): whole = lax.all_gather(moved, 'tensor', axis=1, tiled=True)  28.4 us
    dot_general x2, matrix products, backward_step(): lax.dot_general(grad, weight, (((1,), (1,)), ((), ())), preferred_element...  13.7 us
    dot_general x1, matrix products, contract_rows(): lax.dot_general(left, right, (((0,), (0,)), ((), ())), preferred_element_...  9.87 us
  transfers between devices with their start and end apart: 3, of which 3 were waited for; matrix products, arithmetic and copies ran while one was open for 3% of the time, Pallas kernels for 0%

commit v1 on v0

v1 whole, which is shorter than its diff:
```python
import functools

import jax
import jax.numpy as jnp
from jax import lax
from jax.experimental import pallas as pl
from jax.experimental.pallas import tpu as pltpu
from jax.sharding import Mesh
from jax.sharding import PartitionSpec as P

F32 = jnp.float32
BF16 = jnp.bfloat16
RING = 4
LANES = 128


def block_index(pos, zr, yr, xr):
    z = lax.rem(pos[0] + zr, 2)
    y = lax.rem(pos[1] + yr, RING)
    x = lax.rem(pos[2] + xr, RING)
    return z * (RING * RING) + y * RING + x


SEND_RIGHT = [(0, 2, j) for j in range(RING)] + [(1, 1, j) for j in range(RING)]
SEND_LEFT = [(1, 2, j) for j in range(RING)] + [(0, 3, j) for j in range(RING)]
PASS_ON = [(0, 1, j) for j in range(RING)] + [(1, 3, j) for j in range(RING)]
KEEP = [(0, 0, j) for j in range(RING)] + [(1, 0, j) for j in range(RING)]


def products_kernel(plans, pos_ref, x_ref, stash_ref, head_ref, rel_ref, *rest):
    outs, xt_ref = rest[:-1], rest[-1]
    micro, rows, width = x_ref.shape
    half = width // 2
    pos = (pos_ref[0], pos_ref[1], pos_ref[2])
    tensor, is_last, count = pos_ref[3], pos_ref[4], pos_ref[5]
    for m in range(micro):
        keep = (m >= micro - count).astype(F32)
        masked = jnp.where(keep > 0, x_ref[m].astype(F32), 0.0)
        xt_ref[:, m * rows:(m + 1) * rows] = masked.T.astype(BF16)
    shard_blocks = rel_ref.shape[2] // LANES

    def columns(block):
        at = pl.multiple_of(block * LANES, LANES)
        parts = [stash_ref[m, :, pl.ds(at, LANES)] for m in range(micro - 1)]
        owner = lax.div(block, shard_blocks)
        turn = lax.rem(tensor - owner + RING, RING)
        inner = pl.multiple_of(lax.rem(block, shard_blocks) * LANES, LANES)
        chained = rel_ref[turn, :, pl.ds(inner, LANES)]
        given = head_ref[:, pl.ds(at, LANES)]
        parts.append(jnp.where(is_last > 0, given, chained))
        return jnp.concatenate(parts, axis=0)

    for out, (part, slots) in zip(outs, plans):
        xt = xt_ref[part * half:(part + 1) * half, :]
        for j in range(0, len(slots), 2):
            pair = []
            for zr, along, across in slots[j:j + 2]:
                yr, xr = (across, along) if part == 0 else (along, across)
                pair.append(columns(block_index(pos, zr, yr, xr)))
            both = jnp.dot(xt, jnp.concatenate(pair, axis=1), preferred_element_type=F32)
            out[j * half:(j + 1) * half, :] = both[:, :LANES].astype(out.dtype)
            out[(j + 1) * half:(j + 2) * half, :] = both[:, LANES:].astype(out.dtype)


def products(plans, dtypes, pos, inputs, stash_grad, head_grad, rel):
    micro, rows, width = inputs.shape
    half = width // 2
    whole = pl.BlockSpec(memory_space=pltpu.VMEM)
    shapes = [jax.ShapeDtypeStruct((len(slots) * half, LANES), dtype) for (_, slots), dtype in zip(plans, dtypes)]
    n_slots = sum(len(slots) for _, slots in plans)
    return pl.pallas_call(
        functools.partial(products_kernel, plans),
        out_shape=shapes,
        in_specs=[pl.BlockSpec(memory_space=pltpu.SMEM)] + [whole] * 4,
        out_specs=[whole] * len(shapes),
        scratch_shapes=[pltpu.VMEM((width, micro * rows), BF16)],
        compiler_params=pltpu.CompilerParams(vmem_limit_bytes=40 * 2**20),
        cost_estimate=pl.CostEstimate(
            flops=2 * n_slots * half * LANES * micro * rows,
            bytes_accessed=6 * 2**20 + n_slots * half * LANES * 4,
            transcendentals=0,
        ),
    )(pos, inputs, stash_grad, head_grad, rel)


def shifted(value, axis, by):
    return lax.ppermute(value, axis, [(i, (i + by) % RING) for i in range(RING)])


def local(weights, stash_in, stash_grad, head_grad, pending):
    segment = lax.axis_index("section")
    is_last = segment == lax.axis_size("section") - 1
    tensor = lax.axis_index("z_lo")
    weight = weights[0]
    inputs, grads = stash_in[0], stash_grad[0]
    rows = head_grad.shape[0]

    def backward_step(grad):
        return lax.dot_general(grad, weight, (((1,), (1,)), ((), ())), preferred_element_type=F32)

    first = backward_step(head_grad)
    shard = lax.ppermute(first.astype(BF16), "section", [(1, 0)])
    rel = [shard]
    for by in range(1, RING):
        pairs = [(i, (i + by) % RING) for i in range(RING)]
        rel.append(lax.ppermute(shard, ("section", "z_lo"), pairs))
    rel_stack = jnp.stack(rel, 0)

    count = lax.dynamic_index_in_dim(pending, segment, 0, keepdims=False)
    place = [lax.axis_index("z_hi"), lax.axis_index("y"), lax.axis_index("x"), tensor, is_last, count]
    pos = jnp.stack([v.astype(jnp.int32) for v in place])
    args = (pos, inputs, grads, head_grad, rel_stack)
    axes = ("x", "y")
    sends = products([(part, s) for part in (0, 1) for s in (SEND_RIGHT, SEND_LEFT)], [BF16] * 4, *args)
    got = []
    for part in (0, 1):
        got.append((shifted(sends[2 * part], axes[part], 1), shifted(sends[2 * part + 1], axes[part], -1)))
    own = products([(part, s) for part in (0, 1) for s in (PASS_ON, KEEP)], [F32] * 4, *args)
    mid = own[0].shape[0] // 2
    passed = []
    for part in (0, 1):
        from_left, from_right = got[part]
        going = own[2 * part]
        right = (going[:mid] + from_left[:mid].astype(F32)).astype(BF16)
        left = (going[mid:] + from_right[:mid].astype(F32)).astype(BF16)
        passed.append((shifted(right, axes[part], 1), shifted(left, axes[part], -1)))
    totals = []
    for part in (0, 1):
        from_left, from_right = got[part]
        late_left, late_right = passed[part]
        kept = own[2 * part + 1]
        near = kept[:mid] + from_right[mid:].astype(F32) + late_left.astype(F32)
        far = kept[mid:] + from_left[mid:].astype(F32) + late_right.astype(F32)
        both = jnp.stack([near, far], 0).reshape(2, RING, -1, LANES)
        axis = axes[1 - part]
        total = both[:, 0]
        for by in range(1, RING):
            total = total + shifted(both[:, by], axis, by)
        totals.append(total)
    block = jnp.concatenate(totals, 1)
    block = block[0] + lax.ppermute(block[1], "z_hi", [(0, 1), (1, 0)])
    weight_grad = block[None]

    order = jnp.stack(rel[::-1] + rel[::-1], 0)
    whole = lax.dynamic_slice_in_dim(order, RING - 1 - tensor, RING, 0)
    whole = jnp.moveaxis(whole, 0, 1).reshape(rows, -1)
    second = backward_step(whole)
    input_grad = jnp.where(is_last, first, second)[None]
    return (input_grad, weight_grad)


def solution(mesh):
    fine = Mesh(mesh.devices.reshape(2, 4, 2, 4, 4), ("section", "z_lo", "z_hi", "y", "x"))
    dp = ("z_hi", "y", "x")
    return jax.shard_map(
        local,
        mesh=fine,
        in_specs=(
            P("section", "z_lo", None),
            P("section", None, dp, "z_lo"),
            P("section", None, dp, None),
            P(dp, None),
            P(),
        ),
        out_specs=(P("section", dp, "z_lo"), P("section", "z_lo", dp)),
        check_vma=False,
    )
```

time: 477 us -> 134 us (0.28)
  the two profiles are of different devices: /device:TPU:64 before, /device:TPU:24 now
where the time goes in v1:
time: 134 us; the launch traced here: 133 us
  waiting for transfers between devices  56.6 us (42%)
  starting transfers between devices  38.2 us (29%)
  matrix products  14.5 us (11%)
  Pallas kernels  8.1 us (6%)
  local copies, waits for them, and re-layouts  7.53 us (6%)
  other arithmetic  7.29 us (5%)
    ppermute x14, waiting for transfers between devices, shifted(): lax.ppermute(value, axis, [(i, (i + by) % RING) for i in range(RING)])  44.1 us
    ppermute x14, starting transfers between devices, shifted(): lax.ppermute(value, axis, [(i, (i + by) % RING) for i in range(RING)])  17.7 us
    dot_general x2, matrix products, backward_step(): lax.dot_general(grad, weight, (((1,), (1,)), ((), ())), preferred_element...  14.5 us
    ppermute x3, starting transfers between devices, local(): rel.append(lax.ppermute(shard, ('section', 'z_lo'), pairs))  11.9 us
    pallas_call x2, Pallas kernels, products(): pl.pallas_call(functools.partial(products_kernel, plans), out_shape=shape...  8.1 us
    ppermute x1, starting transfers between devices, local(): block = block[0] + lax.ppermute(block[1], 'z_hi', [(0, 1), (1, 0)])  7.14 us
    ppermute x3, waiting for transfers between devices, local(): rel.append(lax.ppermute(shard, ('section', 'z_lo'), pairs))  5.99 us
    ppermute x1, waiting for transfers between devices, local(): block = block[0] + lax.ppermute(block[1], 'z_hi', [(0, 1), (1, 0)])  4.38 us
  transfers between devices with their start and end apart: 19, of which 9 were waited for; matrix products, arithmetic and copies ran while one was open for 13% of the time, Pallas kernels for 4%

profile of v1, /device:TPU:24, one launch (start us, length us, event | category | flops | bytes accessed | tf_op | source)
XLA Modules:
  0.0 133.1 jit_solution(10556933269548732022)
XLA Ops:
  0.6 7.4 %fusion.35 = (bf16[128,1024]{1,0:T(8,128)(2,1)S(1)}, f32[128,1024]{1,0:T(8,128)}) fusion(bf16[128,4096]{1,0:T(8,128)(2,1)} %head_ref.3, bf16[1,1024,4096]{2,1,0:T(8,128)(2,1)} %param.5), kind=kOutput, calls=%fused_computation.66 | convolution fusion | flops 1073872896 | bytes 10223616 | tf_op jit(solution)/shard_map/dot_general | solution.py:99
  8.1 1.4 %collective-permute-start = (bf16[128,1024]{1,0:T(8,128)(2,1)S(1)}, bf16[128,1024]{1,0:T(8,128)(2,1)S(1)}, u32[]{:S(2)}, u32[]{:S(2)}) collective-permute-start(bf16[128,1024]{1,0:T(8,128)(2,1)S(1)} %get-tuple-element.32), channel_id=1, source_target_pairs={{128,0},{129,1},{130,2},{131,3},{132,4},{133,5},{134,6},{135,7},{1... | collective-permute-start | bytes 786440 | tf_op jit(solution)/shard_map/ppermute | solution.py:102
  9.5 2.1 %collective-permute-done = bf16[128,1024]{1,0:T(8,128)(2,1)S(1)} collective-permute-done((bf16[128,1024]{1,0:T(8,128)(2,1)S(1)}, bf16[128,1024]{1,0:T(8,128)(2,1)S(1)}, u32[]{:S(2)}, u32[]{:S(2)}) %collective-permute-start) | collective-permute-done | bytes 262176 | tf_op jit(solution)/shard_map/ppermute | solution.py:102
  11.6 3.8 %collective-permute-start.3 = (bf16[128,1024]{1,0:T(8,128)(2,1)S(1)}, bf16[128,1024]{1,0:T(8,128)(2,1)S(1)}, u32[]{:S(2)}, u32[]{:S(2)}) collective-permute-start(bf16[128,1024]{1,0:T(8,128)(2,1)S(1)} %collective-permute-done), channel_id=1, source_target_pairs={{0,32},{32,64},{64,96},{96,0},{1,33},{33,65},{65,97},{97,1},{2,34}... | collective-permute-start | bytes 786440 | tf_op jit(solution)/shard_map/ppermute | solution.py:106
  15.4 5.2 %collective-permute-start.2 = (bf16[128,1024]{1,0:T(8,128)(2,1)S(1)}, bf16[128,1024]{1,0:T(8,128)(2,1)S(1)}, u32[]{:S(2)}, u32[]{:S(2)}) collective-permute-start(bf16[128,1024]{1,0:T(8,128)(2,1)S(1)} %collective-permute-done), channel_id=1, source_target_pairs={{0,64},{32,96},{64,0},{96,32},{1,65},{33,97},{65,1},{97,33},{2,66}... | collective-permute-start | bytes 786440 | tf_op jit(solution)/shard_map/ppermute | solution.py:106
  20.6 2.9 %collective-permute-start.1 = (bf16[128,1024]{1,0:T(8,128)(2,1)S(1)}, bf16[128,1024]{1,0:T(8,128)(2,1)S(1)}, u32[]{:S(2)}, u32[]{:S(2)}) collective-permute-start(bf16[128,1024]{1,0:T(8,128)(2,1)S(1)} %collective-permute-done), channel_id=1, source_target_pairs={{0,96},{32,0},{64,32},{96,64},{1,97},{33,1},{65,33},{97,65},{2,98}... | collective-permute-start | bytes 786440 | tf_op jit(solution)/shard_map/ppermute | solution.py:106
  23.6 0.6 dynamic_slice.8
  24.2 0.7 stack.77.pos_ref
  24.9 0.0 collective-permute-done.3
  24.9 3.3 %collective-permute-done.2 = bf16[128,1024]{1,0:T(8,128)(2,1)S(1)} collective-permute-done((bf16[128,1024]{1,0:T(8,128)(2,1)S(1)}, bf16[128,1024]{1,0:T(8,128)(2,1)S(1)}, u32[]{:S(2)}, u32[]{:S(2)}) %collective-permute-start.2) | collective-permute-done | bytes 262176 | tf_op jit(solution)/shard_map/ppermute | solution.py:106
  28.2 2.7 %collective-permute-done.1 = bf16[128,1024]{1,0:T(8,128)(2,1)S(1)} collective-permute-done((bf16[128,1024]{1,0:T(8,128)(2,1)S(1)}, bf16[128,1024]{1,0:T(8,128)(2,1)S(1)}, u32[]{:S(2)}, u32[]{:S(2)}) %collective-permute-start.1) | collective-permute-done | bytes 262176 | tf_op jit(solution)/shard_map/ppermute | solution.py:106
  30.9 0.1 pad_maximum_fusion.rel_ref
  31.1 0.0 copy-start.1
  31.1 1.9 %copy-done.1 = bf16[1,3,128,4096]{3,2,1,0:T(8,128)(2,1)S(1)} copy-done((bf16[1,3,128,4096]{3,2,1,0:T(8,128)(2,1)S(1)}, bf16[1,3,128,4096]{3,2,1,0:T(8,128)(2,1)}, u32[]{:S(2)}) %copy-start.1) | copy-done | bytes 3145752
  33.0 3.4 %shard_map.69 = (bf16[4096,128]{1,0:T(8,128)(2,1)S(1)}, bf16[4096,128]{1,0:T(8,128)(2,1)S(1)}, bf16[4096,128]{1,0:T(8,128)(2,1)S(1)}, bf16[4096,128]{1,0:T(8,128)(2,1)S(1)}) custom-call(s32[6]{0:T(128)S(1)} %stack.77.pos_ref, bf16[4,128,1024]{2,1,0:T(8,128)(2,1)S(1)} %bitcast.89, bf16[3,128,4096]{2,1,0:T(8,128)(2,1)S(1)} %bitcast.88, ...), custom_call_target="tpu_custom_call" | custom-call | flops 2147483648 | bytes 14680064 | tf_op jit(solution)/shard_map/pallas_call | solution.py:71
  36.4 2.8 %collective-permute-start.4 = (bf16[4096,128]{1,0:T(8,128)(2,1)S(1)}, bf16[4096,128]{1,0:T(8,128)(2,1)S(1)}, u32[]{:S(2)}, u32[]{:S(2)}) collective-permute-start(bf16[4096,128]{1,0:T(8,128)(2,1)S(1)} %get-tuple-element.11), channel_id=1, source_target_pairs={{0,3},{1,0},{2,1},{3,2},{4,7},{5,4},{6,5},{7,6},{8,11},{9,8},{10,9... | collective-permute-start | bytes 3145736 | tf_op jit(solution)/shard_map/ppermute | solution.py:87
  39.2 0.7 collective-permute-start.11
  39.9 2.5 %collective-permute-start.12 = (bf16[4096,128]{1,0:T(8,128)(2,1)S(1)}, bf16[4096,128]{1,0:T(8,128)(2,1)S(1)}, u32[]{:S(2)}, u32[]{:S(2)}) collective-permute-start(bf16[4096,128]{1,0:T(8,128)(2,1)S(1)} %get-tuple-element.17), channel_id=1, source_target_pairs={{0,4},{4,8},{8,12},{12,0},{1,5},{5,9},{9,13},{13,1},{2,6},{6,10},{... | collective-permute-start | bytes 3145736 | tf_op jit(solution)/shard_map/ppermute | solution.py:87
  42.6 4.7 %shard_map.68 = (f32[4096,128]{1,0:T(8,128)S(1)}, f32[4096,128]{1,0:T(8,128)S(1)}, f32[4096,128]{1,0:T(8,128)S(1)}, f32[4096,128]{1,0:T(8,128)S(1)}) custom-call(s32[6]{0:T(128)S(1)} %stack.77.pos_ref, bf16[4,128,1024]{2,1,0:T(8,128)(2,1)S(1)} %bitcast.90, bf16[3,128,4096]{2,1,0:T(8,128)(2,1)} %bitcast.87, bf16[128,4096]{1,0:T(8,128)(2,1)S(1)} %copy-done, ...), custom_call_target="tpu_custom_call" | custom-call | flops 2147483648 | bytes 14680064 | tf_op jit(solution)/shard_map/pallas_call | solution.py:71
  47.3 13.5 %collective-permute-done.11 = bf16[4096,128]{1,0:T(8,128)(2,1)S(1)} collective-permute-done((bf16[4096,128]{1,0:T(8,128)(2,1)S(1)}, bf16[4096,128]{1,0:T(8,128)(2,1)S(1)}, u32[]{:S(2)}, u32[]{:S(2)}) %collective-permute-start.11) | collective-permute-done | bytes 1048608 | tf_op jit(solution)/shard_map/ppermute | solution.py:87
  60.8 0.2 add_convert_fusion.1
  61.0 1.2 collective-permute-start.13
  62.2 0.9 collective-permute-start.14
  63.1 0.2 add_convert_fusion.3
  63.3 0.9 collective-permute-start.6
  64.2 2.5 %collective-permute-start.7 = (bf16[2048,128]{1,0:T(8,128)(2,1)S(1)}, bf16[2048,128]{1,0:T(8,128)(2,1)S(1)}, u32[]{:S(2)}, u32[]{:S(2)}) collective-permute-start(bf16[2048,128]{1,0:T(8,128)(2,1)S(1)} %get-tuple-element.24), channel_id=1, source_target_pairs={{0,3},{1,0},{2,1},{3,2},{4,7},{5,4},{6,5},{7,6},{8,11},{9,8},{10,9... | collective-permute-start | bytes 1572872 | tf_op jit(solution)/shard_map/ppermute | solution.py:87
  66.8 8.2 %collective-permute-done.13 = bf16[2048,128]{1,0:T(8,128)(2,1)S(1)} collective-permute-done((bf16[2048,128]{1,0:T(8,128)(2,1)S(1)}, bf16[2048,128]{1,0:T(8,128)(2,1)S(1)}, u32[]{:S(2)}, u32[]{:S(2)}) %collective-permute-start.13) | collective-permute-done | bytes 524320 | tf_op jit(solution)/shard_map/ppermute | solution.py:87
  74.9 8.8 %collective-permute-done.14 = bf16[2048,128]{1,0:T(8,128)(2,1)S(1)} collective-permute-done((bf16[2048,128]{1,0:T(8,128)(2,1)S(1)}, bf16[2048,128]{1,0:T(8,128)(2,1)S(1)}, u32[]{:S(2)}, u32[]{:S(2)}) %collective-permute-start.14) | collective-permute-done | bytes 524320 | tf_op jit(solution)/shard_map/ppermute | solution.py:87
  83.7 0.3 convert_add_fusion.1
  84.0 1.1 fusion.22
  85.1 0.3 collective-permute-start.15
  85.4 2.9 %collective-permute-start.17 = (f32[2,512,128]{2,1,0:T(8,128)}, f32[2,512,128]{2,1,0:T(8,128)}, u32[]{:S(2)}, u32[]{:S(2)}) collective-permute-start(f32[2,512,128]{2,1,0:T(8,128)} %get-tuple-element.26), channel_id=1, source_target_pairs={{0,3},{1,0},{2,1},{3,2},{4,7},{5,4},{6,5},{7,6},{8,11},{9,8},{10,9... | collective-permute-start | bytes 1572872 | tf_op jit(solution)/shard_map/ppermute | solution.py:87
  88.3 0.9 collective-permute-start.16
  89.2 0.3 convert_add_fusion.3
  89.5 1.2 fusion.31
  90.7 2.0 %collective-permute-start.10 = (f32[2,512,128]{2,1,0:T(8,128)}, f32[2,512,128]{2,1,0:T(8,128)}, u32[]{:S(2)}, u32[]{:S(2)}) collective-permute-start(f32[2,512,128]{2,1,0:T(8,128)} %get-tuple-element.19), channel_id=1, source_target_pairs={{0,12},{4,0},{8,4},{12,8},{1,13},{5,1},{9,5},{13,9},{2,14},{6,2},{... | collective-permute-start | bytes 1572872 | tf_op jit(solution)/shard_map/ppermute | solution.py:87
  92.7 8.3 %collective-permute-done.15 = f32[2,512,128]{2,1,0:T(8,128)S(1)} collective-permute-done((f32[2,512,128]{2,1,0:T(8,128)S(1)}, f32[2,512,128]{2,1,0:T(8,128)S(1)}, u32[]{:S(2)}, u32[]{:S(2)}) %collective-permute-start.15) | collective-permute-done | bytes 524320 | tf_op jit(solution)/shard_map/ppermute | solution.py:87
  101.1 0.8 copy-done.7
  101.9 1.1 dynamic-slice_bitcast_fusion
  103.0 2.3 %copy.11 = bf16[128,4,1024]{0,2,1:T(8,128)(2,1)} copy(bf16[128,4,1024]{2,0,1:T(8,128)(2,1)} %dynamic-slice_bitcast_fusion) | data formatting | bytes 2097152 | tf_op jit(solution)/shard_map/transpose | solution.py:146
  105.2 1.5 %fusion.20 = f32[2,512,128]{2,1,0:T(8,128)S(1)} fusion(f32[2,512,128]{2,1,0:T(8,128)} %collective-permute-done.17, f32[2,512,128]{2,1,0:T(8,128)} %collective-permute-done.16, f32[2,512,128]{2,1,0:T(8,128)} %copy-done.7, f32[1,4,512,128]{3,2,0,1:T(8,128)S(1)} %bitcast.92, f32[1,4,512,128]{3,2,0,1:T(8,128)S(1)} %bitcast.94), kind=kLoop, calls=%fused_computation.40 | loop fusion | flops 524288 | bytes 4194304 | tf_op jit(solution)/shard_map/add | solution.py:138
  106.8 0.0 copy-start.6
  106.8 5.2 %collective-permute-done.9 = f32[2,512,128]{2,1,0:T(8,128)} collective-permute-done((f32[2,512,128]{2,1,0:T(8,128)}, f32[2,512,128]{2,1,0:T(8,128)}, u32[]{:S(2)}, u32[]{:S(2)}) %collective-permute-start.9) | collective-permute-done | bytes 524320 | tf_op jit(solution)/shard_map/ppermute | solution.py:87
  112.1 1.5 %fusion.29 = f32[2,512,128]{2,1,0:T(8,128)S(1)} fusion(f32[2,512,128]{2,1,0:T(8,128)} %collective-permute-done.10, f32[2,512,128]{2,1,0:T(8,128)} %collective-permute-done.9, f32[2,512,128]{2,1,0:T(8,128)} %collective-permute-done.8, f32[1,4,512,128]{3,2,0,1:T(8,128)S(1)} %bitcast.96, f32[1,4,512,128]{3,2,0,1:T(8,128)S(1)} %bitcast.98), kind=kLoop, calls=%fused_computation.49 | loop fusion | flops 524288 | bytes 4194304 | tf_op jit(solution)/shard_map/add | solution.py:138
  113.6 7.1 %collective-permute-start.18 = (f32[1024,128]{1,0:T(8,128)S(1)}, f32[1024,128]{1,0:T(8,128)S(1)}, u32[]{:S(2)}, u32[]{:S(2)}) collective-permute-start(f32[1024,128]{1,0:T(8,128)S(1)} %fusion.32), channel_id=1, source_target_pairs={{0,16},{16,0},{1,17},{17,1},{2,18},{18,2},{3,19},{19,3},{4,20},{20... | collective-permute-start | bytes 1572872 | tf_op jit(solution)/shard_map/ppermute | solution.py:141
  120.7 7.1 %fusion.7 = f32[1,128,1024]{2,1,0:T(8,128)} fusion(f32[128,1024]{1,0:T(8,128)S(1)} %copy-done.6, bf16[128,4096]{0,1:T(8,128)(2,1)S(1)} %bitcast.99, bf16[1,1024,4096]{2,1,0:T(8,128)(2,1)} %param.5, pred[]{:T(512)S(6)} %eq.3), kind=kOutput, calls=%fused_computation.17 | convolution fusion | flops 1073872896 | bytes 10485761 | tf_op jit(solution)/shard_map/dot_general | solution.py:99
  127.8 4.4 %collective-permute-done.18 = f32[1024,128]{1,0:T(8,128)S(1)} collective-permute-done((f32[1024,128]{1,0:T(8,128)S(1)}, f32[1024,128]{1,0:T(8,128)S(1)}, u32[]{:S(2)}, u32[]{:S(2)}) %collective-permute-start.18) | collective-permute-done | bytes 524320 | tf_op jit(solution)/shard_map/ppermute | solution.py:141
  132.2 0.8 fusion.13
  (35 shorter events, 0.2 us)
Async XLA Ops:
  0.6 22.9 %copy-start.8 = (s32[2]{0:T(128)S(1)}, s32[2]{0:T(128)}, u32[]{:S(2)}) copy-start(s32[2]{0:T(128)} %param.9) | copy-start | bytes 28
  8.1 23.0 %copy-start = (bf16[128,4096]{1,0:T(8,128)(2,1)S(1)}, bf16[128,4096]{1,0:T(8,128)(2,1)}, u32[]{:S(2)}) copy-start(bf16[128,4096]{1,0:T(8,128)(2,1)} %head_ref.3) | copy-start | bytes 3145732
  8.1 23.0 %copy-start.2 = (bf16[1,4,128,1024]{3,2,1,0:T(8,128)(2,1)S(1)}, bf16[1,4,128,1024]{3,2,1,0:T(8,128)(2,1)}, u32[]{:S(2)}) copy-start(bf16[1,4,128,1024]{3,2,1,0:T(8,128)(2,1)} %param.6) | copy-start | bytes 3145732
  8.1 3.5 %collective-permute-start = (bf16[128,1024]{1,0:T(8,128)(2,1)S(1)}, bf16[128,1024]{1,0:T(8,128)(2,1)S(1)}, u32[]{:S(2)}, u32[]{:S(2)}) collective-permute-start(bf16[128,1024]{1,0:T(8,128)(2,1)S(1)} %get-tuple-element.32), channel_id=1, source_target_pairs={{128,0},{129,1},{130,2},{131,3},{132,4},{133,5},{134,6},{135,7},{1... | collective-permute-start | bytes 786440 | tf_op jit(solution)/shard_map/ppermute | solution.py:102
  11.6 13.3 %collective-permute-start.3 = (bf16[128,1024]{1,0:T(8,128)(2,1)S(1)}, bf16[128,1024]{1,0:T(8,128)(2,1)S(1)}, u32[]{:S(2)}, u32[]{:S(2)}) collective-permute-start(bf16[128,1024]{1,0:T(8,128)(2,1)S(1)} %collective-permute-done), channel_id=1, source_target_pairs={{0,32},{32,64},{64,96},{96,0},{1,33},{33,65},{65,97},{97,1},{2,34}... | collective-permute-start | bytes 786440 | tf_op jit(solution)/shard_map/ppermute | solution.py:106
  15.4 12.8 %collective-permute-start.2 = (bf16[128,1024]{1,0:T(8,128)(2,1)S(1)}, bf16[128,1024]{1,0:T(8,128)(2,1)S(1)}, u32[]{:S(2)}, u32[]{:S(2)}) collective-permute-start(bf16[128,1024]{1,0:T(8,128)(2,1)S(1)} %collective-permute-done), channel_id=1, source_target_pairs={{0,64},{32,96},{64,0},{96,32},{1,65},{33,97},{65,1},{97,33},{2,66}... | collective-permute-start | bytes 786440 | tf_op jit(solution)/shard_map/ppermute | solution.py:106
  20.6 10.3 %collective-permute-start.1 = (bf16[128,1024]{1,0:T(8,128)(2,1)S(1)}, bf16[128,1024]{1,0:T(8,128)(2,1)S(1)}, u32[]{:S(2)}, u32[]{:S(2)}) collective-permute-start(bf16[128,1024]{1,0:T(8,128)(2,1)S(1)} %collective-permute-done), channel_id=1, source_target_pairs={{0,96},{32,0},{64,32},{96,64},{1,97},{33,1},{65,33},{97,65},{2,98}... | collective-permute-start | bytes 786440 | tf_op jit(solution)/shard_map/ppermute | solution.py:106
  31.1 1.9 %copy-start.1 = (bf16[1,3,128,4096]{3,2,1,0:T(8,128)(2,1)S(1)}, bf16[1,3,128,4096]{3,2,1,0:T(8,128)(2,1)}, u32[]{:S(2)}) copy-start(bf16[1,3,128,4096]{3,2,1,0:T(8,128)(2,1)} %param.7) | copy-start | bytes 9437188
  36.4 26.7 %collective-permute-start.4 = (bf16[4096,128]{1,0:T(8,128)(2,1)S(1)}, bf16[4096,128]{1,0:T(8,128)(2,1)S(1)}, u32[]{:S(2)}, u32[]{:S(2)}) collective-permute-start(bf16[4096,128]{1,0:T(8,128)(2,1)S(1)} %get-tuple-element.11), channel_id=1, source_target_pairs={{0,3},{1,0},{2,1},{3,2},{4,7},{5,4},{6,5},{7,6},{8,11},{9,8},{10,9... | collective-permute-start | bytes 3145736 | tf_op jit(solution)/shard_map/ppermute | solution.py:87
  39.2 24.0 %collective-permute-start.5 = (bf16[4096,128]{1,0:T(8,128)(2,1)S(1)}, bf16[4096,128]{1,0:T(8,128)(2,1)S(1)}, u32[]{:S(2)}, u32[]{:S(2)}) collective-permute-start(bf16[4096,128]{1,0:T(8,128)(2,1)S(1)} %get-tuple-element.13), channel_id=1, source_target_pairs={{0,1},{1,2},{2,3},{3,0},{4,5},{5,6},{6,7},{7,4},{8,9},{9,10},{10,1... | collective-permute-start | bytes 3145736 | tf_op jit(solution)/shard_map/ppermute | solution.py:87
  39.2 21.6 %collective-permute-start.11 = (bf16[4096,128]{1,0:T(8,128)(2,1)S(1)}, bf16[4096,128]{1,0:T(8,128)(2,1)S(1)}, u32[]{:S(2)}, u32[]{:S(2)}) collective-permute-start(bf16[4096,128]{1,0:T(8,128)(2,1)S(1)} %get-tuple-element.15), channel_id=1, source_target_pairs={{0,12},{4,0},{8,4},{12,8},{1,13},{5,1},{9,5},{13,9},{2,14},{6,2},{... | collective-permute-start | bytes 3145736 | tf_op jit(solution)/shard_map/ppermute | solution.py:87
  39.9 20.9 %collective-permute-start.12 = (bf16[4096,128]{1,0:T(8,128)(2,1)S(1)}, bf16[4096,128]{1,0:T(8,128)(2,1)S(1)}, u32[]{:S(2)}, u32[]{:S(2)}) collective-permute-start(bf16[4096,128]{1,0:T(8,128)(2,1)S(1)} %get-tuple-element.17), channel_id=1, source_target_pairs={{0,4},{4,8},{8,12},{12,0},{1,5},{5,9},{9,13},{13,1},{2,6},{6,10},{... | collective-permute-start | bytes 3145736 | tf_op jit(solution)/shard_map/ppermute | solution.py:87
  61.0 13.9 %collective-permute-start.13 = (bf16[2048,128]{1,0:T(8,128)(2,1)S(1)}, bf16[2048,128]{1,0:T(8,128)(2,1)S(1)}, u32[]{:S(2)}, u32[]{:S(2)}) collective-permute-start(bf16[2048,128]{1,0:T(8,128)(2,1)S(1)} %get-tuple-element.30), channel_id=1, source_target_pairs={{0,4},{4,8},{8,12},{12,0},{1,5},{5,9},{9,13},{13,1},{2,6},{6,10},{... | collective-permute-start | bytes 1572872 | tf_op jit(solution)/shard_map/ppermute | solution.py:87
  62.2 21.5 %collective-permute-start.14 = (bf16[2048,128]{1,0:T(8,128)(2,1)S(1)}, bf16[2048,128]{1,0:T(8,128)(2,1)S(1)}, u32[]{:S(2)}, u32[]{:S(2)}) collective-permute-start(bf16[2048,128]{1,0:T(8,128)(2,1)S(1)} %get-tuple-element.31), channel_id=1, source_target_pairs={{0,12},{4,0},{8,4},{12,8},{1,13},{5,1},{9,5},{13,9},{2,14},{6,2},{... | collective-permute-start | bytes 1572872 | tf_op jit(solution)/shard_map/ppermute | solution.py:87
  63.3 25.9 %collective-permute-start.6 = (bf16[2048,128]{1,0:T(8,128)(2,1)S(1)}, bf16[2048,128]{1,0:T(8,128)(2,1)S(1)}, u32[]{:S(2)}, u32[]{:S(2)}) collective-permute-start(bf16[2048,128]{1,0:T(8,128)(2,1)S(1)} %get-tuple-element.23), channel_id=1, source_target_pairs={{0,1},{1,2},{2,3},{3,0},{4,5},{5,6},{6,7},{7,4},{8,9},{9,10},{10,1... | collective-permute-start | bytes 1572872 | tf_op jit(solution)/shard_map/ppermute | solution.py:87
  64.2 25.0 %collective-permute-start.7 = (bf16[2048,128]{1,0:T(8,128)(2,1)S(1)}, bf16[2048,128]{1,0:T(8,128)(2,1)S(1)}, u32[]{:S(2)}, u32[]{:S(2)}) collective-permute-start(bf16[2048,128]{1,0:T(8,128)(2,1)S(1)} %get-tuple-element.24), channel_id=1, source_target_pairs={{0,3},{1,0},{2,1},{3,2},{4,7},{5,4},{6,5},{7,6},{8,11},{9,8},{10,9... | collective-permute-start | bytes 1572872 | tf_op jit(solution)/shard_map/ppermute | solution.py:87
  85.1 16.0 %collective-permute-start.15 = (f32[2,512,128]{2,1,0:T(8,128)S(1)}, f32[2,512,128]{2,1,0:T(8,128)S(1)}, u32[]{:S(2)}, u32[]{:S(2)}) collective-permute-start(f32[2,512,128]{2,1,0:T(8,128)S(1)} %get-tuple-element.25), channel_id=1, source_target_pairs={{0,1},{1,2},{2,3},{3,0},{4,5},{5,6},{6,7},{7,4},{8,9},{9,10},{10,1... | collective-permute-start | bytes 1572872 | tf_op jit(solution)/shard_map/ppermute | solution.py:87
  85.4 19.9 %collective-permute-start.17 = (f32[2,512,128]{2,1,0:T(8,128)}, f32[2,512,128]{2,1,0:T(8,128)}, u32[]{:S(2)}, u32[]{:S(2)}) collective-permute-start(f32[2,512,128]{2,1,0:T(8,128)} %get-tuple-element.26), channel_id=1, source_target_pairs={{0,3},{1,0},{2,1},{3,2},{4,7},{5,4},{6,5},{7,6},{8,11},{9,8},{10,9... | collective-permute-start | bytes 1572872 | tf_op jit(solution)/shard_map/ppermute | solution.py:87
  88.3 16.9 %collective-permute-start.16 = (f32[2,512,128]{2,1,0:T(8,128)}, f32[2,512,128]{2,1,0:T(8,128)}, u32[]{:S(2)}, u32[]{:S(2)}) collective-permute-start(f32[2,512,128]{2,1,0:T(8,128)} %get-tuple-element.27), channel_id=1, source_target_pairs={{0,2},{1,3},{2,0},{3,1},{4,6},{5,7},{6,4},{7,5},{8,10},{9,11},{10,... | collective-permute-start | bytes 1572872 | tf_op jit(solution)/shard_map/ppermute | solution.py:87
  89.5 11.6 %copy-start.3 = (f32[2048,128]{1,0:T(8,128)}, f32[2048,128]{1,0:T(8,128)S(1)}, u32[]{:S(2)}) copy-start(f32[2048,128]{1,0:T(8,128)S(1)} %get-tuple-element.22) | copy-start | bytes 3145732
  90.7 16.1 %collective-permute-start.8 = (f32[2,512,128]{2,1,0:T(8,128)}, f32[2,512,128]{2,1,0:T(8,128)}, u32[]{:S(2)}, u32[]{:S(2)}) collective-permute-start(f32[2,512,128]{2,1,0:T(8,128)} %get-tuple-element.18), channel_id=1, source_target_pairs={{0,4},{4,8},{8,12},{12,0},{1,5},{5,9},{9,13},{13,1},{2,6},{6,10},{... | collective-permute-start | bytes 1572872 | tf_op jit(solution)/shard_map/ppermute | solution.py:87
  90.7 16.1 %collective-permute-start.10 = (f32[2,512,128]{2,1,0:T(8,128)}, f32[2,512,128]{2,1,0:T(8,128)}, u32[]{:S(2)}, u32[]{:S(2)}) collective-permute-start(f32[2,512,128]{2,1,0:T(8,128)} %get-tuple-element.19), channel_id=1, source_target_pairs={{0,12},{4,0},{8,4},{12,8},{1,13},{5,1},{9,5},{13,9},{2,14},{6,2},{... | collective-permute-start | bytes 1572872 | tf_op jit(solution)/shard_map/ppermute | solution.py:87
  101.1 0.8 copy-start.7
  101.1 11.0 %collective-permute-start.9 = (f32[2,512,128]{2,1,0:T(8,128)}, f32[2,512,128]{2,1,0:T(8,128)}, u32[]{:S(2)}, u32[]{:S(2)}) collective-permute-start(f32[2,512,128]{2,1,0:T(8,128)} %get-tuple-element.20), channel_id=1, source_target_pairs={{0,8},{4,12},{8,0},{12,4},{1,9},{5,13},{9,1},{13,5},{2,10},{6,14},... | collective-permute-start | bytes 1572872 | tf_op jit(solution)/shard_map/ppermute | solution.py:87
  105.2 6.8 %copy-start.4 = (f32[2048,128]{1,0:T(8,128)S(1)}, f32[2048,128]{1,0:T(8,128)}, u32[]{:S(2)}) copy-start(f32[2048,128]{1,0:T(8,128)} %copy-done.3) | copy-start | bytes 3145732
  106.8 13.9 %copy-start.5 = (bf16[128,4,1024]{0,2,1:T(8,128)(2,1)S(1)}, bf16[128,4,1024]{0,2,1:T(8,128)(2,1)}, u32[]{:S(2)}) copy-start(bf16[128,4,1024]{0,2,1:T(8,128)(2,1)} %copy.11) | copy-start | bytes 3145732
  106.8 13.9 %copy-start.6 = (f32[128,1024]{1,0:T(8,128)S(1)}, f32[128,1024]{1,0:T(8,128)}, u32[]{:S(2)}) copy-start(f32[128,1024]{1,0:T(8,128)} %get-tuple-element.33) | copy-start | bytes 1572868
  113.6 18.6 %collective-permute-start.18 = (f32[1024,128]{1,0:T(8,128)S(1)}, f32[1024,128]{1,0:T(8,128)S(1)}, u32[]{:S(2)}, u32[]{:S(2)}) collective-permute-start(f32[1024,128]{1,0:T(8,128)S(1)} %fusion.32), channel_id=1, source_target_pairs={{0,16},{16,0},{1,17},{17,1},{2,18},{18,2},{3,19},{19,3},{4,20},{20... | collective-permute-start | bytes 1572872 | tf_op jit(solution)/shard_map/ppermute | solution.py:141

commit v2 on v1

v2 whole, which is shorter than its diff:
```python
import functools
import math

import jax
import jax.numpy as jnp
from jax import lax
from jax.experimental import pallas as pl
from jax.experimental.pallas import tpu as pltpu
from jax.sharding import Mesh
from jax.sharding import PartitionSpec as P

F32 = jnp.float32
F16 = jnp.float16
BF16 = jnp.bfloat16
RING = 4
LANES = 128
TAIL = 16
TOP = 15
TINY = 1e-30

SEND_RIGHT = [(0, 2, j) for j in range(RING)] + [(1, 1, j) for j in range(RING)]
SEND_LEFT = [(1, 2, j) for j in range(RING)] + [(0, 3, j) for j in range(RING)]
PASS_RIGHT = [(0, 1, j) for j in range(RING)]
PASS_LEFT = [(1, 3, j) for j in range(RING)]
KEEP_NEAR = [(0, 0, j) for j in range(RING)]
KEEP_FAR = [(1, 0, j) for j in range(RING)]
FIRST = [(part, s) for part in (0, 1) for s in (SEND_RIGHT, SEND_LEFT)]
OWN = [(part, s) for part in (0, 1) for s in (PASS_RIGHT, PASS_LEFT, KEEP_NEAR, KEEP_FAR)]


def on_last():
    return lax.axis_index("section") == lax.axis_size("section") - 1


def block_index(zr, yr, xr):
    z = lax.rem(lax.axis_index("z_hi") + zr, 2)
    y = lax.rem(lax.axis_index("y") + yr, RING)
    x = lax.rem(lax.axis_index("x") + xr, RING)
    return z * (RING * RING) + y * RING + x


def largest(value):
    return jnp.max(jnp.max(jnp.abs(value.astype(F32)), axis=0, keepdims=True), axis=1, keepdims=True)


def products_kernel(plans, scaled, pending_ref, x_ref, stash_ref, head_ref, rel_ref, *rest):
    outs, xt_ref = rest[:-1], rest[-1]
    micro, rows, width = x_ref.shape
    half = width // 2
    tensor, is_last = lax.axis_index("z_lo"), on_last()
    count = pending_ref[lax.axis_index("section")]
    bound = jnp.full((1, 1), TINY, F32)
    for m in range(micro):
        masked = jnp.where(m >= micro - count, x_ref[m].astype(F32), 0.0)
        xt_ref[:, m * rows:(m + 1) * rows] = masked.T.astype(BF16)
        if scaled:
            if m < micro - 1:
                top = largest(stash_ref[m])
            else:
                chained = functools.reduce(jnp.maximum, [largest(rel_ref[k]) for k in range(RING)])
                top = jnp.where(is_last, largest(head_ref[...]), chained)
            bound = bound + rows * largest(masked) * top
    if scaled:
        power = jnp.broadcast_to(jnp.ceil(jnp.log2(bound)) - TOP, (1, LANES))
        factor = jnp.exp2(-power)
    shard_blocks = rel_ref.shape[2] // LANES

    def columns(block):
        at = pl.multiple_of(block * LANES, LANES)
        parts = [stash_ref[m, :, pl.ds(at, LANES)] for m in range(micro - 1)]
        owner = lax.div(block, shard_blocks)
        turn = lax.rem(tensor - owner + RING, RING)
        inner = pl.multiple_of(lax.rem(block, shard_blocks) * LANES, LANES)
        chained = rel_ref[turn, :, pl.ds(inner, LANES)]
        given = head_ref[:, pl.ds(at, LANES)]
        parts.append(jnp.where(is_last, given, chained))
        return jnp.concatenate(parts, axis=0)

    for out, (part, slots) in zip(outs, plans):
        xt = xt_ref[part * half:(part + 1) * half, :]
        for j in range(0, len(slots), 2):
            pair = []
            for zr, along, across in slots[j:j + 2]:
                yr, xr = (across, along) if part == 0 else (along, across)
                pair.append(columns(block_index(zr, yr, xr)))
            both = jnp.dot(xt, jnp.concatenate(pair, axis=1), preferred_element_type=F32)
            for k in range(2):
                tile = both[:, k * LANES:(k + 1) * LANES]
                if scaled:
                    tile = tile * factor
                out[(j + k) * half:(j + k + 1) * half, :] = tile
        if scaled:
            out[len(slots) * half:, :] = jnp.broadcast_to(power, (TAIL, LANES))


def products(plans, scaled, pending, inputs, stash_grad, head_grad, rel):
    micro, rows, width = inputs.shape
    half = width // 2
    whole = pl.BlockSpec(memory_space=pltpu.VMEM)
    extra = TAIL if scaled else 0
    shapes = [jax.ShapeDtypeStruct((len(slots) * half + extra, LANES), F32) for _, slots in plans]
    n_slots = sum(len(slots) for _, slots in plans)
    return pl.pallas_call(
        functools.partial(products_kernel, plans, scaled),
        out_shape=shapes,
        in_specs=[pl.BlockSpec(memory_space=pltpu.SMEM)] + [whole] * 4,
        out_specs=[whole] * len(shapes),
        scratch_shapes=[pltpu.VMEM((width, micro * rows), BF16)],
        compiler_params=pltpu.CompilerParams(vmem_limit_bytes=40 * 2**20),
        cost_estimate=pl.CostEstimate(
            flops=2 * n_slots * half * LANES * micro * rows,
            bytes_accessed=6 * 2**20 + n_slots * half * LANES * 4,
            transcendentals=0,
        ),
    )(pending, inputs, stash_grad, head_grad, rel)


CONTRACT_LAST = (((1,), (1,)), ((), ()))


def first_kernel(grad_ref, weight_ref, out_ref, small_ref):
    out = lax.dot_general(grad_ref[...], weight_ref[...], CONTRACT_LAST, preferred_element_type=F32)
    out_ref[...] = out
    small_ref[...] = out.astype(BF16)


def second_kernel(rel_ref, weight_ref, first_ref, out_ref):
    tensor = lax.axis_index("z_lo")
    share = rel_ref.shape[2]
    total = jnp.zeros(out_ref.shape, F32)
    for k in range(RING):
        owner = lax.rem(tensor - k + RING, RING)
        cols = weight_ref[:, pl.ds(pl.multiple_of(owner * share, share), share)]
        total = total + lax.dot_general(rel_ref[k], cols, CONTRACT_LAST, preferred_element_type=F32)
    out_ref[...] = jnp.where(on_last(), first_ref[...], total)


def chain_call(kernel, out_types, grad, weight, *more, step=256):
    rows = grad.shape[-2]
    width, depth = weight.shape
    tile = pl.BlockSpec((rows, step), lambda i: (0, i))
    outs = [jax.ShapeDtypeStruct((rows, width), t) for t in out_types]
    return pl.pallas_call(
        kernel,
        grid=(width // step,),
        out_shape=outs,
        in_specs=[pl.BlockSpec(memory_space=pltpu.VMEM), pl.BlockSpec((step, depth), lambda i: (i, 0))] + [tile] * len(more),
        out_specs=[tile] * len(outs),
        compiler_params=pltpu.CompilerParams(vmem_limit_bytes=24 * 2**20),
        cost_estimate=pl.CostEstimate(flops=2 * rows * width * depth, bytes_accessed=2 * width * depth + 2**21, transcendentals=0),
    )(grad, weight, *more)


def shifted(value, axis, by):
    return lax.ppermute(value, axis, [(i, (i + by) % RING) for i in range(RING)])


def packed(parts, powers):
    power = functools.reduce(jnp.maximum, powers) + math.ceil(math.log2(len(powers)))
    factor = jnp.exp2(-power)
    rows = [(p * factor).astype(F16) for p in parts]
    return jnp.concatenate(rows + [jnp.broadcast_to(power, (TAIL, LANES)).astype(F16)], 0)


def opened(buffer):
    power = buffer[-1:].astype(F32)
    return buffer[:-TAIL].astype(F32) * jnp.exp2(power), power


def ring(axes, sends, pass_on, keeps, powers):
    got = [(opened(shifted(r, a, 1)), opened(shifted(l, a, -1))) for a, (r, l) in zip(axes, sends)]
    late = []
    for a, ((left, p_left), (right, p_right)), (to_right, to_left), power in zip(axes, got, pass_on, powers):
        mid = left.shape[0] // 2
        go_right = packed([to_right + left[:mid]], power + [p_left])
        go_left = packed([to_left + right[:mid]], power + [p_right])
        late.append((opened(shifted(go_right, a, 1)), opened(shifted(go_left, a, -1))))
    sums, all_powers = [], []
    for near_far, one, two, power in zip(keeps, got, late, powers):
        (left, p_left), (right, p_right) = one
        (left_2, p_left_2), (right_2, p_right_2) = two
        mid = left.shape[0] // 2
        sums.append((near_far[0] + right[mid:] + left_2, near_far[1] + left[mid:] + right_2))
        all_powers.append(power + [p_left, p_right, p_left_2, p_right_2])
    return sums, all_powers


def local(weights, stash_in, stash_grad, head_grad, pending):
    weight = weights[0]
    inputs, grads = stash_in[0], stash_grad[0]

    first, small = chain_call(first_kernel, (F32, BF16), head_grad, weight)
    rel = []
    for by in range(RING):
        pairs = [(RING + i, (i + by) % RING) for i in range(RING)]
        rel.append(lax.ppermute(small, ("section", "z_lo"), pairs))
    rel = jnp.stack(rel, 0)

    args = (pending, inputs, grads, head_grad, rel)
    first_out = products(FIRST, True, *args)
    sends = [[b.astype(F16) for b in first_out[2 * p:2 * p + 2]] for p in (0, 1)]
    power = first_out[0][-1:]
    own = products(OWN, False, *args)
    (second,) = chain_call(second_kernel, (F32,), rel, weight, first)
    own, second = lax.optimization_barrier((own, second))
    powers = [[power], [power]]
    sums, powers = ring(("x", "y"), sends, [own[0:2], own[4:6]], [own[2:4], own[6:8]], powers)

    size = sums[0][0].shape[0] // RING
    cut = [[[v[j * size:(j + 1) * size] for j in range(RING)] for v in pair] for pair in sums]
    sends = [
        (packed([near[2], far[1]], p), packed([far[2], near[3]], p)) for (near, far), p in zip(cut, powers)
    ]
    powers = [[functools.reduce(jnp.maximum, p) + 3] for p in powers]
    pass_on = [(near[1], far[3]) for near, far in cut]
    keeps = [(near[0], far[0]) for near, far in cut]
    sums, powers = ring(("y", "x"), sends, pass_on, keeps, powers)

    far = packed([pair[1] for pair in sums], [functools.reduce(jnp.maximum, p) + 3 for p in powers])
    near = jnp.concatenate([pair[0] for pair in sums], 0)
    other, _ = opened(lax.ppermute(far, "z_hi", [(0, 1), (1, 0)]))
    return (second[None], (near + other)[None])


def solution(mesh):
    fine = Mesh(mesh.devices.reshape(2, 4, 2, 4, 4), ("section", "z_lo", "z_hi", "y", "x"))
    dp = ("z_hi", "y", "x")
    return jax.shard_map(
        local,
        mesh=fine,
        in_specs=(
            P("section", "z_lo", None),
            P("section", None, dp, "z_lo"),
            P("section", None, dp, None),
            P(dp, None),
            P(),
        ),
        out_specs=(P("section", dp, "z_lo"), P("section", "z_lo", dp)),
        check_vma=False,
    )
```

time: 134 us -> 136 us (1.015)
  the two profiles are of different devices: /device:TPU:24 before, /device:TPU:192 now
where the time goes in v2:
time: 136 us; the launch traced here: 135 us
  waiting for transfers between devices  79.3 us (58%)
  starting transfers between devices  20.4 us (15%)
  Pallas kernels  18 us (13%)
  other arithmetic  11.8 us (9%)
  local copies, waits for them, and re-layouts  4.71 us (3%)
    ppermute x16, waiting for transfers between devices, shifted(): lax.ppermute(value, axis, [(i, (i + by) % RING) for i in range(RING)])  58.6 us
    ppermute x16, starting transfers between devices, shifted(): lax.ppermute(value, axis, [(i, (i + by) % RING) for i in range(RING)])  15.1 us
    pallas_call x2, Pallas kernels, products(): pl.pallas_call(functools.partial(products_kernel, plans, scaled), out_sha...  10.5 us
    ppermute x4, waiting for transfers between devices, local(): rel.append(lax.ppermute(small, ('section', 'z_lo'), pairs))  10.3 us
    ppermute x1, waiting for transfers between devices, local(): other, _ = opened(lax.ppermute(far, 'z_hi', [(0, 1), (1, 0)]))  10.3 us
    pallas_call x2, Pallas kernels, chain_call(): pl.pallas_call(kernel, grid=(width // step,), out_shape=outs, in_specs=[p...  7.5 us
    ppermute x4, starting transfers between devices, local(): rel.append(lax.ppermute(small, ('section', 'z_lo'), pairs))  5.3 us
    mul x12, other arithmetic, opened(): return (buffer[:-TAIL].astype(F32) * jnp.exp2(power), power)  4.74 us
  transfers between devices with their start and end apart: 21, of which 19 were waited for; matrix products, arithmetic and copies ran while one was open for 6% of the time, Pallas kernels for 7%

profile of v2, /device:TPU:192, one launch (start us, length us, event | category | flops | bytes accessed | tf_op | source)
XLA Modules:
  0.0 135.4 jit_solution(15699248816844627383)
XLA Ops:
  0.6 3.4 %copy-done = bf16[1,1024,4096]{2,1,0:T(8,128)(2,1)S(1)} copy-done((bf16[1,1024,4096]{2,1,0:T(8,128)(2,1)S(1)}, bf16[1,1024,4096]{2,1,0:T(8,128)(2,1)}, u32[]{:S(2)}) %copy-start) | copy-done | bytes 8388632
  4.0 1.2 copy-done.1
  5.2 3.4 %shard_map.68 = (f32[128,1024]{1,0:T(8,128)S(1)}, bf16[128,1024]{1,0:T(8,128)(2,1)S(1)}) custom-call(bf16[128,4096]{1,0:T(8,128)(2,1)S(1)} %copy-done.1, bf16[1024,4096]{1,0:T(8,128)(2,1)S(1)} %bitcast.88), custom_call_target="tpu_custom_call" | custom-call | flops 1073741824 | bytes 10485760 | tf_op jit(solution)/shard_map/pallas_call | solution.py:143
  8.7 1.4 %collective-permute-start = (bf16[128,1024]{1,0:T(8,128)(2,1)S(1)}, bf16[128,1024]{1,0:T(8,128)(2,1)S(1)}, u32[]{:S(2)}, u32[]{:S(2)}) collective-permute-start(bf16[128,1024]{1,0:T(8,128)(2,1)S(1)} %get-tuple-element.25), channel_id=1, source_target_pairs={{128,0},{160,32},{192,64},{224,96},{129,1},{161,33},{193,65},{225,... | collective-permute-start | bytes 786440 | tf_op jit(solution)/shard_map/ppermute | solution.py:196
  10.1 1.3 collective-permute-start.1
  11.4 1.3 collective-permute-start.2
  12.7 1.3 collective-permute-start.3
  14.0 3.8 %collective-permute-done.1 = bf16[128,1024]{1,0:T(8,128)(2,1)S(1)} collective-permute-done((bf16[128,1024]{1,0:T(8,128)(2,1)S(1)}, bf16[128,1024]{1,0:T(8,128)(2,1)S(1)}, u32[]{:S(2)}, u32[]{:S(2)}) %collective-permute-start.1) | collective-permute-done | bytes 262176 | tf_op jit(solution)/shard_map/ppermute | solution.py:196
  17.8 3.4 %collective-permute-done.2 = bf16[128,1024]{1,0:T(8,128)(2,1)S(1)} collective-permute-done((bf16[128,1024]{1,0:T(8,128)(2,1)S(1)}, bf16[128,1024]{1,0:T(8,128)(2,1)S(1)}, u32[]{:S(2)}, u32[]{:S(2)}) %collective-permute-start.2) | collective-permute-done | bytes 262176 | tf_op jit(solution)/shard_map/ppermute | solution.py:196
  21.1 3.2 %collective-permute-done.3 = bf16[128,1024]{1,0:T(8,128)(2,1)S(1)} collective-permute-done((bf16[128,1024]{1,0:T(8,128)(2,1)S(1)}, bf16[128,1024]{1,0:T(8,128)(2,1)S(1)}, u32[]{:S(2)}, u32[]{:S(2)}) %collective-permute-start.3) | collective-permute-done | bytes 262176 | tf_op jit(solution)/shard_map/ppermute | solution.py:196
  24.5 5.8 %shard_map.71 = (f32[4112,128]{1,0:T(8,128)S(1)}, f32[4112,128]{1,0:T(8,128)S(1)}, f32[4112,128]{1,0:T(8,128)S(1)}, f32[4112,128]{1,0:T(8,128)S(1)}) custom-call(s32[2]{0:T(128)S(1)} %copy-done.4, bf16[4,128,1024]{2,1,0:T(8,128)(2,1)S(1)} %bitcast.92, bf16[3,128,4096]{2,1,0:T(8,128)(2,1)} %bitcast.99, bf16[128,4096]{1,0:T(8,128)(2,1)S(1)} %copy-done.2, ...), custom_call_target="tpu_custom_call" | custom-call | flops 2147483648 | bytes 14680064 | tf_op jit(solution)/shard_map/pallas_call | solution.py:103
  30.5 3.1 %collective-permute-start.11 = (f16[4112,128]{1,0:T(8,128)(2,1)S(1)}, f16[4112,128]{1,0:T(8,128)(2,1)}, u32[]{:S(2)}, u32[]{:S(2)}) collective-permute-start(f16[4112,128]{1,0:T(8,128)(2,1)S(1)} %convert_element_type.278), channel_id=1, source_target_pairs={{0,12},{4,0},{8,4},{12,8},{1,13},{5,1},{9,5},{13,9},{2,14},{6,2},{... | collective-permute-start | bytes 3158024 | tf_op jit(solution)/shard_map/ppermute | solution.py:155
  33.7 2.8 %collective-permute-start.4 = (f16[4112,128]{1,0:T(8,128)(2,1)S(1)}, f16[4112,128]{1,0:T(8,128)(2,1)}, u32[]{:S(2)}, u32[]{:S(2)}) collective-permute-start(f16[4112,128]{1,0:T(8,128)(2,1)S(1)} %convert_element_type.247), channel_id=1, source_target_pairs={{0,3},{1,0},{2,1},{3,2},{4,7},{5,4},{6,5},{7,6},{8,11},{9,8},{10,9... | collective-permute-start | bytes 3158024 | tf_op jit(solution)/shard_map/ppermute | solution.py:155
  37.0 4.1 %shard_map.70 = f32[128,1024]{1,0:T(8,128)} custom-call(bf16[4,128,1024]{2,1,0:T(8,128)(2,1)S(1)} %pad_maximum_fusion.rel_ref, bf16[1024,4096]{1,0:T(8,128)(2,1)S(1)} %bitcast.91, f32[128,1024]{1,0:T(8,128)S(1)} %get-tuple-element.34.first_ref), custom_call_target="tpu_custom_call" | custom-call | flops 1073741824 | bytes 10485760 | tf_op jit(solution)/shard_map/pallas_call | solution.py:143
  41.1 4.7 %shard_map.69 = (f32[2048,128]{1,0:T(8,128)S(1)}, f32[2048,128]{1,0:T(8,128)S(1)}, f32[2048,128]{1,0:T(8,128)S(1)}, f32[2048,128]{1,0:T(8,128)S(1)}, f32[2048,12...) custom-call(s32[2]{0:T(128)S(1)} %copy-done.4, ...), custom_call_target="tpu_custom_call" | custom-call | flops 2147483648 | bytes 14680064 | tf_op jit(solution)/shard_map/pallas_call | solution.py:103
  45.8 10.5 %collective-permute-done.11 = f16[4112,128]{1,0:T(8,128)(2,1)} collective-permute-done((f16[4112,128]{1,0:T(8,128)(2,1)S(1)}, f16[4112,128]{1,0:T(8,128)(2,1)}, u32[]{:S(2)}, u32[]{:S(2)}) %collective-permute-start.11) | collective-permute-done | bytes 1052704 | tf_op jit(solution)/shard_map/ppermute | solution.py:155
  56.3 3.3 %collective-permute-done.4 = f16[4112,128]{1,0:T(8,128)(2,1)} collective-permute-done((f16[4112,128]{1,0:T(8,128)(2,1)S(1)}, f16[4112,128]{1,0:T(8,128)(2,1)}, u32[]{:S(2)}, u32[]{:S(2)}) %collective-permute-start.4) | collective-permute-done | bytes 1052704 | tf_op jit(solution)/shard_map/ppermute | solution.py:155
  59.6 4.2 %collective-permute-done.5 = f16[4112,128]{1,0:T(8,128)(2,1)} collective-permute-done((f16[4112,128]{1,0:T(8,128)(2,1)S(1)}, f16[4112,128]{1,0:T(8,128)(2,1)}, u32[]{:S(2)}, u32[]{:S(2)}) %collective-permute-start.5) | collective-permute-done | bytes 1052704 | tf_op jit(solution)/shard_map/ppermute | solution.py:155
  63.8 0.2 collective-permute-done.12
  64.1 0.7 exponential_bitcast_fusion.24
  64.8 1.8 %convert_multiply_fusion.1 = (f32[4096,128]{1,0:T(8,128)S(1)}, f32[4096,128]{1,0:T(8,128)S(1)}) fusion(f16[4112,128]{1,0:T(8,128)(2,1)} %collective-permute-done.11, f32[128]{0:T(128)S(1)} %get-tuple-element.72, f32[128]{0:T(128)S(1)} %get-tuple-element.74, f16[4112,128]{1,0:T(8,128)(2,1)} %collective-permute-done.4), kind=kLoop, calls=%fused_computation.1 | loop fusion | flops 2097152 | bytes 6292480 | tf_op jit(solution)/shard_map/mul | solution.py:167
  66.9 3.8 %collective-permute-start.7 = (f16[2064,128]{1,0:T(8,128)(2,1)S(1)}, f16[2064,128]{1,0:T(8,128)(2,1)S(1)}, u32[]{:S(2)}, u32[]{:S(2)}) collective-permute-start(f16[2064,128]{1,0:T(8,128)(2,1)S(1)} %pad_maximum_fusion.2), channel_id=1, source_target_pairs={{0,3},{1,0},{2,1},{3,2},{4,7},{5,4},{6,5},{7,6},{8,11},{9,8},{10,9... | collective-permute-start | bytes 1585160 | tf_op jit(solution)/shard_map/ppermute | solution.py:155
  71.1 1.4 %convert_multiply_fusion.2 = f32[4096,128]{1,0:T(8,128)S(1)} fusion(f16[4112,128]{1,0:T(8,128)(2,1)} %collective-permute-done.5, f32[128]{0:T(128)S(1)} %get-tuple-element.75), kind=kLoop, calls=%fused_computation.2 | loop fusion | flops 1048576 | bytes 3146240 | tf_op jit(solution)/shard_map/mul | solution.py:167
  72.5 1.4 %convert_multiply_fusion = f32[4096,128]{1,0:T(8,128)S(1)} fusion(f16[4112,128]{1,0:T(8,128)(2,1)} %collective-permute-done.12, f32[128]{0:T(128)S(1)} %get-tuple-element.73), kind=kLoop, calls=%fused_computation | loop fusion | flops 1048576 | bytes 3146240 | tf_op jit(solution)/shard_map/mul | solution.py:167
  73.8 8.4 %collective-permute-done.7 = f16[2064,128]{1,0:T(8,128)(2,1)S(1)} collective-permute-done((f16[2064,128]{1,0:T(8,128)(2,1)S(1)}, f16[2064,128]{1,0:T(8,128)(2,1)S(1)}, u32[]{:S(2)}, u32[]{:S(2)}) %collective-permute-start.7) | collective-permute-done | bytes 528416 | tf_op jit(solution)/shard_map/ppermute | solution.py:155
  82.2 0.4 fusion.8
  82.9 1.9 %collective-permute-done.14 = f16[2064,128]{1,0:T(8,128)(2,1)S(1)} collective-permute-done((f16[2064,128]{1,0:T(8,128)(2,1)S(1)}, f16[2064,128]{1,0:T(8,128)(2,1)S(1)}, u32[]{:S(2)}, u32[]{:S(2)}) %collective-permute-start.14) | collective-permute-done | bytes 528416 | tf_op jit(solution)/shard_map/ppermute | solution.py:155
  84.8 0.4 fusion.2
  85.5 12.6 %collective-permute-done.6 = f16[2064,128]{1,0:T(8,128)(2,1)S(1)} collective-permute-done((f16[2064,128]{1,0:T(8,128)(2,1)S(1)}, f16[2064,128]{1,0:T(8,128)(2,1)S(1)}, u32[]{:S(2)}, u32[]{:S(2)}) %collective-permute-start.6) | collective-permute-done | bytes 528416 | tf_op jit(solution)/shard_map/ppermute | solution.py:155
  98.0 0.7 exponential_bitcast_fusion.20
  98.7 0.2 fusion.11
  99.1 0.2 pad_maximum_fusion.5
  99.3 2.0 %collective-permute-start.9 = (f16[1040,128]{1,0:T(8,128)(2,1)S(1)}, f16[1040,128]{1,0:T(8,128)(2,1)S(1)}, u32[]{:S(2)}, u32[]{:S(2)}) collective-permute-start(f16[1040,128]{1,0:T(8,128)(2,1)S(1)} %get-tuple-element.104), channel_id=1, source_target_pairs={{0,4},{4,8},{8,12},{12,0},{1,5},{5,9},{9,13},{13,1},{2,6},{6,10},{... | collective-permute-start | bytes 798728 | tf_op jit(solution)/shard_map/ppermute | solution.py:155
  101.4 0.7 exponential_bitcast_fusion.9
  102.1 0.3 fusion.5
  102.6 1.8 %collective-permute-start.15 = (f16[1040,128]{1,0:T(8,128)(2,1)S(1)}, f16[1040,128]{1,0:T(8,128)(2,1)S(1)}, u32[]{:S(2)}, u32[]{:S(2)}) collective-permute-start(f16[1040,128]{1,0:T(8,128)(2,1)S(1)} %get-tuple-element.107), channel_id=1, source_target_pairs={{0,3},{1,0},{2,1},{3,2},{4,7},{5,4},{6,5},{7,6},{8,11},{9,8},{10,9... | collective-permute-start | bytes 798728 | tf_op jit(solution)/shard_map/ppermute | solution.py:155
  104.5 0.3 collective-permute-start.16
  104.7 1.5 %collective-permute-done.8 = f16[1040,128]{1,0:T(8,128)(2,1)S(1)} collective-permute-done((f16[1040,128]{1,0:T(8,128)(2,1)S(1)}, f16[1040,128]{1,0:T(8,128)(2,1)S(1)}, u32[]{:S(2)}, u32[]{:S(2)}) %collective-permute-start.8) | collective-permute-done | bytes 266272 | tf_op jit(solution)/shard_map/ppermute | solution.py:155
  106.3 1.3 collective-permute-done.9
  107.8 0.5 collective-permute-start.10
  108.3 0.9 collective-permute-done.15
  109.1 3.0 %collective-permute-done.16 = f16[1040,128]{1,0:T(8,128)(2,1)S(1)} collective-permute-done((f16[1040,128]{1,0:T(8,128)(2,1)S(1)}, f16[1040,128]{1,0:T(8,128)(2,1)S(1)}, u32[]{:S(2)}, u32[]{:S(2)}) %collective-permute-start.16) | collective-permute-done | bytes 266272 | tf_op jit(solution)/shard_map/ppermute | solution.py:155
  112.4 1.6 %collective-permute-done.10 = f16[528,128]{1,0:T(8,128)(2,1)S(1)} collective-permute-done((f16[528,128]{1,0:T(8,128)(2,1)S(1)}, f16[528,128]{1,0:T(8,128)(2,1)S(1)}, u32[]{:S(2)}, u32[]{:S(2)}) %collective-permute-start.10) | collective-permute-done | bytes 135200 | tf_op jit(solution)/shard_map/ppermute | solution.py:155
  114.3 4.3 %collective-permute-done.17 = f16[528,128]{1,0:T(8,128)(2,1)S(1)} collective-permute-done((f16[528,128]{1,0:T(8,128)(2,1)S(1)}, f16[528,128]{1,0:T(8,128)(2,1)S(1)}, u32[]{:S(2)}, u32[]{:S(2)}) %collective-permute-start.17) | collective-permute-done | bytes 135200 | tf_op jit(solution)/shard_map/ppermute | solution.py:155
  118.8 0.5 collective-permute-done.18
  119.3 4.5 %collective-permute-done.19 = f16[528,128]{1,0:T(8,128)(2,1)S(1)} collective-permute-done((f16[528,128]{1,0:T(8,128)(2,1)S(1)}, f16[528,128]{1,0:T(8,128)(2,1)S(1)}, u32[]{:S(2)}, u32[]{:S(2)}) %collective-permute-start.19) | collective-permute-done | bytes 135200 | tf_op jit(solution)/shard_map/ppermute | solution.py:155
  124.2 10.3 %collective-permute-done.20 = f16[1040,128]{1,0:T(8,128)(2,1)S(1)} collective-permute-done((f16[1040,128]{1,0:T(8,128)(2,1)S(1)}, f16[1040,128]{1,0:T(8,128)(2,1)S(1)}, u32[]{:S(2)}, u32[]{:S(2)}) %collective-permute-start.20) | collective-permute-done | bytes 266272 | tf_op jit(solution)/shard_map/ppermute | solution.py:221
  134.5 0.9 fusion.12
  (78 shorter events, 3.9 us)
Async XLA Ops:
  0.6 3.4 %copy-start = (bf16[1,1024,4096]{2,1,0:T(8,128)(2,1)S(1)}, bf16[1,1024,4096]{2,1,0:T(8,128)(2,1)}, u32[]{:S(2)}) copy-start(bf16[1,1024,4096]{2,1,0:T(8,128)(2,1)} %param.5) | copy-start | bytes 25165828
  4.0 1.2 copy-start.1
  8.6 15.9 %copy-start.2 = (bf16[128,4096]{1,0:T(8,128)(2,1)S(1)}, bf16[128,4096]{1,0:T(8,128)(2,1)}, u32[]{:S(2)}) copy-start(bf16[128,4096]{1,0:T(8,128)(2,1)} %head_ref.3) | copy-start | bytes 3145732
  8.6 15.9 %copy-start.3 = (bf16[1,4,128,1024]{3,2,1,0:T(8,128)(2,1)S(1)}, bf16[1,4,128,1024]{3,2,1,0:T(8,128)(2,1)}, u32[]{:S(2)}) copy-start(bf16[1,4,128,1024]{3,2,1,0:T(8,128)(2,1)} %param.6) | copy-start | bytes 3145732
  8.7 15.9 %copy-start.4 = (s32[2]{0:T(128)S(1)}, s32[2]{0:T(128)}, u32[]{:S(2)}) copy-start(s32[2]{0:T(128)} %pending_ref.3) | copy-start | bytes 28
  8.7 5.3 %collective-permute-start = (bf16[128,1024]{1,0:T(8,128)(2,1)S(1)}, bf16[128,1024]{1,0:T(8,128)(2,1)S(1)}, u32[]{:S(2)}, u32[]{:S(2)}) collective-permute-start(bf16[128,1024]{1,0:T(8,128)(2,1)S(1)} %get-tuple-element.25), channel_id=1, source_target_pairs={{128,0},{160,32},{192,64},{224,96},{129,1},{161,33},{193,65},{225,... | collective-permute-start | bytes 786440 | tf_op jit(solution)/shard_map/ppermute | solution.py:196
  10.1 7.7 %collective-permute-start.1 = (bf16[128,1024]{1,0:T(8,128)(2,1)S(1)}, bf16[128,1024]{1,0:T(8,128)(2,1)S(1)}, u32[]{:S(2)}, u32[]{:S(2)}) collective-permute-start(bf16[128,1024]{1,0:T(8,128)(2,1)S(1)} %get-tuple-element.25), channel_id=1, source_target_pairs={{128,32},{160,64},{192,96},{224,0},{129,33},{161,65},{193,97},{225... | collective-permute-start | bytes 786440 | tf_op jit(solution)/shard_map/ppermute | solution.py:196
  11.4 9.7 %collective-permute-start.2 = (bf16[128,1024]{1,0:T(8,128)(2,1)S(1)}, bf16[128,1024]{1,0:T(8,128)(2,1)S(1)}, u32[]{:S(2)}, u32[]{:S(2)}) collective-permute-start(bf16[128,1024]{1,0:T(8,128)(2,1)S(1)} %get-tuple-element.25), channel_id=1, source_target_pairs={{128,64},{160,96},{192,0},{224,32},{129,65},{161,97},{193,1},{225,... | collective-permute-start | bytes 786440 | tf_op jit(solution)/shard_map/ppermute | solution.py:196
  12.7 11.7 %collective-permute-start.3 = (bf16[128,1024]{1,0:T(8,128)(2,1)S(1)}, bf16[128,1024]{1,0:T(8,128)(2,1)S(1)}, u32[]{:S(2)}, u32[]{:S(2)}) collective-permute-start(bf16[128,1024]{1,0:T(8,128)(2,1)S(1)} %get-tuple-element.25), channel_id=1, source_target_pairs={{128,96},{160,0},{192,32},{224,64},{129,97},{161,1},{193,33},{225,... | collective-permute-start | bytes 786440 | tf_op jit(solution)/shard_map/ppermute | solution.py:196
  24.5 12.5 %slice-start = ((s8[8388608]{0:T(1024)(128)(4,1)}), s8[4194304]{0:T(1024)(128)(4,1)S(1)}, s32[]{:S(2)}) async-start(s8[8388608]{0:T(1024)(128)(4,1)} %bitcast.89), calls=%async_computation | async-start | bytes 8388608
  30.3 6.7 %slice-start.1 = ((s8[8388608]{0:T(1024)(128)(4,1)}), s8[4194304]{0:T(1024)(128)(4,1)S(1)}, s32[]{:S(2)}) async-start(s8[8388608]{0:T(1024)(128)(4,1)} %bitcast.89), calls=%async_computation.1 | async-start | bytes 8388608
  30.5 25.8 %collective-permute-start.11 = (f16[4112,128]{1,0:T(8,128)(2,1)S(1)}, f16[4112,128]{1,0:T(8,128)(2,1)}, u32[]{:S(2)}, u32[]{:S(2)}) collective-permute-start(f16[4112,128]{1,0:T(8,128)(2,1)S(1)} %convert_element_type.278), channel_id=1, source_target_pairs={{0,12},{4,0},{8,4},{12,8},{1,13},{5,1},{9,5},{13,9},{2,14},{6,2},{... | collective-permute-start | bytes 3158024 | tf_op jit(solution)/shard_map/ppermute | solution.py:155
  33.7 25.9 %collective-permute-start.4 = (f16[4112,128]{1,0:T(8,128)(2,1)S(1)}, f16[4112,128]{1,0:T(8,128)(2,1)}, u32[]{:S(2)}, u32[]{:S(2)}) collective-permute-start(f16[4112,128]{1,0:T(8,128)(2,1)S(1)} %convert_element_type.247), channel_id=1, source_target_pairs={{0,3},{1,0},{2,1},{3,2},{4,7},{5,4},{6,5},{7,6},{8,11},{9,8},{10,9... | collective-permute-start | bytes 3158024 | tf_op jit(solution)/shard_map/ppermute | solution.py:155
  36.6 27.2 %collective-permute-start.5 = (f16[4112,128]{1,0:T(8,128)(2,1)S(1)}, f16[4112,128]{1,0:T(8,128)(2,1)}, u32[]{:S(2)}, u32[]{:S(2)}) collective-permute-start(f16[4112,128]{1,0:T(8,128)(2,1)S(1)} %convert_element_type.250), channel_id=1, source_target_pairs={{0,1},{1,2},{2,3},{3,0},{4,5},{5,6},{6,7},{7,4},{8,9},{9,10},{10,1... | collective-permute-start | bytes 3158024 | tf_op jit(solution)/shard_map/ppermute | solution.py:155
  36.9 27.2 %collective-permute-start.12 = (f16[4112,128]{1,0:T(8,128)(2,1)S(1)}, f16[4112,128]{1,0:T(8,128)(2,1)}, u32[]{:S(2)}, u32[]{:S(2)}) collective-permute-start(f16[4112,128]{1,0:T(8,128)(2,1)S(1)} %convert_element_type.281), channel_id=1, source_target_pairs={{0,4},{4,8},{8,12},{12,0},{1,5},{5,9},{9,13},{13,1},{2,6},{6,10},{... | collective-permute-start | bytes 3158024 | tf_op jit(solution)/shard_map/ppermute | solution.py:155
  66.9 15.3 %collective-permute-start.7 = (f16[2064,128]{1,0:T(8,128)(2,1)S(1)}, f16[2064,128]{1,0:T(8,128)(2,1)S(1)}, u32[]{:S(2)}, u32[]{:S(2)}) collective-permute-start(f16[2064,128]{1,0:T(8,128)(2,1)S(1)} %pad_maximum_fusion.2), channel_id=1, source_target_pairs={{0,3},{1,0},{2,1},{3,2},{4,7},{5,4},{6,5},{7,6},{8,11},{9,8},{10,9... | collective-permute-start | bytes 1585160 | tf_op jit(solution)/shard_map/ppermute | solution.py:155
  71.0 13.8 %collective-permute-start.14 = (f16[2064,128]{1,0:T(8,128)(2,1)S(1)}, f16[2064,128]{1,0:T(8,128)(2,1)S(1)}, u32[]{:S(2)}, u32[]{:S(2)}) collective-permute-start(f16[2064,128]{1,0:T(8,128)(2,1)S(1)} %pad_maximum_fusion.4), channel_id=1, source_target_pairs={{0,12},{4,0},{8,4},{12,8},{1,13},{5,1},{9,5},{13,9},{2,14},{6,2},{... | collective-permute-start | bytes 1585160 | tf_op jit(solution)/shard_map/ppermute | solution.py:155
  82.8 15.2 %collective-permute-start.6 = (f16[2064,128]{1,0:T(8,128)(2,1)S(1)}, f16[2064,128]{1,0:T(8,128)(2,1)S(1)}, u32[]{:S(2)}, u32[]{:S(2)}) collective-permute-start(f16[2064,128]{1,0:T(8,128)(2,1)S(1)} %pad_maximum_fusion.1), channel_id=1, source_target_pairs={{0,1},{1,2},{2,3},{3,0},{4,5},{5,6},{6,7},{7,4},{8,9},{9,10},{10,1... | collective-permute-start | bytes 1585160 | tf_op jit(solution)/shard_map/ppermute | solution.py:155
  85.4 16.0 %collective-permute-start.13 = (f16[2064,128]{1,0:T(8,128)(2,1)S(1)}, f16[2064,128]{1,0:T(8,128)(2,1)S(1)}, u32[]{:S(2)}, u32[]{:S(2)}) collective-permute-start(f16[2064,128]{1,0:T(8,128)(2,1)S(1)} %pad_maximum_fusion.3), channel_id=1, source_target_pairs={{0,4},{4,8},{8,12},{12,0},{1,5},{5,9},{9,13},{13,1},{2,6},{6,10},{... | collective-permute-start | bytes 1585160 | tf_op jit(solution)/shard_map/ppermute | solution.py:155
  99.2 7.0 %collective-permute-start.8 = (f16[1040,128]{1,0:T(8,128)(2,1)S(1)}, f16[1040,128]{1,0:T(8,128)(2,1)S(1)}, u32[]{:S(2)}, u32[]{:S(2)}) collective-permute-start(f16[1040,128]{1,0:T(8,128)(2,1)S(1)} %get-tuple-element.105), channel_id=1, source_target_pairs={{0,12},{4,0},{8,4},{12,8},{1,13},{5,1},{9,5},{13,9},{2,14},{6,2},{... | collective-permute-start | bytes 798728 | tf_op jit(solution)/shard_map/ppermute | solution.py:155
  99.3 8.2 %collective-permute-start.9 = (f16[1040,128]{1,0:T(8,128)(2,1)S(1)}, f16[1040,128]{1,0:T(8,128)(2,1)S(1)}, u32[]{:S(2)}, u32[]{:S(2)}) collective-permute-start(f16[1040,128]{1,0:T(8,128)(2,1)S(1)} %get-tuple-element.104), channel_id=1, source_target_pairs={{0,4},{4,8},{8,12},{12,0},{1,5},{5,9},{9,13},{13,1},{2,6},{6,10},{... | collective-permute-start | bytes 798728 | tf_op jit(solution)/shard_map/ppermute | solution.py:155
  102.6 6.5 %collective-permute-start.15 = (f16[1040,128]{1,0:T(8,128)(2,1)S(1)}, f16[1040,128]{1,0:T(8,128)(2,1)S(1)}, u32[]{:S(2)}, u32[]{:S(2)}) collective-permute-start(f16[1040,128]{1,0:T(8,128)(2,1)S(1)} %get-tuple-element.107), channel_id=1, source_target_pairs={{0,3},{1,0},{2,1},{3,2},{4,7},{5,4},{6,5},{7,6},{8,11},{9,8},{10,9... | collective-permute-start | bytes 798728 | tf_op jit(solution)/shard_map/ppermute | solution.py:155
  104.5 7.6 %collective-permute-start.16 = (f16[1040,128]{1,0:T(8,128)(2,1)S(1)}, f16[1040,128]{1,0:T(8,128)(2,1)S(1)}, u32[]{:S(2)}, u32[]{:S(2)}) collective-permute-start(f16[1040,128]{1,0:T(8,128)(2,1)S(1)} %get-tuple-element.106), channel_id=1, source_target_pairs={{0,1},{1,2},{2,3},{3,0},{4,5},{5,6},{6,7},{7,4},{8,9},{9,10},{10,1... | collective-permute-start | bytes 798728 | tf_op jit(solution)/shard_map/ppermute | solution.py:155
  107.8 6.3 %collective-permute-start.10 = (f16[528,128]{1,0:T(8,128)(2,1)S(1)}, f16[528,128]{1,0:T(8,128)(2,1)S(1)}, u32[]{:S(2)}, u32[]{:S(2)}) collective-permute-start(f16[528,128]{1,0:T(8,128)(2,1)S(1)} %pad_maximum_fusion.10), channel_id=1, source_target_pairs={{0,4},{4,8},{8,12},{12,0},{1,5},{5,9},{9,13},{13,1},{2,6},{6,10},{... | collective-permute-start | bytes 405512 | tf_op jit(solution)/shard_map/ppermute | solution.py:155
  112.3 6.3 %collective-permute-start.17 = (f16[528,128]{1,0:T(8,128)(2,1)S(1)}, f16[528,128]{1,0:T(8,128)(2,1)S(1)}, u32[]{:S(2)}, u32[]{:S(2)}) collective-permute-start(f16[528,128]{1,0:T(8,128)(2,1)S(1)} %pad_maximum_fusion.11), channel_id=1, source_target_pairs={{0,1},{1,2},{2,3},{3,0},{4,5},{5,6},{6,7},{7,4},{8,9},{9,10},{10,1... | collective-permute-start | bytes 405512 | tf_op jit(solution)/shard_map/ppermute | solution.py:155
  114.2 5.1 %collective-permute-start.18 = (f16[528,128]{1,0:T(8,128)(2,1)S(1)}, f16[528,128]{1,0:T(8,128)(2,1)S(1)}, u32[]{:S(2)}, u32[]{:S(2)}) collective-permute-start(f16[528,128]{1,0:T(8,128)(2,1)S(1)} %pad_maximum_fusion.12), channel_id=1, source_target_pairs={{0,12},{4,0},{8,4},{12,8},{1,13},{5,1},{9,5},{13,9},{2,14},{6,2},{... | collective-permute-start | bytes 405512 | tf_op jit(solution)/shard_map/ppermute | solution.py:155
  118.7 5.1 %collective-permute-start.19 = (f16[528,128]{1,0:T(8,128)(2,1)S(1)}, f16[528,128]{1,0:T(8,128)(2,1)S(1)}, u32[]{:S(2)}, u32[]{:S(2)}) collective-permute-start(f16[528,128]{1,0:T(8,128)(2,1)S(1)} %pad_maximum_fusion.13), channel_id=1, source_target_pairs={{0,3},{1,0},{2,1},{3,2},{4,7},{5,4},{6,5},{7,6},{8,11},{9,8},{10,9... | collective-permute-start | bytes 405512 | tf_op jit(solution)/shard_map/ppermute | solution.py:155
  124.1 10.4 %collective-permute-start.20 = (f16[1040,128]{1,0:T(8,128)(2,1)S(1)}, f16[1040,128]{1,0:T(8,128)(2,1)S(1)}, u32[]{:S(2)}, u32[]{:S(2)}) collective-permute-start(f16[1040,128]{1,0:T(8,128)(2,1)S(1)} %pad_maximum_fusion.9), channel_id=1, source_target_pairs={{0,16},{16,0},{1,17},{17,1},{2,18},{18,2},{3,19},{19,3},{4,20},{20... | collective-permute-start | bytes 798728 | tf_op jit(solution)/shard_map/ppermute | solution.py:221

commit v3 on v0

v3 whole, which is shorter than its diff:
```python
import functools

import jax
import jax.numpy as jnp
from jax import lax
from jax.experimental import pallas as pl
from jax.experimental.pallas import tpu as pltpu
from jax.sharding import Mesh
from jax.sharding import PartitionSpec as P

F32 = jnp.float32
F16 = jnp.float16
BF16 = jnp.bfloat16
RING = 4
LANES = 128
TAIL = 16
TOP = 15
TINY = 1e-30


def section():
    return lax.axis_index("section")


def on_last():
    return section() == lax.axis_size("section") - 1


def block_start(z_off, along, across):
    first = section() == 0
    y_off, x_off = jnp.where(first, across, along), jnp.where(first, along, across)
    z = lax.rem(lax.axis_index("z_hi") + z_off, 2)
    y = lax.rem(lax.axis_index("y") + y_off, RING)
    x = lax.rem(lax.axis_index("x") + x_off, RING)
    return pl.multiple_of((z * (RING * RING) + y * RING + x) * LANES, LANES)


def pairs_over(along, by):
    size, pairs = RING * RING, []
    for s in range(2):
        for y in range(RING):
            for x in range(RING):
                on_x = (s == 0) == along
                there = (y, (x + by) % RING) if on_x else ((y + by) % RING, x)
                pairs.append((s * size + y * RING + x, s * size + there[0] * RING + there[1]))
    return pairs


def shifted(value, along, by):
    return lax.ppermute(value, ("section", "y", "x"), pairs_over(along, by))


def whole(n=1):
    return [pl.BlockSpec(memory_space=pltpu.VMEM)] * n


def call(kernel, out_shapes, operands, specs, scratch=(), flops=0, moved=0, limit=32):
    return pl.pallas_call(
        kernel,
        out_shape=[jax.ShapeDtypeStruct(s, t) for s, t in out_shapes],
        in_specs=specs,
        out_specs=whole(len(out_shapes)),
        scratch_shapes=list(scratch),
        compiler_params=pltpu.CompilerParams(vmem_limit_bytes=limit * 2**20),
        cost_estimate=pl.CostEstimate(flops=flops, bytes_accessed=moved, transcendentals=0),
    )(*operands)


def pack_stash_kernel(pending_ref, x_ref, stash_ref, right_ref, left_ref, own_ref):
    micro, rows, width = x_ref.shape
    count = pending_ref[section()]
    for m in range(micro):
        turned = jnp.where(m >= micro - count, x_ref[m].astype(F32), 0.0).T.astype(BF16)
        right_ref[:width, m * rows:(m + 1) * rows] = turned
        left_ref[:width, m * rows:(m + 1) * rows] = turned
    depth = stash_ref.shape[0] * rows
    for out, base, along in ((right_ref, width, 1), (left_ref, width, RING - 1), (own_ref, 0, 0)):
        for z in range(2):
            for b in range(RING):
                at = block_start(z, along, b)
                for m in range(stash_ref.shape[0]):
                    top = base + z * depth + m * rows
                    out[top:top + rows, b * LANES:(b + 1) * LANES] = stash_ref[m, :, pl.ds(at, LANES)]


def pack_last_kernel(stash_ref, head_ref, rel_ref, right_ref, left_ref, own_ref, far_ref):
    tensor = lax.axis_index("z_lo")
    rows, share = rel_ref.shape[1], rel_ref.shape[2]
    earlier = stash_ref.shape[0]

    def last(at):
        owner = lax.div(at, share)
        inner = pl.multiple_of(lax.rem(at, share), LANES)
        chained = rel_ref[lax.rem(tensor - owner + RING, RING), :, pl.ds(inner, LANES)]
        return jnp.where(on_last(), head_ref[:, pl.ds(at, LANES)], chained)

    for z in range(2):
        for b in range(RING):
            lanes = slice(b * LANES, (b + 1) * LANES)
            for out, along in ((right_ref, 1), (left_ref, RING - 1), (own_ref, 0)):
                out[z * rows:(z + 1) * rows, lanes] = last(block_start(z, along, b))
            at = block_start(z, 2, b)
            top = z * (earlier + 1) * rows
            for m in range(earlier):
                far_ref[top + m * rows:top + (m + 1) * rows, lanes] = stash_ref[m, :, pl.ds(at, LANES)]
            far_ref[top + earlier * rows:top + (earlier + 1) * rows, lanes] = last(at)


def early_kernel(mine_ref, own_ref, left_ref, right_ref, acc_ref):
    width, depth = acc_ref.shape[0], own_ref.shape[0] // 2
    half = acc_ref.shape[1] // 2
    step = width // 2
    for r in range(0, width, step):
        lhs = jnp.concatenate([ref[r:r + step, :depth] for ref in (mine_ref, left_ref, right_ref)], axis=1)
        for z in range(2):
            sides = [own_ref[z * depth:(z + 1) * depth, :]]
            sides += [ref[width + z * depth:width + (z + 1) * depth, :] for ref in (left_ref, right_ref)]
            rhs = jnp.concatenate(sides, axis=0)
            acc_ref[r:r + step, z * half:(z + 1) * half] = jnp.dot(lhs, rhs, preferred_element_type=F32)


def late_kernel(acc_ref, mine_ref, left_ref, right_ref, top_ref, low_ref, own_last_ref, left_last_ref, right_last_ref,
                far_ref, keep_ref, *rest):
    sends, sum_ref = rest[:-1], rest[-1]
    width, rows = acc_ref.shape[0], own_last_ref.shape[0] // 2
    half = acc_ref.shape[1] // 2
    step = width // 2
    full = far_ref.shape[0] // 2
    largest = jnp.full((1, half), TINY, F32)
    for r, there in ((0, top_ref), (step, low_ref)):
        lhs = [ref[r:r + step, full - rows:] for ref in (mine_ref, left_ref, right_ref)]
        lhs = jnp.concatenate(lhs + [there[...]], axis=1)
        for z in range(2):
            rhs = [ref[z * rows:(z + 1) * rows, :] for ref in (own_last_ref, left_last_ref, right_last_ref)]
            rhs = jnp.concatenate(rhs + [far_ref[z * full:(z + 1) * full, :]], axis=0)
            total = acc_ref[r:r + step, z * half:(z + 1) * half] + jnp.dot(lhs, rhs, preferred_element_type=F32)
            largest = jnp.maximum(largest, jnp.max(jnp.abs(total), axis=0, keepdims=True))
            sum_ref[r:r + step, z * half:(z + 1) * half] = total
    power = jnp.ceil(jnp.log2(jnp.max(largest, axis=1, keepdims=True))) - TOP
    power = jnp.broadcast_to(power, (1, LANES))
    factor = jnp.exp2(-power)
    for z in range(2):
        keep_ref[z * width:(z + 1) * width, :] = sum_ref[:, z * half:z * half + LANES]
        for b, out in enumerate(sends, 1):
            lanes = slice(z * half + b * LANES, z * half + (b + 1) * LANES)
            out[z * width:(z + 1) * width, :] = sum_ref[:, lanes] * factor
    for out in sends:
        out[2 * width:, :] = jnp.broadcast_to(power, (TAIL, LANES))


def combine_kernel(keep_ref, one_ref, two_ref, three_ref, near_ref, far_ref):
    rows = near_ref.shape[0]
    totals = []
    for z in range(2):
        total = keep_ref[z * rows:(z + 1) * rows, :]
        for ref in (one_ref, two_ref, three_ref):
            total = total + ref[z * rows:(z + 1) * rows, :] * jnp.exp2(ref[2 * rows:2 * rows + 1, :])
        totals.append(total)
    near_ref[...] = totals[0]
    largest = jnp.maximum(jnp.max(jnp.abs(totals[1]), axis=0, keepdims=True), TINY)
    power = jnp.ceil(jnp.log2(jnp.max(largest, axis=1, keepdims=True))) - TOP
    power = jnp.broadcast_to(power, (1, LANES))
    far_ref[:rows, :] = totals[1] * jnp.exp2(-power)
    far_ref[rows:, :] = jnp.broadcast_to(power, (TAIL, LANES))


CONTRACT_LAST = (((1,), (1,)), ((), ()))


def weight_copies(weight_ref, held_ref, sems):
    copies = [pltpu.make_async_copy(weight_ref.at[pl.ds(i * held_ref.shape[1], held_ref.shape[1])], held_ref.at[i], sems.at[i])
              for i in range(held_ref.shape[0])]
    for copy in copies:
        copy.start()
    return copies


def first_kernel(grad_ref, weight_ref, out_ref, small_ref, held_ref, sems):
    step = held_ref.shape[1]
    for i, copy in enumerate(weight_copies(weight_ref, held_ref, sems)):
        copy.wait()
        out = lax.dot_general(grad_ref[...], held_ref[i], CONTRACT_LAST, preferred_element_type=F32)
        out_ref[:, i * step:(i + 1) * step] = out
        small_ref[:, i * step:(i + 1) * step] = out.astype(BF16)


def second_kernel(rel_ref, first_ref, weight_ref, out_ref, held_ref, sems):
    step, share = held_ref.shape[1], rel_ref.shape[2]
    tensor = lax.axis_index("z_lo")
    for i, copy in enumerate(weight_copies(weight_ref, held_ref, sems)):
        copy.wait()
        total = jnp.zeros((rel_ref.shape[1], step), F32)
        for k in range(RING):
            owner = lax.rem(tensor - k + RING, RING)
            cols = held_ref[i, :, pl.ds(pl.multiple_of(owner * share, share), share)]
            total = total + lax.dot_general(rel_ref[k], cols, CONTRACT_LAST, preferred_element_type=F32)
        lanes = slice(i * step, (i + 1) * step)
        out_ref[:, lanes] = jnp.where(on_last(), first_ref[:, lanes], total)


def chain_call(kernel, out_types, operands, weight, rows):
    width, depth = weight.shape
    parts = 4
    return call(
        kernel,
        [((rows, width), t) for t in out_types],
        operands + [weight],
        whole(len(operands)) + [pl.BlockSpec(memory_space=pltpu.HBM)],
        scratch=[pltpu.VMEM((parts, width // parts, depth), weight.dtype), pltpu.SemaphoreType.DMA((parts,))],
        flops=2 * rows * width * depth,
        moved=2 * width * depth, limit=48,
    )


def local(weights, stash_in, stash_grad, head_grad, pending):
    weight = weights[0]
    inputs, grads = stash_in[0], stash_grad[0]
    micro, rows, width = inputs.shape
    depth = (micro - 1) * rows
    half = RING * LANES
    smem = [pl.BlockSpec(memory_space=pltpu.SMEM)]

    side = ((width + 2 * depth, half), BF16)
    right, left, own = call(
        pack_stash_kernel, [side, side, ((2 * depth, half), BF16)], (pending, inputs, grads), smem + whole(2),
        moved=12 * 2**20,
    )
    right, left, head = lax.optimization_barrier((right, left, head_grad))
    from_left, from_right = shifted(right, True, 1), shifted(left, True, -1)

    first, small = chain_call(first_kernel, (F32, BF16), [head], weight, rows)
    shard = lax.ppermute(small, "section", [(1, 0)])
    rel = [shard]
    for by in range(1, RING):
        rel.append(lax.ppermute(shard, ("section", "z_lo"), [(i, (i + by) % RING) for i in range(RING)]))
    rel = jnp.stack(rel, 0)

    edge = ((2 * rows, half), BF16)
    edge_right, edge_left, own_last, far = call(
        pack_last_kernel, [edge, edge, edge, ((2 * micro * rows, half), BF16)], (grads, head_grad, rel), whole(3),
        moved=8 * 2**20,
    )
    from_left, from_right, edge_right, edge_left, far = lax.optimization_barrier(
        (from_left, from_right, edge_right, edge_left, far)
    )
    top = shifted(from_left[:width // 2], True, 1)
    low = shifted(from_right[width // 2:width], True, -1)
    last_left, last_right = shifted(edge_right, True, 1), shifted(edge_left, True, -1)
    far = shifted(far, True, 2)
    (acc,) = call(
        early_kernel, [((width, 2 * half), F32)], (right, own, from_left, from_right), whole(4),
        flops=2 * width * 2 * half * 3 * depth, moved=12 * 2**20,
    )
    (second,) = chain_call(second_kernel, (F32,), [rel, first], weight, rows)
    acc, second = lax.optimization_barrier((acc, second))
    send = ((2 * width + TAIL, LANES), F32)
    keep, *sends = call(
        late_kernel, [((2 * width, LANES), F32)] + [send] * 3,
        (acc, right, from_left, from_right, top, low, own_last, last_left, last_right, far), whole(10),
        scratch=[pltpu.VMEM((width, 2 * half), F32)],
        flops=2 * width * 2 * half * (3 * rows + micro * rows), moved=12 * 2**20,
    )
    got = [shifted(s.astype(F16), False, by).astype(F32) for by, s in enumerate(sends, 1)]
    near, far = call(
        combine_kernel, [((width, LANES), F32), ((width + TAIL, LANES), F32)], (keep, *got), whole(4), moved=6 * 2**20,
    )
    other = lax.ppermute(far.astype(F16), "z_hi", [(0, 1), (1, 0)])
    block = near + other[:width].astype(F32) * jnp.exp2(other[width:width + 1].astype(F32))
    return (second[None], block[None])


def solution(mesh):
    fine = Mesh(mesh.devices.reshape(2, 4, 2, 4, 4), ("section", "z_lo", "z_hi", "y", "x"))
    dp = ("z_hi", "y", "x")
    return jax.shard_map(
        local,
        mesh=fine,
        in_specs=(
            P("section", "z_lo", None),
            P("section", None, dp, "z_lo"),
            P("section", None, dp, None),
            P(dp, None),
            P(),
        ),
        out_specs=(P("section", dp, "z_lo"), P("section", "z_lo", dp)),
        check_vma=False,
    )
```

time: 477 us -> 108 us (0.23)
  the two profiles are of different devices: /device:TPU:64 before, /device:TPU:82 now
where the time goes in v3:
time: 108 us
  waiting for transfers between devices  52 us (48%)
  starting transfers between devices  26.4 us (24%)
  Pallas kernels  23.7 us (22%)
  local copies, waits for them, and re-layouts  3.84 us (4%)
  other arithmetic  1.46 us (1%)
    ppermute x10, waiting for transfers between devices, shifted(): return lax.ppermute(value, ('section', 'y', 'x'), pairs_over(along, by))  31.5 us
    pallas_call x7, Pallas kernels, call(): pl.pallas_call(kernel, out_shape=[jax.ShapeDtypeStruct(s, t) for s, t in...  23.7 us
    ppermute x10, starting transfers between devices, shifted(): return lax.ppermute(value, ('section', 'y', 'x'), pairs_over(along, by))  11.4 us
    ppermute x3, starting transfers between devices, local(): lax.ppermute(shard, ('section', 'z_lo'), [(i, (i + by) % RING) for i in r...  10 us
    ppermute x1, waiting for transfers between devices, local(): other = lax.ppermute(far.astype(F16), 'z_hi', [(0, 1), (1, 0)])  9.49 us
    ppermute x3, waiting for transfers between devices, local(): lax.ppermute(shard, ('section', 'z_lo'), [(i, (i + by) % RING) for i in r...  8.94 us
    unnamed x10, local copies, waits for them, and re-layouts  3.77 us
    ppermute x1, starting transfers between devices, local(): other = lax.ppermute(far.astype(F16), 'z_hi', [(0, 1), (1, 0)])  3.7 us
  transfers between devices with their start and end apart: 15, of which 8 were waited for; matrix products, arithmetic and copies ran while one was open for 0% of the time, Pallas kernels for 18%

profile of v3, /device:TPU:82, one launch (start us, length us, event | category | flops | bytes accessed | tf_op | source)
XLA Modules:
  0.0 108.2 jit_solution(12838783987168693196)
XLA Ops:
  0.6 0.0 copy-start
  0.6 1.9 %copy-done = bf16[1,3,128,4096]{3,2,1,0:T(8,128)(2,1)S(1)} copy-done((bf16[1,3,128,4096]{3,2,1,0:T(8,128)(2,1)S(1)}, bf16[1,3,128,4096]{3,2,1,0:T(8,128)(2,1)}, u32[]{:S(2)}) %copy-start) | copy-done | bytes 3145752
  2.5 1.2 %copy-done.3 = bf16[1,4,128,1024]{3,2,1,0:T(8,128)(2,1)S(1)} copy-done((bf16[1,4,128,1024]{3,2,1,0:T(8,128)(2,1)S(1)}, bf16[1,4,128,1024]{3,2,1,0:T(8,128)(2,1)}, u32[]{:S(2)}) %copy-start.3) | copy-done | bytes 1048600
  3.8 0.7 copy-done.4
  4.4 1.6 %shard_map.68 = (bf16[1792,512]{1,0:T(8,128)(2,1)S(1)}, bf16[1792,512]{1,0:T(8,128)(2,1)S(1)}, bf16[768,512]{1,0:T(8,128)(2,1)S(1)}) custom-call(s32[2]{0:T(128)S(1)} %copy-done.4, bf16[4,128,1024]{2,1,0:T(8,128)(2,1)S(1)} %bitcast.14, bf16[3,128,4096]{2,1,0:T(8,128)(2,1)S(1)} %bitcast.12), custom_call_target="tpu_custom_call" | custom-call | bytes 12582912 | tf_op jit(solution)/shard_map/pallas_call | solution.py:58
  6.0 1.6 %collective-permute-start = (bf16[1792,512]{1,0:T(8,128)(2,1)S(1)}, bf16[1792,512]{1,0:T(8,128)(2,1)S(1)}, u32[]{:S(2)}, u32[]{:S(2)}) collective-permute-start(bf16[1792,512]{1,0:T(8,128)(2,1)S(1)} %get-tuple-element.29.mine_ref), channel_id=1, source_target_pairs={{0,1},{1,2},{2,3},{3,0},{4,5},{5,6},{6,7},{7,4},{8,9},{9,10},{10,1... | collective-permute-start | bytes 5505032 | tf_op jit(solution)/shard_map/ppermute | solution.py:50
  7.6 0.5 collective-permute-start.1
  8.1 6.8 %shard_map.69 = (f32[128,1024]{1,0:T(8,128)S(1)}, bf16[128,1024]{1,0:T(8,128)(2,1)S(1)}) custom-call(bf16[128,4096]{1,0:T(8,128)(2,1)S(1)} %copy-done.2, bf16[1024,4096]{1,0:T(8,128)(2,1)} %bitcast.15), custom_call_target="tpu_custom_call" | custom-call | flops 1073741824 | bytes 8388608 | tf_op jit(solution)/shard_map/pallas_call | solution.py:58
  14.9 1.3 %collective-permute-start.2 = (bf16[128,1024]{1,0:T(8,128)(2,1)S(1)}, bf16[128,1024]{1,0:T(8,128)(2,1)S(1)}, u32[]{:S(2)}, u32[]{:S(2)}) collective-permute-start(bf16[128,1024]{1,0:T(8,128)(2,1)S(1)} %get-tuple-element.33), channel_id=1, source_target_pairs={{128,0},{129,1},{130,2},{131,3},{132,4},{133,5},{134,6},{135,7},{1... | collective-permute-start | bytes 786440 | tf_op jit(solution)/shard_map/ppermute | solution.py:232
  16.2 2.1 %collective-permute-done.2 = bf16[128,1024]{1,0:T(8,128)(2,1)S(1)} collective-permute-done((bf16[128,1024]{1,0:T(8,128)(2,1)S(1)}, bf16[128,1024]{1,0:T(8,128)(2,1)S(1)}, u32[]{:S(2)}, u32[]{:S(2)}) %collective-permute-start.2) | collective-permute-done | bytes 262176 | tf_op jit(solution)/shard_map/ppermute | solution.py:232
  18.4 2.0 %collective-permute-start.5 = (bf16[128,1024]{1,0:T(8,128)(2,1)S(1)}, bf16[128,1024]{1,0:T(8,128)(2,1)S(1)}, u32[]{:S(2)}, u32[]{:S(2)}) collective-permute-start(bf16[128,1024]{1,0:T(8,128)(2,1)S(1)} %collective-permute-done.2), channel_id=1, source_target_pairs={{0,96},{32,0},{64,32},{96,64},{1,97},{33,1},{65,33},{97,65},{2,98}... | collective-permute-start | bytes 786440 | tf_op jit(solution)/shard_map/ppermute | solution.py:235
  20.4 6.1 %collective-permute-start.4 = (bf16[128,1024]{1,0:T(8,128)(2,1)S(1)}, bf16[128,1024]{1,0:T(8,128)(2,1)S(1)}, u32[]{:S(2)}, u32[]{:S(2)}) collective-permute-start(bf16[128,1024]{1,0:T(8,128)(2,1)S(1)} %collective-permute-done.2), channel_id=1, source_target_pairs={{0,64},{32,96},{64,0},{96,32},{1,65},{33,97},{65,1},{97,33},{2,66}... | collective-permute-start | bytes 786440 | tf_op jit(solution)/shard_map/ppermute | solution.py:235
  26.5 1.9 %collective-permute-start.3 = (bf16[128,1024]{1,0:T(8,128)(2,1)S(1)}, bf16[128,1024]{1,0:T(8,128)(2,1)S(1)}, u32[]{:S(2)}, u32[]{:S(2)}) collective-permute-start(bf16[128,1024]{1,0:T(8,128)(2,1)S(1)} %collective-permute-done.2), channel_id=1, source_target_pairs={{0,32},{32,64},{64,96},{96,0},{1,33},{33,65},{65,97},{97,1},{2,34}... | collective-permute-start | bytes 786440 | tf_op jit(solution)/shard_map/ppermute | solution.py:235
  28.4 0.0 collective-permute-done.5
  28.4 5.6 %collective-permute-done.4 = bf16[128,1024]{1,0:T(8,128)(2,1)S(1)} collective-permute-done((bf16[128,1024]{1,0:T(8,128)(2,1)S(1)}, bf16[128,1024]{1,0:T(8,128)(2,1)S(1)}, u32[]{:S(2)}, u32[]{:S(2)}) %collective-permute-start.4) | collective-permute-done | bytes 262176 | tf_op jit(solution)/shard_map/ppermute | solution.py:235
  34.0 3.3 %collective-permute-done.3 = bf16[128,1024]{1,0:T(8,128)(2,1)S(1)} collective-permute-done((bf16[128,1024]{1,0:T(8,128)(2,1)S(1)}, bf16[128,1024]{1,0:T(8,128)(2,1)S(1)}, u32[]{:S(2)}, u32[]{:S(2)}) %collective-permute-start.3) | collective-permute-done | bytes 262176 | tf_op jit(solution)/shard_map/ppermute | solution.py:235
  37.3 0.1 pad_maximum_fusion.rel_ref
  37.5 1.8 %shard_map.70 = (bf16[256,512]{1,0:T(8,128)(2,1)S(1)}, bf16[256,512]{1,0:T(8,128)(2,1)S(1)}, bf16[256,512]{1,0:T(8,128)(2,1)S(1)}, bf16[1024,512]{1,0:T(8,128)(2,1)}) custom-call(bf16[3,128,4096]{2,1,0:T(8,128)(2,1)S(1)} %bitcast.13, bf16[128,4096]{1,0:T(8,128)(2,1)S(1)} %copy-done.2, bf16[4,128,1024]{2,1,0:T(8,128)(2,1)S(1)} %pad_maximum_fusion.rel_ref), custom_call_target="tpu_custom_call" | custom-call | bytes 8388608 | tf_op jit(solution)/shard_map/pallas_call | solution.py:58
  39.3 0.0 collective-permute-done.left_ref
  39.3 0.0 collective-permute-done.1.right_ref
  39.3 2.1 %collective-permute-start.10 = (bf16[1024,512]{1,0:T(8,128)(2,1)}, bf16[1024,512]{1,0:T(8,128)(2,1)S(1)}, u32[]{:S(2)}, u32[]{:S(2)}) collective-permute-start(bf16[1024,512]{1,0:T(8,128)(2,1)} %get-tuple-element.45), channel_id=1, source_target_pairs={{0,2},{1,3},{2,0},{3,1},{4,6},{5,7},{6,4},{7,5},{8,10},{9,11},{10,... | collective-permute-start | bytes 3145736 | tf_op jit(solution)/shard_map/ppermute | solution.py:50
  41.5 1.2 %collective-permute-start.6 = (bf16[512,512]{1,0:T(8,128)(2,1)S(1)}, bf16[512,512]{1,0:T(8,128)(2,1)S(1)}, u32[]{:S(2)}, u32[]{:S(2)}) collective-permute-start(bf16[512,512]{1,0:T(8,128)(2,1)S(1)} %slice.12), channel_id=1, source_target_pairs={{0,1},{1,2},{2,3},{3,0},{4,5},{5,6},{6,7},{7,4},{8,9},{9,10},{10,1... | collective-permute-start | bytes 1572872 | tf_op jit(solution)/shard_map/ppermute | solution.py:50
  42.7 1.0 collective-permute-start.7
  43.7 1.1 collective-permute-start.8
  44.8 1.6 %collective-permute-start.9 = (bf16[256,512]{1,0:T(8,128)(2,1)S(1)}, bf16[256,512]{1,0:T(8,128)(2,1)S(1)}, u32[]{:S(2)}, u32[]{:S(2)}) collective-permute-start(bf16[256,512]{1,0:T(8,128)(2,1)S(1)} %get-tuple-element.44), channel_id=1, source_target_pairs={{0,3},{1,0},{2,1},{3,2},{4,7},{5,4},{6,5},{7,6},{8,11},{9,8},{10,9... | collective-permute-start | bytes 786440 | tf_op jit(solution)/shard_map/ppermute | solution.py:50
  46.4 7.5 %shard_map.72 = f32[128,1024]{1,0:T(8,128)} custom-call(bf16[4,128,1024]{2,1,0:T(8,128)(2,1)S(1)} %pad_maximum_fusion.rel_ref, f32[128,1024]{1,0:T(8,128)S(1)} %get-tuple-element.39.first_ref, bf16[1024,4096]{1,0:T(8,128)(2,1)} %bitcast.16), custom_call_target="tpu_custom_call" | custom-call | flops 1073741824 | bytes 8388608 | tf_op jit(solution)/shard_map/pallas_call | solution.py:58
  53.8 2.9 %shard_map.71.acc_ref = f32[1024,1024]{1,0:T(8,128)S(1)} custom-call(bf16[1792,512]{1,0:T(8,128)(2,1)S(1)} %get-tuple-element.29.mine_ref, bf16[768,512]{1,0:T(8,128)(2,1)S(1)} %get-tuple-element.30.own_ref, bf16[1792,512]{1,0:T(8,128)(2,1)S(1)} %collective-permute-done.left_ref, bf16[1792,512]{1,0:T(8,128)(2,1)S(1)} %collective-permute-done.1.right_ref), custom_call_target="tpu_custom_call" | custom-call | flops 2415919104 | bytes 12582912 | tf_op jit(solution)/shard_map/pallas_call | solution.py:58
  56.7 13.8 %collective-permute-done.8.left_last_ref = bf16[256,512]{1,0:T(8,128)(2,1)S(1)} collective-permute-done((bf16[256,512]{1,0:T(8,128)(2,1)S(1)}, bf16[256,512]{1,0:T(8,128)(2,1)S(1)}, u32[]{:S(2)}, u32[]{:S(2)}) %collective-permute-start.8) | collective-permute-done | bytes 262176 | tf_op jit(solution)/shard_map/ppermute | solution.py:50
  70.5 3.0 %collective-permute-done.9.right_last_ref = bf16[256,512]{1,0:T(8,128)(2,1)S(1)} collective-permute-done((bf16[256,512]{1,0:T(8,128)(2,1)S(1)}, bf16[256,512]{1,0:T(8,128)(2,1)S(1)}, u32[]{:S(2)}, u32[]{:S(2)}) %collective-permute-start.9) | collective-permute-done | bytes 262176 | tf_op jit(solution)/shard_map/ppermute | solution.py:50
  73.5 0.0 collective-permute-done.7.low_ref
  73.5 0.0 collective-permute-done.10.far_ref
  73.5 2.6 %shard_map.73 = (f32[2048,128]{1,0:T(8,128)S(1)}, f32[2064,128]{1,0:T(8,128)S(1)}, f32[2064,128]{1,0:T(8,128)S(1)}, f32[2064,128]{1,0:T(8,128)S(1)}) custom-call(f32[1024,1024]{1,0:T(8,128)S(1)} %shard_map.71.acc_ref, bf16[1792,512]{1,0:T(8,128)(2,1)S(1)} %get-tuple-element.29.mine_ref, bf16[1792,512]{1,0:T(8,128)(2,1)S(1)} %collective-permute-done.left_ref, ...), custom_call_target="tpu_custom_call" | custom-call | flops 1879048192 | bytes 12582912 | tf_op jit(solution)/shard_map/pallas_call | solution.py:58
  76.2 0.1 convert_element_type.27
  76.2 0.5 collective-permute-start.11
  76.8 0.1 convert_element_type.29
  76.8 0.7 collective-permute-start.12
  77.6 0.1 convert_element_type.31
  77.6 1.1 collective-permute-start.13
  78.7 12.5 %collective-permute-done.11 = f16[2064,128]{1,0:T(8,128)(2,1)S(1)} collective-permute-done((f16[2064,128]{1,0:T(8,128)(2,1)S(1)}, f16[2064,128]{1,0:T(8,128)(2,1)S(1)}, u32[]{:S(2)}, u32[]{:S(2)}) %collective-permute-start.11) | collective-permute-done | bytes 528416 | tf_op jit(solution)/shard_map/ppermute | solution.py:50
  91.2 0.1 convert_element_type.28.one_ref
  91.3 0.0 collective-permute-done.12
  91.3 0.1 convert_element_type.30.two_ref
  91.4 2.1 %collective-permute-done.13 = f16[2064,128]{1,0:T(8,128)(2,1)S(1)} collective-permute-done((f16[2064,128]{1,0:T(8,128)(2,1)S(1)}, f16[2064,128]{1,0:T(8,128)(2,1)S(1)}, u32[]{:S(2)}, u32[]{:S(2)}) %collective-permute-start.13) | collective-permute-done | bytes 528416 | tf_op jit(solution)/shard_map/ppermute | solution.py:50
  93.5 0.1 convert_element_type.32.three_ref
  93.6 0.5 shard_map.74
  94.1 3.7 %collective-permute-start.14 = (f16[1040,128]{1,0:T(8,128)(2,1)S(1)}, f16[1040,128]{1,0:T(8,128)(2,1)S(1)}, u32[]{:S(2)}, u32[]{:S(2)}) collective-permute-start(f16[1040,128]{1,0:T(8,128)(2,1)S(1)} %convert_element_type.33), channel_id=1, source_target_pairs={{0,16},{16,0},{1,17},{17,1},{2,18},{18,2},{3,19},{19,3},{4,20},{20... | collective-permute-start | bytes 798728 | tf_op jit(solution)/shard_map/ppermute | solution.py:267
  97.8 9.5 %collective-permute-done.14 = f16[1040,128]{1,0:T(8,128)(2,1)S(1)} collective-permute-done((f16[1040,128]{1,0:T(8,128)(2,1)S(1)}, f16[1040,128]{1,0:T(8,128)(2,1)S(1)}, u32[]{:S(2)}, u32[]{:S(2)}) %collective-permute-start.14) | collective-permute-done | bytes 266272 | tf_op jit(solution)/shard_map/ppermute | solution.py:267
  107.3 0.9 add_bitcast_fusion
  (11 shorter events, 0.1 us)
Async XLA Ops:
  0.6 1.9 %copy-start = (bf16[1,3,128,4096]{3,2,1,0:T(8,128)(2,1)S(1)}, bf16[1,3,128,4096]{3,2,1,0:T(8,128)(2,1)}, u32[]{:S(2)}) copy-start(bf16[1,3,128,4096]{3,2,1,0:T(8,128)(2,1)} %param.7) | copy-start | bytes 9437188
  2.5 1.2 %copy-start.3 = (bf16[1,4,128,1024]{3,2,1,0:T(8,128)(2,1)S(1)}, bf16[1,4,128,1024]{3,2,1,0:T(8,128)(2,1)}, u32[]{:S(2)}) copy-start(bf16[1,4,128,1024]{3,2,1,0:T(8,128)(2,1)} %param.6) | copy-start | bytes 3145732
  3.7 0.7 copy-start.4
  4.4 3.7 %copy-start.2 = (bf16[128,4096]{1,0:T(8,128)(2,1)S(1)}, bf16[128,4096]{1,0:T(8,128)(2,1)}, u32[]{:S(2)}) copy-start(bf16[128,4096]{1,0:T(8,128)(2,1)} %head_ref.1) | copy-start | bytes 3145732
  6.0 33.3 %collective-permute-start = (bf16[1792,512]{1,0:T(8,128)(2,1)S(1)}, bf16[1792,512]{1,0:T(8,128)(2,1)S(1)}, u32[]{:S(2)}, u32[]{:S(2)}) collective-permute-start(bf16[1792,512]{1,0:T(8,128)(2,1)S(1)} %get-tuple-element.29.mine_ref), channel_id=1, source_target_pairs={{0,1},{1,2},{2,3},{3,0},{4,5},{5,6},{6,7},{7,4},{8,9},{9,10},{10,1... | collective-permute-start | bytes 5505032 | tf_op jit(solution)/shard_map/ppermute | solution.py:50
  7.6 31.7 %collective-permute-start.1 = (bf16[1792,512]{1,0:T(8,128)(2,1)S(1)}, bf16[1792,512]{1,0:T(8,128)(2,1)S(1)}, u32[]{:S(2)}, u32[]{:S(2)}) collective-permute-start(bf16[1792,512]{1,0:T(8,128)(2,1)S(1)} %get-tuple-element.31), channel_id=1, source_target_pairs={{0,3},{1,0},{2,1},{3,2},{4,7},{5,4},{6,5},{7,6},{8,11},{9,8},{10,9... | collective-permute-start | bytes 5505032 | tf_op jit(solution)/shard_map/ppermute | solution.py:50
  8.1 29.4 %copy-start.1 = (bf16[1,3,128,4096]{3,2,1,0:T(8,128)(2,1)S(1)}, bf16[1,3,128,4096]{3,2,1,0:T(8,128)(2,1)}, u32[]{:S(2)}) copy-start(bf16[1,3,128,4096]{3,2,1,0:T(8,128)(2,1)} %param.7) | copy-start | bytes 9437188
  14.9 3.4 %collective-permute-start.2 = (bf16[128,1024]{1,0:T(8,128)(2,1)S(1)}, bf16[128,1024]{1,0:T(8,128)(2,1)S(1)}, u32[]{:S(2)}, u32[]{:S(2)}) collective-permute-start(bf16[128,1024]{1,0:T(8,128)(2,1)S(1)} %get-tuple-element.33), channel_id=1, source_target_pairs={{128,0},{129,1},{130,2},{131,3},{132,4},{133,5},{134,6},{135,7},{1... | collective-permute-start | bytes 786440 | tf_op jit(solution)/shard_map/ppermute | solution.py:232
  18.4 10.0 %collective-permute-start.5 = (bf16[128,1024]{1,0:T(8,128)(2,1)S(1)}, bf16[128,1024]{1,0:T(8,128)(2,1)S(1)}, u32[]{:S(2)}, u32[]{:S(2)}) collective-permute-start(bf16[128,1024]{1,0:T(8,128)(2,1)S(1)} %collective-permute-done.2), channel_id=1, source_target_pairs={{0,96},{32,0},{64,32},{96,64},{1,97},{33,1},{65,33},{97,65},{2,98}... | collective-permute-start | bytes 786440 | tf_op jit(solution)/shard_map/ppermute | solution.py:235
  20.4 13.6 %collective-permute-start.4 = (bf16[128,1024]{1,0:T(8,128)(2,1)S(1)}, bf16[128,1024]{1,0:T(8,128)(2,1)S(1)}, u32[]{:S(2)}, u32[]{:S(2)}) collective-permute-start(bf16[128,1024]{1,0:T(8,128)(2,1)S(1)} %collective-permute-done.2), channel_id=1, source_target_pairs={{0,64},{32,96},{64,0},{96,32},{1,65},{33,97},{65,1},{97,33},{2,66}... | collective-permute-start | bytes 786440 | tf_op jit(solution)/shard_map/ppermute | solution.py:235
  26.5 10.9 %collective-permute-start.3 = (bf16[128,1024]{1,0:T(8,128)(2,1)S(1)}, bf16[128,1024]{1,0:T(8,128)(2,1)S(1)}, u32[]{:S(2)}, u32[]{:S(2)}) collective-permute-start(bf16[128,1024]{1,0:T(8,128)(2,1)S(1)} %collective-permute-done.2), channel_id=1, source_target_pairs={{0,32},{32,64},{64,96},{96,0},{1,33},{33,65},{65,97},{97,1},{2,34}... | collective-permute-start | bytes 786440 | tf_op jit(solution)/shard_map/ppermute | solution.py:235
  39.3 34.2 %collective-permute-start.10 = (bf16[1024,512]{1,0:T(8,128)(2,1)}, bf16[1024,512]{1,0:T(8,128)(2,1)S(1)}, u32[]{:S(2)}, u32[]{:S(2)}) collective-permute-start(bf16[1024,512]{1,0:T(8,128)(2,1)} %get-tuple-element.45), channel_id=1, source_target_pairs={{0,2},{1,3},{2,0},{3,1},{4,6},{5,7},{6,4},{7,5},{8,10},{9,11},{10,... | collective-permute-start | bytes 3145736 | tf_op jit(solution)/shard_map/ppermute | solution.py:50
  41.5 32.0 %collective-permute-start.6 = (bf16[512,512]{1,0:T(8,128)(2,1)S(1)}, bf16[512,512]{1,0:T(8,128)(2,1)S(1)}, u32[]{:S(2)}, u32[]{:S(2)}) collective-permute-start(bf16[512,512]{1,0:T(8,128)(2,1)S(1)} %slice.12), channel_id=1, source_target_pairs={{0,1},{1,2},{2,3},{3,0},{4,5},{5,6},{6,7},{7,4},{8,9},{9,10},{10,1... | collective-permute-start | bytes 1572872 | tf_op jit(solution)/shard_map/ppermute | solution.py:50
  42.7 30.9 %collective-permute-start.7 = (bf16[512,512]{1,0:T(8,128)(2,1)S(1)}, bf16[512,512]{1,0:T(8,128)(2,1)S(1)}, u32[]{:S(2)}, u32[]{:S(2)}) collective-permute-start(bf16[512,512]{1,0:T(8,128)(2,1)S(1)} %slice.13), channel_id=1, source_target_pairs={{0,3},{1,0},{2,1},{3,2},{4,7},{5,4},{6,5},{7,6},{8,11},{9,8},{10,9... | collective-permute-start | bytes 1572872 | tf_op jit(solution)/shard_map/ppermute | solution.py:50
  43.7 26.8 %collective-permute-start.8 = (bf16[256,512]{1,0:T(8,128)(2,1)S(1)}, bf16[256,512]{1,0:T(8,128)(2,1)S(1)}, u32[]{:S(2)}, u32[]{:S(2)}) collective-permute-start(bf16[256,512]{1,0:T(8,128)(2,1)S(1)} %get-tuple-element.43), channel_id=1, source_target_pairs={{0,1},{1,2},{2,3},{3,0},{4,5},{5,6},{6,7},{7,4},{8,9},{9,10},{10,1... | collective-permute-start | bytes 786440 | tf_op jit(solution)/shard_map/ppermute | solution.py:50
  44.8 28.8 %collective-permute-start.9 = (bf16[256,512]{1,0:T(8,128)(2,1)S(1)}, bf16[256,512]{1,0:T(8,128)(2,1)S(1)}, u32[]{:S(2)}, u32[]{:S(2)}) collective-permute-start(bf16[256,512]{1,0:T(8,128)(2,1)S(1)} %get-tuple-element.44), channel_id=1, source_target_pairs={{0,3},{1,0},{2,1},{3,2},{4,7},{5,4},{6,5},{7,6},{8,11},{9,8},{10,9... | collective-permute-start | bytes 786440 | tf_op jit(solution)/shard_map/ppermute | solution.py:50
  76.2 15.0 %collective-permute-start.11 = (f16[2064,128]{1,0:T(8,128)(2,1)S(1)}, f16[2064,128]{1,0:T(8,128)(2,1)S(1)}, u32[]{:S(2)}, u32[]{:S(2)}) collective-permute-start(f16[2064,128]{1,0:T(8,128)(2,1)S(1)} %convert_element_type.27), channel_id=1, source_target_pairs={{0,4},{1,5},{2,6},{3,7},{4,8},{5,9},{6,10},{7,11},{8,12},{9,13},{1... | collective-permute-start | bytes 1585160 | tf_op jit(solution)/shard_map/ppermute | solution.py:50
  76.8 14.5 %collective-permute-start.12 = (f16[2064,128]{1,0:T(8,128)(2,1)S(1)}, f16[2064,128]{1,0:T(8,128)(2,1)S(1)}, u32[]{:S(2)}, u32[]{:S(2)}) collective-permute-start(f16[2064,128]{1,0:T(8,128)(2,1)S(1)} %convert_element_type.29), channel_id=1, source_target_pairs={{0,8},{1,9},{2,10},{3,11},{4,12},{5,13},{6,14},{7,15},{8,0},{9,1},... | collective-permute-start | bytes 1585160 | tf_op jit(solution)/shard_map/ppermute | solution.py:50
  77.6 15.9 %collective-permute-start.13 = (f16[2064,128]{1,0:T(8,128)(2,1)S(1)}, f16[2064,128]{1,0:T(8,128)(2,1)S(1)}, u32[]{:S(2)}, u32[]{:S(2)}) collective-permute-start(f16[2064,128]{1,0:T(8,128)(2,1)S(1)} %convert_element_type.31), channel_id=1, source_target_pairs={{0,12},{1,13},{2,14},{3,15},{4,0},{5,1},{6,2},{7,3},{8,4},{9,5},{1... | collective-permute-start | bytes 1585160 | tf_op jit(solution)/shard_map/ppermute | solution.py:50
  94.1 13.2 %collective-permute-start.14 = (f16[1040,128]{1,0:T(8,128)(2,1)S(1)}, f16[1040,128]{1,0:T(8,128)(2,1)S(1)}, u32[]{:S(2)}, u32[]{:S(2)}) collective-permute-start(f16[1040,128]{1,0:T(8,128)(2,1)S(1)} %convert_element_type.33), channel_id=1, source_target_pairs={{0,16},{16,0},{1,17},{17,1},{2,18},{18,2},{3,19},{19,3},{4,20},{20... | collective-permute-start | bytes 798728 | tf_op jit(solution)/shard_map/ppermute | solution.py:267

commit v4 on v0

v4 whole, which is shorter than its diff:
```python
import functools

import jax
import jax.numpy as jnp
from jax import lax
from jax.experimental import pallas as pl
from jax.experimental.pallas import tpu as pltpu
from jax.sharding import Mesh
from jax.sharding import PartitionSpec as P

F32 = jnp.float32
F16 = jnp.float16
BF16 = jnp.bfloat16
RING = 4
LANES = 128
TAIL = 16
TOP = 15
TINY = 1e-30
ENTRY_LIMIT = 40
SECOND_LIMIT = 40


def section():
    return lax.axis_index("section")


def on_last():
    return section() == lax.axis_size("section") - 1


def block_start(z_off, along, across):
    first = section() == 0
    y_off, x_off = jnp.where(first, across, along), jnp.where(first, along, across)
    z = lax.rem(lax.axis_index("z_hi") + z_off, 2)
    y = lax.rem(lax.axis_index("y") + y_off, RING)
    x = lax.rem(lax.axis_index("x") + x_off, RING)
    return pl.multiple_of((z * (RING * RING) + y * RING + x) * LANES, LANES)


def pairs_over(along, by):
    size, pairs = RING * RING, []
    for s in range(2):
        for y in range(RING):
            for x in range(RING):
                on_x = (s == 0) == along
                there = (y, (x + by) % RING) if on_x else ((y + by) % RING, x)
                pairs.append((s * size + y * RING + x, s * size + there[0] * RING + there[1]))
    return pairs


def shifted(value, along, by):
    return lax.ppermute(value, ("section", "y", "x"), pairs_over(along, by))


def whole(n=1):
    return [pl.BlockSpec(memory_space=pltpu.VMEM)] * n


def in_hbm(value):
    return pltpu.with_memory_space_constraint(value, pltpu.HBM)


def call(kernel, out_shapes, operands, specs, scratch=(), flops=0, moved=0, limit=32):
    return pl.pallas_call(
        kernel,
        out_shape=[jax.ShapeDtypeStruct(s, t) for s, t in out_shapes],
        in_specs=specs,
        out_specs=whole(len(out_shapes)),
        scratch_shapes=list(scratch),
        compiler_params=pltpu.CompilerParams(vmem_limit_bytes=limit * 2**20),
        cost_estimate=pl.CostEstimate(flops=flops, bytes_accessed=moved, transcendentals=0),
    )(*operands)


CONTRACT_LAST = (((1,), (1,)), ((), ()))


def entry_kernel(pending_ref, x_ref, stash_ref, head_ref, weight_ref, right_ref, left_ref, own_ref, first_ref, pieces_ref,
                 x_in, stash_in, head_in, weight_in, sems, count_in):
    micro, rows, width = x_ref.shape
    half = width // 2
    counts = pltpu.make_async_copy(pending_ref, count_in, sems.at[micro + 5])
    counts.start()
    pieces = [(x_ref, x_in)]
    pieces += [(stash_ref.at[m], stash_in.at[m]) for m in range(micro - 1)] + [(head_ref, head_in)]
    parts = 4
    share = width // parts
    pieces += [(weight_ref.at[pl.ds(i * share, share)], weight_in.at[i]) for i in range(parts)]
    copies = [pltpu.make_async_copy(a, b, sems.at[i]) for i, (a, b) in enumerate(pieces)]
    stashes, weights = copies[1:1 + micro], copies[1 + micro:]
    for copy in copies[:1 + micro]:
        copy.start()
    copies[0].wait()
    weights[0].start()
    counts.wait()
    count = count_in[section()]
    for m in range(micro):
        turned = jnp.where(m >= micro - count, x_in[m].astype(F32), 0.0).T.astype(BF16)
        lanes = slice(m * rows, (m + 1) * rows)
        for out, order in ((right_ref, (half, 0)), (left_ref, (0, half))):
            for at, top in zip((0, half), order):
                out[at:at + half, lanes] = turned[top:top + half]
    full = micro * rows
    plans = [(right_ref, width, 0, 2), (left_ref, width, 1, 2)]
    for z in range(2):
        plans += [(right_ref, width + (1 + z) * full, z, 1), (left_ref, width + (1 + z) * full, z, RING - 1), (own_ref, z * full, z, 0)]
    for m in range(micro):
        stashes[m].wait()
        if m < parts - 1:
            weights[m + 1].start()
        source = stash_in.at[m] if m < micro - 1 else head_in
        for out, base, z, along in plans:
            for b in range(RING):
                top = base + m * rows
                out[top:top + rows, b * LANES:(b + 1) * LANES] = source[:, pl.ds(block_start(z, along, b), LANES)]
    for i in range(parts):
        weights[i].wait()
        out = lax.dot_general(head_in[...], weight_in[i], CONTRACT_LAST, preferred_element_type=F32)
        first_ref[:, i * share:(i + 1) * share] = out
    for p in range(RING):
        x_at = lax.rem(lax.axis_index("x") + p, RING)
        for inner in range(2):
            cols = pl.ds(pl.multiple_of((inner * RING + x_at) * LANES, LANES), LANES)
            pieces_ref[p * rows:(p + 1) * rows, inner * LANES:(inner + 1) * LANES] = first_ref[:, cols].astype(BF16)


def halves(ref, half, swapped):
    return (ref.at[half:2 * half], ref.at[0:half]) if swapped else (ref.at[0:half], ref.at[half:2 * half])


def early_kernel(depth, mine_ref, own_ref, left_ref, right_ref, acc_ref):
    width, full = acc_ref.shape[0], own_ref.shape[0] // 2
    half, lanes = width // 2, acc_ref.shape[1] // 2
    sides = [halves(mine_ref, half, True), halves(left_ref, half, True), halves(right_ref, half, False)]
    for r in range(2):
        lhs = jnp.concatenate([side[r][:, :depth] for side in sides], axis=1)
        for z in range(2):
            rhs = [own_ref[z * full:z * full + depth, :]]
            at = width + (1 + z) * full
            rhs = jnp.concatenate(rhs + [ref[at:at + depth, :] for ref in (left_ref, right_ref)], axis=0)
            acc_ref[r * half:(r + 1) * half, z * lanes:(z + 1) * lanes] = jnp.dot(lhs, rhs, preferred_element_type=F32)


def late_kernel(depth, acc_ref, mine_ref, own_ref, left_ref, right_ref, upper_ref, lower_ref, chain_ref, keep_ref, *rest):
    sends, sum_ref, last_ref = rest[:-2], rest[-2], rest[-1]
    width, full = acc_ref.shape[0], own_ref.shape[0] // 2
    half, lanes, rows = width // 2, acc_ref.shape[1] // 2, own_ref.shape[0] // 2 - depth
    tensor = lax.axis_index("z_lo")
    far = (upper_ref, lower_ref)
    for z in range(2):
        at = width + (1 + z) * full
        given = [own_ref[z * full + depth:(z + 1) * full, :], left_ref[at + depth:at + full, :],
                 far[z][half + depth:half + full, :], right_ref[at + depth:at + full, :]]
        for b in range(RING):
            z_at = lax.rem(lax.axis_index("z_hi") + z, 2)
            y_at = lax.rem(lax.axis_index("y") + b, RING)
            turn = lax.rem(tensor - (z_at * 2 + lax.div(y_at, 2)) + RING, RING)
            inner = pl.multiple_of(lax.rem(y_at, 2) * LANES, LANES)
            cols = slice(b * LANES, (b + 1) * LANES)
            for p in range(RING):
                chained = chain_ref[turn, p * rows:(p + 1) * rows, pl.ds(inner, LANES)]
                last_ref[z, p * rows:(p + 1) * rows, cols] = jnp.where(on_last(), given[p][:, cols], chained)
    mine, left, right = halves(mine_ref, half, True), halves(left_ref, half, True), halves(right_ref, half, False)
    largest = jnp.full((1, lanes), TINY, F32)
    for r in range(2):
        lhs = [mine[r][:, depth:], left[r][:, depth:], far[r][:half, depth:], right[r][:, depth:], far[r][:half, :depth]]
        lhs = jnp.concatenate(lhs, axis=1)
        for z in range(2):
            rhs = jnp.concatenate([last_ref[z], far[z][half:half + depth, :]], axis=0)
            total = acc_ref[r * half:(r + 1) * half, z * lanes:(z + 1) * lanes]
            total = total + jnp.dot(lhs, rhs, preferred_element_type=F32)
            largest = jnp.maximum(largest, jnp.max(jnp.abs(total), axis=0, keepdims=True))
            sum_ref[r * half:(r + 1) * half, z * lanes:(z + 1) * lanes] = total
    power = jnp.ceil(jnp.log2(jnp.max(largest, axis=1, keepdims=True))) - TOP
    power = jnp.broadcast_to(power, (1, LANES))
    factor = jnp.exp2(-power)
    for z in range(2):
        keep_ref[z * width:(z + 1) * width, :] = sum_ref[:, z * lanes:z * lanes + LANES]
        for b, out in enumerate(sends, 1):
            cols = slice(z * lanes + b * LANES, z * lanes + (b + 1) * LANES)
            out[z * width:(z + 1) * width, :] = sum_ref[:, cols] * factor
    for out in sends:
        out[2 * width:, :] = jnp.broadcast_to(power, (TAIL, LANES))


def combine_kernel(keep_ref, one_ref, two_ref, three_ref, near_ref, far_ref):
    rows = near_ref.shape[0]
    totals = []
    for z in range(2):
        total = keep_ref[z * rows:(z + 1) * rows, :]
        for ref in (one_ref, two_ref, three_ref):
            total = total + ref[z * rows:(z + 1) * rows, :] * jnp.exp2(ref[2 * rows:2 * rows + 1, :])
        totals.append(total)
    near_ref[...] = totals[0]
    largest = jnp.maximum(jnp.max(jnp.abs(totals[1]), axis=0, keepdims=True), TINY)
    power = jnp.ceil(jnp.log2(jnp.max(largest, axis=1, keepdims=True))) - TOP
    power = jnp.broadcast_to(power, (1, LANES))
    far_ref[:rows, :] = totals[1] * jnp.exp2(-power)
    far_ref[rows:, :] = jnp.broadcast_to(power, (TAIL, LANES))


def second_kernel(own_ref, near_ref, far_ref, first_ref, weight_ref, out_ref, whole_ref, weight_in, sems):
    rows, size = out_ref.shape[0], own_ref.shape[0]
    parts, share = weight_in.shape[:2]
    copies = [pltpu.make_async_copy(weight_ref.at[pl.ds(i * share, share)], weight_in.at[i], sems.at[i]) for i in range(parts)]
    for copy in copies:
        copy.start()
    for j in range(RING):
        ref, base = ((own_ref, 0), (near_ref, 0), (far_ref, 0), (far_ref, size))[j]
        owner = jnp.bitwise_xor(lax.axis_index("z_lo"), j)
        for p in range(RING):
            x_at = lax.rem(lax.axis_index("x") + p, RING)
            for inner in range(2):
                at = pl.multiple_of(((owner * 2 + inner) * RING + x_at) * LANES, LANES)
                piece = ref[base + p * rows:base + (p + 1) * rows, inner * LANES:(inner + 1) * LANES]
                whole_ref[:, pl.ds(at, LANES)] = piece
    for i in range(parts):
        copies[i].wait()
        out = lax.dot_general(whole_ref[...], weight_in[i], CONTRACT_LAST, preferred_element_type=F32)
        cols = slice(i * share, (i + 1) * share)
        out_ref[:, cols] = jnp.where(on_last(), first_ref[:, cols], out)


def on_first(value, axis, by):
    return lax.ppermute(value, ("section", axis), [(i, (i + by) % RING) for i in range(RING)])


def swapped(value, bit):
    return lax.ppermute(value, ("section", "z_lo"), [(i, i ^ bit) for i in range(RING)])


def local(weights, stash_in, stash_grad, head_grad, pending):
    inputs, grads = stash_in[0], stash_grad[0]
    micro, rows, width = inputs.shape
    full, depth, half, lanes = micro * rows, (micro - 1) * rows, width // 2, RING * LANES
    columns = head_grad.shape[1]
    hbm = pl.BlockSpec(memory_space=pltpu.HBM)

    held = [pltpu.VMEM((4, width // 4, columns), BF16), pltpu.SemaphoreType.DMA((micro + 6,))]
    matmul = dict(flops=2 * rows * width * columns, moved=10 * 2**20)
    side = ((width + 3 * full, lanes), BF16)
    right, left, own, first, pieces = call(
        entry_kernel, [side, side, ((2 * full, lanes), BF16), ((rows, width), F32), ((full, 2 * LANES), BF16)],
        [in_hbm(v) for v in (pending, inputs, grads, head_grad, weights[0])], [hbm] * 5,
        scratch=[pltpu.VMEM(inputs.shape, BF16), pltpu.VMEM(grads.shape, BF16), pltpu.VMEM(head_grad.shape, BF16)] + held
        + [pltpu.SMEM(pending.shape, pending.dtype)],
        limit=ENTRY_LIMIT, **matmul,
    )
    from_left, from_right = shifted(right, True, 1), shifted(left, True, -1)

    pieces = lax.ppermute(pieces, "section", [(1, 0)])
    gathered = [pieces[:rows]]
    for by in range(1, RING):
        gathered.append(on_first(pieces[by * rows:(by + 1) * rows], "x", by))
    gathered = jnp.concatenate(gathered, 0)
    chain = [gathered] + [on_first(gathered, "z_lo", by) for by in range(1, RING)]
    from_left, from_right, *chain = lax.optimization_barrier((from_left, from_right, *chain))

    upper = shifted(from_left[half:width + full], True, 1)
    lower = shifted(from_right[half:width + full], True, -1)
    (acc,) = call(
        functools.partial(early_kernel, depth), [((width, 2 * lanes), F32)], (right, own, from_left, from_right), whole(4),
        flops=2 * width * 2 * lanes * 3 * depth, moved=12 * 2**20,
    )
    acc, pieces, *chain = lax.optimization_barrier((acc, pieces, *chain))
    near_pieces = swapped(pieces, 1)
    far_pieces = swapped(jnp.concatenate([pieces, near_pieces], 0), 2)
    send = ((2 * width + TAIL, LANES), F32)
    keep, *sends = call(
        functools.partial(late_kernel, depth), [((2 * width, LANES), F32)] + [send] * 3,
        (acc, right, own, from_left, from_right, upper, lower, jnp.stack(chain, 0)), whole(8),
        scratch=[pltpu.VMEM((width, 2 * lanes), F32), pltpu.VMEM((2, full, lanes), BF16)],
        flops=2 * width * 2 * lanes * (3 * rows + full), moved=12 * 2**20,
    )
    got = [shifted(s.astype(F16), False, by).astype(F32) for by, s in enumerate(sends, 1)]
    near, far = call(
        combine_kernel, [((width, LANES), F32), ((width + TAIL, LANES), F32)], (keep, *got), whole(4), moved=6 * 2**20,
    )
    far = far.astype(F16)
    far, pieces, near_pieces, far_pieces = lax.optimization_barrier((far, pieces, near_pieces, far_pieces))
    other = lax.ppermute(far, "z_hi", [(0, 1), (1, 0)])
    (second,) = call(
        second_kernel, [((rows, width), F32)], (pieces, near_pieces, far_pieces, first, in_hbm(weights[0])), whole(4) + [hbm],
        scratch=[pltpu.VMEM((rows, columns), BF16)] + held, limit=SECOND_LIMIT, **matmul,
    )
    block = near + other[:width].astype(F32) * jnp.exp2(other[width:width + 1].astype(F32))
    return (second[None], block[None])


def solution(mesh):
    fine = Mesh(mesh.devices.reshape(2, 4, 2, 4, 4), ("section", "z_lo", "z_hi", "y", "x"))
    dp = ("z_hi", "y", "x")
    return jax.shard_map(
        local,
        mesh=fine,
        in_specs=(
            P("section", "z_lo", None),
            P("section", None, dp, "z_lo"),
            P("section", None, dp, None),
            P(dp, None),
            P(),
        ),
        out_specs=(P("section", dp, "z_lo"), P("section", "z_lo", dp)),
        check_vma=False,
    )
```

time: 477 us -> 132 us (0.28)
  the two profiles are of different devices: /device:TPU:64 before, /device:TPU:24 now
where the time goes in v4:
time: 132 us; the launch traced here: 131 us
  waiting for transfers between devices  58.3 us (44%)
  starting transfers between devices  47.8 us (36%)
  Pallas kernels  22.6 us (17%)
  other arithmetic  1.51 us (1%)
    ppermute x6, waiting for transfers between devices, on_first(): lax.ppermute(value, ('section', axis), [(i, (i + by) % RING) for i in ran...  29.3 us
    pallas_call x5, Pallas kernels, call(): pl.pallas_call(kernel, out_shape=[jax.ShapeDtypeStruct(s, t) for s, t in...  22.6 us
    ppermute x7, waiting for transfers between devices, shifted(): return lax.ppermute(value, ('section', 'y', 'x'), pairs_over(along, by))  21.6 us
    ppermute x6, starting transfers between devices, on_first(): lax.ppermute(value, ('section', axis), [(i, (i + by) % RING) for i in ran...  20.9 us
    ppermute x7, starting transfers between devices, shifted(): return lax.ppermute(value, ('section', 'y', 'x'), pairs_over(along, by))  11 us
    ppermute x2, starting transfers between devices, swapped(): lax.ppermute(value, ('section', 'z_lo'), [(i, i ^ bit) for i in range(RIN...  7.59 us
    ppermute x1, starting transfers between devices, local(): other = lax.ppermute(far, 'z_hi', [(0, 1), (1, 0)])  7.11 us
    ppermute x2, waiting for transfers between devices, swapped(): lax.ppermute(value, ('section', 'z_lo'), [(i, i ^ bit) for i in range(RIN...  5.21 us
  transfers between devices with their start and end apart: 17, of which 9 were waited for; matrix products, arithmetic and copies ran while one was open for 1% of the time, Pallas kernels for 11%

profile of v4, /device:TPU:24, one launch (start us, length us, event | category | flops | bytes accessed | tf_op | source)
XLA Modules:
  0.0 131.2 jit_solution(8939028697073000661)
XLA Ops:
  0.6 8.6 %shard_map.68 = (bf16[2560,512]{1,0:T(8,128)(2,1)S(1)}, bf16[2560,512]{1,0:T(8,128)(2,1)S(1)}, bf16[1024,512]{1,0:T(8,128)(2,1)S(1)}, f32[128,1024]{1,0:T(8,128)S(1)}, bf16[512,256]{1,0:T(8,128)(2,1)S(1)}) custom-call(s32[2]{0:T(128)} %pending_ref.1, bf16[4,128,1024]{2,1,0:T(8,128)(2,1)} %bitcast.16, bf16[3,128,4096]{2,1,0:T(8,128)(2,1)} %bitcast.14, ...), custom_call_target="tpu_custom_call" | custom-call | flops 1073741824 | bytes 10485760 | tf_op jit(solution)/shard_map/pallas_call | solution.py:64
  9.3 2.8 %collective-permute-start.1 = (bf16[2560,512]{1,0:T(8,128)(2,1)S(1)}, bf16[2560,512]{1,0:T(8,128)(2,1)S(1)}, u32[]{:S(2)}, u32[]{:S(2)}) collective-permute-start(bf16[2560,512]{1,0:T(8,128)(2,1)S(1)} %get-tuple-element.31), channel_id=1, source_target_pairs={{0,3},{1,0},{2,1},{3,2},{4,7},{5,4},{6,5},{7,6},{8,11},{9,8},{10,9... | collective-permute-start | bytes 7864328 | tf_op jit(solution)/shard_map/ppermute | solution.py:52
  12.1 0.0 collective-permute-start
  12.1 1.3 collective-permute-start.2
  13.4 2.1 %collective-permute-done.2.own_ref = bf16[512,256]{1,0:T(8,128)(2,1)S(1)} collective-permute-done((bf16[512,256]{1,0:T(8,128)(2,1)S(1)}, bf16[512,256]{1,0:T(8,128)(2,1)S(1)}, u32[]{:S(2)}, u32[]{:S(2)}) %collective-permute-start.2) | collective-permute-done | bytes 262176 | tf_op jit(solution)/shard_map/ppermute | solution.py:251
  15.6 5.1 %collective-permute-start.5 = (bf16[128,256]{1,0:T(8,128)(2,1)S(1)}, bf16[128,256]{1,0:T(8,128)(2,1)S(1)}, u32[]{:S(2)}, u32[]{:S(2)}) collective-permute-start(bf16[128,256]{1,0:T(8,128)(2,1)S(1)} %get-tuple-element.57), channel_id=1, source_target_pairs={{0,3},{1,0},{2,1},{3,2},{4,7},{5,4},{6,5},{7,6},{8,11},{9,8},{10,9... | collective-permute-start | bytes 196616 | tf_op jit(solution)/shard_map/ppermute | solution.py:225
  20.7 1.9 %collective-permute-start.4 = (bf16[128,256]{1,0:T(8,128)(2,1)S(1)}, bf16[128,256]{1,0:T(8,128)(2,1)S(1)}, u32[]{:S(2)}, u32[]{:S(2)}) collective-permute-start(bf16[128,256]{1,0:T(8,128)(2,1)S(1)} %get-tuple-element.58), channel_id=1, source_target_pairs={{0,2},{1,3},{2,0},{3,1},{4,6},{5,7},{6,4},{7,5},{8,10},{9,11},{10,... | collective-permute-start | bytes 196616 | tf_op jit(solution)/shard_map/ppermute | solution.py:225
  22.6 2.8 %collective-permute-start.3 = (bf16[128,256]{1,0:T(8,128)(2,1)S(1)}, bf16[128,256]{1,0:T(8,128)(2,1)S(1)}, u32[]{:S(2)}, u32[]{:S(2)}) collective-permute-start(bf16[128,256]{1,0:T(8,128)(2,1)S(1)} %get-tuple-element.59), channel_id=1, source_target_pairs={{0,1},{1,2},{2,3},{3,0},{4,5},{5,6},{6,7},{7,4},{8,9},{9,10},{10,1... | collective-permute-start | bytes 196616 | tf_op jit(solution)/shard_map/ppermute | solution.py:225
  25.4 17.3 %collective-permute-done.5 = bf16[128,256]{1,0:T(8,128)(2,1)S(1)} collective-permute-done((bf16[128,256]{1,0:T(8,128)(2,1)S(1)}, bf16[128,256]{1,0:T(8,128)(2,1)S(1)}, u32[]{:S(2)}, u32[]{:S(2)}) %collective-permute-start.5) | collective-permute-done | bytes 65568 | tf_op jit(solution)/shard_map/ppermute | solution.py:225
  42.7 2.1 %collective-permute-done.4 = bf16[128,256]{1,0:T(8,128)(2,1)S(1)} collective-permute-done((bf16[128,256]{1,0:T(8,128)(2,1)S(1)}, bf16[128,256]{1,0:T(8,128)(2,1)S(1)}, u32[]{:S(2)}, u32[]{:S(2)}) %collective-permute-start.4) | collective-permute-done | bytes 65568 | tf_op jit(solution)/shard_map/ppermute | solution.py:225
  44.8 1.5 %collective-permute-done.3 = bf16[128,256]{1,0:T(8,128)(2,1)S(1)} collective-permute-done((bf16[128,256]{1,0:T(8,128)(2,1)S(1)}, bf16[128,256]{1,0:T(8,128)(2,1)S(1)}, u32[]{:S(2)}, u32[]{:S(2)}) %collective-permute-start.3) | collective-permute-done | bytes 65568 | tf_op jit(solution)/shard_map/ppermute | solution.py:225
  46.4 6.5 %collective-permute-start.8 = (bf16[512,256]{1,0:T(8,128)(2,1)S(1)}, bf16[512,256]{1,0:T(8,128)(2,1)S(1)}, u32[]{:S(2)}, u32[]{:S(2)}) collective-permute-start(bf16[512,256]{1,0:T(8,128)(2,1)S(1)} %pad_maximum_fusion.2), channel_id=1, source_target_pairs={{0,96},{32,0},{64,32},{96,64},{1,97},{33,1},{65,33},{97,65},{2,98}... | collective-permute-start | bytes 786440 | tf_op jit(solution)/shard_map/ppermute | solution.py:225
  52.9 1.9 %collective-permute-start.7 = (bf16[512,256]{1,0:T(8,128)(2,1)S(1)}, bf16[512,256]{1,0:T(8,128)(2,1)S(1)}, u32[]{:S(2)}, u32[]{:S(2)}) collective-permute-start(bf16[512,256]{1,0:T(8,128)(2,1)S(1)} %pad_maximum_fusion.2), channel_id=1, source_target_pairs={{0,64},{32,96},{64,0},{96,32},{1,65},{33,97},{65,1},{97,33},{2,66}... | collective-permute-start | bytes 786440 | tf_op jit(solution)/shard_map/ppermute | solution.py:225
  54.9 2.6 %collective-permute-start.6 = (bf16[512,256]{1,0:T(8,128)(2,1)S(1)}, bf16[512,256]{1,0:T(8,128)(2,1)S(1)}, u32[]{:S(2)}, u32[]{:S(2)}) collective-permute-start(bf16[512,256]{1,0:T(8,128)(2,1)S(1)} %pad_maximum_fusion.2), channel_id=1, source_target_pairs={{0,32},{32,64},{64,96},{96,0},{1,33},{33,65},{65,97},{97,1},{2,34}... | collective-permute-start | bytes 786440 | tf_op jit(solution)/shard_map/ppermute | solution.py:225
  57.4 0.0 collective-permute-done.8
  57.5 8.3 %collective-permute-done.7 = bf16[512,256]{1,0:T(8,128)(2,1)S(1)} collective-permute-done((bf16[512,256]{1,0:T(8,128)(2,1)S(1)}, bf16[512,256]{1,0:T(8,128)(2,1)S(1)}, u32[]{:S(2)}, u32[]{:S(2)}) %collective-permute-start.7) | collective-permute-done | bytes 262176 | tf_op jit(solution)/shard_map/ppermute | solution.py:225
  65.8 0.0 collective-permute-done.6
  65.8 0.0 collective-permute-done.1.right_ref
  65.8 0.0 collective-permute-done.left_ref
  65.8 0.1 slice.28
  65.9 0.1 slice.29
  66.0 0.1 collective-permute-start.10
  66.1 2.0 %collective-permute-start.9 = (bf16[1024,512]{1,0:T(8,128)(2,1)S(1)}, bf16[1024,512]{1,0:T(8,128)(2,1)S(1)}, u32[]{:S(2)}, u32[]{:S(2)}) collective-permute-start(bf16[1024,512]{1,0:T(8,128)(2,1)S(1)} %slice.28), channel_id=1, source_target_pairs={{0,1},{1,2},{2,3},{3,0},{4,5},{5,6},{6,7},{7,4},{8,9},{9,10},{10,1... | collective-permute-start | bytes 3145736 | tf_op jit(solution)/shard_map/ppermute | solution.py:52
  68.1 2.9 %shard_map.69.acc_ref = f32[1024,1024]{1,0:T(8,128)S(1)} custom-call(bf16[2560,512]{1,0:T(8,128)(2,1)S(1)} %get-tuple-element.29.mine_ref, bf16[1024,512]{1,0:T(8,128)(2,1)S(1)} %get-tuple-element.30.own_ref, bf16[2560,512]{1,0:T(8,128)(2,1)S(1)} %collective-permute-done.left_ref, bf16[2560,512]{1,0:T(8,128)(2,1)S(1)} %collective-permute-done.1.right_ref), custom_call_target="tpu_custom_call" | custom-call | flops 2415919104 | bytes 12582912 | tf_op jit(solution)/shard_map/pallas_call | solution.py:64
  70.9 2.8 %collective-permute-start.14 = (bf16[512,256]{1,0:T(8,128)(2,1)S(1)}, bf16[512,256]{1,0:T(8,128)(2,1)S(1)}, u32[]{:S(2)}, u32[]{:S(2)}) collective-permute-start(bf16[512,256]{1,0:T(8,128)(2,1)S(1)} %collective-permute-done.2.own_ref), channel_id=1, source_target_pairs={{0,32},{32,0},{64,96},{96,64},{1,33},{33,1},{65,97},{97,65},{2,34}... | collective-permute-start | bytes 786440 | tf_op jit(solution)/shard_map/ppermute | solution.py:229
  73.8 0.1 pad_maximum_fusion.chain_ref
  73.9 11.1 %collective-permute-done.10.lower_ref = bf16[1024,512]{1,0:T(8,128)(2,1)S(1)} collective-permute-done((bf16[1024,512]{1,0:T(8,128)(2,1)S(1)}, bf16[1024,512]{1,0:T(8,128)(2,1)S(1)}, u32[]{:S(2)}, u32[]{:S(2)}) %collective-permute-start.10) | collective-permute-done | bytes 1048608 | tf_op jit(solution)/shard_map/ppermute | solution.py:52
  85.0 3.7 %collective-permute-done.9.upper_ref = bf16[1024,512]{1,0:T(8,128)(2,1)S(1)} collective-permute-done((bf16[1024,512]{1,0:T(8,128)(2,1)S(1)}, bf16[1024,512]{1,0:T(8,128)(2,1)S(1)}, u32[]{:S(2)}, u32[]{:S(2)}) %collective-permute-start.9) | collective-permute-done | bytes 1048608 | tf_op jit(solution)/shard_map/ppermute | solution.py:52
  88.7 2.8 %shard_map.70 = (f32[2048,128]{1,0:T(8,128)S(1)}, f32[2064,128]{1,0:T(8,128)S(1)}, f32[2064,128]{1,0:T(8,128)S(1)}, f32[2064,128]{1,0:T(8,128)S(1)}) custom-call(f32[1024,1024]{1,0:T(8,128)S(1)} %shard_map.69.acc_ref, bf16[2560,512]{1,0:T(8,128)(2,1)S(1)} %get-tuple-element.29.mine_ref, bf16[1024,512]{1,0:T(8,128)(2,1)S(1)} %get-tuple-element.30.own_ref, ...), custom_call_target="tpu_custom_call" | custom-call | flops 1879048192 | bytes 12582912 | tf_op jit(solution)/shard_map/pallas_call | solution.py:64
  91.5 0.1 convert_element_type.27
  91.6 0.1 convert_element_type.29
  91.7 0.1 convert_element_type.31
  91.8 1.6 %collective-permute-start.13 = (f16[2064,128]{1,0:T(8,128)(2,1)S(1)}, f16[2064,128]{1,0:T(8,128)(2,1)S(1)}, u32[]{:S(2)}, u32[]{:S(2)}) collective-permute-start(f16[2064,128]{1,0:T(8,128)(2,1)S(1)} %convert_element_type.31), channel_id=1, source_target_pairs={{0,12},{1,13},{2,14},{3,15},{4,0},{5,1},{6,2},{7,3},{8,4},{9,5},{1... | collective-permute-start | bytes 1585160 | tf_op jit(solution)/shard_map/ppermute | solution.py:52
  93.3 3.3 %collective-permute-start.12 = (f16[2064,128]{1,0:T(8,128)(2,1)S(1)}, f16[2064,128]{1,0:T(8,128)(2,1)S(1)}, u32[]{:S(2)}, u32[]{:S(2)}) collective-permute-start(f16[2064,128]{1,0:T(8,128)(2,1)S(1)} %convert_element_type.29), channel_id=1, source_target_pairs={{0,8},{1,9},{2,10},{3,11},{4,12},{5,13},{6,14},{7,15},{8,0},{9,1},... | collective-permute-start | bytes 1585160 | tf_op jit(solution)/shard_map/ppermute | solution.py:52
  96.6 1.1 collective-permute-start.11
  97.8 0.0 collective-permute-done.14.near_ref
  97.8 4.8 %collective-permute-start.15 = (bf16[1024,256]{1,0:T(8,128)(2,1)S(1)}, bf16[1024,256]{1,0:T(8,128)(2,1)S(1)}, u32[]{:S(2)}, u32[]{:S(2)}) collective-permute-start(bf16[1024,256]{1,0:T(8,128)(2,1)S(1)} %pad_maximum_fusion.1), channel_id=1, source_target_pairs={{0,64},{32,96},{64,0},{96,32},{1,65},{33,97},{65,1},{97,33},{2,66}... | collective-permute-start | bytes 1572872 | tf_op jit(solution)/shard_map/ppermute | solution.py:229
  102.6 0.0 collective-permute-done.13
  102.6 0.1 convert_element_type.32.three_ref
  102.7 6.8 %collective-permute-done.12 = f16[2064,128]{1,0:T(8,128)(2,1)S(1)} collective-permute-done((f16[2064,128]{1,0:T(8,128)(2,1)S(1)}, f16[2064,128]{1,0:T(8,128)(2,1)S(1)}, u32[]{:S(2)}, u32[]{:S(2)}) %collective-permute-start.12) | collective-permute-done | bytes 528416 | tf_op jit(solution)/shard_map/ppermute | solution.py:52
  109.5 0.1 convert_element_type.30.two_ref
  109.6 0.1 convert_element_type.28.one_ref
  109.7 0.5 shard_map.71
  110.2 5.2 %collective-permute-done.15.far_ref = bf16[1024,256]{1,0:T(8,128)(2,1)S(1)} collective-permute-done((bf16[1024,256]{1,0:T(8,128)(2,1)S(1)}, bf16[1024,256]{1,0:T(8,128)(2,1)S(1)}, u32[]{:S(2)}, u32[]{:S(2)}) %collective-permute-start.15) | collective-permute-done | bytes 524320 | tf_op jit(solution)/shard_map/ppermute | solution.py:229
  115.4 7.1 %collective-permute-start.16 = (f16[1040,128]{1,0:T(8,128)(2,1)S(1)}, f16[1040,128]{1,0:T(8,128)(2,1)S(1)}, u32[]{:S(2)}, u32[]{:S(2)}) collective-permute-start(f16[1040,128]{1,0:T(8,128)(2,1)S(1)} %convert_element_type.33), channel_id=1, source_target_pairs={{0,16},{16,0},{1,17},{17,1},{2,18},{18,2},{3,19},{19,3},{4,20},{20... | collective-permute-start | bytes 798728 | tf_op jit(solution)/shard_map/ppermute | solution.py:281
  122.5 7.8 %shard_map.72 = f32[128,1024]{1,0:T(8,128)} custom-call(bf16[512,256]{1,0:T(8,128)(2,1)S(1)} %collective-permute-done.2.own_ref, bf16[512,256]{1,0:T(8,128)(2,1)S(1)} %collective-permute-done.14.near_ref, bf16[1024,256]{1,0:T(8,128)(2,1)S(1)} %collective-permute-done.15.far_ref, f32[128,1024]{1,0:T(8,128)S(1)} %get-tuple-element.53.first_ref, ...), custom_call_target="tpu_custom_call" | custom-call | flops 1073741824 | bytes 10485760 | tf_op jit(solution)/shard_map/pallas_call | solution.py:64
  130.3 0.0 collective-permute-done.16
  130.3 0.9 add_bitcast_fusion
  (6 shorter events, 0.1 us)
Async XLA Ops:
  9.3 56.5 %collective-permute-start.1 = (bf16[2560,512]{1,0:T(8,128)(2,1)S(1)}, bf16[2560,512]{1,0:T(8,128)(2,1)S(1)}, u32[]{:S(2)}, u32[]{:S(2)}) collective-permute-start(bf16[2560,512]{1,0:T(8,128)(2,1)S(1)} %get-tuple-element.31), channel_id=1, source_target_pairs={{0,3},{1,0},{2,1},{3,2},{4,7},{5,4},{6,5},{7,6},{8,11},{9,8},{10,9... | collective-permute-start | bytes 7864328 | tf_op jit(solution)/shard_map/ppermute | solution.py:52
  12.1 53.7 %collective-permute-start = (bf16[2560,512]{1,0:T(8,128)(2,1)S(1)}, bf16[2560,512]{1,0:T(8,128)(2,1)S(1)}, u32[]{:S(2)}, u32[]{:S(2)}) collective-permute-start(bf16[2560,512]{1,0:T(8,128)(2,1)S(1)} %get-tuple-element.29.mine_ref), channel_id=1, source_target_pairs={{0,1},{1,2},{2,3},{3,0},{4,5},{5,6},{6,7},{7,4},{8,9},{9,10},{10,1... | collective-permute-start | bytes 7864328 | tf_op jit(solution)/shard_map/ppermute | solution.py:52
  12.1 3.4 %collective-permute-start.2 = (bf16[512,256]{1,0:T(8,128)(2,1)S(1)}, bf16[512,256]{1,0:T(8,128)(2,1)S(1)}, u32[]{:S(2)}, u32[]{:S(2)}) collective-permute-start(bf16[512,256]{1,0:T(8,128)(2,1)S(1)} %get-tuple-element.32), channel_id=1, source_target_pairs={{128,0},{129,1},{130,2},{131,3},{132,4},{133,5},{134,6},{135,7},{1... | collective-permute-start | bytes 786440 | tf_op jit(solution)/shard_map/ppermute | solution.py:251
  15.6 27.2 %collective-permute-start.5 = (bf16[128,256]{1,0:T(8,128)(2,1)S(1)}, bf16[128,256]{1,0:T(8,128)(2,1)S(1)}, u32[]{:S(2)}, u32[]{:S(2)}) collective-permute-start(bf16[128,256]{1,0:T(8,128)(2,1)S(1)} %get-tuple-element.57), channel_id=1, source_target_pairs={{0,3},{1,0},{2,1},{3,2},{4,7},{5,4},{6,5},{7,6},{8,11},{9,8},{10,9... | collective-permute-start | bytes 196616 | tf_op jit(solution)/shard_map/ppermute | solution.py:225
  20.7 24.1 %collective-permute-start.4 = (bf16[128,256]{1,0:T(8,128)(2,1)S(1)}, bf16[128,256]{1,0:T(8,128)(2,1)S(1)}, u32[]{:S(2)}, u32[]{:S(2)}) collective-permute-start(bf16[128,256]{1,0:T(8,128)(2,1)S(1)} %get-tuple-element.58), channel_id=1, source_target_pairs={{0,2},{1,3},{2,0},{3,1},{4,6},{5,7},{6,4},{7,5},{8,10},{9,11},{10,... | collective-permute-start | bytes 196616 | tf_op jit(solution)/shard_map/ppermute | solution.py:225
  22.6 23.7 %collective-permute-start.3 = (bf16[128,256]{1,0:T(8,128)(2,1)S(1)}, bf16[128,256]{1,0:T(8,128)(2,1)S(1)}, u32[]{:S(2)}, u32[]{:S(2)}) collective-permute-start(bf16[128,256]{1,0:T(8,128)(2,1)S(1)} %get-tuple-element.59), channel_id=1, source_target_pairs={{0,1},{1,2},{2,3},{3,0},{4,5},{5,6},{6,7},{7,4},{8,9},{9,10},{10,1... | collective-permute-start | bytes 196616 | tf_op jit(solution)/shard_map/ppermute | solution.py:225
  46.4 11.1 %collective-permute-start.8 = (bf16[512,256]{1,0:T(8,128)(2,1)S(1)}, bf16[512,256]{1,0:T(8,128)(2,1)S(1)}, u32[]{:S(2)}, u32[]{:S(2)}) collective-permute-start(bf16[512,256]{1,0:T(8,128)(2,1)S(1)} %pad_maximum_fusion.2), channel_id=1, source_target_pairs={{0,96},{32,0},{64,32},{96,64},{1,97},{33,1},{65,33},{97,65},{2,98}... | collective-permute-start | bytes 786440 | tf_op jit(solution)/shard_map/ppermute | solution.py:225
  52.9 12.9 %collective-permute-start.7 = (bf16[512,256]{1,0:T(8,128)(2,1)S(1)}, bf16[512,256]{1,0:T(8,128)(2,1)S(1)}, u32[]{:S(2)}, u32[]{:S(2)}) collective-permute-start(bf16[512,256]{1,0:T(8,128)(2,1)S(1)} %pad_maximum_fusion.2), channel_id=1, source_target_pairs={{0,64},{32,96},{64,0},{96,32},{1,65},{33,97},{65,1},{97,33},{2,66}... | collective-permute-start | bytes 786440 | tf_op jit(solution)/shard_map/ppermute | solution.py:225
  54.9 10.9 %collective-permute-start.6 = (bf16[512,256]{1,0:T(8,128)(2,1)S(1)}, bf16[512,256]{1,0:T(8,128)(2,1)S(1)}, u32[]{:S(2)}, u32[]{:S(2)}) collective-permute-start(bf16[512,256]{1,0:T(8,128)(2,1)S(1)} %pad_maximum_fusion.2), channel_id=1, source_target_pairs={{0,32},{32,64},{64,96},{96,0},{1,33},{33,65},{65,97},{97,1},{2,34}... | collective-permute-start | bytes 786440 | tf_op jit(solution)/shard_map/ppermute | solution.py:225
  66.0 19.1 %collective-permute-start.10 = (bf16[1024,512]{1,0:T(8,128)(2,1)S(1)}, bf16[1024,512]{1,0:T(8,128)(2,1)S(1)}, u32[]{:S(2)}, u32[]{:S(2)}) collective-permute-start(bf16[1024,512]{1,0:T(8,128)(2,1)S(1)} %slice.29), channel_id=1, source_target_pairs={{0,3},{1,0},{2,1},{3,2},{4,7},{5,4},{6,5},{7,6},{8,11},{9,8},{10,9... | collective-permute-start | bytes 3145736 | tf_op jit(solution)/shard_map/ppermute | solution.py:52
  66.1 22.7 %collective-permute-start.9 = (bf16[1024,512]{1,0:T(8,128)(2,1)S(1)}, bf16[1024,512]{1,0:T(8,128)(2,1)S(1)}, u32[]{:S(2)}, u32[]{:S(2)}) collective-permute-start(bf16[1024,512]{1,0:T(8,128)(2,1)S(1)} %slice.28), channel_id=1, source_target_pairs={{0,1},{1,2},{2,3},{3,0},{4,5},{5,6},{6,7},{7,4},{8,9},{9,10},{10,1... | collective-permute-start | bytes 3145736 | tf_op jit(solution)/shard_map/ppermute | solution.py:52
  70.9 26.8 %collective-permute-start.14 = (bf16[512,256]{1,0:T(8,128)(2,1)S(1)}, bf16[512,256]{1,0:T(8,128)(2,1)S(1)}, u32[]{:S(2)}, u32[]{:S(2)}) collective-permute-start(bf16[512,256]{1,0:T(8,128)(2,1)S(1)} %collective-permute-done.2.own_ref), channel_id=1, source_target_pairs={{0,32},{32,0},{64,96},{96,64},{1,33},{33,1},{65,97},{97,65},{2,34}... | collective-permute-start | bytes 786440 | tf_op jit(solution)/shard_map/ppermute | solution.py:229
  91.8 10.8 %collective-permute-start.13 = (f16[2064,128]{1,0:T(8,128)(2,1)S(1)}, f16[2064,128]{1,0:T(8,128)(2,1)S(1)}, u32[]{:S(2)}, u32[]{:S(2)}) collective-permute-start(f16[2064,128]{1,0:T(8,128)(2,1)S(1)} %convert_element_type.31), channel_id=1, source_target_pairs={{0,12},{1,13},{2,14},{3,15},{4,0},{5,1},{6,2},{7,3},{8,4},{9,5},{1... | collective-permute-start | bytes 1585160 | tf_op jit(solution)/shard_map/ppermute | solution.py:52
  93.3 16.2 %collective-permute-start.12 = (f16[2064,128]{1,0:T(8,128)(2,1)S(1)}, f16[2064,128]{1,0:T(8,128)(2,1)S(1)}, u32[]{:S(2)}, u32[]{:S(2)}) collective-permute-start(f16[2064,128]{1,0:T(8,128)(2,1)S(1)} %convert_element_type.29), channel_id=1, source_target_pairs={{0,8},{1,9},{2,10},{3,11},{4,12},{5,13},{6,14},{7,15},{8,0},{9,1},... | collective-permute-start | bytes 1585160 | tf_op jit(solution)/shard_map/ppermute | solution.py:52
  96.6 12.9 %collective-permute-start.11 = (f16[2064,128]{1,0:T(8,128)(2,1)S(1)}, f16[2064,128]{1,0:T(8,128)(2,1)S(1)}, u32[]{:S(2)}, u32[]{:S(2)}) collective-permute-start(f16[2064,128]{1,0:T(8,128)(2,1)S(1)} %convert_element_type.27), channel_id=1, source_target_pairs={{0,4},{1,5},{2,6},{3,7},{4,8},{5,9},{6,10},{7,11},{8,12},{9,13},{1... | collective-permute-start | bytes 1585160 | tf_op jit(solution)/shard_map/ppermute | solution.py:52
  97.8 17.6 %collective-permute-start.15 = (bf16[1024,256]{1,0:T(8,128)(2,1)S(1)}, bf16[1024,256]{1,0:T(8,128)(2,1)S(1)}, u32[]{:S(2)}, u32[]{:S(2)}) collective-permute-start(bf16[1024,256]{1,0:T(8,128)(2,1)S(1)} %pad_maximum_fusion.1), channel_id=1, source_target_pairs={{0,64},{32,96},{64,0},{96,32},{1,65},{33,97},{65,1},{97,33},{2,66}... | collective-permute-start | bytes 1572872 | tf_op jit(solution)/shard_map/ppermute | solution.py:229
  115.4 14.9 %collective-permute-start.16 = (f16[1040,128]{1,0:T(8,128)(2,1)S(1)}, f16[1040,128]{1,0:T(8,128)(2,1)S(1)}, u32[]{:S(2)}, u32[]{:S(2)}) collective-permute-start(f16[1040,128]{1,0:T(8,128)(2,1)S(1)} %convert_element_type.33), channel_id=1, source_target_pairs={{0,16},{16,0},{1,17},{17,1},{2,18},{18,2},{3,19},{19,3},{4,20},{20... | collective-permute-start | bytes 798728 | tf_op jit(solution)/shard_map/ppermute | solution.py:281

commit v5 on v4

v5 whole, which is shorter than its diff:
```python
import functools

import jax
import jax.numpy as jnp
from jax import lax
from jax.experimental import pallas as pl
from jax.experimental.pallas import tpu as pltpu
from jax.sharding import Mesh
from jax.sharding import PartitionSpec as P

F32 = jnp.float32
F16 = jnp.float16
BF16 = jnp.bfloat16
RING = 4
LANES = 128
TAIL = 16
TOP = 15
TINY = 1e-30
ENTRY_LIMIT = 26


def section():
    return lax.axis_index("section")


def on_last():
    return section() == lax.axis_size("section") - 1


def block_start(z_off, along, across):
    first = section() == 0
    y_off, x_off = jnp.where(first, across, along), jnp.where(first, along, across)
    z = lax.rem(lax.axis_index("z_hi") + z_off, 2)
    y = lax.rem(lax.axis_index("y") + y_off, RING)
    x = lax.rem(lax.axis_index("x") + x_off, RING)
    return pl.multiple_of((z * (RING * RING) + y * RING + x) * LANES, LANES)


def pairs_over(along, by):
    size, pairs = RING * RING, []
    for s in range(2):
        for y in range(RING):
            for x in range(RING):
                on_x = (s == 0) == along
                there = (y, (x + by) % RING) if on_x else ((y + by) % RING, x)
                pairs.append((s * size + y * RING + x, s * size + there[0] * RING + there[1]))
    return pairs


def shifted(value, along, by):
    return lax.ppermute(value, ("section", "y", "x"), pairs_over(along, by))


def whole(n=1):
    return [pl.BlockSpec(memory_space=pltpu.VMEM)] * n


def in_hbm(value):
    return pltpu.with_memory_space_constraint(value, pltpu.HBM)


def call(kernel, out_shapes, operands, specs, scratch=(), flops=0, moved=0, limit=20):
    return pl.pallas_call(
        kernel,
        out_shape=[jax.ShapeDtypeStruct(s, t) for s, t in out_shapes],
        in_specs=specs,
        out_specs=whole(len(out_shapes)),
        scratch_shapes=list(scratch),
        compiler_params=pltpu.CompilerParams(vmem_limit_bytes=limit * 2**20),
        cost_estimate=pl.CostEstimate(flops=flops, bytes_accessed=moved, transcendentals=0),
    )(*operands)


CONTRACT_LAST = (((1,), (1,)), ((), ()))


def entry_kernel(pending_ref, x_ref, stash_ref, head_ref, weight_ref, right_ref, left_ref, own_ref, head_out, weight_out,
                 x_in, stash_in, count_in, sems):
    micro, rows, width = x_ref.shape
    half, depth = width // 2, (micro - 1) * rows
    pieces = [(pending_ref, count_in), (x_ref, x_in)]
    pieces += [(stash_ref.at[m], stash_in.at[m]) for m in range(micro - 1)]
    pieces += [(head_ref, head_out)]
    parts = 4
    share = width // parts
    pieces += [(weight_ref.at[pl.ds(i * share, share)], weight_out.at[pl.ds(i * share, share)]) for i in range(parts)]
    copies = [pltpu.make_async_copy(a, b, sems.at[i]) for i, (a, b) in enumerate(pieces)]
    for copy in copies:
        copy.start()
    copies[0].wait()
    copies[1].wait()
    count = count_in[section()]
    for m in range(micro):
        turned = jnp.where(m >= micro - count, x_in[m].astype(F32), 0.0).T.astype(BF16)
        lanes = slice(m * rows, (m + 1) * rows)
        for out, order in ((right_ref, (half, 0)), (left_ref, (0, half))):
            for at, top in zip((0, half), order):
                out[at:at + half, lanes] = turned[top:top + half]
    plans = [(right_ref, width, 0, 2), (left_ref, width, 1, 2)]
    for z in range(2):
        at = width + (1 + z) * depth
        plans += [(right_ref, at, z, 1), (left_ref, at, z, RING - 1), (own_ref, z * depth, z, 0)]
    for m in range(micro - 1):
        copies[2 + m].wait()
        for out, base, z, along in plans:
            for b in range(RING):
                top = base + m * rows
                source = stash_in[m, :, pl.ds(block_start(z, along, b), LANES)]
                out[top:top + rows, b * LANES:(b + 1) * LANES] = source
    for copy in copies[1 + micro:]:
        copy.wait()


def first_kernel(grad_ref, weight_ref, out_ref, small_ref):
    step = 256
    for i in range(0, weight_ref.shape[0], step):
        out = lax.dot_general(grad_ref[...], weight_ref[i:i + step, :], CONTRACT_LAST, preferred_element_type=F32)
        out_ref[:, i:i + step] = out
        small_ref[:, i:i + step] = out.astype(BF16)


def second_kernel(rel_ref, first_ref, weight_ref, out_ref):
    step, share = 256, rel_ref.shape[2]
    tensor = lax.axis_index("z_lo")
    for i in range(0, weight_ref.shape[0], step):
        total = jnp.zeros((rel_ref.shape[1], step), F32)
        for k in range(RING):
            owner = lax.rem(tensor - k + RING, RING)
            cols = weight_ref[i:i + step, pl.ds(pl.multiple_of(owner * share, share), share)]
            total = total + lax.dot_general(rel_ref[k], cols, CONTRACT_LAST, preferred_element_type=F32)
        out_ref[:, i:i + step] = jnp.where(on_last(), first_ref[:, i:i + step], total)


def pack_last_kernel(head_ref, rel_ref, right_ref, left_ref, own_ref, far_ref):
    tensor = lax.axis_index("z_lo")
    rows, share = rel_ref.shape[1], rel_ref.shape[2]
    for z in range(2):
        for b in range(RING):
            for out, along in ((right_ref, 1), (left_ref, RING - 1), (own_ref, 0), (far_ref, 2)):
                at = block_start(z, along, b)
                inner = pl.multiple_of(lax.rem(at, share), LANES)
                chained = rel_ref[lax.rem(tensor - lax.div(at, share) + RING, RING), :, pl.ds(inner, LANES)]
                last = jnp.where(on_last(), head_ref[:, pl.ds(at, LANES)], chained)
                out[z * rows:(z + 1) * rows, b * LANES:(b + 1) * LANES] = last


def halves(ref, half, swapped):
    return (ref.at[half:2 * half], ref.at[0:half]) if swapped else (ref.at[0:half], ref.at[half:2 * half])


def early_kernel(mine_ref, own_ref, left_ref, right_ref, acc_ref):
    width, depth = acc_ref.shape[0], own_ref.shape[0] // 2
    half, lanes = width // 2, acc_ref.shape[1] // 2
    sides = [halves(mine_ref, half, True), halves(left_ref, half, True), halves(right_ref, half, False)]
    for r in range(2):
        lhs = jnp.concatenate([side[r][:, :depth] for side in sides], axis=1)
        for z in range(2):
            at = width + (1 + z) * depth
            rhs = [own_ref[z * depth:(z + 1) * depth, :], left_ref[at:at + depth, :], right_ref[at:at + depth, :]]
            rhs = jnp.concatenate(rhs, axis=0)
            acc_ref[r * half:(r + 1) * half, z * lanes:(z + 1) * lanes] = jnp.dot(lhs, rhs, preferred_element_type=F32)


def late_kernel(acc_ref, mine_ref, left_ref, right_ref, upper_ref, lower_ref, own_last, left_last, right_last, far_last,
                keep_far, keep_near, *rest):
    sends, sum_ref = rest[:-1], rest[-1]
    width, rows = acc_ref.shape[0], own_last.shape[0] // 2
    half, lanes = width // 2, acc_ref.shape[1] // 2
    depth = mine_ref.shape[1] - rows
    mine, left, right = halves(mine_ref, half, True), halves(left_ref, half, True), halves(right_ref, half, False)
    far = (upper_ref, lower_ref)
    largest = jnp.full((1, lanes), TINY, F32)
    for r in range(2):
        lhs = [mine[r][:, depth:], left[r][:, depth:], right[r][:, depth:], far[r][:half, depth:], far[r][:half, :depth]]
        lhs = jnp.concatenate(lhs, axis=1)
        for z in range(2):
            rhs = [ref[z * rows:(z + 1) * rows, :] for ref in (own_last, left_last, right_last, far_last)]
            rhs = jnp.concatenate(rhs + [far[z][half:, :]], axis=0)
            total = acc_ref[r * half:(r + 1) * half, z * lanes:(z + 1) * lanes]
            total = total + jnp.dot(lhs, rhs, preferred_element_type=F32)
            largest = jnp.maximum(largest, jnp.max(jnp.abs(total), axis=0, keepdims=True))
            sum_ref[r * half:(r + 1) * half, z * lanes:(z + 1) * lanes] = total
    power = jnp.ceil(jnp.log2(jnp.max(largest, axis=1, keepdims=True))) - TOP
    power = jnp.broadcast_to(power, (1, LANES))
    factor = jnp.exp2(-power)
    for z, keep, outs in ((1, keep_far, sends[:RING - 1]), (0, keep_near, sends[RING - 1:])):
        keep[...] = sum_ref[:, z * lanes:z * lanes + LANES]
        for b, out in enumerate(outs, 1):
            cols = slice(z * lanes + b * LANES, z * lanes + (b + 1) * LANES)
            out[:width, :] = sum_ref[:, cols] * factor
            out[width:, :] = jnp.broadcast_to(power, (TAIL, LANES))


def summed(keep_ref, refs):
    rows = keep_ref.shape[0]
    total = keep_ref[...]
    for ref in refs:
        total = total + ref[:rows, :] * jnp.exp2(ref[rows:rows + 1, :])
    return total


def far_kernel(keep_ref, one_ref, two_ref, three_ref, out_ref):
    rows = keep_ref.shape[0]
    total = summed(keep_ref, (one_ref, two_ref, three_ref))
    largest = jnp.maximum(jnp.max(jnp.abs(total), axis=0, keepdims=True), TINY)
    power = jnp.ceil(jnp.log2(jnp.max(largest, axis=1, keepdims=True))) - TOP
    power = jnp.broadcast_to(power, (1, LANES))
    out_ref[:rows, :] = total * jnp.exp2(-power)
    out_ref[rows:, :] = jnp.broadcast_to(power, (TAIL, LANES))


def near_kernel(keep_ref, one_ref, two_ref, three_ref, other_ref, out_ref):
    out_ref[...] = summed(keep_ref, (one_ref, two_ref, three_ref, other_ref))


def on_first(value, by):
    return lax.ppermute(value, ("section", "z_lo"), [(i, (i + by) % RING) for i in range(RING)])


def local(weights, stash_in, stash_grad, head_grad, pending):
    inputs, grads = stash_in[0], stash_grad[0]
    micro, rows, width = inputs.shape
    depth, half, lanes = (micro - 1) * rows, width // 2, RING * LANES
    columns = head_grad.shape[1]
    matmul = dict(flops=2 * rows * width * columns, moved=2 * 2**20)

    side = ((width + 3 * depth, lanes), BF16)
    right, left, own, head, weight = call(
        entry_kernel, [side, side, ((2 * depth, lanes), BF16), (head_grad.shape, BF16), ((width, columns), BF16)],
        [in_hbm(v) for v in (pending, inputs, grads, head_grad, weights[0])], [pl.BlockSpec(memory_space=pltpu.HBM)] * 5,
        scratch=[pltpu.VMEM(inputs.shape, BF16), pltpu.VMEM(grads.shape, BF16), pltpu.SMEM(pending.shape, pending.dtype),
                 pltpu.SemaphoreType.DMA((micro + 6,))],
        moved=13 * 2**20, limit=ENTRY_LIMIT,
    )
    from_left, from_right = shifted(right, True, 1), shifted(left, True, -1)

    first, small = call(first_kernel, [((rows, width), F32), ((rows, width), BF16)], (head, weight), whole(2), **matmul)
    shard = lax.ppermute(small, "section", [(1, 0)])
    rel = [shard] + [on_first(shard, by) for by in range(1, RING)]
    from_left, from_right, *rel = lax.optimization_barrier((from_left, from_right, *rel))
    rel = jnp.stack(rel, 0)

    upper = shifted(from_left[half:width + depth], True, 1)
    lower = shifted(from_right[half:width + depth], True, -1)
    edge = ((2 * rows, lanes), BF16)
    last_right, last_left, last_own, last_far = call(
        pack_last_kernel, [edge] * 4, (head, rel), whole(2), moved=4 * 2**20
    )
    last = [last_own, shifted(last_right, True, 1), shifted(last_left, True, -1), shifted(last_far, True, 2)]
    (acc,) = call(
        early_kernel, [((width, 2 * lanes), F32)], (right, own, from_left, from_right), whole(4),
        flops=2 * width * 2 * lanes * 3 * depth, moved=12 * 2**20,
    )
    send = ((width + TAIL, LANES), F32)
    keep_far, keep_near, *sends = call(
        late_kernel, [((width, LANES), F32)] * 2 + [send] * 6,
        (acc, right, from_left, from_right, upper, lower, *last), whole(10),
        scratch=[pltpu.VMEM((width, 2 * lanes), F32)],
        flops=2 * width * 2 * lanes * (3 * rows + micro * rows), moved=12 * 2**20,
    )
    keep_far, rel = lax.optimization_barrier((keep_far, rel))
    (second,) = call(second_kernel, [((rows, width), F32)], (rel, first, weights[0]), whole(3), **matmul)
    got = [shifted(s.astype(F16), False, by).astype(F32) for by, s in zip((1, 2, 3, 1, 2, 3), sends)]
    (far,) = call(far_kernel, [send], (keep_far, *got[:3]), whole(4), moved=4 * 2**20)
    other = lax.ppermute(far.astype(F16), "z_hi", [(0, 1), (1, 0)]).astype(F32)
    (block,) = call(near_kernel, [((width, LANES), F32)], (keep_near, *got[3:], other), whole(5), moved=4 * 2**20)
    return (second[None], block[None])


def solution(mesh):
    fine = Mesh(mesh.devices.reshape(2, 4, 2, 4, 4), ("section", "z_lo", "z_hi", "y", "x"))
    dp = ("z_hi", "y", "x")
    return jax.shard_map(
        local,
        mesh=fine,
        in_specs=(
            P("section", "z_lo", None),
            P("section", None, dp, "z_lo"),
            P("section", None, dp, None),
            P(dp, None),
            P(),
        ),
        out_specs=(P("section", dp, "z_lo"), P("section", "z_lo", dp)),
        check_vma=False,
    )
```

time: 132 us -> 91.2 us (0.69)
  the two profiles are of different devices: /device:TPU:24 before, /device:TPU:32 now
where the time goes in v5:
time: 91.2 us; the launch traced here: 91 us
  starting transfers between devices  36.7 us (40%)
  waiting for transfers between devices  33.6 us (37%)
  Pallas kernels  19 us (21%)
    ppermute x13, waiting for transfers between devices, shifted(): return lax.ppermute(value, ('section', 'y', 'x'), pairs_over(along, by))  20 us
    pallas_call x8, Pallas kernels, call(): pl.pallas_call(kernel, out_shape=[jax.ShapeDtypeStruct(s, t) for s, t in...  19 us
    ppermute x13, starting transfers between devices, shifted(): return lax.ppermute(value, ('section', 'y', 'x'), pairs_over(along, by))  17.1 us
    ppermute x3, starting transfers between devices, on_first(): lax.ppermute(value, ('section', 'z_lo'), [(i, (i + by) % RING) for i in r...  11.9 us
    ppermute x3, waiting for transfers between devices, on_first(): lax.ppermute(value, ('section', 'z_lo'), [(i, (i + by) % RING) for i in r...  6.47 us
    ppermute x1, starting transfers between devices, local(): other = lax.ppermute(far.astype(F16), 'z_hi', [(0, 1), (1, 0)]).astype(F32)  6.38 us
    ppermute x1, waiting for transfers between devices, local(): other = lax.ppermute(far.astype(F16), 'z_hi', [(0, 1), (1, 0)]).astype(F32)  4.98 us
    ppermute x1, waiting for transfers between devices, local(): shard = lax.ppermute(small, 'section', [(1, 0)])  2.13 us
  transfers between devices with their start and end apart: 18, of which 10 were waited for; matrix products, arithmetic and copies ran while one was open for 1% of the time, Pallas kernels for 11%

profile of v5, /device:TPU:32, one launch (start us, length us, event | category | flops | bytes accessed | tf_op | source)
XLA Modules:
  0.0 91.0 jit_solution(6403078744738467461)
XLA Ops:
  0.6 5.1 %shard_map.68 = (bf16[2176,512]{1,0:T(8,128)(2,1)S(1)}, bf16[2176,512]{1,0:T(8,128)(2,1)S(1)}, bf16[768,512]{1,0:T(8,128)(2,1)S(1)}, bf16[128,4096]{1,0:T(8,128)(2,1)S(1)}, bf16[1024,4096]{1,0:T(8,128)(2,1)S(1)}) custom-call(s32[2]{0:T(128)} %pending_ref.1, bf16[4,128,1024]{2,1,0:T(8,128)(2,1)} %bitcast.14, bf16[3,128,4096]{2,1,0:T(8,128)(2,1)} %bitcast.13, ...), custom_call_target="tpu_custom_call" | custom-call | bytes 13631488 | tf_op jit(solution)/shard_map/pallas_call | solution.py:63
  5.7 2.8 %collective-permute-start.1 = (bf16[2176,512]{1,0:T(8,128)(2,1)S(1)}, bf16[2176,512]{1,0:T(8,128)(2,1)S(1)}, u32[]{:S(2)}, u32[]{:S(2)}) collective-permute-start(bf16[2176,512]{1,0:T(8,128)(2,1)S(1)} %get-tuple-element.31), channel_id=1, source_target_pairs={{0,3},{1,0},{2,1},{3,2},{4,7},{5,4},{6,5},{7,6},{8,11},{9,8},{10,9... | collective-permute-start | bytes 6684680 | tf_op jit(solution)/shard_map/ppermute | solution.py:51
  8.5 0.0 collective-permute-start
  8.5 2.9 %shard_map.69 = (f32[128,1024]{1,0:T(8,128)S(1)}, bf16[128,1024]{1,0:T(8,128)(2,1)S(1)}) custom-call(bf16[128,4096]{1,0:T(8,128)(2,1)S(1)} %get-tuple-element.32.grad_ref.head_ref, bf16[1024,4096]{1,0:T(8,128)(2,1)S(1)} %get-tuple-element.33.weight_ref), custom_call_target="tpu_custom_call" | custom-call | flops 1073741824 | bytes 2097152 | tf_op jit(solution)/shard_map/pallas_call | solution.py:63
  11.4 1.3 %collective-permute-start.2 = (bf16[128,1024]{1,0:T(8,128)(2,1)S(1)}, bf16[128,1024]{1,0:T(8,128)(2,1)S(1)}, u32[]{:S(2)}, u32[]{:S(2)}) collective-permute-start(bf16[128,1024]{1,0:T(8,128)(2,1)S(1)} %get-tuple-element.34), channel_id=1, source_target_pairs={{128,0},{129,1},{130,2},{131,3},{132,4},{133,5},{134,6},{135,7},{1... | collective-permute-start | bytes 786440 | tf_op jit(solution)/shard_map/ppermute | solution.py:238
  12.7 2.1 %collective-permute-done.2 = bf16[128,1024]{1,0:T(8,128)(2,1)S(1)} collective-permute-done((bf16[128,1024]{1,0:T(8,128)(2,1)S(1)}, bf16[128,1024]{1,0:T(8,128)(2,1)S(1)}, u32[]{:S(2)}, u32[]{:S(2)}) %collective-permute-start.2) | collective-permute-done | bytes 262176 | tf_op jit(solution)/shard_map/ppermute | solution.py:238
  14.9 3.0 %collective-permute-start.5 = (bf16[128,1024]{1,0:T(8,128)(2,1)S(1)}, bf16[128,1024]{1,0:T(8,128)(2,1)S(1)}, u32[]{:S(2)}, u32[]{:S(2)}) collective-permute-start(bf16[128,1024]{1,0:T(8,128)(2,1)S(1)} %collective-permute-done.2), channel_id=1, source_target_pairs={{0,96},{32,0},{64,32},{96,64},{1,97},{33,1},{65,33},{97,65},{2,98}... | collective-permute-start | bytes 786440 | tf_op jit(solution)/shard_map/ppermute | solution.py:217
  17.9 4.2 %collective-permute-start.4 = (bf16[128,1024]{1,0:T(8,128)(2,1)S(1)}, bf16[128,1024]{1,0:T(8,128)(2,1)S(1)}, u32[]{:S(2)}, u32[]{:S(2)}) collective-permute-start(bf16[128,1024]{1,0:T(8,128)(2,1)S(1)} %collective-permute-done.2), channel_id=1, source_target_pairs={{0,64},{32,96},{64,0},{96,32},{1,65},{33,97},{65,1},{97,33},{2,66}... | collective-permute-start | bytes 786440 | tf_op jit(solution)/shard_map/ppermute | solution.py:217
  22.1 4.7 %collective-permute-start.3 = (bf16[128,1024]{1,0:T(8,128)(2,1)S(1)}, bf16[128,1024]{1,0:T(8,128)(2,1)S(1)}, u32[]{:S(2)}, u32[]{:S(2)}) collective-permute-start(bf16[128,1024]{1,0:T(8,128)(2,1)S(1)} %collective-permute-done.2), channel_id=1, source_target_pairs={{0,32},{32,64},{64,96},{96,0},{1,33},{33,65},{65,97},{97,1},{2,34}... | collective-permute-start | bytes 786440 | tf_op jit(solution)/shard_map/ppermute | solution.py:217
  26.8 0.0 collective-permute-done.5
  26.8 3.7 %collective-permute-done.4 = bf16[128,1024]{1,0:T(8,128)(2,1)S(1)} collective-permute-done((bf16[128,1024]{1,0:T(8,128)(2,1)S(1)}, bf16[128,1024]{1,0:T(8,128)(2,1)S(1)}, u32[]{:S(2)}, u32[]{:S(2)}) %collective-permute-start.4) | collective-permute-done | bytes 262176 | tf_op jit(solution)/shard_map/ppermute | solution.py:217
  30.5 2.8 %collective-permute-done.3 = bf16[128,1024]{1,0:T(8,128)(2,1)S(1)} collective-permute-done((bf16[128,1024]{1,0:T(8,128)(2,1)S(1)}, bf16[128,1024]{1,0:T(8,128)(2,1)S(1)}, u32[]{:S(2)}, u32[]{:S(2)}) %collective-permute-start.3) | collective-permute-done | bytes 262176 | tf_op jit(solution)/shard_map/ppermute | solution.py:217
  33.3 0.2 collective-permute-done.1.right_ref
  33.5 3.7 %collective-permute-done.left_ref = bf16[2176,512]{1,0:T(8,128)(2,1)S(1)} collective-permute-done((bf16[2176,512]{1,0:T(8,128)(2,1)S(1)}, bf16[2176,512]{1,0:T(8,128)(2,1)S(1)}, u32[]{:S(2)}, u32[]{:S(2)}) %collective-permute-start) | collective-permute-done | bytes 2228256 | tf_op jit(solution)/shard_map/ppermute | solution.py:51
  37.2 0.1 slice.6
  37.3 0.1 slice.7
  37.3 0.1 collective-permute-start.7
  37.4 2.0 %collective-permute-start.6 = (bf16[896,512]{1,0:T(8,128)(2,1)S(1)}, bf16[896,512]{1,0:T(8,128)(2,1)S(1)}, u32[]{:S(2)}, u32[]{:S(2)}) collective-permute-start(bf16[896,512]{1,0:T(8,128)(2,1)S(1)} %slice.6), channel_id=1, source_target_pairs={{0,1},{1,2},{2,3},{3,0},{4,5},{5,6},{6,7},{7,4},{8,9},{9,10},{10,1... | collective-permute-start | bytes 2752520 | tf_op jit(solution)/shard_map/ppermute | solution.py:51
  39.4 0.1 pad_maximum_fusion.rel_ref
  39.6 0.6 shard_map.71
  40.2 0.1 collective-permute-start.8
  40.3 3.2 %collective-permute-start.9 = (bf16[256,512]{1,0:T(8,128)(2,1)S(1)}, bf16[256,512]{1,0:T(8,128)(2,1)S(1)}, u32[]{:S(2)}, u32[]{:S(2)}) collective-permute-start(bf16[256,512]{1,0:T(8,128)(2,1)S(1)} %get-tuple-element.43), channel_id=1, source_target_pairs={{0,3},{1,0},{2,1},{3,2},{4,7},{5,4},{6,5},{7,6},{8,11},{9,8},{10,9... | collective-permute-start | bytes 786440 | tf_op jit(solution)/shard_map/ppermute | solution.py:51
  43.5 0.0 collective-permute-start.10
  43.5 2.9 %shard_map.70.acc_ref = f32[1024,1024]{1,0:T(8,128)S(1)} custom-call(bf16[2176,512]{1,0:T(8,128)(2,1)S(1)} %get-tuple-element.29.mine_ref, bf16[768,512]{1,0:T(8,128)(2,1)S(1)} %get-tuple-element.30.own_ref, bf16[2176,512]{1,0:T(8,128)(2,1)S(1)} %collective-permute-done.left_ref, bf16[2176,512]{1,0:T(8,128)(2,1)S(1)} %collective-permute-done.1.right_ref), custom_call_target="tpu_custom_call" | custom-call | flops 2415919104 | bytes 12582912 | tf_op jit(solution)/shard_map/pallas_call | solution.py:63
  46.4 11.3 %collective-permute-done.8.left_last = bf16[256,512]{1,0:T(8,128)(2,1)S(1)} collective-permute-done((bf16[256,512]{1,0:T(8,128)(2,1)S(1)}, bf16[256,512]{1,0:T(8,128)(2,1)S(1)}, u32[]{:S(2)}, u32[]{:S(2)}) %collective-permute-start.8) | collective-permute-done | bytes 262176 | tf_op jit(solution)/shard_map/ppermute | solution.py:51
  57.7 0.0 collective-permute-done.9.right_last
  57.7 0.0 collective-permute-done.10.far_last
  57.7 0.0 collective-permute-done.7.lower_ref
  57.7 0.0 collective-permute-done.6.upper_ref
  57.7 0.0 slice-start.1
  57.8 2.6 %shard_map.72 = (f32[1024,128]{1,0:T(8,128)S(1)}, f32[1024,128]{1,0:T(8,128)S(1)}, f32[1040,128]{1,0:T(8,128)S(1)}, f32[1040,128]{1,0:T(8,128)S(1)}, f32[1040,12...) custom-call(f32[1024,1024]{1,0:T(8,128)S(1)} %shard_map.70.acc_ref, ...), custom_call_target="tpu_custom_call" | custom-call | flops 1879048192 | bytes 12582912 | tf_op jit(solution)/shard_map/pallas_call | solution.py:63
  60.4 3.1 %collective-permute-start.16 = (f16[1040,128]{1,0:T(8,128)(2,1)S(1)}, f16[1040,128]{1,0:T(8,128)(2,1)S(1)}, u32[]{:S(2)}, u32[]{:S(2)}) collective-permute-start(f16[1040,128]{1,0:T(8,128)(2,1)S(1)} %convert_element_type.52), channel_id=1, source_target_pairs={{0,12},{1,13},{2,14},{3,15},{4,0},{5,1},{6,2},{7,3},{8,4},{9,5},{1... | collective-permute-start | bytes 798728 | tf_op jit(solution)/shard_map/ppermute | solution.py:51
  63.6 0.7 collective-permute-start.15
  64.3 1.0 %collective-permute-start.14 = (f16[1040,128]{1,0:T(8,128)(2,1)S(1)}, f16[1040,128]{1,0:T(8,128)(2,1)S(1)}, u32[]{:S(2)}, u32[]{:S(2)}) collective-permute-start(f16[1040,128]{1,0:T(8,128)(2,1)S(1)} %convert_element_type.48), channel_id=1, source_target_pairs={{0,4},{1,5},{2,6},{3,7},{4,8},{5,9},{6,10},{7,11},{8,12},{9,13},{1... | collective-permute-start | bytes 798728 | tf_op jit(solution)/shard_map/ppermute | solution.py:51
  65.5 2.3 %collective-permute-start.13 = (f16[1040,128]{1,0:T(8,128)(2,1)S(1)}, f16[1040,128]{1,0:T(8,128)(2,1)S(1)}, u32[]{:S(2)}, u32[]{:S(2)}) collective-permute-start(f16[1040,128]{1,0:T(8,128)(2,1)S(1)} %convert_element_type.46), channel_id=1, source_target_pairs={{0,12},{1,13},{2,14},{3,15},{4,0},{5,1},{6,2},{7,3},{8,4},{9,5},{1... | collective-permute-start | bytes 798728 | tf_op jit(solution)/shard_map/ppermute | solution.py:51
  67.9 1.7 %collective-permute-start.12 = (f16[1040,128]{1,0:T(8,128)(2,1)S(1)}, f16[1040,128]{1,0:T(8,128)(2,1)S(1)}, u32[]{:S(2)}, u32[]{:S(2)}) collective-permute-start(f16[1040,128]{1,0:T(8,128)(2,1)S(1)} %convert_element_type.44), channel_id=1, source_target_pairs={{0,8},{1,9},{2,10},{3,11},{4,12},{5,13},{6,14},{7,15},{8,0},{9,1},... | collective-permute-start | bytes 798728 | tf_op jit(solution)/shard_map/ppermute | solution.py:51
  69.6 0.8 collective-permute-done.16
  70.3 0.0 collective-permute-start.11
  70.4 1.3 %collective-permute-done.15 = f16[1040,128]{1,0:T(8,128)(2,1)S(1)} collective-permute-done((f16[1040,128]{1,0:T(8,128)(2,1)S(1)}, f16[1040,128]{1,0:T(8,128)(2,1)S(1)}, u32[]{:S(2)}, u32[]{:S(2)}) %collective-permute-start.15) | collective-permute-done | bytes 266272 | tf_op jit(solution)/shard_map/ppermute | solution.py:51
  71.7 2.7 %collective-permute-done.14 = f16[1040,128]{1,0:T(8,128)(2,1)S(1)} collective-permute-done((f16[1040,128]{1,0:T(8,128)(2,1)S(1)}, f16[1040,128]{1,0:T(8,128)(2,1)S(1)}, u32[]{:S(2)}, u32[]{:S(2)}) %collective-permute-start.14) | collective-permute-done | bytes 266272 | tf_op jit(solution)/shard_map/ppermute | solution.py:51
  74.5 0.3 shard_map.74
  74.8 6.4 %collective-permute-start.17 = (f16[1040,128]{1,0:T(8,128)(2,1)S(1)}, f16[1040,128]{1,0:T(8,128)(2,1)S(1)}, u32[]{:S(2)}, u32[]{:S(2)}) collective-permute-start(f16[1040,128]{1,0:T(8,128)(2,1)S(1)} %convert_element_type.54), channel_id=1, source_target_pairs={{0,16},{16,0},{1,17},{17,1},{2,18},{18,2},{3,19},{19,3},{4,20},{20... | collective-permute-start | bytes 798728 | tf_op jit(solution)/shard_map/ppermute | solution.py:265
  81.2 3.7 %shard_map.73 = f32[128,1024]{1,0:T(8,128)} custom-call(bf16[4,128,1024]{2,1,0:T(8,128)(2,1)S(1)} %pad_maximum_fusion.rel_ref, f32[128,1024]{1,0:T(8,128)S(1)} %get-tuple-element.47.first_ref, bf16[1024,4096]{1,0:T(8,128)(2,1)S(1)} %bitcast.12), custom_call_target="tpu_custom_call" | custom-call | flops 1073741824 | bytes 2097152 | tf_op jit(solution)/shard_map/pallas_call | solution.py:63
  84.9 0.0 collective-permute-done.13
  84.9 0.0 collective-permute-done.12
  85.0 0.0 collective-permute-done.11
  85.0 5.0 %collective-permute-done.17 = f16[1040,128]{1,0:T(8,128)(2,1)S(1)} collective-permute-done((f16[1040,128]{1,0:T(8,128)(2,1)S(1)}, f16[1040,128]{1,0:T(8,128)(2,1)S(1)}, u32[]{:S(2)}, u32[]{:S(2)}) %collective-permute-start.17) | collective-permute-done | bytes 266272 | tf_op jit(solution)/shard_map/ppermute | solution.py:265
  90.0 1.0 %shard_map.75 = f32[1024,128]{1,0:T(8,128)} custom-call(f32[1024,128]{1,0:T(8,128)S(1)} %get-tuple-element.48.keep_ref, f32[1040,128]{1,0:T(8,128)S(1)} %convert_element_type.43.one_ref, f32[1040,128]{1,0:T(8,128)S(1)} %convert_element_type.45.two_ref, f32[1040,128]{1,0:T(8,128)S(1)} %convert_element_type.47.three_ref, ...), custom_call_target="tpu_custom_call" | custom-call | bytes 4194304 | tf_op jit(solution)/shard_map/pallas_call | solution.py:63
  (18 shorter events, 0.5 us)
Async XLA Ops:
  5.7 27.8 %collective-permute-start.1 = (bf16[2176,512]{1,0:T(8,128)(2,1)S(1)}, bf16[2176,512]{1,0:T(8,128)(2,1)S(1)}, u32[]{:S(2)}, u32[]{:S(2)}) collective-permute-start(bf16[2176,512]{1,0:T(8,128)(2,1)S(1)} %get-tuple-element.31), channel_id=1, source_target_pairs={{0,3},{1,0},{2,1},{3,2},{4,7},{5,4},{6,5},{7,6},{8,11},{9,8},{10,9... | collective-permute-start | bytes 6684680 | tf_op jit(solution)/shard_map/ppermute | solution.py:51
  8.5 28.6 %collective-permute-start = (bf16[2176,512]{1,0:T(8,128)(2,1)S(1)}, bf16[2176,512]{1,0:T(8,128)(2,1)S(1)}, u32[]{:S(2)}, u32[]{:S(2)}) collective-permute-start(bf16[2176,512]{1,0:T(8,128)(2,1)S(1)} %get-tuple-element.29.mine_ref), channel_id=1, source_target_pairs={{0,1},{1,2},{2,3},{3,0},{4,5},{5,6},{6,7},{7,4},{8,9},{9,10},{10,1... | collective-permute-start | bytes 6684680 | tf_op jit(solution)/shard_map/ppermute | solution.py:51
  11.4 3.4 %collective-permute-start.2 = (bf16[128,1024]{1,0:T(8,128)(2,1)S(1)}, bf16[128,1024]{1,0:T(8,128)(2,1)S(1)}, u32[]{:S(2)}, u32[]{:S(2)}) collective-permute-start(bf16[128,1024]{1,0:T(8,128)(2,1)S(1)} %get-tuple-element.34), channel_id=1, source_target_pairs={{128,0},{129,1},{130,2},{131,3},{132,4},{133,5},{134,6},{135,7},{1... | collective-permute-start | bytes 786440 | tf_op jit(solution)/shard_map/ppermute | solution.py:238
  14.9 11.9 %collective-permute-start.5 = (bf16[128,1024]{1,0:T(8,128)(2,1)S(1)}, bf16[128,1024]{1,0:T(8,128)(2,1)S(1)}, u32[]{:S(2)}, u32[]{:S(2)}) collective-permute-start(bf16[128,1024]{1,0:T(8,128)(2,1)S(1)} %collective-permute-done.2), channel_id=1, source_target_pairs={{0,96},{32,0},{64,32},{96,64},{1,97},{33,1},{65,33},{97,65},{2,98}... | collective-permute-start | bytes 786440 | tf_op jit(solution)/shard_map/ppermute | solution.py:217
  17.9 12.6 %collective-permute-start.4 = (bf16[128,1024]{1,0:T(8,128)(2,1)S(1)}, bf16[128,1024]{1,0:T(8,128)(2,1)S(1)}, u32[]{:S(2)}, u32[]{:S(2)}) collective-permute-start(bf16[128,1024]{1,0:T(8,128)(2,1)S(1)} %collective-permute-done.2), channel_id=1, source_target_pairs={{0,64},{32,96},{64,0},{96,32},{1,65},{33,97},{65,1},{97,33},{2,66}... | collective-permute-start | bytes 786440 | tf_op jit(solution)/shard_map/ppermute | solution.py:217
  22.1 11.2 %collective-permute-start.3 = (bf16[128,1024]{1,0:T(8,128)(2,1)S(1)}, bf16[128,1024]{1,0:T(8,128)(2,1)S(1)}, u32[]{:S(2)}, u32[]{:S(2)}) collective-permute-start(bf16[128,1024]{1,0:T(8,128)(2,1)S(1)} %collective-permute-done.2), channel_id=1, source_target_pairs={{0,32},{32,64},{64,96},{96,0},{1,33},{33,65},{65,97},{97,1},{2,34}... | collective-permute-start | bytes 786440 | tf_op jit(solution)/shard_map/ppermute | solution.py:217
  37.3 20.4 %collective-permute-start.7 = (bf16[896,512]{1,0:T(8,128)(2,1)S(1)}, bf16[896,512]{1,0:T(8,128)(2,1)S(1)}, u32[]{:S(2)}, u32[]{:S(2)}) collective-permute-start(bf16[896,512]{1,0:T(8,128)(2,1)S(1)} %slice.7), channel_id=1, source_target_pairs={{0,3},{1,0},{2,1},{3,2},{4,7},{5,4},{6,5},{7,6},{8,11},{9,8},{10,9... | collective-permute-start | bytes 2752520 | tf_op jit(solution)/shard_map/ppermute | solution.py:51
  37.4 20.3 %collective-permute-start.6 = (bf16[896,512]{1,0:T(8,128)(2,1)S(1)}, bf16[896,512]{1,0:T(8,128)(2,1)S(1)}, u32[]{:S(2)}, u32[]{:S(2)}) collective-permute-start(bf16[896,512]{1,0:T(8,128)(2,1)S(1)} %slice.6), channel_id=1, source_target_pairs={{0,1},{1,2},{2,3},{3,0},{4,5},{5,6},{6,7},{7,4},{8,9},{9,10},{10,1... | collective-permute-start | bytes 2752520 | tf_op jit(solution)/shard_map/ppermute | solution.py:51
  40.2 17.5 %collective-permute-start.8 = (bf16[256,512]{1,0:T(8,128)(2,1)S(1)}, bf16[256,512]{1,0:T(8,128)(2,1)S(1)}, u32[]{:S(2)}, u32[]{:S(2)}) collective-permute-start(bf16[256,512]{1,0:T(8,128)(2,1)S(1)} %get-tuple-element.42), channel_id=1, source_target_pairs={{0,1},{1,2},{2,3},{3,0},{4,5},{5,6},{6,7},{7,4},{8,9},{9,10},{10,1... | collective-permute-start | bytes 786440 | tf_op jit(solution)/shard_map/ppermute | solution.py:51
  40.3 17.4 %collective-permute-start.9 = (bf16[256,512]{1,0:T(8,128)(2,1)S(1)}, bf16[256,512]{1,0:T(8,128)(2,1)S(1)}, u32[]{:S(2)}, u32[]{:S(2)}) collective-permute-start(bf16[256,512]{1,0:T(8,128)(2,1)S(1)} %get-tuple-element.43), channel_id=1, source_target_pairs={{0,3},{1,0},{2,1},{3,2},{4,7},{5,4},{6,5},{7,6},{8,11},{9,8},{10,9... | collective-permute-start | bytes 786440 | tf_op jit(solution)/shard_map/ppermute | solution.py:51
  43.5 14.2 %collective-permute-start.10 = (bf16[256,512]{1,0:T(8,128)(2,1)S(1)}, bf16[256,512]{1,0:T(8,128)(2,1)S(1)}, u32[]{:S(2)}, u32[]{:S(2)}) collective-permute-start(bf16[256,512]{1,0:T(8,128)(2,1)S(1)} %get-tuple-element.44), channel_id=1, source_target_pairs={{0,2},{1,3},{2,0},{3,1},{4,6},{5,7},{6,4},{7,5},{8,10},{9,11},{10,... | collective-permute-start | bytes 786440 | tf_op jit(solution)/shard_map/ppermute | solution.py:51
  43.5 37.6 %slice-start = ((s8[8388608]{0:T(1024)(128)(4,1)}), s8[4194304]{0:T(1024)(128)(4,1)S(1)}, s32[]{:S(2)}) async-start(s8[8388608]{0:T(1024)(128)(4,1)} %bitcast.10), calls=%async_computation | async-start | bytes 8388608
  57.7 23.4 %slice-start.1 = ((s8[8388608]{0:T(1024)(128)(4,1)}), s8[4194304]{0:T(1024)(128)(4,1)S(1)}, s32[]{:S(2)}) async-start(s8[8388608]{0:T(1024)(128)(4,1)} %bitcast.10), calls=%async_computation.1 | async-start | bytes 8388608
  60.4 9.9 %collective-permute-start.16 = (f16[1040,128]{1,0:T(8,128)(2,1)S(1)}, f16[1040,128]{1,0:T(8,128)(2,1)S(1)}, u32[]{:S(2)}, u32[]{:S(2)}) collective-permute-start(f16[1040,128]{1,0:T(8,128)(2,1)S(1)} %convert_element_type.52), channel_id=1, source_target_pairs={{0,12},{1,13},{2,14},{3,15},{4,0},{5,1},{6,2},{7,3},{8,4},{9,5},{1... | collective-permute-start | bytes 798728 | tf_op jit(solution)/shard_map/ppermute | solution.py:51
  63.6 8.1 %collective-permute-start.15 = (f16[1040,128]{1,0:T(8,128)(2,1)S(1)}, f16[1040,128]{1,0:T(8,128)(2,1)S(1)}, u32[]{:S(2)}, u32[]{:S(2)}) collective-permute-start(f16[1040,128]{1,0:T(8,128)(2,1)S(1)} %convert_element_type.50), channel_id=1, source_target_pairs={{0,8},{1,9},{2,10},{3,11},{4,12},{5,13},{6,14},{7,15},{8,0},{9,1},... | collective-permute-start | bytes 798728 | tf_op jit(solution)/shard_map/ppermute | solution.py:51
  64.3 10.1 %collective-permute-start.14 = (f16[1040,128]{1,0:T(8,128)(2,1)S(1)}, f16[1040,128]{1,0:T(8,128)(2,1)S(1)}, u32[]{:S(2)}, u32[]{:S(2)}) collective-permute-start(f16[1040,128]{1,0:T(8,128)(2,1)S(1)} %convert_element_type.48), channel_id=1, source_target_pairs={{0,4},{1,5},{2,6},{3,7},{4,8},{5,9},{6,10},{7,11},{8,12},{9,13},{1... | collective-permute-start | bytes 798728 | tf_op jit(solution)/shard_map/ppermute | solution.py:51
  65.5 19.3 %collective-permute-start.13 = (f16[1040,128]{1,0:T(8,128)(2,1)S(1)}, f16[1040,128]{1,0:T(8,128)(2,1)S(1)}, u32[]{:S(2)}, u32[]{:S(2)}) collective-permute-start(f16[1040,128]{1,0:T(8,128)(2,1)S(1)} %convert_element_type.46), channel_id=1, source_target_pairs={{0,12},{1,13},{2,14},{3,15},{4,0},{5,1},{6,2},{7,3},{8,4},{9,5},{1... | collective-permute-start | bytes 798728 | tf_op jit(solution)/shard_map/ppermute | solution.py:51
  67.9 17.0 %collective-permute-start.12 = (f16[1040,128]{1,0:T(8,128)(2,1)S(1)}, f16[1040,128]{1,0:T(8,128)(2,1)S(1)}, u32[]{:S(2)}, u32[]{:S(2)}) collective-permute-start(f16[1040,128]{1,0:T(8,128)(2,1)S(1)} %convert_element_type.44), channel_id=1, source_target_pairs={{0,8},{1,9},{2,10},{3,11},{4,12},{5,13},{6,14},{7,15},{8,0},{9,1},... | collective-permute-start | bytes 798728 | tf_op jit(solution)/shard_map/ppermute | solution.py:51
  70.3 14.6 %collective-permute-start.11 = (f16[1040,128]{1,0:T(8,128)(2,1)S(1)}, f16[1040,128]{1,0:T(8,128)(2,1)S(1)}, u32[]{:S(2)}, u32[]{:S(2)}) collective-permute-start(f16[1040,128]{1,0:T(8,128)(2,1)S(1)} %convert_element_type.42), channel_id=1, source_target_pairs={{0,4},{1,5},{2,6},{3,7},{4,8},{5,9},{6,10},{7,11},{8,12},{9,13},{1... | collective-permute-start | bytes 798728 | tf_op jit(solution)/shard_map/ppermute | solution.py:51
  74.8 15.2 %collective-permute-start.17 = (f16[1040,128]{1,0:T(8,128)(2,1)S(1)}, f16[1040,128]{1,0:T(8,128)(2,1)S(1)}, u32[]{:S(2)}, u32[]{:S(2)}) collective-permute-start(f16[1040,128]{1,0:T(8,128)(2,1)S(1)} %convert_element_type.54), channel_id=1, source_target_pairs={{0,16},{16,0},{1,17},{17,1},{2,18},{18,2},{3,19},{19,3},{4,20},{20... | collective-permute-start | bytes 798728 | tf_op jit(solution)/shard_map/ppermute | solution.py:265

commit v6 on v5

--- a/solution.py
+++ b/solution.py
@@ -74,8 +74,8 @@
 CONTRACT_LAST = (((1,), (1,)), ((), ()))
 
 
-def entry_kernel(pending_ref, x_ref, stash_ref, head_ref, weight_ref, right_ref, left_ref, own_ref, head_out, weight_out,
-                 x_in, stash_in, count_in, sems):
+def entry_kernel(pending_ref, x_ref, stash_ref, head_ref, weight_ref, right_ref, left_ref, own_ref, two_ref, head_out,
+                 weight_out, x_in, stash_in, count_in, sems):
     micro, rows, width = x_ref.shape
     half, depth = width // 2, (micro - 1) * rows
     pieces = [(pending_ref, count_in), (x_ref, x_in)]
@@ -96,17 +96,20 @@
         for out, order in ((right_ref, (half, 0)), (left_ref, (0, half))):
             for at, top in zip((0, half), order):
                 out[at:at + half, lanes] = turned[top:top + half]
-    plans = [(right_ref, width, 0, 2), (left_ref, width, 1, 2)]
+    share = depth // 2
+    plans = [(right_ref, width, 1, 2, 0, share), (left_ref, width, 1, 2, share, depth), (two_ref, 0, 0, 2, 0, depth)]
     for z in range(2):
-        at = width + (1 + z) * depth
-        plans += [(right_ref, at, z, 1), (left_ref, at, z, RING - 1), (own_ref, z * depth, z, 0)]
+        at = width + share + z * depth
+        plans += [(right_ref, at, z, 1, 0, depth), (left_ref, at, z, RING - 1, 0, depth), (own_ref, z * depth, z, 0, 0, depth)]
     for m in range(micro - 1):
         copies[2 + m].wait()
-        for out, base, z, along in plans:
+        for out, base, z, along, begin, end in plans:
+            begin_m, end_m = max(begin, m * rows), min(end, (m + 1) * rows)
+            if begin_m >= end_m:
+                continue
             for b in range(RING):
-                top = base + m * rows
-                source = stash_in[m, :, pl.ds(block_start(z, along, b), LANES)]
-                out[top:top + rows, b * LANES:(b + 1) * LANES] = source
+                source = stash_in[m, begin_m - m * rows:end_m - m * rows, pl.ds(block_start(z, along, b), LANES)]
+                out[base + begin_m - begin:base + end_m - begin, b * LANES:(b + 1) * LANES] = source
     for copy in copies[1 + micro:]:
         copy.wait()
 
@@ -131,17 +134,20 @@
         out_ref[:, i:i + step] = jnp.where(on_last(), first_ref[:, i:i + step], total)
 
 
-def pack_last_kernel(head_ref, rel_ref, right_ref, left_ref, own_ref, far_ref):
+def pack_last_kernel(head_ref, rel_ref, two_ref, right_ref, left_ref, own_ref, far_ref, direct_ref):
     tensor = lax.axis_index("z_lo")
     rows, share = rel_ref.shape[1], rel_ref.shape[2]
+    depth = two_ref.shape[0]
+    direct_ref[:depth, :] = two_ref[...]
     for z in range(2):
         for b in range(RING):
-            for out, along in ((right_ref, 1), (left_ref, RING - 1), (own_ref, 0), (far_ref, 2)):
+            two, base = ((direct_ref, depth), (far_ref, 0))[z]
+            for out, top, along in ((right_ref, z * rows, 1), (left_ref, z * rows, RING - 1), (own_ref, z * rows, 0), (two, base, 2)):
                 at = block_start(z, along, b)
                 inner = pl.multiple_of(lax.rem(at, share), LANES)
                 chained = rel_ref[lax.rem(tensor - lax.div(at, share) + RING, RING), :, pl.ds(inner, LANES)]
                 last = jnp.where(on_last(), head_ref[:, pl.ds(at, LANES)], chained)
-                out[z * rows:(z + 1) * rows, b * LANES:(b + 1) * LANES] = last
+                out[top:top + rows, b * LANES:(b + 1) * LANES] = last
 
 
 def halves(ref, half, swapped):
@@ -155,40 +161,40 @@
     for r in range(2):
         lhs = jnp.concatenate([side[r][:, :depth] for side in sides], axis=1)
         for z in range(2):
-            at = width + (1 + z) * depth
+            at = width + depth // 2 + z * depth
             rhs = [own_ref[z * depth:(z + 1) * depth, :], left_ref[at:at + depth, :], right_ref[at:at + depth, :]]
             rhs = jnp.concatenate(rhs, axis=0)
             acc_ref[r * half:(r + 1) * half, z * lanes:(z + 1) * lanes] = jnp.dot(lhs, rhs, preferred_element_type=F32)
 
 
-def late_kernel(acc_ref, mine_ref, left_ref, right_ref, upper_ref, lower_ref, own_last, left_last, right_last, far_last,
-                keep_far, keep_near, *rest):
+def late_kernel(z, acc_ref, mine_ref, left_ref, right_ref, upper_ref, lower_ref, own_last, left_last, right_last, two_ref,
+                keep_ref, *rest):
     sends, sum_ref = rest[:-1], rest[-1]
     width, rows = acc_ref.shape[0], own_last.shape[0] // 2
     half, lanes = width // 2, acc_ref.shape[1] // 2
     depth = mine_ref.shape[1] - rows
     mine, left, right = halves(mine_ref, half, True), halves(left_ref, half, True), halves(right_ref, half, False)
     far = (upper_ref, lower_ref)
+    rhs = [ref[z * rows:(z + 1) * rows, :] for ref in (own_last, left_last, right_last)]
+    if z:
+        rhs += [two_ref[...], upper_ref[half:, :], lower_ref[half:, :]]
+    else:
+        rhs += [two_ref[depth:, :], two_ref[:depth, :]]
+    rhs = jnp.concatenate(rhs, axis=0)
     largest = jnp.full((1, lanes), TINY, F32)
     for r in range(2):
         lhs = [mine[r][:, depth:], left[r][:, depth:], right[r][:, depth:], far[r][:half, depth:], far[r][:half, :depth]]
-        lhs = jnp.concatenate(lhs, axis=1)
-        for z in range(2):
-            rhs = [ref[z * rows:(z + 1) * rows, :] for ref in (own_last, left_last, right_last, far_last)]
-            rhs = jnp.concatenate(rhs + [far[z][half:, :]], axis=0)
-            total = acc_ref[r * half:(r + 1) * half, z * lanes:(z + 1) * lanes]
-            total = total + jnp.dot(lhs, rhs, preferred_element_type=F32)
-            largest = jnp.maximum(largest, jnp.max(jnp.abs(total), axis=0, keepdims=True))
-            sum_ref[r * half:(r + 1) * half, z * lanes:(z + 1) * lanes] = total
+        total = jnp.dot(jnp.concatenate(lhs, axis=1), rhs, preferred_element_type=F32)
+        total = total + acc_ref[r * half:(r + 1) * half, z * lanes:(z + 1) * lanes]
+        largest = jnp.maximum(largest, jnp.max(jnp.abs(total), axis=0, keepdims=True))
+        sum_ref[r * half:(r + 1) * half, :] = total
     power = jnp.ceil(jnp.log2(jnp.max(largest, axis=1, keepdims=True))) - TOP
     power = jnp.broadcast_to(power, (1, LANES))
     factor = jnp.exp2(-power)
-    for z, keep, outs in ((1, keep_far, sends[:RING - 1]), (0, keep_near, sends[RING - 1:])):
-        keep[...] = sum_ref[:, z * lanes:z * lanes + LANES]
-        for b, out in enumerate(outs, 1):
-            cols = slice(z * lanes + b * LANES, z * lanes + (b + 1) * LANES)
-            out[:width, :] = sum_ref[:, cols] * factor
-            out[width:, :] = jnp.broadcast_to(power, (TAIL, LANES))
+    keep_ref[...] = sum_ref[:, :LANES]
+    for b, out in enumerate(sends, 1):
+        out[:width, :] = sum_ref[:, b * LANES:(b + 1) * LANES] * factor
+        out[width:, :] = jnp.broadcast_to(power, (TAIL, LANES))
 
 
 def summed(keep_ref, refs):
@@ -224,9 +230,10 @@
     columns = head_grad.shape[1]
     matmul = dict(flops=2 * rows * width * columns, moved=2 * 2**20)
 
-    side = ((width + 3 * depth, lanes), BF16)
-    right, left, own, head, weight = call(
-        entry_kernel, [side, side, ((2 * depth, lanes), BF16), (head_grad.shape, BF16), ((width, columns), BF16)],
+    side = ((width + depth // 2 + 2 * depth, lanes), BF16)
+    right, left, own, two, head, weight = call(
+        entry_kernel,
+        [side, side, ((2 * depth, lanes), BF16), ((depth, lanes), BF16), (head_grad.shape, BF16), ((width, columns), BF16)],
         [in_hbm(v) for v in (pending, inputs, grads, head_grad, weights[0])], [pl.BlockSpec(memory_space=pltpu.HBM)] * 5,
         scratch=[pltpu.VMEM(inputs.shape, BF16), pltpu.VMEM(grads.shape, BF16), pltpu.SMEM(pending.shape, pending.dtype),
                  pltpu.SemaphoreType.DMA((micro + 6,))],
@@ -240,25 +247,36 @@
     from_left, from_right, *rel = lax.optimization_barrier((from_left, from_right, *rel))
     rel = jnp.stack(rel, 0)
 
-    upper = shifted(from_left[half:width + depth], True, 1)
-    lower = shifted(from_right[half:width + depth], True, -1)
+    passed = half + depth // 2
+    upper = shifted(from_left[half:half + passed], True, 1)
+    lower = shifted(from_right[half:half + passed], True, -1)
     edge = ((2 * rows, lanes), BF16)
-    last_right, last_left, last_own, last_far = call(
-        pack_last_kernel, [edge] * 4, (head, rel), whole(2), moved=4 * 2**20
+    last_right, last_left, last_own, last_far, direct = call(
+        pack_last_kernel, [edge] * 3 + [((rows, lanes), BF16), ((micro * rows, lanes), BF16)], (head, rel, two), whole(3),
+        moved=4 * 2**20,
     )
-    last = [last_own, shifted(last_right, True, 1), shifted(last_left, True, -1), shifted(last_far, True, 2)]
+    last = [last_own, shifted(last_right, True, 1), shifted(last_left, True, -1)]
+    last_far = shifted(last_far, True, 2)
     (acc,) = call(
         early_kernel, [((width, 2 * lanes), F32)], (right, own, from_left, from_right), whole(4),
         flops=2 * width * 2 * lanes * 3 * depth, moved=12 * 2**20,
     )
+    upper, lower, direct = lax.optimization_barrier((upper, lower, direct))
+    direct = shifted(direct, True, 2)
     send = ((width + TAIL, LANES), F32)
-    keep_far, keep_near, *sends = call(
-        late_kernel, [((width, LANES), F32)] * 2 + [send] * 6,
-        (acc, right, from_left, from_right, upper, lower, *last), whole(10),
-        scratch=[pltpu.VMEM((width, 2 * lanes), F32)],
-        flops=2 * width * 2 * lanes * (3 * rows + micro * rows), moved=12 * 2**20,
-    )
-    keep_far, rel = lax.optimization_barrier((keep_far, rel))
+
+    def late(z, two):
+        return call(
+            functools.partial(late_kernel, z), [((width, LANES), F32)] + [send] * 3,
+            (acc, right, from_left, from_right, upper, lower, *last, two), whole(10),
+            scratch=[pltpu.VMEM((width, lanes), F32)],
+            flops=2 * width * lanes * (3 * rows + micro * rows), moved=8 * 2**20,
+        )
+
+    keep_far, *far_sends = late(1, last_far)
+    keep_near, *near_sends = late(0, direct)
+    sends = far_sends + near_sends
+    keep_far, keep_near, rel = lax.optimization_barrier((keep_far, keep_near, rel))
     (second,) = call(second_kernel, [((rows, width), F32)], (rel, first, weights[0]), whole(3), **matmul)
     got = [shifted(s.astype(F16), False, by).astype(F32) for by, s in zip((1, 2, 3, 1, 2, 3), sends)]
     (far,) = call(far_kernel, [send], (keep_far, *got[:3]), whole(4), moved=4 * 2**20)

time: 91.2 us -> 89.7 us (0.984)
  the two profiles are of different devices: /device:TPU:32 before, /device:TPU:24 now
where the time goes in v6:
time: 89.7 us; the launch traced here: 87.9 us
  starting transfers between devices  36.7 us (41%)
  waiting for transfers between devices  30.2 us (34%)
  Pallas kernels  19.3 us (22%)
  between operations  0.92 us (1%)
    ppermute x14, waiting for transfers between devices, shifted(): return lax.ppermute(value, ('section', 'y', 'x'), pairs_over(along, by))  19.7 us
    pallas_call x9, Pallas kernels, call(): pl.pallas_call(kernel, out_shape=[jax.ShapeDtypeStruct(s, t) for s, t in...  19.3 us
    ppermute x14, starting transfers between devices, shifted(): return lax.ppermute(value, ('section', 'y', 'x'), pairs_over(along, by))  18.4 us
    ppermute x3, starting transfers between devices, on_first(): lax.ppermute(value, ('section', 'z_lo'), [(i, (i + by) % RING) for i in r...  11 us
    ppermute x3, waiting for transfers between devices, on_first(): lax.ppermute(value, ('section', 'z_lo'), [(i, (i + by) % RING) for i in r...  8.35 us
    ppermute x1, starting transfers between devices, local(): other = lax.ppermute(far.astype(F16), 'z_hi', [(0, 1), (1, 0)]).astype(F32)  6.03 us
    ppermute x1, waiting for transfers between devices, local(): shard = lax.ppermute(small, 'section', [(1, 0)])  2.13 us
  transfers between devices with their start and end apart: 19, of which 9 were waited for; matrix products, arithmetic and copies ran while one was open for 1% of the time, Pallas kernels for 13%

profile of v6, /device:TPU:24, one launch (start us, length us, event | category | flops | bytes accessed | tf_op | source)
XLA Modules:
  0.0 87.9 jit_solution(3240783312655374554)
XLA Ops:
  0.6 5.1 %shard_map.68 = (bf16[1984,512]{1,0:T(8,128)(2,1)S(1)}, bf16[1984,512]{1,0:T(8,128)(2,1)S(1)}, bf16[768,512]{1,0:T(8,128)(2,1)S(1)}, bf16[384,512]{1,0:T(8,128)(...) custom-call(s32[2]{0:T(128)} %pending_ref.1, bf16[4,128,1024]{2,1,0:T(8,128)(2,1)} %bitcast.14, ...), custom_call_target="tpu_custom_call" | custom-call | bytes 13631488 | tf_op jit(solution)/shard_map/pallas_call | solution.py:63
  5.7 2.8 %collective-permute-start.1 = (bf16[1984,512]{1,0:T(8,128)(2,1)S(1)}, bf16[1984,512]{1,0:T(8,128)(2,1)S(1)}, u32[]{:S(2)}, u32[]{:S(2)}) collective-permute-start(bf16[1984,512]{1,0:T(8,128)(2,1)S(1)} %get-tuple-element.37), channel_id=1, source_target_pairs={{0,3},{1,0},{2,1},{3,2},{4,7},{5,4},{6,5},{7,6},{8,11},{9,8},{10,9... | collective-permute-start | bytes 6094856 | tf_op jit(solution)/shard_map/ppermute | solution.py:51
  8.5 0.0 collective-permute-start
  8.5 2.9 %shard_map.69 = (f32[128,1024]{1,0:T(8,128)S(1)}, bf16[128,1024]{1,0:T(8,128)(2,1)S(1)}) custom-call(bf16[128,4096]{1,0:T(8,128)(2,1)S(1)} %get-tuple-element.38.grad_ref.head_ref, bf16[1024,4096]{1,0:T(8,128)(2,1)S(1)} %get-tuple-element.39.weight_ref), custom_call_target="tpu_custom_call" | custom-call | flops 1073741824 | bytes 2097152 | tf_op jit(solution)/shard_map/pallas_call | solution.py:63
  11.4 1.3 %collective-permute-start.2 = (bf16[128,1024]{1,0:T(8,128)(2,1)S(1)}, bf16[128,1024]{1,0:T(8,128)(2,1)S(1)}, u32[]{:S(2)}, u32[]{:S(2)}) collective-permute-start(bf16[128,1024]{1,0:T(8,128)(2,1)S(1)} %get-tuple-element.40), channel_id=1, source_target_pairs={{128,0},{129,1},{130,2},{131,3},{132,4},{133,5},{134,6},{135,7},{1... | collective-permute-start | bytes 786440 | tf_op jit(solution)/shard_map/ppermute | solution.py:245
  12.7 2.1 %collective-permute-done.2 = bf16[128,1024]{1,0:T(8,128)(2,1)S(1)} collective-permute-done((bf16[128,1024]{1,0:T(8,128)(2,1)S(1)}, bf16[128,1024]{1,0:T(8,128)(2,1)S(1)}, u32[]{:S(2)}, u32[]{:S(2)}) %collective-permute-start.2) | collective-permute-done | bytes 262176 | tf_op jit(solution)/shard_map/ppermute | solution.py:245
  14.9 6.5 %collective-permute-start.5 = (bf16[128,1024]{1,0:T(8,128)(2,1)S(1)}, bf16[128,1024]{1,0:T(8,128)(2,1)S(1)}, u32[]{:S(2)}, u32[]{:S(2)}) collective-permute-start(bf16[128,1024]{1,0:T(8,128)(2,1)S(1)} %collective-permute-done.2), channel_id=1, source_target_pairs={{0,96},{32,0},{64,32},{96,64},{1,97},{33,1},{65,33},{97,65},{2,98}... | collective-permute-start | bytes 786440 | tf_op jit(solution)/shard_map/ppermute | solution.py:223
  21.4 1.9 %collective-permute-start.4 = (bf16[128,1024]{1,0:T(8,128)(2,1)S(1)}, bf16[128,1024]{1,0:T(8,128)(2,1)S(1)}, u32[]{:S(2)}, u32[]{:S(2)}) collective-permute-start(bf16[128,1024]{1,0:T(8,128)(2,1)S(1)} %collective-permute-done.2), channel_id=1, source_target_pairs={{0,64},{32,96},{64,0},{96,32},{1,65},{33,97},{65,1},{97,33},{2,66}... | collective-permute-start | bytes 786440 | tf_op jit(solution)/shard_map/ppermute | solution.py:223
  23.3 2.6 %collective-permute-start.3 = (bf16[128,1024]{1,0:T(8,128)(2,1)S(1)}, bf16[128,1024]{1,0:T(8,128)(2,1)S(1)}, u32[]{:S(2)}, u32[]{:S(2)}) collective-permute-start(bf16[128,1024]{1,0:T(8,128)(2,1)S(1)} %collective-permute-done.2), channel_id=1, source_target_pairs={{0,32},{32,64},{64,96},{96,0},{1,33},{33,65},{65,97},{97,1},{2,34}... | collective-permute-start | bytes 786440 | tf_op jit(solution)/shard_map/ppermute | solution.py:223
  25.9 0.0 collective-permute-done.5
  25.9 8.3 %collective-permute-done.4 = bf16[128,1024]{1,0:T(8,128)(2,1)S(1)} collective-permute-done((bf16[128,1024]{1,0:T(8,128)(2,1)S(1)}, bf16[128,1024]{1,0:T(8,128)(2,1)S(1)}, u32[]{:S(2)}, u32[]{:S(2)}) %collective-permute-start.4) | collective-permute-done | bytes 262176 | tf_op jit(solution)/shard_map/ppermute | solution.py:223
  34.3 0.0 collective-permute-done.3
  34.3 0.0 collective-permute-done.1.right_ref
  34.3 0.8 collective-permute-done.left_ref
  35.2 2.5 %collective-permute-start.7 = (bf16[704,512]{1,0:T(8,128)(2,1)S(1)}, bf16[704,512]{1,0:T(8,128)(2,1)S(1)}, u32[]{:S(2)}, u32[]{:S(2)}) collective-permute-start(bf16[704,512]{1,0:T(8,128)(2,1)S(1)} %slice.7), channel_id=1, source_target_pairs={{0,3},{1,0},{2,1},{3,2},{4,7},{5,4},{6,5},{7,6},{8,11},{9,8},{10,9... | collective-permute-start | bytes 2162696 | tf_op jit(solution)/shard_map/ppermute | solution.py:51
  37.7 0.0 collective-permute-start.6
  37.7 0.1 pad_maximum_fusion.rel_ref
  37.8 0.6 shard_map.71
  38.5 0.1 collective-permute-start.8
  38.6 3.3 %collective-permute-start.9 = (bf16[256,512]{1,0:T(8,128)(2,1)S(1)}, bf16[256,512]{1,0:T(8,128)(2,1)S(1)}, u32[]{:S(2)}, u32[]{:S(2)}) collective-permute-start(bf16[256,512]{1,0:T(8,128)(2,1)S(1)} %get-tuple-element.53), channel_id=1, source_target_pairs={{0,3},{1,0},{2,1},{3,2},{4,7},{5,4},{6,5},{7,6},{8,11},{9,8},{10,9... | collective-permute-start | bytes 786440 | tf_op jit(solution)/shard_map/ppermute | solution.py:51
  41.9 1.4 %collective-permute-start.10 = (bf16[128,512]{1,0:T(8,128)(2,1)S(1)}, bf16[128,512]{1,0:T(8,128)(2,1)S(1)}, u32[]{:S(2)}, u32[]{:S(2)}) collective-permute-start(bf16[128,512]{1,0:T(8,128)(2,1)S(1)} %get-tuple-element.54), channel_id=1, source_target_pairs={{0,2},{1,3},{2,0},{3,1},{4,6},{5,7},{6,4},{7,5},{8,10},{9,11},{10,... | collective-permute-start | bytes 393224 | tf_op jit(solution)/shard_map/ppermute | solution.py:51
  43.3 3.3 %collective-permute-done.7.lower_ref = bf16[704,512]{1,0:T(8,128)(2,1)S(1)} collective-permute-done((bf16[704,512]{1,0:T(8,128)(2,1)S(1)}, bf16[704,512]{1,0:T(8,128)(2,1)S(1)}, u32[]{:S(2)}, u32[]{:S(2)}) %collective-permute-start.7) | collective-permute-done | bytes 720928 | tf_op jit(solution)/shard_map/ppermute | solution.py:51
  46.6 3.6 %collective-permute-done.6.upper_ref = bf16[704,512]{1,0:T(8,128)(2,1)S(1)} collective-permute-done((bf16[704,512]{1,0:T(8,128)(2,1)S(1)}, bf16[704,512]{1,0:T(8,128)(2,1)S(1)}, u32[]{:S(2)}, u32[]{:S(2)}) %collective-permute-start.6) | collective-permute-done | bytes 720928 | tf_op jit(solution)/shard_map/ppermute | solution.py:51
  50.2 0.0 collective-permute-start.11
  50.2 2.9 %shard_map.70.acc_ref = f32[1024,1024]{1,0:T(8,128)S(1)} custom-call(bf16[1984,512]{1,0:T(8,128)(2,1)S(1)} %get-tuple-element.35.mine_ref, bf16[768,512]{1,0:T(8,128)(2,1)S(1)} %get-tuple-element.36.own_ref, bf16[1984,512]{1,0:T(8,128)(2,1)S(1)} %collective-permute-done.left_ref, bf16[1984,512]{1,0:T(8,128)(2,1)S(1)} %collective-permute-done.1.right_ref), custom_call_target="tpu_custom_call" | custom-call | flops 2415919104 | bytes 12582912 | tf_op jit(solution)/shard_map/pallas_call | solution.py:63
  53.1 0.0 collective-permute-done.10.two_ref
  53.1 1.3 %collective-permute-done.8.left_last = bf16[256,512]{1,0:T(8,128)(2,1)S(1)} collective-permute-done((bf16[256,512]{1,0:T(8,128)(2,1)S(1)}, bf16[256,512]{1,0:T(8,128)(2,1)S(1)}, u32[]{:S(2)}, u32[]{:S(2)}) %collective-permute-start.8) | collective-permute-done | bytes 262176 | tf_op jit(solution)/shard_map/ppermute | solution.py:51
  54.4 0.0 collective-permute-done.9.right_last
  54.4 1.5 %shard_map.72 = (f32[1024,128]{1,0:T(8,128)S(1)}, f32[1040,128]{1,0:T(8,128)S(1)}, f32[1040,128]{1,0:T(8,128)S(1)}, f32[1040,128]{1,0:T(8,128)S(1)}) custom-call(f32[1024,1024]{1,0:T(8,128)S(1)} %shard_map.70.acc_ref, bf16[1984,512]{1,0:T(8,128)(2,1)S(1)} %get-tuple-element.35.mine_ref, bf16[1984,512]{1,0:T(8,128)(2,1)S(1)} %collective-permute-done.left_ref, ...), custom_call_target="tpu_custom_call" | custom-call | flops 939524096 | bytes 8388608 | tf_op jit(solution)/shard_map/pallas_call | solution.py:63
  56.0 0.8 collective-permute-start.17
  56.8 0.9 %collective-permute-start.16 = (f16[1040,128]{1,0:T(8,128)(2,1)S(1)}, f16[1040,128]{1,0:T(8,128)(2,1)S(1)}, u32[]{:S(2)}, u32[]{:S(2)}) collective-permute-start(f16[1040,128]{1,0:T(8,128)(2,1)S(1)} %convert_element_type.50), channel_id=1, source_target_pairs={{0,8},{1,9},{2,10},{3,11},{4,12},{5,13},{6,14},{7,15},{8,0},{9,1},... | collective-permute-start | bytes 798728 | tf_op jit(solution)/shard_map/ppermute | solution.py:51
  57.8 2.3 %collective-permute-start.15 = (f16[1040,128]{1,0:T(8,128)(2,1)S(1)}, f16[1040,128]{1,0:T(8,128)(2,1)S(1)}, u32[]{:S(2)}, u32[]{:S(2)}) collective-permute-start(f16[1040,128]{1,0:T(8,128)(2,1)S(1)} %convert_element_type.48), channel_id=1, source_target_pairs={{0,4},{1,5},{2,6},{3,7},{4,8},{5,9},{6,10},{7,11},{8,12},{9,13},{1... | collective-permute-start | bytes 798728 | tf_op jit(solution)/shard_map/ppermute | solution.py:51
  60.0 6.5 %collective-permute-done.17 = f16[1040,128]{1,0:T(8,128)(2,1)S(1)} collective-permute-done((f16[1040,128]{1,0:T(8,128)(2,1)S(1)}, f16[1040,128]{1,0:T(8,128)(2,1)S(1)}, u32[]{:S(2)}, u32[]{:S(2)}) %collective-permute-start.17) | collective-permute-done | bytes 266272 | tf_op jit(solution)/shard_map/ppermute | solution.py:51
  66.6 0.0 collective-permute-done.16
  66.6 0.8 collective-permute-done.15
  67.5 0.0 slice-start.1
  67.5 0.0 collective-permute-done.11.two_ref
  67.5 1.5 %shard_map.73 = (f32[1024,128]{1,0:T(8,128)S(1)}, f32[1040,128]{1,0:T(8,128)S(1)}, f32[1040,128]{1,0:T(8,128)S(1)}, f32[1040,128]{1,0:T(8,128)S(1)}) custom-call(f32[1024,1024]{1,0:T(8,128)S(1)} %shard_map.70.acc_ref, bf16[1984,512]{1,0:T(8,128)(2,1)S(1)} %get-tuple-element.35.mine_ref, bf16[1984,512]{1,0:T(8,128)(2,1)S(1)} %collective-permute-done.left_ref, ...), custom_call_target="tpu_custom_call" | custom-call | flops 939524096 | bytes 8388608 | tf_op jit(solution)/shard_map/pallas_call | solution.py:63
  69.0 0.3 shard_map.75
  69.3 6.0 %collective-permute-start.18 = (f16[1040,128]{1,0:T(8,128)(2,1)S(1)}, f16[1040,128]{1,0:T(8,128)(2,1)S(1)}, u32[]{:S(2)}, u32[]{:S(2)}) collective-permute-start(f16[1040,128]{1,0:T(8,128)(2,1)S(1)} %convert_element_type.54), channel_id=1, source_target_pairs={{0,16},{16,0},{1,17},{17,1},{2,18},{18,2},{3,19},{19,3},{4,20},{20... | collective-permute-start | bytes 798728 | tf_op jit(solution)/shard_map/ppermute | solution.py:283
  75.4 0.7 collective-permute-start.14
  76.1 3.5 %collective-permute-start.13 = (f16[1040,128]{1,0:T(8,128)(2,1)S(1)}, f16[1040,128]{1,0:T(8,128)(2,1)S(1)}, u32[]{:S(2)}, u32[]{:S(2)}) collective-permute-start(f16[1040,128]{1,0:T(8,128)(2,1)S(1)} %convert_element_type.44), channel_id=1, source_target_pairs={{0,8},{1,9},{2,10},{3,11},{4,12},{5,13},{6,14},{7,15},{8,0},{9,1},... | collective-permute-start | bytes 798728 | tf_op jit(solution)/shard_map/ppermute | solution.py:51
  79.6 0.1 collective-permute-start.12
  79.7 3.7 %shard_map.74 = f32[128,1024]{1,0:T(8,128)} custom-call(bf16[4,128,1024]{2,1,0:T(8,128)(2,1)S(1)} %pad_maximum_fusion.rel_ref, f32[128,1024]{1,0:T(8,128)S(1)} %get-tuple-element.59.first_ref, bf16[1024,4096]{1,0:T(8,128)(2,1)S(1)} %bitcast.12), custom_call_target="tpu_custom_call" | custom-call | flops 1073741824 | bytes 2097152 | tf_op jit(solution)/shard_map/pallas_call | solution.py:63
  83.4 0.0 collective-permute-done.18
  83.5 3.3 %collective-permute-done.13 = f16[1040,128]{1,0:T(8,128)(2,1)S(1)} collective-permute-done((f16[1040,128]{1,0:T(8,128)(2,1)S(1)}, f16[1040,128]{1,0:T(8,128)(2,1)S(1)}, u32[]{:S(2)}, u32[]{:S(2)}) %collective-permute-start.13) | collective-permute-done | bytes 266272 | tf_op jit(solution)/shard_map/ppermute | solution.py:51
  86.8 0.0 collective-permute-done.12
  86.9 1.0 %shard_map.76 = f32[1024,128]{1,0:T(8,128)} custom-call(f32[1024,128]{1,0:T(8,128)S(1)} %get-tuple-element.60.keep_ref, f32[1040,128]{1,0:T(8,128)S(1)} %convert_element_type.43.one_ref, f32[1040,128]{1,0:T(8,128)S(1)} %convert_element_type.45.two_ref, f32[1040,128]{1,0:T(8,128)S(1)} %convert_element_type.47.three_ref, ...), custom_call_target="tpu_custom_call" | custom-call | bytes 4194304 | tf_op jit(solution)/shard_map/pallas_call | solution.py:63
  (21 shorter events, 0.6 us)
Async XLA Ops:
  5.7 28.6 %collective-permute-start.1 = (bf16[1984,512]{1,0:T(8,128)(2,1)S(1)}, bf16[1984,512]{1,0:T(8,128)(2,1)S(1)}, u32[]{:S(2)}, u32[]{:S(2)}) collective-permute-start(bf16[1984,512]{1,0:T(8,128)(2,1)S(1)} %get-tuple-element.37), channel_id=1, source_target_pairs={{0,3},{1,0},{2,1},{3,2},{4,7},{5,4},{6,5},{7,6},{8,11},{9,8},{10,9... | collective-permute-start | bytes 6094856 | tf_op jit(solution)/shard_map/ppermute | solution.py:51
  8.5 26.5 %collective-permute-start = (bf16[1984,512]{1,0:T(8,128)(2,1)S(1)}, bf16[1984,512]{1,0:T(8,128)(2,1)S(1)}, u32[]{:S(2)}, u32[]{:S(2)}) collective-permute-start(bf16[1984,512]{1,0:T(8,128)(2,1)S(1)} %get-tuple-element.35.mine_ref), channel_id=1, source_target_pairs={{0,1},{1,2},{2,3},{3,0},{4,5},{5,6},{6,7},{7,4},{8,9},{9,10},{10,1... | collective-permute-start | bytes 6094856 | tf_op jit(solution)/shard_map/ppermute | solution.py:51
  11.4 3.4 %collective-permute-start.2 = (bf16[128,1024]{1,0:T(8,128)(2,1)S(1)}, bf16[128,1024]{1,0:T(8,128)(2,1)S(1)}, u32[]{:S(2)}, u32[]{:S(2)}) collective-permute-start(bf16[128,1024]{1,0:T(8,128)(2,1)S(1)} %get-tuple-element.40), channel_id=1, source_target_pairs={{128,0},{129,1},{130,2},{131,3},{132,4},{133,5},{134,6},{135,7},{1... | collective-permute-start | bytes 786440 | tf_op jit(solution)/shard_map/ppermute | solution.py:245
  14.9 11.0 %collective-permute-start.5 = (bf16[128,1024]{1,0:T(8,128)(2,1)S(1)}, bf16[128,1024]{1,0:T(8,128)(2,1)S(1)}, u32[]{:S(2)}, u32[]{:S(2)}) collective-permute-start(bf16[128,1024]{1,0:T(8,128)(2,1)S(1)} %collective-permute-done.2), channel_id=1, source_target_pairs={{0,96},{32,0},{64,32},{96,64},{1,97},{33,1},{65,33},{97,65},{2,98}... | collective-permute-start | bytes 786440 | tf_op jit(solution)/shard_map/ppermute | solution.py:223
  21.4 12.9 %collective-permute-start.4 = (bf16[128,1024]{1,0:T(8,128)(2,1)S(1)}, bf16[128,1024]{1,0:T(8,128)(2,1)S(1)}, u32[]{:S(2)}, u32[]{:S(2)}) collective-permute-start(bf16[128,1024]{1,0:T(8,128)(2,1)S(1)} %collective-permute-done.2), channel_id=1, source_target_pairs={{0,64},{32,96},{64,0},{96,32},{1,65},{33,97},{65,1},{97,33},{2,66}... | collective-permute-start | bytes 786440 | tf_op jit(solution)/shard_map/ppermute | solution.py:223
  23.3 10.9 %collective-permute-start.3 = (bf16[128,1024]{1,0:T(8,128)(2,1)S(1)}, bf16[128,1024]{1,0:T(8,128)(2,1)S(1)}, u32[]{:S(2)}, u32[]{:S(2)}) collective-permute-start(bf16[128,1024]{1,0:T(8,128)(2,1)S(1)} %collective-permute-done.2), channel_id=1, source_target_pairs={{0,32},{32,64},{64,96},{96,0},{1,33},{33,65},{65,97},{97,1},{2,34}... | collective-permute-start | bytes 786440 | tf_op jit(solution)/shard_map/ppermute | solution.py:223
  35.2 11.4 %collective-permute-start.7 = (bf16[704,512]{1,0:T(8,128)(2,1)S(1)}, bf16[704,512]{1,0:T(8,128)(2,1)S(1)}, u32[]{:S(2)}, u32[]{:S(2)}) collective-permute-start(bf16[704,512]{1,0:T(8,128)(2,1)S(1)} %slice.7), channel_id=1, source_target_pairs={{0,3},{1,0},{2,1},{3,2},{4,7},{5,4},{6,5},{7,6},{8,11},{9,8},{10,9... | collective-permute-start | bytes 2162696 | tf_op jit(solution)/shard_map/ppermute | solution.py:51
  37.7 12.5 %collective-permute-start.6 = (bf16[704,512]{1,0:T(8,128)(2,1)S(1)}, bf16[704,512]{1,0:T(8,128)(2,1)S(1)}, u32[]{:S(2)}, u32[]{:S(2)}) collective-permute-start(bf16[704,512]{1,0:T(8,128)(2,1)S(1)} %slice.6), channel_id=1, source_target_pairs={{0,1},{1,2},{2,3},{3,0},{4,5},{5,6},{6,7},{7,4},{8,9},{9,10},{10,1... | collective-permute-start | bytes 2162696 | tf_op jit(solution)/shard_map/ppermute | solution.py:51
  38.5 15.9 %collective-permute-start.8 = (bf16[256,512]{1,0:T(8,128)(2,1)S(1)}, bf16[256,512]{1,0:T(8,128)(2,1)S(1)}, u32[]{:S(2)}, u32[]{:S(2)}) collective-permute-start(bf16[256,512]{1,0:T(8,128)(2,1)S(1)} %get-tuple-element.52), channel_id=1, source_target_pairs={{0,1},{1,2},{2,3},{3,0},{4,5},{5,6},{6,7},{7,4},{8,9},{9,10},{10,1... | collective-permute-start | bytes 786440 | tf_op jit(solution)/shard_map/ppermute | solution.py:51
  38.6 15.8 %collective-permute-start.9 = (bf16[256,512]{1,0:T(8,128)(2,1)S(1)}, bf16[256,512]{1,0:T(8,128)(2,1)S(1)}, u32[]{:S(2)}, u32[]{:S(2)}) collective-permute-start(bf16[256,512]{1,0:T(8,128)(2,1)S(1)} %get-tuple-element.53), channel_id=1, source_target_pairs={{0,3},{1,0},{2,1},{3,2},{4,7},{5,4},{6,5},{7,6},{8,11},{9,8},{10,9... | collective-permute-start | bytes 786440 | tf_op jit(solution)/shard_map/ppermute | solution.py:51
  41.9 11.2 %collective-permute-start.10 = (bf16[128,512]{1,0:T(8,128)(2,1)S(1)}, bf16[128,512]{1,0:T(8,128)(2,1)S(1)}, u32[]{:S(2)}, u32[]{:S(2)}) collective-permute-start(bf16[128,512]{1,0:T(8,128)(2,1)S(1)} %get-tuple-element.54), channel_id=1, source_target_pairs={{0,2},{1,3},{2,0},{3,1},{4,6},{5,7},{6,4},{7,5},{8,10},{9,11},{10,... | collective-permute-start | bytes 393224 | tf_op jit(solution)/shard_map/ppermute | solution.py:51
  50.2 17.3 %collective-permute-start.11 = (bf16[512,512]{1,0:T(8,128)(2,1)S(1)}, bf16[512,512]{1,0:T(8,128)(2,1)S(1)}, u32[]{:S(2)}, u32[]{:S(2)}) collective-permute-start(bf16[512,512]{1,0:T(8,128)(2,1)S(1)} %get-tuple-element.56), channel_id=1, source_target_pairs={{0,2},{1,3},{2,0},{3,1},{4,6},{5,7},{6,4},{7,5},{8,10},{9,11},{10,... | collective-permute-start | bytes 1572872 | tf_op jit(solution)/shard_map/ppermute | solution.py:51
  56.0 10.6 %collective-permute-start.17 = (f16[1040,128]{1,0:T(8,128)(2,1)S(1)}, f16[1040,128]{1,0:T(8,128)(2,1)S(1)}, u32[]{:S(2)}, u32[]{:S(2)}) collective-permute-start(f16[1040,128]{1,0:T(8,128)(2,1)S(1)} %convert_element_type.52), channel_id=1, source_target_pairs={{0,12},{1,13},{2,14},{3,15},{4,0},{5,1},{6,2},{7,3},{8,4},{9,5},{1... | collective-permute-start | bytes 798728 | tf_op jit(solution)/shard_map/ppermute | solution.py:51
  56.8 9.8 %collective-permute-start.16 = (f16[1040,128]{1,0:T(8,128)(2,1)S(1)}, f16[1040,128]{1,0:T(8,128)(2,1)S(1)}, u32[]{:S(2)}, u32[]{:S(2)}) collective-permute-start(f16[1040,128]{1,0:T(8,128)(2,1)S(1)} %convert_element_type.50), channel_id=1, source_target_pairs={{0,8},{1,9},{2,10},{3,11},{4,12},{5,13},{6,14},{7,15},{8,0},{9,1},... | collective-permute-start | bytes 798728 | tf_op jit(solution)/shard_map/ppermute | solution.py:51
  57.8 9.7 %collective-permute-start.15 = (f16[1040,128]{1,0:T(8,128)(2,1)S(1)}, f16[1040,128]{1,0:T(8,128)(2,1)S(1)}, u32[]{:S(2)}, u32[]{:S(2)}) collective-permute-start(f16[1040,128]{1,0:T(8,128)(2,1)S(1)} %convert_element_type.48), channel_id=1, source_target_pairs={{0,4},{1,5},{2,6},{3,7},{4,8},{5,9},{6,10},{7,11},{8,12},{9,13},{1... | collective-permute-start | bytes 798728 | tf_op jit(solution)/shard_map/ppermute | solution.py:51
  67.4 12.3 %slice-start = ((s8[8388608]{0:T(1024)(128)(4,1)}), s8[4194304]{0:T(1024)(128)(4,1)S(1)}, s32[]{:S(2)}) async-start(s8[8388608]{0:T(1024)(128)(4,1)} %bitcast.10), calls=%async_computation | async-start | bytes 8388608
  67.5 12.2 %slice-start.1 = ((s8[8388608]{0:T(1024)(128)(4,1)}), s8[4194304]{0:T(1024)(128)(4,1)S(1)}, s32[]{:S(2)}) async-start(s8[8388608]{0:T(1024)(128)(4,1)} %bitcast.10), calls=%async_computation.1 | async-start | bytes 8388608
  69.3 14.1 %collective-permute-start.18 = (f16[1040,128]{1,0:T(8,128)(2,1)S(1)}, f16[1040,128]{1,0:T(8,128)(2,1)S(1)}, u32[]{:S(2)}, u32[]{:S(2)}) collective-permute-start(f16[1040,128]{1,0:T(8,128)(2,1)S(1)} %convert_element_type.54), channel_id=1, source_target_pairs={{0,16},{16,0},{1,17},{17,1},{2,18},{18,2},{3,19},{19,3},{4,20},{20... | collective-permute-start | bytes 798728 | tf_op jit(solution)/shard_map/ppermute | solution.py:283
  75.4 8.1 %collective-permute-start.14 = (f16[1040,128]{1,0:T(8,128)(2,1)S(1)}, f16[1040,128]{1,0:T(8,128)(2,1)S(1)}, u32[]{:S(2)}, u32[]{:S(2)}) collective-permute-start(f16[1040,128]{1,0:T(8,128)(2,1)S(1)} %convert_element_type.46), channel_id=1, source_target_pairs={{0,12},{1,13},{2,14},{3,15},{4,0},{5,1},{6,2},{7,3},{8,4},{9,5},{1... | collective-permute-start | bytes 798728 | tf_op jit(solution)/shard_map/ppermute | solution.py:51
  76.1 10.7 %collective-permute-start.13 = (f16[1040,128]{1,0:T(8,128)(2,1)S(1)}, f16[1040,128]{1,0:T(8,128)(2,1)S(1)}, u32[]{:S(2)}, u32[]{:S(2)}) collective-permute-start(f16[1040,128]{1,0:T(8,128)(2,1)S(1)} %convert_element_type.44), channel_id=1, source_target_pairs={{0,8},{1,9},{2,10},{3,11},{4,12},{5,13},{6,14},{7,15},{8,0},{9,1},... | collective-permute-start | bytes 798728 | tf_op jit(solution)/shard_map/ppermute | solution.py:51
  79.6 7.2 %collective-permute-start.12 = (f16[1040,128]{1,0:T(8,128)(2,1)S(1)}, f16[1040,128]{1,0:T(8,128)(2,1)S(1)}, u32[]{:S(2)}, u32[]{:S(2)}) collective-permute-start(f16[1040,128]{1,0:T(8,128)(2,1)S(1)} %convert_element_type.42), channel_id=1, source_target_pairs={{0,4},{1,5},{2,6},{3,7},{4,8},{5,9},{6,10},{7,11},{8,12},{9,13},{1... | collective-permute-start | bytes 798728 | tf_op jit(solution)/shard_map/ppermute | solution.py:51

commit v7 on v6

--- a/solution.py
+++ b/solution.py
@@ -17,6 +17,7 @@
 TOP = 15
 TINY = 1e-30
 ENTRY_LIMIT = 26
+ENTRY_FLOPS = 10**10
 
 
 def section():
@@ -74,16 +75,11 @@
 CONTRACT_LAST = (((1,), (1,)), ((), ()))
 
 
-def entry_kernel(pending_ref, x_ref, stash_ref, head_ref, weight_ref, right_ref, left_ref, own_ref, two_ref, head_out,
-                 weight_out, x_in, stash_in, count_in, sems):
+def entry_kernel(pending_ref, x_ref, stash_ref, right_ref, left_ref, own_ref, two_ref, x_in, stash_in, count_in, sems):
     micro, rows, width = x_ref.shape
     half, depth = width // 2, (micro - 1) * rows
     pieces = [(pending_ref, count_in), (x_ref, x_in)]
     pieces += [(stash_ref.at[m], stash_in.at[m]) for m in range(micro - 1)]
-    pieces += [(head_ref, head_out)]
-    parts = 4
-    share = width // parts
-    pieces += [(weight_ref.at[pl.ds(i * share, share)], weight_out.at[pl.ds(i * share, share)]) for i in range(parts)]
     copies = [pltpu.make_async_copy(a, b, sems.at[i]) for i, (a, b) in enumerate(pieces)]
     for copy in copies:
         copy.start()
@@ -110,8 +106,6 @@
             for b in range(RING):
                 source = stash_in[m, begin_m - m * rows:end_m - m * rows, pl.ds(block_start(z, along, b), LANES)]
                 out[base + begin_m - begin:base + end_m - begin, b * LANES:(b + 1) * LANES] = source
-    for copy in copies[1 + micro:]:
-        copy.wait()
 
 
 def first_kernel(grad_ref, weight_ref, out_ref, small_ref):
@@ -231,17 +225,17 @@
     matmul = dict(flops=2 * rows * width * columns, moved=2 * 2**20)
 
     side = ((width + depth // 2 + 2 * depth, lanes), BF16)
-    right, left, own, two, head, weight = call(
+    right, left, own, two = call(
         entry_kernel,
-        [side, side, ((2 * depth, lanes), BF16), ((depth, lanes), BF16), (head_grad.shape, BF16), ((width, columns), BF16)],
-        [in_hbm(v) for v in (pending, inputs, grads, head_grad, weights[0])], [pl.BlockSpec(memory_space=pltpu.HBM)] * 5,
+        [side, side, ((2 * depth, lanes), BF16), ((depth, lanes), BF16)],
+        [in_hbm(v) for v in (pending, inputs, grads)], [pl.BlockSpec(memory_space=pltpu.HBM)] * 3,
         scratch=[pltpu.VMEM(inputs.shape, BF16), pltpu.VMEM(grads.shape, BF16), pltpu.SMEM(pending.shape, pending.dtype),
                  pltpu.SemaphoreType.DMA((micro + 6,))],
-        moved=13 * 2**20, limit=ENTRY_LIMIT,
+        flops=ENTRY_FLOPS, moved=12 * 2**20, limit=ENTRY_LIMIT,
     )
     from_left, from_right = shifted(right, True, 1), shifted(left, True, -1)
 
-    first, small = call(first_kernel, [((rows, width), F32), ((rows, width), BF16)], (head, weight), whole(2), **matmul)
+    first, small = call(first_kernel, [((rows, width), F32), ((rows, width), BF16)], (head_grad, weights[0]), whole(2), **matmul)
     shard = lax.ppermute(small, "section", [(1, 0)])
     rel = [shard] + [on_first(shard, by) for by in range(1, RING)]
     from_left, from_right, *rel = lax.optimization_barrier((from_left, from_right, *rel))
@@ -252,7 +246,7 @@
     lower = shifted(from_right[half:half + passed], True, -1)
     edge = ((2 * rows, lanes), BF16)
     last_right, last_left, last_own, last_far, direct = call(
-        pack_last_kernel, [edge] * 3 + [((rows, lanes), BF16), ((micro * rows, lanes), BF16)], (head, rel, two), whole(3),
+        pack_last_kernel, [edge] * 3 + [((rows, lanes), BF16), ((micro * rows, lanes), BF16)], (head_grad, rel, two), whole(3),
         moved=4 * 2**20,
     )
     last = [last_own, shifted(last_right, True, 1), shifted(last_left, True, -1)]
@@ -261,7 +255,7 @@
         early_kernel, [((width, 2 * lanes), F32)], (right, own, from_left, from_right), whole(4),
         flops=2 * width * 2 * lanes * 3 * depth, moved=12 * 2**20,
     )
-    upper, lower, direct = lax.optimization_barrier((upper, lower, direct))
+    acc, upper, lower, last_far, direct, *last = lax.optimization_barrier((acc, upper, lower, last_far, direct, *last))
     direct = shifted(direct, True, 2)
     send = ((width + TAIL, LANES), F32)
 
@@ -276,9 +270,10 @@
     keep_far, *far_sends = late(1, last_far)
     keep_near, *near_sends = late(0, direct)
     sends = far_sends + near_sends
-    keep_far, keep_near, rel = lax.optimization_barrier((keep_far, keep_near, rel))
+    got = [shifted(s.astype(F16), False, by) for by, s in zip((1, 2, 3, 1, 2, 3), sends)]
+    rel, *got[:4] = lax.optimization_barrier((rel, *got[:4]))
+    got = [v.astype(F32) for v in got]
     (second,) = call(second_kernel, [((rows, width), F32)], (rel, first, weights[0]), whole(3), **matmul)
-    got = [shifted(s.astype(F16), False, by).astype(F32) for by, s in zip((1, 2, 3, 1, 2, 3), sends)]
     (far,) = call(far_kernel, [send], (keep_far, *got[:3]), whole(4), moved=4 * 2**20)
     other = lax.ppermute(far.astype(F16), "z_hi", [(0, 1), (1, 0)]).astype(F32)
     (block,) = call(near_kernel, [((width, LANES), F32)], (keep_near, *got[3:], other), whole(5), moved=4 * 2**20)

time: 89.7 us -> 91.2 us (1.017)
  the two profiles are of different devices: /device:TPU:24 before, /device:TPU:50 now
where the time goes in v7:
time: 91.2 us; the launch traced here: 91 us
  starting transfers between devices  37.2 us (41%)
  waiting for transfers between devices  35.1 us (38%)
  Pallas kernels  16.9 us (19%)
    ppermute x14, waiting for transfers between devices, shifted(): return lax.ppermute(value, ('section', 'y', 'x'), pairs_over(along, by))  22.6 us
    ppermute x14, starting transfers between devices, shifted(): return lax.ppermute(value, ('section', 'y', 'x'), pairs_over(along, by))  18.5 us
    pallas_call x9, Pallas kernels, call(): pl.pallas_call(kernel, out_shape=[jax.ShapeDtypeStruct(s, t) for s, t in...  16.9 us
    ppermute x3, starting transfers between devices, on_first(): lax.ppermute(value, ('section', 'z_lo'), [(i, (i + by) % RING) for i in r...  11 us
    ppermute x3, waiting for transfers between devices, on_first(): lax.ppermute(value, ('section', 'z_lo'), [(i, (i + by) % RING) for i in r...  6.94 us
    ppermute x1, starting transfers between devices, local(): other = lax.ppermute(far.astype(F16), 'z_hi', [(0, 1), (1, 0)]).astype(F32)  6.38 us
    ppermute x1, waiting for transfers between devices, local(): other = lax.ppermute(far.astype(F16), 'z_hi', [(0, 1), (1, 0)]).astype(F32)  3.45 us
    ppermute x1, waiting for transfers between devices, local(): shard = lax.ppermute(small, 'section', [(1, 0)])  2.13 us
  transfers between devices with their start and end apart: 19, of which 8 were waited for; matrix products, arithmetic and copies ran while one was open for 1% of the time, Pallas kernels for 15%

profile of v7, /device:TPU:50, one launch (start us, length us, event | category | flops | bytes accessed | tf_op | source)
XLA Modules:
  0.0 91.0 jit_solution(12217561665448771429)
XLA Ops:
  0.6 0.0 slice-start
  0.6 0.0 slice-start.1
  0.7 2.7 %shard_map.68 = (bf16[1984,512]{1,0:T(8,128)(2,1)S(1)}, bf16[1984,512]{1,0:T(8,128)(2,1)S(1)}, bf16[768,512]{1,0:T(8,128)(2,1)S(1)}, bf16[384,512]{1,0:T(8,128)(2,1)S(1)}) custom-call(s32[2]{0:T(128)} %pending_ref.1, bf16[4,128,1024]{2,1,0:T(8,128)(2,1)} %bitcast.20, bf16[3,128,4096]{2,1,0:T(8,128)(2,1)} %bitcast.19), custom_call_target="tpu_custom_call" | custom-call | flops 10000000000 | bytes 12582912 | tf_op jit(solution)/shard_map/pallas_call | solution.py:64
  3.4 1.6 %collective-permute-start = (bf16[1984,512]{1,0:T(8,128)(2,1)S(1)}, bf16[1984,512]{1,0:T(8,128)(2,1)S(1)}, u32[]{:S(2)}, u32[]{:S(2)}) collective-permute-start(bf16[1984,512]{1,0:T(8,128)(2,1)S(1)} %get-tuple-element.40.mine_ref), channel_id=1, source_target_pairs={{0,1},{1,2},{2,3},{3,0},{4,5},{5,6},{6,7},{7,4},{8,9},{9,10},{10,1... | collective-permute-start | bytes 6094856 | tf_op jit(solution)/shard_map/ppermute | solution.py:52
  4.9 0.5 collective-permute-start.1
  5.5 0.1 copy-done
  5.6 2.9 %shard_map.69 = (f32[128,1024]{1,0:T(8,128)S(1)}, bf16[128,1024]{1,0:T(8,128)(2,1)S(1)}) custom-call(bf16[128,4096]{1,0:T(8,128)(2,1)S(1)} %copy-done, bf16[1024,4096]{1,0:T(8,128)(2,1)S(1)} %bitcast.11), custom_call_target="tpu_custom_call" | custom-call | flops 1073741824 | bytes 2097152 | tf_op jit(solution)/shard_map/pallas_call | solution.py:64
  8.5 1.3 %collective-permute-start.2 = (bf16[128,1024]{1,0:T(8,128)(2,1)S(1)}, bf16[128,1024]{1,0:T(8,128)(2,1)S(1)}, u32[]{:S(2)}, u32[]{:S(2)}) collective-permute-start(bf16[128,1024]{1,0:T(8,128)(2,1)S(1)} %get-tuple-element.42), channel_id=1, source_target_pairs={{128,0},{129,1},{130,2},{131,3},{132,4},{133,5},{134,6},{135,7},{1... | collective-permute-start | bytes 786440 | tf_op jit(solution)/shard_map/ppermute | solution.py:239
  9.8 2.1 %collective-permute-done.2 = bf16[128,1024]{1,0:T(8,128)(2,1)S(1)} collective-permute-done((bf16[128,1024]{1,0:T(8,128)(2,1)S(1)}, bf16[128,1024]{1,0:T(8,128)(2,1)S(1)}, u32[]{:S(2)}, u32[]{:S(2)}) %collective-permute-start.2) | collective-permute-done | bytes 262176 | tf_op jit(solution)/shard_map/ppermute | solution.py:239
  11.9 3.8 %collective-permute-start.3 = (bf16[128,1024]{1,0:T(8,128)(2,1)S(1)}, bf16[128,1024]{1,0:T(8,128)(2,1)S(1)}, u32[]{:S(2)}, u32[]{:S(2)}) collective-permute-start(bf16[128,1024]{1,0:T(8,128)(2,1)S(1)} %collective-permute-done.2), channel_id=1, source_target_pairs={{0,32},{32,64},{64,96},{96,0},{1,33},{33,65},{65,97},{97,1},{2,34}... | collective-permute-start | bytes 786440 | tf_op jit(solution)/shard_map/ppermute | solution.py:217
  15.7 3.3 %collective-permute-start.4 = (bf16[128,1024]{1,0:T(8,128)(2,1)S(1)}, bf16[128,1024]{1,0:T(8,128)(2,1)S(1)}, u32[]{:S(2)}, u32[]{:S(2)}) collective-permute-start(bf16[128,1024]{1,0:T(8,128)(2,1)S(1)} %collective-permute-done.2), channel_id=1, source_target_pairs={{0,64},{32,96},{64,0},{96,32},{1,65},{33,97},{65,1},{97,33},{2,66}... | collective-permute-start | bytes 786440 | tf_op jit(solution)/shard_map/ppermute | solution.py:217
  19.0 3.9 %collective-permute-start.5 = (bf16[128,1024]{1,0:T(8,128)(2,1)S(1)}, bf16[128,1024]{1,0:T(8,128)(2,1)S(1)}, u32[]{:S(2)}, u32[]{:S(2)}) collective-permute-start(bf16[128,1024]{1,0:T(8,128)(2,1)S(1)} %collective-permute-done.2), channel_id=1, source_target_pairs={{0,96},{32,0},{64,32},{96,64},{1,97},{33,1},{65,33},{97,65},{2,98}... | collective-permute-start | bytes 786440 | tf_op jit(solution)/shard_map/ppermute | solution.py:217
  23.0 0.0 collective-permute-done.3
  23.0 5.5 %collective-permute-done.4 = bf16[128,1024]{1,0:T(8,128)(2,1)S(1)} collective-permute-done((bf16[128,1024]{1,0:T(8,128)(2,1)S(1)}, bf16[128,1024]{1,0:T(8,128)(2,1)S(1)}, u32[]{:S(2)}, u32[]{:S(2)}) %collective-permute-start.4) | collective-permute-done | bytes 262176 | tf_op jit(solution)/shard_map/ppermute | solution.py:217
  28.5 1.4 %collective-permute-done.5 = bf16[128,1024]{1,0:T(8,128)(2,1)S(1)} collective-permute-done((bf16[128,1024]{1,0:T(8,128)(2,1)S(1)}, bf16[128,1024]{1,0:T(8,128)(2,1)S(1)}, u32[]{:S(2)}, u32[]{:S(2)}) %collective-permute-start.5) | collective-permute-done | bytes 262176 | tf_op jit(solution)/shard_map/ppermute | solution.py:217
  29.9 0.0 collective-permute-done.left_ref
  29.9 0.4 collective-permute-done.1.right_ref
  30.3 1.3 %collective-permute-start.6 = (bf16[704,512]{1,0:T(8,128)(2,1)S(1)}, bf16[704,512]{1,0:T(8,128)(2,1)S(1)}, u32[]{:S(2)}, u32[]{:S(2)}) collective-permute-start(bf16[704,512]{1,0:T(8,128)(2,1)S(1)} %slice.6), channel_id=1, source_target_pairs={{0,1},{1,2},{2,3},{3,0},{4,5},{5,6},{6,7},{7,4},{8,9},{9,10},{10,1... | collective-permute-start | bytes 2162696 | tf_op jit(solution)/shard_map/ppermute | solution.py:52
  31.6 0.9 collective-permute-start.7
  32.5 0.1 pad_maximum_fusion.rel_ref
  32.7 0.6 shard_map.71
  33.3 1.3 %collective-permute-start.9 = (bf16[256,512]{1,0:T(8,128)(2,1)S(1)}, bf16[256,512]{1,0:T(8,128)(2,1)S(1)}, u32[]{:S(2)}, u32[]{:S(2)}) collective-permute-start(bf16[256,512]{1,0:T(8,128)(2,1)S(1)} %get-tuple-element.54), channel_id=1, source_target_pairs={{0,1},{1,2},{2,3},{3,0},{4,5},{5,6},{6,7},{7,4},{8,9},{9,10},{10,1... | collective-permute-start | bytes 786440 | tf_op jit(solution)/shard_map/ppermute | solution.py:52
  34.6 1.4 %collective-permute-start.10 = (bf16[256,512]{1,0:T(8,128)(2,1)S(1)}, bf16[256,512]{1,0:T(8,128)(2,1)S(1)}, u32[]{:S(2)}, u32[]{:S(2)}) collective-permute-start(bf16[256,512]{1,0:T(8,128)(2,1)S(1)} %get-tuple-element.55), channel_id=1, source_target_pairs={{0,3},{1,0},{2,1},{3,2},{4,7},{5,4},{6,5},{7,6},{8,11},{9,8},{10,9... | collective-permute-start | bytes 786440 | tf_op jit(solution)/shard_map/ppermute | solution.py:52
  36.0 2.0 %collective-permute-start.8 = (bf16[128,512]{1,0:T(8,128)(2,1)S(1)}, bf16[128,512]{1,0:T(8,128)(2,1)S(1)}, u32[]{:S(2)}, u32[]{:S(2)}) collective-permute-start(bf16[128,512]{1,0:T(8,128)(2,1)S(1)} %get-tuple-element.51), channel_id=1, source_target_pairs={{0,2},{1,3},{2,0},{3,1},{4,6},{5,7},{6,4},{7,5},{8,10},{9,11},{10,... | collective-permute-start | bytes 393224 | tf_op jit(solution)/shard_map/ppermute | solution.py:52
  38.0 2.9 %shard_map.70.acc_ref = f32[1024,1024]{1,0:T(8,128)S(1)} custom-call(bf16[1984,512]{1,0:T(8,128)(2,1)S(1)} %get-tuple-element.40.mine_ref, bf16[768,512]{1,0:T(8,128)(2,1)S(1)} %get-tuple-element.47.own_ref, bf16[1984,512]{1,0:T(8,128)(2,1)S(1)} %collective-permute-done.left_ref, bf16[1984,512]{1,0:T(8,128)(2,1)S(1)} %collective-permute-done.1.right_ref), custom_call_target="tpu_custom_call" | custom-call | flops 2415919104 | bytes 12582912 | tf_op jit(solution)/shard_map/pallas_call | solution.py:64
  40.8 7.5 %collective-permute-done.8.two_ref = bf16[128,512]{1,0:T(8,128)(2,1)S(1)} collective-permute-done((bf16[128,512]{1,0:T(8,128)(2,1)S(1)}, bf16[128,512]{1,0:T(8,128)(2,1)S(1)}, u32[]{:S(2)}, u32[]{:S(2)}) %collective-permute-start.8) | collective-permute-done | bytes 131104 | tf_op jit(solution)/shard_map/ppermute | solution.py:52
  48.3 0.0 collective-permute-done.9.left_last
  48.3 0.0 collective-permute-done.10.right_last
  48.3 0.0 collective-permute-done.6.upper_ref
  48.3 0.0 collective-permute-done.7.lower_ref
  48.4 2.2 %collective-permute-start.14 = (bf16[512,512]{1,0:T(8,128)(2,1)S(1)}, bf16[512,512]{1,0:T(8,128)(2,1)S(1)}, u32[]{:S(2)}, u32[]{:S(2)}) collective-permute-start(bf16[512,512]{1,0:T(8,128)(2,1)S(1)} %get-tuple-element.66), channel_id=1, source_target_pairs={{0,2},{1,3},{2,0},{3,1},{4,6},{5,7},{6,4},{7,5},{8,10},{9,11},{10,... | collective-permute-start | bytes 1572872 | tf_op jit(solution)/shard_map/ppermute | solution.py:52
  50.6 1.5 %shard_map.72 = (f32[1024,128]{1,0:T(8,128)S(1)}, f32[1040,128]{1,0:T(8,128)S(1)}, f32[1040,128]{1,0:T(8,128)S(1)}, f32[1040,128]{1,0:T(8,128)S(1)}) custom-call(f32[1024,1024]{1,0:T(8,128)S(1)} %shard_map.70.acc_ref, bf16[1984,512]{1,0:T(8,128)(2,1)S(1)} %get-tuple-element.40.mine_ref, bf16[1984,512]{1,0:T(8,128)(2,1)S(1)} %collective-permute-done.left_ref, ...), custom_call_target="tpu_custom_call" | custom-call | flops 939524096 | bytes 8388608 | tf_op jit(solution)/shard_map/pallas_call | solution.py:64
  52.1 1.4 %collective-permute-start.11 = (f16[1040,128]{1,0:T(8,128)(2,1)S(1)}, f16[1040,128]{1,0:T(8,128)(2,1)S(1)}, u32[]{:S(2)}, u32[]{:S(2)}) collective-permute-start(f16[1040,128]{1,0:T(8,128)(2,1)S(1)} %convert_element_type.42), channel_id=1, source_target_pairs={{0,4},{1,5},{2,6},{3,7},{4,8},{5,9},{6,10},{7,11},{8,12},{9,13},{1... | collective-permute-start | bytes 798728 | tf_op jit(solution)/shard_map/ppermute | solution.py:52
  53.5 0.7 collective-permute-start.12
  54.3 2.1 %collective-permute-start.13 = (f16[1040,128]{1,0:T(8,128)(2,1)S(1)}, f16[1040,128]{1,0:T(8,128)(2,1)S(1)}, u32[]{:S(2)}, u32[]{:S(2)}) collective-permute-start(f16[1040,128]{1,0:T(8,128)(2,1)S(1)} %convert_element_type.44), channel_id=1, source_target_pairs={{0,12},{1,13},{2,14},{3,15},{4,0},{5,1},{6,2},{7,3},{8,4},{9,5},{1... | collective-permute-start | bytes 798728 | tf_op jit(solution)/shard_map/ppermute | solution.py:52
  56.3 8.7 %collective-permute-done.14.two_ref = bf16[512,512]{1,0:T(8,128)(2,1)S(1)} collective-permute-done((bf16[512,512]{1,0:T(8,128)(2,1)S(1)}, bf16[512,512]{1,0:T(8,128)(2,1)S(1)}, u32[]{:S(2)}, u32[]{:S(2)}) %collective-permute-start.14) | collective-permute-done | bytes 524320 | tf_op jit(solution)/shard_map/ppermute | solution.py:52
  65.0 1.5 %shard_map.73 = (f32[1024,128]{1,0:T(8,128)S(1)}, f32[1040,128]{1,0:T(8,128)S(1)}, f32[1040,128]{1,0:T(8,128)S(1)}, f32[1040,128]{1,0:T(8,128)S(1)}) custom-call(f32[1024,1024]{1,0:T(8,128)S(1)} %shard_map.70.acc_ref, bf16[1984,512]{1,0:T(8,128)(2,1)S(1)} %get-tuple-element.40.mine_ref, bf16[1984,512]{1,0:T(8,128)(2,1)S(1)} %collective-permute-done.left_ref, ...), custom_call_target="tpu_custom_call" | custom-call | flops 939524096 | bytes 8388608 | tf_op jit(solution)/shard_map/pallas_call | solution.py:64
  66.5 1.1 %collective-permute-start.15 = (f16[1040,128]{1,0:T(8,128)(2,1)S(1)}, f16[1040,128]{1,0:T(8,128)(2,1)S(1)}, u32[]{:S(2)}, u32[]{:S(2)}) collective-permute-start(f16[1040,128]{1,0:T(8,128)(2,1)S(1)} %convert_element_type.45), channel_id=1, source_target_pairs={{0,4},{1,5},{2,6},{3,7},{4,8},{5,9},{6,10},{7,11},{8,12},{9,13},{1... | collective-permute-start | bytes 798728 | tf_op jit(solution)/shard_map/ppermute | solution.py:52
  67.6 0.6 collective-permute-start.16
  68.3 1.5 %collective-permute-start.17 = (f16[1040,128]{1,0:T(8,128)(2,1)S(1)}, f16[1040,128]{1,0:T(8,128)(2,1)S(1)}, u32[]{:S(2)}, u32[]{:S(2)}) collective-permute-start(f16[1040,128]{1,0:T(8,128)(2,1)S(1)} %convert_element_type.49), channel_id=1, source_target_pairs={{0,12},{1,13},{2,14},{3,15},{4,0},{5,1},{6,2},{7,3},{8,4},{9,5},{1... | collective-permute-start | bytes 798728 | tf_op jit(solution)/shard_map/ppermute | solution.py:52
  69.8 6.0 %collective-permute-done.15 = f16[1040,128]{1,0:T(8,128)(2,1)S(1)} collective-permute-done((f16[1040,128]{1,0:T(8,128)(2,1)S(1)}, f16[1040,128]{1,0:T(8,128)(2,1)S(1)}, u32[]{:S(2)}, u32[]{:S(2)}) %collective-permute-start.15) | collective-permute-done | bytes 266272 | tf_op jit(solution)/shard_map/ppermute | solution.py:52
  76.0 0.3 shard_map.75
  76.3 6.4 %collective-permute-start.18 = (f16[1040,128]{1,0:T(8,128)(2,1)S(1)}, f16[1040,128]{1,0:T(8,128)(2,1)S(1)}, u32[]{:S(2)}, u32[]{:S(2)}) collective-permute-start(f16[1040,128]{1,0:T(8,128)(2,1)S(1)} %convert_element_type.54), channel_id=1, source_target_pairs={{0,16},{16,0},{1,17},{17,1},{2,18},{18,2},{3,19},{19,3},{4,20},{20... | collective-permute-start | bytes 798728 | tf_op jit(solution)/shard_map/ppermute | solution.py:278
  82.7 0.0 collective-permute-done.16
  82.7 0.0 collective-permute-done.17
  82.8 3.7 %shard_map.74 = f32[128,1024]{1,0:T(8,128)} custom-call(bf16[4,128,1024]{2,1,0:T(8,128)(2,1)S(1)} %pad_maximum_fusion.rel_ref, f32[128,1024]{1,0:T(8,128)S(1)} %get-tuple-element.69.first_ref, bf16[1024,4096]{1,0:T(8,128)(2,1)S(1)} %bitcast.12), custom_call_target="tpu_custom_call" | custom-call | flops 1073741824 | bytes 2097152 | tf_op jit(solution)/shard_map/pallas_call | solution.py:64
  86.5 3.5 %collective-permute-done.18 = f16[1040,128]{1,0:T(8,128)(2,1)S(1)} collective-permute-done((f16[1040,128]{1,0:T(8,128)(2,1)S(1)}, f16[1040,128]{1,0:T(8,128)(2,1)S(1)}, u32[]{:S(2)}, u32[]{:S(2)}) %collective-permute-start.18) | collective-permute-done | bytes 266272 | tf_op jit(solution)/shard_map/ppermute | solution.py:278
  90.0 1.0 %shard_map.76 = f32[1024,128]{1,0:T(8,128)} custom-call(f32[1024,128]{1,0:T(8,128)S(1)} %get-tuple-element.70.keep_ref, f32[1040,128]{1,0:T(8,128)S(1)} %convert_element_type.46.one_ref, f32[1040,128]{1,0:T(8,128)S(1)} %convert_element_type.48.two_ref, f32[1040,128]{1,0:T(8,128)S(1)} %convert_element_type.50.three_ref, ...), custom_call_target="tpu_custom_call" | custom-call | bytes 4194304 | tf_op jit(solution)/shard_map/pallas_call | solution.py:64
  (23 shorter events, 0.6 us)
Async XLA Ops:
  0.6 4.8 %slice-start = ((s8[8388608]{0:T(1024)(128)(4,1)}), s8[4194304]{0:T(1024)(128)(4,1)S(1)}, s32[]{:S(2)}) async-start(s8[8388608]{0:T(1024)(128)(4,1)} %bitcast.9), calls=%async_computation | async-start | bytes 8388608
  0.6 4.8 %slice-start.1 = ((s8[8388608]{0:T(1024)(128)(4,1)}), s8[4194304]{0:T(1024)(128)(4,1)S(1)}, s32[]{:S(2)}) async-start(s8[8388608]{0:T(1024)(128)(4,1)} %bitcast.9), calls=%async_computation.1 | async-start | bytes 8388608
  0.7 4.9 %copy-start = (bf16[128,4096]{1,0:T(8,128)(2,1)S(1)}, bf16[128,4096]{1,0:T(8,128)(2,1)}, u32[]{:S(2)}) copy-start(bf16[128,4096]{1,0:T(8,128)(2,1)} %head_ref.1) | copy-start | bytes 3145732
  3.4 26.5 %collective-permute-start = (bf16[1984,512]{1,0:T(8,128)(2,1)S(1)}, bf16[1984,512]{1,0:T(8,128)(2,1)S(1)}, u32[]{:S(2)}, u32[]{:S(2)}) collective-permute-start(bf16[1984,512]{1,0:T(8,128)(2,1)S(1)} %get-tuple-element.40.mine_ref), channel_id=1, source_target_pairs={{0,1},{1,2},{2,3},{3,0},{4,5},{5,6},{6,7},{7,4},{8,9},{9,10},{10,1... | collective-permute-start | bytes 6094856 | tf_op jit(solution)/shard_map/ppermute | solution.py:52
  4.9 25.3 %collective-permute-start.1 = (bf16[1984,512]{1,0:T(8,128)(2,1)S(1)}, bf16[1984,512]{1,0:T(8,128)(2,1)S(1)}, u32[]{:S(2)}, u32[]{:S(2)}) collective-permute-start(bf16[1984,512]{1,0:T(8,128)(2,1)S(1)} %get-tuple-element.41), channel_id=1, source_target_pairs={{0,3},{1,0},{2,1},{3,2},{4,7},{5,4},{6,5},{7,6},{8,11},{9,8},{10,9... | collective-permute-start | bytes 6094856 | tf_op jit(solution)/shard_map/ppermute | solution.py:52
  8.5 3.4 %collective-permute-start.2 = (bf16[128,1024]{1,0:T(8,128)(2,1)S(1)}, bf16[128,1024]{1,0:T(8,128)(2,1)S(1)}, u32[]{:S(2)}, u32[]{:S(2)}) collective-permute-start(bf16[128,1024]{1,0:T(8,128)(2,1)S(1)} %get-tuple-element.42), channel_id=1, source_target_pairs={{128,0},{129,1},{130,2},{131,3},{132,4},{133,5},{134,6},{135,7},{1... | collective-permute-start | bytes 786440 | tf_op jit(solution)/shard_map/ppermute | solution.py:239
  11.9 11.0 %collective-permute-start.3 = (bf16[128,1024]{1,0:T(8,128)(2,1)S(1)}, bf16[128,1024]{1,0:T(8,128)(2,1)S(1)}, u32[]{:S(2)}, u32[]{:S(2)}) collective-permute-start(bf16[128,1024]{1,0:T(8,128)(2,1)S(1)} %collective-permute-done.2), channel_id=1, source_target_pairs={{0,32},{32,64},{64,96},{96,0},{1,33},{33,65},{65,97},{97,1},{2,34}... | collective-permute-start | bytes 786440 | tf_op jit(solution)/shard_map/ppermute | solution.py:217
  15.7 12.8 %collective-permute-start.4 = (bf16[128,1024]{1,0:T(8,128)(2,1)S(1)}, bf16[128,1024]{1,0:T(8,128)(2,1)S(1)}, u32[]{:S(2)}, u32[]{:S(2)}) collective-permute-start(bf16[128,1024]{1,0:T(8,128)(2,1)S(1)} %collective-permute-done.2), channel_id=1, source_target_pairs={{0,64},{32,96},{64,0},{96,32},{1,65},{33,97},{65,1},{97,33},{2,66}... | collective-permute-start | bytes 786440 | tf_op jit(solution)/shard_map/ppermute | solution.py:217
  19.0 10.9 %collective-permute-start.5 = (bf16[128,1024]{1,0:T(8,128)(2,1)S(1)}, bf16[128,1024]{1,0:T(8,128)(2,1)S(1)}, u32[]{:S(2)}, u32[]{:S(2)}) collective-permute-start(bf16[128,1024]{1,0:T(8,128)(2,1)S(1)} %collective-permute-done.2), channel_id=1, source_target_pairs={{0,96},{32,0},{64,32},{96,64},{1,97},{33,1},{65,33},{97,65},{2,98}... | collective-permute-start | bytes 786440 | tf_op jit(solution)/shard_map/ppermute | solution.py:217
  30.3 18.0 %collective-permute-start.6 = (bf16[704,512]{1,0:T(8,128)(2,1)S(1)}, bf16[704,512]{1,0:T(8,128)(2,1)S(1)}, u32[]{:S(2)}, u32[]{:S(2)}) collective-permute-start(bf16[704,512]{1,0:T(8,128)(2,1)S(1)} %slice.6), channel_id=1, source_target_pairs={{0,1},{1,2},{2,3},{3,0},{4,5},{5,6},{6,7},{7,4},{8,9},{9,10},{10,1... | collective-permute-start | bytes 2162696 | tf_op jit(solution)/shard_map/ppermute | solution.py:52
  31.6 16.7 %collective-permute-start.7 = (bf16[704,512]{1,0:T(8,128)(2,1)S(1)}, bf16[704,512]{1,0:T(8,128)(2,1)S(1)}, u32[]{:S(2)}, u32[]{:S(2)}) collective-permute-start(bf16[704,512]{1,0:T(8,128)(2,1)S(1)} %slice.7), channel_id=1, source_target_pairs={{0,3},{1,0},{2,1},{3,2},{4,7},{5,4},{6,5},{7,6},{8,11},{9,8},{10,9... | collective-permute-start | bytes 2162696 | tf_op jit(solution)/shard_map/ppermute | solution.py:52
  33.3 15.0 %collective-permute-start.9 = (bf16[256,512]{1,0:T(8,128)(2,1)S(1)}, bf16[256,512]{1,0:T(8,128)(2,1)S(1)}, u32[]{:S(2)}, u32[]{:S(2)}) collective-permute-start(bf16[256,512]{1,0:T(8,128)(2,1)S(1)} %get-tuple-element.54), channel_id=1, source_target_pairs={{0,1},{1,2},{2,3},{3,0},{4,5},{5,6},{6,7},{7,4},{8,9},{9,10},{10,1... | collective-permute-start | bytes 786440 | tf_op jit(solution)/shard_map/ppermute | solution.py:52
  34.6 13.7 %collective-permute-start.10 = (bf16[256,512]{1,0:T(8,128)(2,1)S(1)}, bf16[256,512]{1,0:T(8,128)(2,1)S(1)}, u32[]{:S(2)}, u32[]{:S(2)}) collective-permute-start(bf16[256,512]{1,0:T(8,128)(2,1)S(1)} %get-tuple-element.55), channel_id=1, source_target_pairs={{0,3},{1,0},{2,1},{3,2},{4,7},{5,4},{6,5},{7,6},{8,11},{9,8},{10,9... | collective-permute-start | bytes 786440 | tf_op jit(solution)/shard_map/ppermute | solution.py:52
  36.0 12.3 %collective-permute-start.8 = (bf16[128,512]{1,0:T(8,128)(2,1)S(1)}, bf16[128,512]{1,0:T(8,128)(2,1)S(1)}, u32[]{:S(2)}, u32[]{:S(2)}) collective-permute-start(bf16[128,512]{1,0:T(8,128)(2,1)S(1)} %get-tuple-element.51), channel_id=1, source_target_pairs={{0,2},{1,3},{2,0},{3,1},{4,6},{5,7},{6,4},{7,5},{8,10},{9,11},{10,... | collective-permute-start | bytes 393224 | tf_op jit(solution)/shard_map/ppermute | solution.py:52
  48.4 16.6 %collective-permute-start.14 = (bf16[512,512]{1,0:T(8,128)(2,1)S(1)}, bf16[512,512]{1,0:T(8,128)(2,1)S(1)}, u32[]{:S(2)}, u32[]{:S(2)}) collective-permute-start(bf16[512,512]{1,0:T(8,128)(2,1)S(1)} %get-tuple-element.66), channel_id=1, source_target_pairs={{0,2},{1,3},{2,0},{3,1},{4,6},{5,7},{6,4},{7,5},{8,10},{9,11},{10,... | collective-permute-start | bytes 1572872 | tf_op jit(solution)/shard_map/ppermute | solution.py:52
  52.1 16.2 %collective-permute-start.11 = (f16[1040,128]{1,0:T(8,128)(2,1)S(1)}, f16[1040,128]{1,0:T(8,128)(2,1)S(1)}, u32[]{:S(2)}, u32[]{:S(2)}) collective-permute-start(f16[1040,128]{1,0:T(8,128)(2,1)S(1)} %convert_element_type.42), channel_id=1, source_target_pairs={{0,4},{1,5},{2,6},{3,7},{4,8},{5,9},{6,10},{7,11},{8,12},{9,13},{1... | collective-permute-start | bytes 798728 | tf_op jit(solution)/shard_map/ppermute | solution.py:52
  53.5 16.3 %collective-permute-start.12 = (f16[1040,128]{1,0:T(8,128)(2,1)S(1)}, f16[1040,128]{1,0:T(8,128)(2,1)S(1)}, u32[]{:S(2)}, u32[]{:S(2)}) collective-permute-start(f16[1040,128]{1,0:T(8,128)(2,1)S(1)} %convert_element_type.43), channel_id=1, source_target_pairs={{0,8},{1,9},{2,10},{3,11},{4,12},{5,13},{6,14},{7,15},{8,0},{9,1},... | collective-permute-start | bytes 798728 | tf_op jit(solution)/shard_map/ppermute | solution.py:52
  54.3 15.5 %collective-permute-start.13 = (f16[1040,128]{1,0:T(8,128)(2,1)S(1)}, f16[1040,128]{1,0:T(8,128)(2,1)S(1)}, u32[]{:S(2)}, u32[]{:S(2)}) collective-permute-start(f16[1040,128]{1,0:T(8,128)(2,1)S(1)} %convert_element_type.44), channel_id=1, source_target_pairs={{0,12},{1,13},{2,14},{3,15},{4,0},{5,1},{6,2},{7,3},{8,4},{9,5},{1... | collective-permute-start | bytes 798728 | tf_op jit(solution)/shard_map/ppermute | solution.py:52
  66.5 9.3 %collective-permute-start.15 = (f16[1040,128]{1,0:T(8,128)(2,1)S(1)}, f16[1040,128]{1,0:T(8,128)(2,1)S(1)}, u32[]{:S(2)}, u32[]{:S(2)}) collective-permute-start(f16[1040,128]{1,0:T(8,128)(2,1)S(1)} %convert_element_type.45), channel_id=1, source_target_pairs={{0,4},{1,5},{2,6},{3,7},{4,8},{5,9},{6,10},{7,11},{8,12},{9,13},{1... | collective-permute-start | bytes 798728 | tf_op jit(solution)/shard_map/ppermute | solution.py:52
  67.6 15.0 %collective-permute-start.16 = (f16[1040,128]{1,0:T(8,128)(2,1)S(1)}, f16[1040,128]{1,0:T(8,128)(2,1)S(1)}, u32[]{:S(2)}, u32[]{:S(2)}) collective-permute-start(f16[1040,128]{1,0:T(8,128)(2,1)S(1)} %convert_element_type.47), channel_id=1, source_target_pairs={{0,8},{1,9},{2,10},{3,11},{4,12},{5,13},{6,14},{7,15},{8,0},{9,1},... | collective-permute-start | bytes 798728 | tf_op jit(solution)/shard_map/ppermute | solution.py:52
  68.3 14.5 %collective-permute-start.17 = (f16[1040,128]{1,0:T(8,128)(2,1)S(1)}, f16[1040,128]{1,0:T(8,128)(2,1)S(1)}, u32[]{:S(2)}, u32[]{:S(2)}) collective-permute-start(f16[1040,128]{1,0:T(8,128)(2,1)S(1)} %convert_element_type.49), channel_id=1, source_target_pairs={{0,12},{1,13},{2,14},{3,15},{4,0},{5,1},{6,2},{7,3},{8,4},{9,5},{1... | collective-permute-start | bytes 798728 | tf_op jit(solution)/shard_map/ppermute | solution.py:52
  76.3 13.7 %collective-permute-start.18 = (f16[1040,128]{1,0:T(8,128)(2,1)S(1)}, f16[1040,128]{1,0:T(8,128)(2,1)S(1)}, u32[]{:S(2)}, u32[]{:S(2)}) collective-permute-start(f16[1040,128]{1,0:T(8,128)(2,1)S(1)} %convert_element_type.54), channel_id=1, source_target_pairs={{0,16},{16,0},{1,17},{17,1},{2,18},{18,2},{3,19},{19,3},{4,20},{20... | collective-permute-start | bytes 798728 | tf_op jit(solution)/shard_map/ppermute | solution.py:278

commit v8 on v7

--- a/solution.py
+++ b/solution.py
@@ -128,20 +128,17 @@
         out_ref[:, i:i + step] = jnp.where(on_last(), first_ref[:, i:i + step], total)
 
 
-def pack_last_kernel(head_ref, rel_ref, two_ref, right_ref, left_ref, own_ref, far_ref, direct_ref):
+def pack_last_kernel(head_ref, rel_ref, right_ref, left_ref, own_ref, two_ref):
     tensor = lax.axis_index("z_lo")
     rows, share = rel_ref.shape[1], rel_ref.shape[2]
-    depth = two_ref.shape[0]
-    direct_ref[:depth, :] = two_ref[...]
     for z in range(2):
         for b in range(RING):
-            two, base = ((direct_ref, depth), (far_ref, 0))[z]
-            for out, top, along in ((right_ref, z * rows, 1), (left_ref, z * rows, RING - 1), (own_ref, z * rows, 0), (two, base, 2)):
+            for out, along in ((right_ref, 1), (left_ref, RING - 1), (own_ref, 0), (two_ref, 2)):
                 at = block_start(z, along, b)
                 inner = pl.multiple_of(lax.rem(at, share), LANES)
                 chained = rel_ref[lax.rem(tensor - lax.div(at, share) + RING, RING), :, pl.ds(inner, LANES)]
                 last = jnp.where(on_last(), head_ref[:, pl.ds(at, LANES)], chained)
-                out[top:top + rows, b * LANES:(b + 1) * LANES] = last
+                out[z * rows:(z + 1) * rows, b * LANES:(b + 1) * LANES] = last
 
 
 def halves(ref, half, swapped):
@@ -161,19 +158,17 @@
             acc_ref[r * half:(r + 1) * half, z * lanes:(z + 1) * lanes] = jnp.dot(lhs, rhs, preferred_element_type=F32)
 
 
-def late_kernel(z, acc_ref, mine_ref, left_ref, right_ref, upper_ref, lower_ref, own_last, left_last, right_last, two_ref,
-                keep_ref, *rest):
-    sends, sum_ref = rest[:-1], rest[-1]
+def late_kernel(z, acc_ref, mine_ref, left_ref, right_ref, upper_ref, lower_ref, own_last, left_last, right_last, two_last,
+                *rest):
+    earlier = (upper_ref, lower_ref) if z else rest[:1]
+    keep_ref, *sends, sum_ref = rest[1 - z:]
     width, rows = acc_ref.shape[0], own_last.shape[0] // 2
     half, lanes = width // 2, acc_ref.shape[1] // 2
     depth = mine_ref.shape[1] - rows
     mine, left, right = halves(mine_ref, half, True), halves(left_ref, half, True), halves(right_ref, half, False)
     far = (upper_ref, lower_ref)
-    rhs = [ref[z * rows:(z + 1) * rows, :] for ref in (own_last, left_last, right_last)]
-    if z:
-        rhs += [two_ref[...], upper_ref[half:, :], lower_ref[half:, :]]
-    else:
-        rhs += [two_ref[depth:, :], two_ref[:depth, :]]
+    rhs = [ref[z * rows:(z + 1) * rows, :] for ref in (own_last, left_last, right_last, two_last)]
+    rhs += [ref[half if z else 0:, :] for ref in earlier]
     rhs = jnp.concatenate(rhs, axis=0)
     largest = jnp.full((1, lanes), TINY, F32)
     for r in range(2):
@@ -233,45 +228,44 @@
                  pltpu.SemaphoreType.DMA((micro + 6,))],
         flops=ENTRY_FLOPS, moved=12 * 2**20, limit=ENTRY_LIMIT,
     )
-    from_left, from_right = shifted(right, True, 1), shifted(left, True, -1)
+    from_left, from_right, two = shifted(right, True, 1), shifted(left, True, -1), shifted(two, True, 2)
 
     first, small = call(first_kernel, [((rows, width), F32), ((rows, width), BF16)], (head_grad, weights[0]), whole(2), **matmul)
     shard = lax.ppermute(small, "section", [(1, 0)])
-    rel = [shard] + [on_first(shard, by) for by in range(1, RING)]
-    from_left, from_right, *rel = lax.optimization_barrier((from_left, from_right, *rel))
+    one, three = on_first(shard, 1), on_first(shard, 3)
+    shard, one = lax.optimization_barrier((shard, one))
+    rel = [shard, one, on_first(shard, 2), three]
+    from_left, from_right, two, *rel = lax.optimization_barrier((from_left, from_right, two, *rel))
     rel = jnp.stack(rel, 0)
 
     passed = half + depth // 2
     upper = shifted(from_left[half:half + passed], True, 1)
     lower = shifted(from_right[half:half + passed], True, -1)
     edge = ((2 * rows, lanes), BF16)
-    last_right, last_left, last_own, last_far, direct = call(
-        pack_last_kernel, [edge] * 3 + [((rows, lanes), BF16), ((micro * rows, lanes), BF16)], (head_grad, rel, two), whole(3),
-        moved=4 * 2**20,
-    )
-    last = [last_own, shifted(last_right, True, 1), shifted(last_left, True, -1)]
-    last_far = shifted(last_far, True, 2)
+    last_right, last_left, last_own, last_two = call(
+        pack_last_kernel, [edge] * 4, (head_grad, rel), whole(2), moved=4 * 2**20
+    )
+    last = [last_own, shifted(last_right, True, 1), shifted(last_left, True, -1), shifted(last_two, True, 2)]
     (acc,) = call(
         early_kernel, [((width, 2 * lanes), F32)], (right, own, from_left, from_right), whole(4),
         flops=2 * width * 2 * lanes * 3 * depth, moved=12 * 2**20,
     )
-    acc, upper, lower, last_far, direct, *last = lax.optimization_barrier((acc, upper, lower, last_far, direct, *last))
-    direct = shifted(direct, True, 2)
+    acc, upper, lower, *last = lax.optimization_barrier((acc, upper, lower, *last))
     send = ((width + TAIL, LANES), F32)
 
-    def late(z, two):
+    def late(z, *more):
         return call(
             functools.partial(late_kernel, z), [((width, LANES), F32)] + [send] * 3,
-            (acc, right, from_left, from_right, upper, lower, *last, two), whole(10),
+            (acc, right, from_left, from_right, upper, lower, *last, *more), whole(10 + len(more)),
             scratch=[pltpu.VMEM((width, lanes), F32)],
             flops=2 * width * lanes * (3 * rows + micro * rows), moved=8 * 2**20,
         )
 
-    keep_far, *far_sends = late(1, last_far)
-    keep_near, *near_sends = late(0, direct)
+    keep_far, *far_sends = late(1)
+    keep_near, *near_sends = late(0, two)
     sends = far_sends + near_sends
     got = [shifted(s.astype(F16), False, by) for by, s in zip((1, 2, 3, 1, 2, 3), sends)]
-    rel, *got[:4] = lax.optimization_barrier((rel, *got[:4]))
+    rel, *got[:3] = lax.optimization_barrier((rel, *got[:3]))
     got = [v.astype(F32) for v in got]
     (second,) = call(second_kernel, [((rows, width), F32)], (rel, first, weights[0]), whole(3), **matmul)
     (far,) = call(far_kernel, [send], (keep_far, *got[:3]), whole(4), moved=4 * 2**20)

time: 91.2 us -> 84.5 us (0.927)
  the two profiles are of different devices: /device:TPU:50 before, /device:TPU:58 now
where the time goes in v8:
time: 84.5 us; the launch traced here: 84.4 us
  starting transfers between devices  37.1 us (44%)
  waiting for transfers between devices  28.5 us (34%)
  Pallas kernels  16.9 us (20%)
  between operations  0.89 us (1%)
    ppermute x14, waiting for transfers between devices, shifted(): return lax.ppermute(value, ('section', 'y', 'x'), pairs_over(along, by))  20.9 us
    ppermute x14, starting transfers between devices, shifted(): return lax.ppermute(value, ('section', 'y', 'x'), pairs_over(along, by))  18.5 us
    pallas_call x9, Pallas kernels, call(): pl.pallas_call(kernel, out_shape=[jax.ShapeDtypeStruct(s, t) for s, t in...  16.9 us
    ppermute x3, starting transfers between devices, on_first(): lax.ppermute(value, ('section', 'z_lo'), [(i, (i + by) % RING) for i in r...  11 us
    ppermute x1, starting transfers between devices, local(): other = lax.ppermute(far.astype(F16), 'z_hi', [(0, 1), (1, 0)]).astype(F32)  6.38 us
    ppermute x1, waiting for transfers between devices, local(): other = lax.ppermute(far.astype(F16), 'z_hi', [(0, 1), (1, 0)]).astype(F32)  5.31 us
    ppermute x1, waiting for transfers between devices, local(): shard = lax.ppermute(small, 'section', [(1, 0)])  2.13 us
  transfers between devices with their start and end apart: 19, of which 9 were waited for; matrix products, arithmetic and copies ran while one was open for 1% of the time, Pallas kernels for 14%

profile of v8, /device:TPU:58, one launch (start us, length us, event | category | flops | bytes accessed | tf_op | source)
XLA Modules:
  0.0 84.4 jit_solution(5779904149862690090)
XLA Ops:
  0.6 0.0 slice-start
  0.6 0.0 slice-start.1
  0.7 2.7 %shard_map.68 = (bf16[1984,512]{1,0:T(8,128)(2,1)S(1)}, bf16[1984,512]{1,0:T(8,128)(2,1)S(1)}, bf16[768,512]{1,0:T(8,128)(2,1)S(1)}, bf16[384,512]{1,0:T(8,128)(2,1)S(1)}) custom-call(s32[2]{0:T(128)} %pending_ref.1, bf16[4,128,1024]{2,1,0:T(8,128)(2,1)} %bitcast.20, bf16[3,128,4096]{2,1,0:T(8,128)(2,1)} %bitcast.19), custom_call_target="tpu_custom_call" | custom-call | flops 10000000000 | bytes 12582912 | tf_op jit(solution)/shard_map/pallas_call | solution.py:64
  3.4 1.6 %collective-permute-start = (bf16[1984,512]{1,0:T(8,128)(2,1)S(1)}, bf16[1984,512]{1,0:T(8,128)(2,1)S(1)}, u32[]{:S(2)}, u32[]{:S(2)}) collective-permute-start(bf16[1984,512]{1,0:T(8,128)(2,1)S(1)} %get-tuple-element.40.mine_ref), channel_id=1, source_target_pairs={{0,1},{1,2},{2,3},{3,0},{4,5},{5,6},{6,7},{7,4},{8,9},{9,10},{10,1... | collective-permute-start | bytes 6094856 | tf_op jit(solution)/shard_map/ppermute | solution.py:52
  4.9 0.5 collective-permute-start.1
  5.5 0.1 copy-done
  5.6 2.9 %shard_map.69 = (f32[128,1024]{1,0:T(8,128)S(1)}, bf16[128,1024]{1,0:T(8,128)(2,1)S(1)}) custom-call(bf16[128,4096]{1,0:T(8,128)(2,1)S(1)} %copy-done, bf16[1024,4096]{1,0:T(8,128)(2,1)S(1)} %bitcast.11), custom_call_target="tpu_custom_call" | custom-call | flops 1073741824 | bytes 2097152 | tf_op jit(solution)/shard_map/pallas_call | solution.py:64
  8.5 1.3 %collective-permute-start.3 = (bf16[128,1024]{1,0:T(8,128)(2,1)S(1)}, bf16[128,1024]{1,0:T(8,128)(2,1)S(1)}, u32[]{:S(2)}, u32[]{:S(2)}) collective-permute-start(bf16[128,1024]{1,0:T(8,128)(2,1)S(1)} %get-tuple-element.43), channel_id=1, source_target_pairs={{128,0},{129,1},{130,2},{131,3},{132,4},{133,5},{134,6},{135,7},{1... | collective-permute-start | bytes 786440 | tf_op jit(solution)/shard_map/ppermute | solution.py:234
  9.8 2.1 %collective-permute-done.3 = bf16[128,1024]{1,0:T(8,128)(2,1)S(1)} collective-permute-done((bf16[128,1024]{1,0:T(8,128)(2,1)S(1)}, bf16[128,1024]{1,0:T(8,128)(2,1)S(1)}, u32[]{:S(2)}, u32[]{:S(2)}) %collective-permute-start.3) | collective-permute-done | bytes 262176 | tf_op jit(solution)/shard_map/ppermute | solution.py:234
  11.9 3.8 %collective-permute-start.4 = (bf16[128,1024]{1,0:T(8,128)(2,1)S(1)}, bf16[128,1024]{1,0:T(8,128)(2,1)S(1)}, u32[]{:S(2)}, u32[]{:S(2)}) collective-permute-start(bf16[128,1024]{1,0:T(8,128)(2,1)S(1)} %collective-permute-done.3), channel_id=1, source_target_pairs={{0,32},{32,64},{64,96},{96,0},{1,33},{33,65},{65,97},{97,1},{2,34}... | collective-permute-start | bytes 786440 | tf_op jit(solution)/shard_map/ppermute | solution.py:212
  15.7 2.2 %collective-permute-start.2 = (bf16[384,512]{1,0:T(8,128)(2,1)S(1)}, bf16[384,512]{1,0:T(8,128)(2,1)S(1)}, u32[]{:S(2)}, u32[]{:S(2)}) collective-permute-start(bf16[384,512]{1,0:T(8,128)(2,1)S(1)} %get-tuple-element.42), channel_id=1, source_target_pairs={{0,2},{1,3},{2,0},{3,1},{4,6},{5,7},{6,4},{7,5},{8,10},{9,11},{10,... | collective-permute-start | bytes 1179656 | tf_op jit(solution)/shard_map/ppermute | solution.py:52
  17.9 2.0 %collective-permute-start.6 = (bf16[128,1024]{1,0:T(8,128)(2,1)S(1)}, bf16[128,1024]{1,0:T(8,128)(2,1)S(1)}, u32[]{:S(2)}, u32[]{:S(2)}) collective-permute-start(bf16[128,1024]{1,0:T(8,128)(2,1)S(1)} %collective-permute-done.3), channel_id=1, source_target_pairs={{0,96},{32,0},{64,32},{96,64},{1,97},{33,1},{65,33},{97,65},{2,98}... | collective-permute-start | bytes 786440 | tf_op jit(solution)/shard_map/ppermute | solution.py:212
  20.0 0.2 collective-permute-done.4
  20.2 5.2 %collective-permute-start.5 = (bf16[128,1024]{1,0:T(8,128)(2,1)S(1)}, bf16[128,1024]{1,0:T(8,128)(2,1)S(1)}, u32[]{:S(2)}, u32[]{:S(2)}) collective-permute-start(bf16[128,1024]{1,0:T(8,128)(2,1)S(1)} %collective-permute-done.3), channel_id=1, source_target_pairs={{0,64},{32,96},{64,0},{96,32},{1,65},{33,97},{65,1},{97,33},{2,66}... | collective-permute-start | bytes 786440 | tf_op jit(solution)/shard_map/ppermute | solution.py:212
  25.3 9.8 %collective-permute-done.2.rest_0_ = bf16[384,512]{1,0:T(8,128)(2,1)S(1)} collective-permute-done((bf16[384,512]{1,0:T(8,128)(2,1)S(1)}, bf16[384,512]{1,0:T(8,128)(2,1)S(1)}, u32[]{:S(2)}, u32[]{:S(2)}) %collective-permute-start.2) | collective-permute-done | bytes 393248 | tf_op jit(solution)/shard_map/ppermute | solution.py:52
  35.1 0.0 collective-permute-done.6
  35.1 0.0 collective-permute-done.5
  35.1 0.0 collective-permute-done.1.right_ref
  35.2 0.1 collective-permute-start.7
  35.3 2.1 %collective-permute-start.8 = (bf16[704,512]{1,0:T(8,128)(2,1)S(1)}, bf16[704,512]{1,0:T(8,128)(2,1)S(1)}, u32[]{:S(2)}, u32[]{:S(2)}) collective-permute-start(bf16[704,512]{1,0:T(8,128)(2,1)S(1)} %slice.7), channel_id=1, source_target_pairs={{0,3},{1,0},{2,1},{3,2},{4,7},{5,4},{6,5},{7,6},{8,11},{9,8},{10,9... | collective-permute-start | bytes 2162696 | tf_op jit(solution)/shard_map/ppermute | solution.py:52
  37.4 0.1 pad_maximum_fusion.rel_ref
  37.5 0.6 shard_map.71
  38.2 0.3 collective-permute-start.9
  38.5 1.8 %collective-permute-start.10 = (bf16[256,512]{1,0:T(8,128)(2,1)S(1)}, bf16[256,512]{1,0:T(8,128)(2,1)S(1)}, u32[]{:S(2)}, u32[]{:S(2)}) collective-permute-start(bf16[256,512]{1,0:T(8,128)(2,1)S(1)} %get-tuple-element.55), channel_id=1, source_target_pairs={{0,3},{1,0},{2,1},{3,2},{4,7},{5,4},{6,5},{7,6},{8,11},{9,8},{10,9... | collective-permute-start | bytes 786440 | tf_op jit(solution)/shard_map/ppermute | solution.py:52
  40.3 1.9 %collective-permute-start.11 = (bf16[256,512]{1,0:T(8,128)(2,1)S(1)}, bf16[256,512]{1,0:T(8,128)(2,1)S(1)}, u32[]{:S(2)}, u32[]{:S(2)}) collective-permute-start(bf16[256,512]{1,0:T(8,128)(2,1)S(1)} %get-tuple-element.56), channel_id=1, source_target_pairs={{0,2},{1,3},{2,0},{3,1},{4,6},{5,7},{6,4},{7,5},{8,10},{9,11},{10,... | collective-permute-start | bytes 786440 | tf_op jit(solution)/shard_map/ppermute | solution.py:52
  42.2 2.9 %shard_map.70.acc_ref = f32[1024,1024]{1,0:T(8,128)S(1)} custom-call(bf16[1984,512]{1,0:T(8,128)(2,1)S(1)} %get-tuple-element.40.mine_ref, bf16[768,512]{1,0:T(8,128)(2,1)S(1)} %get-tuple-element.50.own_ref, bf16[1984,512]{1,0:T(8,128)(2,1)S(1)} %collective-permute-done.left_ref, bf16[1984,512]{1,0:T(8,128)(2,1)S(1)} %collective-permute-done.1.right_ref), custom_call_target="tpu_custom_call" | custom-call | flops 2415919104 | bytes 12582912 | tf_op jit(solution)/shard_map/pallas_call | solution.py:64
  45.0 4.3 %collective-permute-done.9.left_last = bf16[256,512]{1,0:T(8,128)(2,1)S(1)} collective-permute-done((bf16[256,512]{1,0:T(8,128)(2,1)S(1)}, bf16[256,512]{1,0:T(8,128)(2,1)S(1)}, u32[]{:S(2)}, u32[]{:S(2)}) %collective-permute-start.9) | collective-permute-done | bytes 262176 | tf_op jit(solution)/shard_map/ppermute | solution.py:52
  49.4 0.3 collective-permute-done.10.right_last
  49.7 4.3 %collective-permute-done.11.two_last = bf16[256,512]{1,0:T(8,128)(2,1)S(1)} collective-permute-done((bf16[256,512]{1,0:T(8,128)(2,1)S(1)}, bf16[256,512]{1,0:T(8,128)(2,1)S(1)}, u32[]{:S(2)}, u32[]{:S(2)}) %collective-permute-start.11) | collective-permute-done | bytes 262176 | tf_op jit(solution)/shard_map/ppermute | solution.py:52
  54.0 1.5 %shard_map.72 = (f32[1024,128]{1,0:T(8,128)S(1)}, f32[1040,128]{1,0:T(8,128)S(1)}, f32[1040,128]{1,0:T(8,128)S(1)}, f32[1040,128]{1,0:T(8,128)S(1)}) custom-call(f32[1024,1024]{1,0:T(8,128)S(1)} %shard_map.70.acc_ref, bf16[1984,512]{1,0:T(8,128)(2,1)S(1)} %get-tuple-element.40.mine_ref, bf16[1984,512]{1,0:T(8,128)(2,1)S(1)} %collective-permute-done.left_ref, ...), custom_call_target="tpu_custom_call" | custom-call | flops 939524096 | bytes 8388608 | tf_op jit(solution)/shard_map/pallas_call | solution.py:64
  55.5 0.3 collective-permute-start.12
  55.8 2.7 %collective-permute-start.13 = (f16[1040,128]{1,0:T(8,128)(2,1)S(1)}, f16[1040,128]{1,0:T(8,128)(2,1)S(1)}, u32[]{:S(2)}, u32[]{:S(2)}) collective-permute-start(f16[1040,128]{1,0:T(8,128)(2,1)S(1)} %convert_element_type.43), channel_id=1, source_target_pairs={{0,8},{1,9},{2,10},{3,11},{4,12},{5,13},{6,14},{7,15},{8,0},{9,1},... | collective-permute-start | bytes 798728 | tf_op jit(solution)/shard_map/ppermute | solution.py:52
  58.5 0.1 collective-permute-start.14
  58.6 1.5 %shard_map.74 = (f32[1024,128]{1,0:T(8,128)S(1)}, f32[1040,128]{1,0:T(8,128)S(1)}, f32[1040,128]{1,0:T(8,128)S(1)}, f32[1040,128]{1,0:T(8,128)S(1)}) custom-call(f32[1024,1024]{1,0:T(8,128)S(1)} %shard_map.70.acc_ref, bf16[1984,512]{1,0:T(8,128)(2,1)S(1)} %get-tuple-element.40.mine_ref, bf16[1984,512]{1,0:T(8,128)(2,1)S(1)} %collective-permute-done.left_ref, ...), custom_call_target="tpu_custom_call" | custom-call | flops 939524096 | bytes 8388608 | tf_op jit(solution)/shard_map/pallas_call | solution.py:64
  60.1 3.3 %collective-permute-start.15 = (f16[1040,128]{1,0:T(8,128)(2,1)S(1)}, f16[1040,128]{1,0:T(8,128)(2,1)S(1)}, u32[]{:S(2)}, u32[]{:S(2)}) collective-permute-start(f16[1040,128]{1,0:T(8,128)(2,1)S(1)} %convert_element_type.45), channel_id=1, source_target_pairs={{0,4},{1,5},{2,6},{3,7},{4,8},{5,9},{6,10},{7,11},{8,12},{9,13},{1... | collective-permute-start | bytes 798728 | tf_op jit(solution)/shard_map/ppermute | solution.py:52
  63.5 0.2 collective-permute-start.16
  63.7 0.0 collective-permute-done.12
  63.7 1.5 %collective-permute-start.17 = (f16[1040,128]{1,0:T(8,128)(2,1)S(1)}, f16[1040,128]{1,0:T(8,128)(2,1)S(1)}, u32[]{:S(2)}, u32[]{:S(2)}) collective-permute-start(f16[1040,128]{1,0:T(8,128)(2,1)S(1)} %convert_element_type.49), channel_id=1, source_target_pairs={{0,12},{1,13},{2,14},{3,15},{4,0},{5,1},{6,2},{7,3},{8,4},{9,5},{1... | collective-permute-start | bytes 798728 | tf_op jit(solution)/shard_map/ppermute | solution.py:52
  65.2 0.0 collective-permute-done.13
  65.2 1.5 %collective-permute-done.14 = f16[1040,128]{1,0:T(8,128)(2,1)S(1)} collective-permute-done((f16[1040,128]{1,0:T(8,128)(2,1)S(1)}, f16[1040,128]{1,0:T(8,128)(2,1)S(1)}, u32[]{:S(2)}, u32[]{:S(2)}) %collective-permute-start.14) | collective-permute-done | bytes 266272 | tf_op jit(solution)/shard_map/ppermute | solution.py:52
  66.8 0.3 shard_map.75
  67.1 6.4 %collective-permute-start.18 = (f16[1040,128]{1,0:T(8,128)(2,1)S(1)}, f16[1040,128]{1,0:T(8,128)(2,1)S(1)}, u32[]{:S(2)}, u32[]{:S(2)}) collective-permute-start(f16[1040,128]{1,0:T(8,128)(2,1)S(1)} %convert_element_type.54), channel_id=1, source_target_pairs={{0,16},{16,0},{1,17},{17,1},{2,18},{18,2},{3,19},{19,3},{4,20},{20... | collective-permute-start | bytes 798728 | tf_op jit(solution)/shard_map/ppermute | solution.py:272
  73.5 0.0 collective-permute-done.15
  73.5 0.0 collective-permute-done.16
  73.6 0.7 collective-permute-done.17
  74.3 3.7 %shard_map.73 = f32[128,1024]{1,0:T(8,128)} custom-call(bf16[4,128,1024]{2,1,0:T(8,128)(2,1)S(1)} %pad_maximum_fusion.rel_ref, f32[128,1024]{1,0:T(8,128)S(1)} %get-tuple-element.68.first_ref, bf16[1024,4096]{1,0:T(8,128)(2,1)S(1)} %bitcast.12), custom_call_target="tpu_custom_call" | custom-call | flops 1073741824 | bytes 2097152 | tf_op jit(solution)/shard_map/pallas_call | solution.py:64
  78.0 5.3 %collective-permute-done.18 = f16[1040,128]{1,0:T(8,128)(2,1)S(1)} collective-permute-done((f16[1040,128]{1,0:T(8,128)(2,1)S(1)}, f16[1040,128]{1,0:T(8,128)(2,1)S(1)}, u32[]{:S(2)}, u32[]{:S(2)}) %collective-permute-start.18) | collective-permute-done | bytes 266272 | tf_op jit(solution)/shard_map/ppermute | solution.py:272
  83.4 1.0 %shard_map.76 = f32[1024,128]{1,0:T(8,128)} custom-call(f32[1024,128]{1,0:T(8,128)S(1)} %get-tuple-element.70.keep_ref, f32[1040,128]{1,0:T(8,128)S(1)} %convert_element_type.46.one_ref, f32[1040,128]{1,0:T(8,128)S(1)} %convert_element_type.48.two_ref, f32[1040,128]{1,0:T(8,128)S(1)} %convert_element_type.50.three_ref, ...), custom_call_target="tpu_custom_call" | custom-call | bytes 4194304 | tf_op jit(solution)/shard_map/pallas_call | solution.py:64
  (23 shorter events, 0.6 us)
Async XLA Ops:
  0.6 4.8 %slice-start = ((s8[8388608]{0:T(1024)(128)(4,1)}), s8[4194304]{0:T(1024)(128)(4,1)S(1)}, s32[]{:S(2)}) async-start(s8[8388608]{0:T(1024)(128)(4,1)} %bitcast.9), calls=%async_computation | async-start | bytes 8388608
  0.6 4.8 %slice-start.1 = ((s8[8388608]{0:T(1024)(128)(4,1)}), s8[4194304]{0:T(1024)(128)(4,1)S(1)}, s32[]{:S(2)}) async-start(s8[8388608]{0:T(1024)(128)(4,1)} %bitcast.9), calls=%async_computation.1 | async-start | bytes 8388608
  0.7 4.9 %copy-start = (bf16[128,4096]{1,0:T(8,128)(2,1)S(1)}, bf16[128,4096]{1,0:T(8,128)(2,1)}, u32[]{:S(2)}) copy-start(bf16[128,4096]{1,0:T(8,128)(2,1)} %head_ref.1) | copy-start | bytes 3145732
  3.4 31.8 %collective-permute-start = (bf16[1984,512]{1,0:T(8,128)(2,1)S(1)}, bf16[1984,512]{1,0:T(8,128)(2,1)S(1)}, u32[]{:S(2)}, u32[]{:S(2)}) collective-permute-start(bf16[1984,512]{1,0:T(8,128)(2,1)S(1)} %get-tuple-element.40.mine_ref), channel_id=1, source_target_pairs={{0,1},{1,2},{2,3},{3,0},{4,5},{5,6},{6,7},{7,4},{8,9},{9,10},{10,1... | collective-permute-start | bytes 6094856 | tf_op jit(solution)/shard_map/ppermute | solution.py:52
  4.9 30.2 %collective-permute-start.1 = (bf16[1984,512]{1,0:T(8,128)(2,1)S(1)}, bf16[1984,512]{1,0:T(8,128)(2,1)S(1)}, u32[]{:S(2)}, u32[]{:S(2)}) collective-permute-start(bf16[1984,512]{1,0:T(8,128)(2,1)S(1)} %get-tuple-element.41), channel_id=1, source_target_pairs={{0,3},{1,0},{2,1},{3,2},{4,7},{5,4},{6,5},{7,6},{8,11},{9,8},{10,9... | collective-permute-start | bytes 6094856 | tf_op jit(solution)/shard_map/ppermute | solution.py:52
  8.5 3.4 %collective-permute-start.3 = (bf16[128,1024]{1,0:T(8,128)(2,1)S(1)}, bf16[128,1024]{1,0:T(8,128)(2,1)S(1)}, u32[]{:S(2)}, u32[]{:S(2)}) collective-permute-start(bf16[128,1024]{1,0:T(8,128)(2,1)S(1)} %get-tuple-element.43), channel_id=1, source_target_pairs={{128,0},{129,1},{130,2},{131,3},{132,4},{133,5},{134,6},{135,7},{1... | collective-permute-start | bytes 786440 | tf_op jit(solution)/shard_map/ppermute | solution.py:234
  11.9 8.3 %collective-permute-start.4 = (bf16[128,1024]{1,0:T(8,128)(2,1)S(1)}, bf16[128,1024]{1,0:T(8,128)(2,1)S(1)}, u32[]{:S(2)}, u32[]{:S(2)}) collective-permute-start(bf16[128,1024]{1,0:T(8,128)(2,1)S(1)} %collective-permute-done.3), channel_id=1, source_target_pairs={{0,32},{32,64},{64,96},{96,0},{1,33},{33,65},{65,97},{97,1},{2,34}... | collective-permute-start | bytes 786440 | tf_op jit(solution)/shard_map/ppermute | solution.py:212
  15.7 19.4 %collective-permute-start.2 = (bf16[384,512]{1,0:T(8,128)(2,1)S(1)}, bf16[384,512]{1,0:T(8,128)(2,1)S(1)}, u32[]{:S(2)}, u32[]{:S(2)}) collective-permute-start(bf16[384,512]{1,0:T(8,128)(2,1)S(1)} %get-tuple-element.42), channel_id=1, source_target_pairs={{0,2},{1,3},{2,0},{3,1},{4,6},{5,7},{6,4},{7,5},{8,10},{9,11},{10,... | collective-permute-start | bytes 1179656 | tf_op jit(solution)/shard_map/ppermute | solution.py:52
  17.9 17.2 %collective-permute-start.6 = (bf16[128,1024]{1,0:T(8,128)(2,1)S(1)}, bf16[128,1024]{1,0:T(8,128)(2,1)S(1)}, u32[]{:S(2)}, u32[]{:S(2)}) collective-permute-start(bf16[128,1024]{1,0:T(8,128)(2,1)S(1)} %collective-permute-done.3), channel_id=1, source_target_pairs={{0,96},{32,0},{64,32},{96,64},{1,97},{33,1},{65,33},{97,65},{2,98}... | collective-permute-start | bytes 786440 | tf_op jit(solution)/shard_map/ppermute | solution.py:212
  20.2 14.9 %collective-permute-start.5 = (bf16[128,1024]{1,0:T(8,128)(2,1)S(1)}, bf16[128,1024]{1,0:T(8,128)(2,1)S(1)}, u32[]{:S(2)}, u32[]{:S(2)}) collective-permute-start(bf16[128,1024]{1,0:T(8,128)(2,1)S(1)} %collective-permute-done.3), channel_id=1, source_target_pairs={{0,64},{32,96},{64,0},{96,32},{1,65},{33,97},{65,1},{97,33},{2,66}... | collective-permute-start | bytes 786440 | tf_op jit(solution)/shard_map/ppermute | solution.py:212
  35.2 18.8 %collective-permute-start.7 = (bf16[704,512]{1,0:T(8,128)(2,1)S(1)}, bf16[704,512]{1,0:T(8,128)(2,1)S(1)}, u32[]{:S(2)}, u32[]{:S(2)}) collective-permute-start(bf16[704,512]{1,0:T(8,128)(2,1)S(1)} %slice.6), channel_id=1, source_target_pairs={{0,1},{1,2},{2,3},{3,0},{4,5},{5,6},{6,7},{7,4},{8,9},{9,10},{10,1... | collective-permute-start | bytes 2162696 | tf_op jit(solution)/shard_map/ppermute | solution.py:52
  35.3 18.6 %collective-permute-start.8 = (bf16[704,512]{1,0:T(8,128)(2,1)S(1)}, bf16[704,512]{1,0:T(8,128)(2,1)S(1)}, u32[]{:S(2)}, u32[]{:S(2)}) collective-permute-start(bf16[704,512]{1,0:T(8,128)(2,1)S(1)} %slice.7), channel_id=1, source_target_pairs={{0,3},{1,0},{2,1},{3,2},{4,7},{5,4},{6,5},{7,6},{8,11},{9,8},{10,9... | collective-permute-start | bytes 2162696 | tf_op jit(solution)/shard_map/ppermute | solution.py:52
  38.2 11.2 %collective-permute-start.9 = (bf16[256,512]{1,0:T(8,128)(2,1)S(1)}, bf16[256,512]{1,0:T(8,128)(2,1)S(1)}, u32[]{:S(2)}, u32[]{:S(2)}) collective-permute-start(bf16[256,512]{1,0:T(8,128)(2,1)S(1)} %get-tuple-element.54), channel_id=1, source_target_pairs={{0,1},{1,2},{2,3},{3,0},{4,5},{5,6},{6,7},{7,4},{8,9},{9,10},{10,1... | collective-permute-start | bytes 786440 | tf_op jit(solution)/shard_map/ppermute | solution.py:52
  38.5 11.2 %collective-permute-start.10 = (bf16[256,512]{1,0:T(8,128)(2,1)S(1)}, bf16[256,512]{1,0:T(8,128)(2,1)S(1)}, u32[]{:S(2)}, u32[]{:S(2)}) collective-permute-start(bf16[256,512]{1,0:T(8,128)(2,1)S(1)} %get-tuple-element.55), channel_id=1, source_target_pairs={{0,3},{1,0},{2,1},{3,2},{4,7},{5,4},{6,5},{7,6},{8,11},{9,8},{10,9... | collective-permute-start | bytes 786440 | tf_op jit(solution)/shard_map/ppermute | solution.py:52
  40.3 13.7 %collective-permute-start.11 = (bf16[256,512]{1,0:T(8,128)(2,1)S(1)}, bf16[256,512]{1,0:T(8,128)(2,1)S(1)}, u32[]{:S(2)}, u32[]{:S(2)}) collective-permute-start(bf16[256,512]{1,0:T(8,128)(2,1)S(1)} %get-tuple-element.56), channel_id=1, source_target_pairs={{0,2},{1,3},{2,0},{3,1},{4,6},{5,7},{6,4},{7,5},{8,10},{9,11},{10,... | collective-permute-start | bytes 786440 | tf_op jit(solution)/shard_map/ppermute | solution.py:52
  55.5 8.3 %collective-permute-start.12 = (f16[1040,128]{1,0:T(8,128)(2,1)S(1)}, f16[1040,128]{1,0:T(8,128)(2,1)S(1)}, u32[]{:S(2)}, u32[]{:S(2)}) collective-permute-start(f16[1040,128]{1,0:T(8,128)(2,1)S(1)} %convert_element_type.42), channel_id=1, source_target_pairs={{0,4},{1,5},{2,6},{3,7},{4,8},{5,9},{6,10},{7,11},{8,12},{9,13},{1... | collective-permute-start | bytes 798728 | tf_op jit(solution)/shard_map/ppermute | solution.py:52
  55.8 9.4 %collective-permute-start.13 = (f16[1040,128]{1,0:T(8,128)(2,1)S(1)}, f16[1040,128]{1,0:T(8,128)(2,1)S(1)}, u32[]{:S(2)}, u32[]{:S(2)}) collective-permute-start(f16[1040,128]{1,0:T(8,128)(2,1)S(1)} %convert_element_type.43), channel_id=1, source_target_pairs={{0,8},{1,9},{2,10},{3,11},{4,12},{5,13},{6,14},{7,15},{8,0},{9,1},... | collective-permute-start | bytes 798728 | tf_op jit(solution)/shard_map/ppermute | solution.py:52
  58.5 8.1 %collective-permute-start.14 = (f16[1040,128]{1,0:T(8,128)(2,1)S(1)}, f16[1040,128]{1,0:T(8,128)(2,1)S(1)}, u32[]{:S(2)}, u32[]{:S(2)}) collective-permute-start(f16[1040,128]{1,0:T(8,128)(2,1)S(1)} %convert_element_type.44), channel_id=1, source_target_pairs={{0,12},{1,13},{2,14},{3,15},{4,0},{5,1},{6,2},{7,3},{8,4},{9,5},{1... | collective-permute-start | bytes 798728 | tf_op jit(solution)/shard_map/ppermute | solution.py:52
  60.1 13.4 %collective-permute-start.15 = (f16[1040,128]{1,0:T(8,128)(2,1)S(1)}, f16[1040,128]{1,0:T(8,128)(2,1)S(1)}, u32[]{:S(2)}, u32[]{:S(2)}) collective-permute-start(f16[1040,128]{1,0:T(8,128)(2,1)S(1)} %convert_element_type.45), channel_id=1, source_target_pairs={{0,4},{1,5},{2,6},{3,7},{4,8},{5,9},{6,10},{7,11},{8,12},{9,13},{1... | collective-permute-start | bytes 798728 | tf_op jit(solution)/shard_map/ppermute | solution.py:52
  63.5 10.1 %collective-permute-start.16 = (f16[1040,128]{1,0:T(8,128)(2,1)S(1)}, f16[1040,128]{1,0:T(8,128)(2,1)S(1)}, u32[]{:S(2)}, u32[]{:S(2)}) collective-permute-start(f16[1040,128]{1,0:T(8,128)(2,1)S(1)} %convert_element_type.47), channel_id=1, source_target_pairs={{0,8},{1,9},{2,10},{3,11},{4,12},{5,13},{6,14},{7,15},{8,0},{9,1},... | collective-permute-start | bytes 798728 | tf_op jit(solution)/shard_map/ppermute | solution.py:52
  63.7 10.6 %collective-permute-start.17 = (f16[1040,128]{1,0:T(8,128)(2,1)S(1)}, f16[1040,128]{1,0:T(8,128)(2,1)S(1)}, u32[]{:S(2)}, u32[]{:S(2)}) collective-permute-start(f16[1040,128]{1,0:T(8,128)(2,1)S(1)} %convert_element_type.49), channel_id=1, source_target_pairs={{0,12},{1,13},{2,14},{3,15},{4,0},{5,1},{6,2},{7,3},{8,4},{9,5},{1... | collective-permute-start | bytes 798728 | tf_op jit(solution)/shard_map/ppermute | solution.py:52
  67.1 16.2 %collective-permute-start.18 = (f16[1040,128]{1,0:T(8,128)(2,1)S(1)}, f16[1040,128]{1,0:T(8,128)(2,1)S(1)}, u32[]{:S(2)}, u32[]{:S(2)}) collective-permute-start(f16[1040,128]{1,0:T(8,128)(2,1)S(1)} %convert_element_type.54), channel_id=1, source_target_pairs={{0,16},{16,0},{1,17},{17,1},{2,18},{18,2},{3,19},{19,3},{4,20},{20... | collective-permute-start | bytes 798728 | tf_op jit(solution)/shard_map/ppermute | solution.py:272

commit v9 on v8

--- a/solution.py
+++ b/solution.py
@@ -75,7 +75,7 @@
 CONTRACT_LAST = (((1,), (1,)), ((), ()))
 
 
-def entry_kernel(pending_ref, x_ref, stash_ref, right_ref, left_ref, own_ref, two_ref, x_in, stash_in, count_in, sems):
+def entry_kernel(pending_ref, x_ref, stash_ref, right_ref, left_ref, own_ref, x_in, stash_in, count_in, sems):
     micro, rows, width = x_ref.shape
     half, depth = width // 2, (micro - 1) * rows
     pieces = [(pending_ref, count_in), (x_ref, x_in)]
@@ -93,9 +93,11 @@
             for at, top in zip((0, half), order):
                 out[at:at + half, lanes] = turned[top:top + half]
     share = depth // 2
-    plans = [(right_ref, width, 1, 2, 0, share), (left_ref, width, 1, 2, share, depth), (two_ref, 0, 0, 2, 0, depth)]
+    plans = []
     for z in range(2):
-        at = width + share + z * depth
+        at = width + z * share
+        plans += [(right_ref, at, z, 2, 0, share), (left_ref, at, z, 2, share, depth)]
+        at = width + (1 + z) * depth
         plans += [(right_ref, at, z, 1, 0, depth), (left_ref, at, z, RING - 1, 0, depth), (own_ref, z * depth, z, 0, 0, depth)]
     for m in range(micro - 1):
         copies[2 + m].wait()
@@ -152,23 +154,23 @@
     for r in range(2):
         lhs = jnp.concatenate([side[r][:, :depth] for side in sides], axis=1)
         for z in range(2):
-            at = width + depth // 2 + z * depth
+            at = width + (1 + z) * depth
             rhs = [own_ref[z * depth:(z + 1) * depth, :], left_ref[at:at + depth, :], right_ref[at:at + depth, :]]
             rhs = jnp.concatenate(rhs, axis=0)
             acc_ref[r * half:(r + 1) * half, z * lanes:(z + 1) * lanes] = jnp.dot(lhs, rhs, preferred_element_type=F32)
 
 
 def late_kernel(z, acc_ref, mine_ref, left_ref, right_ref, upper_ref, lower_ref, own_last, left_last, right_last, two_last,
-                *rest):
-    earlier = (upper_ref, lower_ref) if z else rest[:1]
-    keep_ref, *sends, sum_ref = rest[1 - z:]
+                keep_ref, *rest):
+    sends, sum_ref = rest[:-1], rest[-1]
     width, rows = acc_ref.shape[0], own_last.shape[0] // 2
     half, lanes = width // 2, acc_ref.shape[1] // 2
     depth = mine_ref.shape[1] - rows
     mine, left, right = halves(mine_ref, half, True), halves(left_ref, half, True), halves(right_ref, half, False)
     far = (upper_ref, lower_ref)
     rhs = [ref[z * rows:(z + 1) * rows, :] for ref in (own_last, left_last, right_last, two_last)]
-    rhs += [ref[half if z else 0:, :] for ref in earlier]
+    at = half + z * depth // 2
+    rhs += [ref[at:at + depth // 2, :] for ref in far]
     rhs = jnp.concatenate(rhs, axis=0)
     largest = jnp.full((1, lanes), TINY, F32)
     for r in range(2):
@@ -219,26 +221,24 @@
     columns = head_grad.shape[1]
     matmul = dict(flops=2 * rows * width * columns, moved=2 * 2**20)
 
-    side = ((width + depth // 2 + 2 * depth, lanes), BF16)
-    right, left, own, two = call(
+    side = ((width + 3 * depth, lanes), BF16)
+    right, left, own = call(
         entry_kernel,
-        [side, side, ((2 * depth, lanes), BF16), ((depth, lanes), BF16)],
+        [side, side, ((2 * depth, lanes), BF16)],
         [in_hbm(v) for v in (pending, inputs, grads)], [pl.BlockSpec(memory_space=pltpu.HBM)] * 3,
         scratch=[pltpu.VMEM(inputs.shape, BF16), pltpu.VMEM(grads.shape, BF16), pltpu.SMEM(pending.shape, pending.dtype),
                  pltpu.SemaphoreType.DMA((micro + 6,))],
         flops=ENTRY_FLOPS, moved=12 * 2**20, limit=ENTRY_LIMIT,
     )
-    from_left, from_right, two = shifted(right, True, 1), shifted(left, True, -1), shifted(two, True, 2)
+    from_left, from_right = shifted(right, True, 1), shifted(left, True, -1)
 
     first, small = call(first_kernel, [((rows, width), F32), ((rows, width), BF16)], (head_grad, weights[0]), whole(2), **matmul)
     shard = lax.ppermute(small, "section", [(1, 0)])
-    one, three = on_first(shard, 1), on_first(shard, 3)
-    shard, one = lax.optimization_barrier((shard, one))
-    rel = [shard, one, on_first(shard, 2), three]
-    from_left, from_right, two, *rel = lax.optimization_barrier((from_left, from_right, two, *rel))
+    rel = [shard] + [on_first(shard, by) for by in range(1, RING)]
+    from_left, from_right, *rel = lax.optimization_barrier((from_left, from_right, *rel))
     rel = jnp.stack(rel, 0)
 
-    passed = half + depth // 2
+    passed = half + depth
     upper = shifted(from_left[half:half + passed], True, 1)
     lower = shifted(from_right[half:half + passed], True, -1)
     edge = ((2 * rows, lanes), BF16)
@@ -253,16 +253,16 @@
     acc, upper, lower, *last = lax.optimization_barrier((acc, upper, lower, *last))
     send = ((width + TAIL, LANES), F32)
 
-    def late(z, *more):
+    def late(z):
         return call(
             functools.partial(late_kernel, z), [((width, LANES), F32)] + [send] * 3,
-            (acc, right, from_left, from_right, upper, lower, *last, *more), whole(10 + len(more)),
+            (acc, right, from_left, from_right, upper, lower, *last), whole(10),
             scratch=[pltpu.VMEM((width, lanes), F32)],
             flops=2 * width * lanes * (3 * rows + micro * rows), moved=8 * 2**20,
         )
 
     keep_far, *far_sends = late(1)
-    keep_near, *near_sends = late(0, two)
+    keep_near, *near_sends = late(0)
     sends = far_sends + near_sends
     got = [shifted(s.astype(F16), False, by) for by, s in zip((1, 2, 3, 1, 2, 3), sends)]
     rel, *got[:3] = lax.optimization_barrier((rel, *got[:3]))

time: 84.5 us -> 84.5 us (level)
  the two profiles are of different devices: /device:TPU:58 before, /device:TPU:42 now
where the time goes in v9:
time: 84.5 us; the launch traced here: 84.4 us
  starting transfers between devices  36.4 us (43%)
  waiting for transfers between devices  29.2 us (35%)
  Pallas kernels  17 us (20%)
  between operations  0.9 us (1%)
    ppermute x13, starting transfers between devices, shifted(): return lax.ppermute(value, ('section', 'y', 'x'), pairs_over(along, by))  17.7 us
    pallas_call x9, Pallas kernels, call(): pl.pallas_call(kernel, out_shape=[jax.ShapeDtypeStruct(s, t) for s, t in...  17 us
    ppermute x13, waiting for transfers between devices, shifted(): return lax.ppermute(value, ('section', 'y', 'x'), pairs_over(along, by))  15.4 us
    ppermute x3, starting transfers between devices, on_first(): lax.ppermute(value, ('section', 'z_lo'), [(i, (i + by) % RING) for i in r...  11 us
    ppermute x3, waiting for transfers between devices, on_first(): lax.ppermute(value, ('section', 'z_lo'), [(i, (i + by) % RING) for i in r...  6.94 us
    ppermute x1, starting transfers between devices, local(): other = lax.ppermute(far.astype(F16), 'z_hi', [(0, 1), (1, 0)]).astype(F32)  6.38 us
    ppermute x1, waiting for transfers between devices, local(): other = lax.ppermute(far.astype(F16), 'z_hi', [(0, 1), (1, 0)]).astype(F32)  4.8 us
    ppermute x1, waiting for transfers between devices, local(): shard = lax.ppermute(small, 'section', [(1, 0)])  2.13 us
  transfers between devices with their start and end apart: 18, of which 10 were waited for; matrix products, arithmetic and copies ran while one was open for 1% of the time, Pallas kernels for 14%

profile of v9, /device:TPU:42, one launch (start us, length us, event | category | flops | bytes accessed | tf_op | source)
XLA Modules:
  0.0 84.4 jit_solution(5319930076401374408)
XLA Ops:
  0.6 0.0 slice-start
  0.6 0.0 slice-start.1
  0.7 2.8 %shard_map.68 = (bf16[2176,512]{1,0:T(8,128)(2,1)S(1)}, bf16[2176,512]{1,0:T(8,128)(2,1)S(1)}, bf16[768,512]{1,0:T(8,128)(2,1)S(1)}) custom-call(s32[2]{0:T(128)} %pending_ref.1, bf16[4,128,1024]{2,1,0:T(8,128)(2,1)} %bitcast.20, bf16[3,128,4096]{2,1,0:T(8,128)(2,1)} %bitcast.19), custom_call_target="tpu_custom_call" | custom-call | flops 10000000000 | bytes 12582912 | tf_op jit(solution)/shard_map/pallas_call | solution.py:64
  3.4 1.6 %collective-permute-start = (bf16[2176,512]{1,0:T(8,128)(2,1)S(1)}, bf16[2176,512]{1,0:T(8,128)(2,1)S(1)}, u32[]{:S(2)}, u32[]{:S(2)}) collective-permute-start(bf16[2176,512]{1,0:T(8,128)(2,1)S(1)} %get-tuple-element.36.mine_ref), channel_id=1, source_target_pairs={{0,1},{1,2},{2,3},{3,0},{4,5},{5,6},{6,7},{7,4},{8,9},{9,10},{10,1... | collective-permute-start | bytes 6684680 | tf_op jit(solution)/shard_map/ppermute | solution.py:52
  5.0 0.5 collective-permute-start.1
  5.5 0.0 copy-done
  5.6 2.9 %shard_map.69 = (f32[128,1024]{1,0:T(8,128)S(1)}, bf16[128,1024]{1,0:T(8,128)(2,1)S(1)}) custom-call(bf16[128,4096]{1,0:T(8,128)(2,1)S(1)} %copy-done, bf16[1024,4096]{1,0:T(8,128)(2,1)S(1)} %bitcast.11), custom_call_target="tpu_custom_call" | custom-call | flops 1073741824 | bytes 2097152 | tf_op jit(solution)/shard_map/pallas_call | solution.py:64
  8.5 1.3 %collective-permute-start.2 = (bf16[128,1024]{1,0:T(8,128)(2,1)S(1)}, bf16[128,1024]{1,0:T(8,128)(2,1)S(1)}, u32[]{:S(2)}, u32[]{:S(2)}) collective-permute-start(bf16[128,1024]{1,0:T(8,128)(2,1)S(1)} %get-tuple-element.38), channel_id=1, source_target_pairs={{128,0},{129,1},{130,2},{131,3},{132,4},{133,5},{134,6},{135,7},{1... | collective-permute-start | bytes 786440 | tf_op jit(solution)/shard_map/ppermute | solution.py:236
  9.8 2.1 %collective-permute-done.2 = bf16[128,1024]{1,0:T(8,128)(2,1)S(1)} collective-permute-done((bf16[128,1024]{1,0:T(8,128)(2,1)S(1)}, bf16[128,1024]{1,0:T(8,128)(2,1)S(1)}, u32[]{:S(2)}, u32[]{:S(2)}) %collective-permute-start.2) | collective-permute-done | bytes 262176 | tf_op jit(solution)/shard_map/ppermute | solution.py:236
  11.9 3.8 %collective-permute-start.3 = (bf16[128,1024]{1,0:T(8,128)(2,1)S(1)}, bf16[128,1024]{1,0:T(8,128)(2,1)S(1)}, u32[]{:S(2)}, u32[]{:S(2)}) collective-permute-start(bf16[128,1024]{1,0:T(8,128)(2,1)S(1)} %collective-permute-done.2), channel_id=1, source_target_pairs={{0,32},{32,64},{64,96},{96,0},{1,33},{33,65},{65,97},{97,1},{2,34}... | collective-permute-start | bytes 786440 | tf_op jit(solution)/shard_map/ppermute | solution.py:214
  15.7 3.3 %collective-permute-start.4 = (bf16[128,1024]{1,0:T(8,128)(2,1)S(1)}, bf16[128,1024]{1,0:T(8,128)(2,1)S(1)}, u32[]{:S(2)}, u32[]{:S(2)}) collective-permute-start(bf16[128,1024]{1,0:T(8,128)(2,1)S(1)} %collective-permute-done.2), channel_id=1, source_target_pairs={{0,64},{32,96},{64,0},{96,32},{1,65},{33,97},{65,1},{97,33},{2,66}... | collective-permute-start | bytes 786440 | tf_op jit(solution)/shard_map/ppermute | solution.py:214
  19.0 3.9 %collective-permute-start.5 = (bf16[128,1024]{1,0:T(8,128)(2,1)S(1)}, bf16[128,1024]{1,0:T(8,128)(2,1)S(1)}, u32[]{:S(2)}, u32[]{:S(2)}) collective-permute-start(bf16[128,1024]{1,0:T(8,128)(2,1)S(1)} %collective-permute-done.2), channel_id=1, source_target_pairs={{0,96},{32,0},{64,32},{96,64},{1,97},{33,1},{65,33},{97,65},{2,98}... | collective-permute-start | bytes 786440 | tf_op jit(solution)/shard_map/ppermute | solution.py:214
  23.0 0.0 collective-permute-done.3
  23.0 5.5 %collective-permute-done.4 = bf16[128,1024]{1,0:T(8,128)(2,1)S(1)} collective-permute-done((bf16[128,1024]{1,0:T(8,128)(2,1)S(1)}, bf16[128,1024]{1,0:T(8,128)(2,1)S(1)}, u32[]{:S(2)}, u32[]{:S(2)}) %collective-permute-start.4) | collective-permute-done | bytes 262176 | tf_op jit(solution)/shard_map/ppermute | solution.py:214
  28.5 1.4 %collective-permute-done.5 = bf16[128,1024]{1,0:T(8,128)(2,1)S(1)} collective-permute-done((bf16[128,1024]{1,0:T(8,128)(2,1)S(1)}, bf16[128,1024]{1,0:T(8,128)(2,1)S(1)}, u32[]{:S(2)}, u32[]{:S(2)}) %collective-permute-start.5) | collective-permute-done | bytes 262176 | tf_op jit(solution)/shard_map/ppermute | solution.py:214
  29.9 1.0 %collective-permute-done.left_ref = bf16[2176,512]{1,0:T(8,128)(2,1)S(1)} collective-permute-done((bf16[2176,512]{1,0:T(8,128)(2,1)S(1)}, bf16[2176,512]{1,0:T(8,128)(2,1)S(1)}, u32[]{:S(2)}, u32[]{:S(2)}) %collective-permute-start) | collective-permute-done | bytes 2228256 | tf_op jit(solution)/shard_map/ppermute | solution.py:52
  30.9 1.5 %collective-permute-done.1.right_ref = bf16[2176,512]{1,0:T(8,128)(2,1)S(1)} collective-permute-done((bf16[2176,512]{1,0:T(8,128)(2,1)S(1)}, bf16[2176,512]{1,0:T(8,128)(2,1)S(1)}, u32[]{:S(2)}, u32[]{:S(2)}) %collective-permute-start.1) | collective-permute-done | bytes 2228256 | tf_op jit(solution)/shard_map/ppermute | solution.py:52
  32.4 0.1 slice.6
  32.5 1.3 %collective-permute-start.6 = (bf16[896,512]{1,0:T(8,128)(2,1)S(1)}, bf16[896,512]{1,0:T(8,128)(2,1)S(1)}, u32[]{:S(2)}, u32[]{:S(2)}) collective-permute-start(bf16[896,512]{1,0:T(8,128)(2,1)S(1)} %slice.6), channel_id=1, source_target_pairs={{0,1},{1,2},{2,3},{3,0},{4,5},{5,6},{6,7},{7,4},{8,9},{9,10},{10,1... | collective-permute-start | bytes 2752520 | tf_op jit(solution)/shard_map/ppermute | solution.py:52
  33.8 0.1 slice.7
  33.8 0.9 %collective-permute-start.7 = (bf16[896,512]{1,0:T(8,128)(2,1)S(1)}, bf16[896,512]{1,0:T(8,128)(2,1)S(1)}, u32[]{:S(2)}, u32[]{:S(2)}) collective-permute-start(bf16[896,512]{1,0:T(8,128)(2,1)S(1)} %slice.7), channel_id=1, source_target_pairs={{0,3},{1,0},{2,1},{3,2},{4,7},{5,4},{6,5},{7,6},{8,11},{9,8},{10,9... | collective-permute-start | bytes 2752520 | tf_op jit(solution)/shard_map/ppermute | solution.py:52
  34.7 0.1 pad_maximum_fusion.rel_ref
  34.9 0.6 shard_map.71
  35.5 1.3 %collective-permute-start.8 = (bf16[256,512]{1,0:T(8,128)(2,1)S(1)}, bf16[256,512]{1,0:T(8,128)(2,1)S(1)}, u32[]{:S(2)}, u32[]{:S(2)}) collective-permute-start(bf16[256,512]{1,0:T(8,128)(2,1)S(1)} %get-tuple-element.47), channel_id=1, source_target_pairs={{0,1},{1,2},{2,3},{3,0},{4,5},{5,6},{6,7},{7,4},{8,9},{9,10},{10,1... | collective-permute-start | bytes 786440 | tf_op jit(solution)/shard_map/ppermute | solution.py:52
  36.8 0.8 collective-permute-start.9
  37.6 2.3 %collective-permute-start.10 = (bf16[256,512]{1,0:T(8,128)(2,1)S(1)}, bf16[256,512]{1,0:T(8,128)(2,1)S(1)}, u32[]{:S(2)}, u32[]{:S(2)}) collective-permute-start(bf16[256,512]{1,0:T(8,128)(2,1)S(1)} %get-tuple-element.49), channel_id=1, source_target_pairs={{0,2},{1,3},{2,0},{3,1},{4,6},{5,7},{6,4},{7,5},{8,10},{9,11},{10,... | collective-permute-start | bytes 786440 | tf_op jit(solution)/shard_map/ppermute | solution.py:52
  39.9 2.9 %shard_map.70.acc_ref = f32[1024,1024]{1,0:T(8,128)S(1)} custom-call(bf16[2176,512]{1,0:T(8,128)(2,1)S(1)} %get-tuple-element.36.mine_ref, bf16[768,512]{1,0:T(8,128)(2,1)S(1)} %get-tuple-element.43.own_ref, bf16[2176,512]{1,0:T(8,128)(2,1)S(1)} %collective-permute-done.left_ref, bf16[2176,512]{1,0:T(8,128)(2,1)S(1)} %collective-permute-done.1.right_ref), custom_call_target="tpu_custom_call" | custom-call | flops 2415919104 | bytes 12582912 | tf_op jit(solution)/shard_map/pallas_call | solution.py:64
  42.8 6.0 %collective-permute-done.8.left_last = bf16[256,512]{1,0:T(8,128)(2,1)S(1)} collective-permute-done((bf16[256,512]{1,0:T(8,128)(2,1)S(1)}, bf16[256,512]{1,0:T(8,128)(2,1)S(1)}, u32[]{:S(2)}, u32[]{:S(2)}) %collective-permute-start.8) | collective-permute-done | bytes 262176 | tf_op jit(solution)/shard_map/ppermute | solution.py:52
  48.8 1.3 %collective-permute-done.9.right_last = bf16[256,512]{1,0:T(8,128)(2,1)S(1)} collective-permute-done((bf16[256,512]{1,0:T(8,128)(2,1)S(1)}, bf16[256,512]{1,0:T(8,128)(2,1)S(1)}, u32[]{:S(2)}, u32[]{:S(2)}) %collective-permute-start.9) | collective-permute-done | bytes 262176 | tf_op jit(solution)/shard_map/ppermute | solution.py:52
  50.1 3.9 %collective-permute-done.10.two_last = bf16[256,512]{1,0:T(8,128)(2,1)S(1)} collective-permute-done((bf16[256,512]{1,0:T(8,128)(2,1)S(1)}, bf16[256,512]{1,0:T(8,128)(2,1)S(1)}, u32[]{:S(2)}, u32[]{:S(2)}) %collective-permute-start.10) | collective-permute-done | bytes 262176 | tf_op jit(solution)/shard_map/ppermute | solution.py:52
  54.1 0.0 collective-permute-done.7.lower_ref
  54.1 1.5 %shard_map.72 = (f32[1024,128]{1,0:T(8,128)S(1)}, f32[1040,128]{1,0:T(8,128)S(1)}, f32[1040,128]{1,0:T(8,128)S(1)}, f32[1040,128]{1,0:T(8,128)S(1)}) custom-call(f32[1024,1024]{1,0:T(8,128)S(1)} %shard_map.70.acc_ref, bf16[2176,512]{1,0:T(8,128)(2,1)S(1)} %get-tuple-element.36.mine_ref, bf16[2176,512]{1,0:T(8,128)(2,1)S(1)} %collective-permute-done.left_ref, ...), custom_call_target="tpu_custom_call" | custom-call | flops 939524096 | bytes 8388608 | tf_op jit(solution)/shard_map/pallas_call | solution.py:64
  55.6 1.8 %collective-permute-start.11 = (f16[1040,128]{1,0:T(8,128)(2,1)S(1)}, f16[1040,128]{1,0:T(8,128)(2,1)S(1)}, u32[]{:S(2)}, u32[]{:S(2)}) collective-permute-start(f16[1040,128]{1,0:T(8,128)(2,1)S(1)} %convert_element_type.42), channel_id=1, source_target_pairs={{0,4},{1,5},{2,6},{3,7},{4,8},{5,9},{6,10},{7,11},{8,12},{9,13},{1... | collective-permute-start | bytes 798728 | tf_op jit(solution)/shard_map/ppermute | solution.py:52
  57.4 1.0 %collective-permute-start.12 = (f16[1040,128]{1,0:T(8,128)(2,1)S(1)}, f16[1040,128]{1,0:T(8,128)(2,1)S(1)}, u32[]{:S(2)}, u32[]{:S(2)}) collective-permute-start(f16[1040,128]{1,0:T(8,128)(2,1)S(1)} %convert_element_type.43), channel_id=1, source_target_pairs={{0,8},{1,9},{2,10},{3,11},{4,12},{5,13},{6,14},{7,15},{8,0},{9,1},... | collective-permute-start | bytes 798728 | tf_op jit(solution)/shard_map/ppermute | solution.py:52
  58.5 2.5 %collective-permute-start.13 = (f16[1040,128]{1,0:T(8,128)(2,1)S(1)}, f16[1040,128]{1,0:T(8,128)(2,1)S(1)}, u32[]{:S(2)}, u32[]{:S(2)}) collective-permute-start(f16[1040,128]{1,0:T(8,128)(2,1)S(1)} %convert_element_type.44), channel_id=1, source_target_pairs={{0,12},{1,13},{2,14},{3,15},{4,0},{5,1},{6,2},{7,3},{8,4},{9,5},{1... | collective-permute-start | bytes 798728 | tf_op jit(solution)/shard_map/ppermute | solution.py:52
  61.0 1.5 %shard_map.74 = (f32[1024,128]{1,0:T(8,128)S(1)}, f32[1040,128]{1,0:T(8,128)S(1)}, f32[1040,128]{1,0:T(8,128)S(1)}, f32[1040,128]{1,0:T(8,128)S(1)}) custom-call(f32[1024,1024]{1,0:T(8,128)S(1)} %shard_map.70.acc_ref, bf16[2176,512]{1,0:T(8,128)(2,1)S(1)} %get-tuple-element.36.mine_ref, bf16[2176,512]{1,0:T(8,128)(2,1)S(1)} %collective-permute-done.left_ref, ...), custom_call_target="tpu_custom_call" | custom-call | flops 939524096 | bytes 8388608 | tf_op jit(solution)/shard_map/pallas_call | solution.py:64
  62.5 0.1 collective-permute-start.14
  62.6 3.5 %collective-permute-start.15 = (f16[1040,128]{1,0:T(8,128)(2,1)S(1)}, f16[1040,128]{1,0:T(8,128)(2,1)S(1)}, u32[]{:S(2)}, u32[]{:S(2)}) collective-permute-start(f16[1040,128]{1,0:T(8,128)(2,1)S(1)} %convert_element_type.47), channel_id=1, source_target_pairs={{0,8},{1,9},{2,10},{3,11},{4,12},{5,13},{6,14},{7,15},{8,0},{9,1},... | collective-permute-start | bytes 798728 | tf_op jit(solution)/shard_map/ppermute | solution.py:52
  66.2 0.0 collective-permute-done.11
  66.2 0.1 collective-permute-start.16
  66.3 0.0 collective-permute-done.12
  66.3 1.6 %collective-permute-done.13 = f16[1040,128]{1,0:T(8,128)(2,1)S(1)} collective-permute-done((f16[1040,128]{1,0:T(8,128)(2,1)S(1)}, f16[1040,128]{1,0:T(8,128)(2,1)S(1)}, u32[]{:S(2)}, u32[]{:S(2)}) %collective-permute-start.13) | collective-permute-done | bytes 266272 | tf_op jit(solution)/shard_map/ppermute | solution.py:52
  68.0 0.3 shard_map.75
  68.3 6.4 %collective-permute-start.17 = (f16[1040,128]{1,0:T(8,128)(2,1)S(1)}, f16[1040,128]{1,0:T(8,128)(2,1)S(1)}, u32[]{:S(2)}, u32[]{:S(2)}) collective-permute-start(f16[1040,128]{1,0:T(8,128)(2,1)S(1)} %convert_element_type.54), channel_id=1, source_target_pairs={{0,16},{16,0},{1,17},{17,1},{2,18},{18,2},{3,19},{19,3},{4,20},{20... | collective-permute-start | bytes 798728 | tf_op jit(solution)/shard_map/ppermute | solution.py:272
  74.8 0.0 collective-permute-done.16
  74.8 3.7 %shard_map.73 = f32[128,1024]{1,0:T(8,128)} custom-call(bf16[4,128,1024]{2,1,0:T(8,128)(2,1)S(1)} %pad_maximum_fusion.rel_ref, f32[128,1024]{1,0:T(8,128)S(1)} %get-tuple-element.61.first_ref, bf16[1024,4096]{1,0:T(8,128)(2,1)S(1)} %bitcast.12), custom_call_target="tpu_custom_call" | custom-call | flops 1073741824 | bytes 2097152 | tf_op jit(solution)/shard_map/pallas_call | solution.py:64
  78.5 4.8 %collective-permute-done.17 = f16[1040,128]{1,0:T(8,128)(2,1)S(1)} collective-permute-done((f16[1040,128]{1,0:T(8,128)(2,1)S(1)}, f16[1040,128]{1,0:T(8,128)(2,1)S(1)}, u32[]{:S(2)}, u32[]{:S(2)}) %collective-permute-start.17) | collective-permute-done | bytes 266272 | tf_op jit(solution)/shard_map/ppermute | solution.py:272
  83.4 1.0 %shard_map.76 = f32[1024,128]{1,0:T(8,128)} custom-call(f32[1024,128]{1,0:T(8,128)S(1)} %get-tuple-element.62.keep_ref, f32[1040,128]{1,0:T(8,128)S(1)} %convert_element_type.46.one_ref, f32[1040,128]{1,0:T(8,128)S(1)} %convert_element_type.48.two_ref, f32[1040,128]{1,0:T(8,128)S(1)} %convert_element_type.50.three_ref, ...), custom_call_target="tpu_custom_call" | custom-call | bytes 4194304 | tf_op jit(solution)/shard_map/pallas_call | solution.py:64
  (21 shorter events, 0.5 us)
Async XLA Ops:
  0.6 4.9 %slice-start = ((s8[8388608]{0:T(1024)(128)(4,1)}), s8[4194304]{0:T(1024)(128)(4,1)S(1)}, s32[]{:S(2)}) async-start(s8[8388608]{0:T(1024)(128)(4,1)} %bitcast.9), calls=%async_computation | async-start | bytes 8388608
  0.6 4.9 %slice-start.1 = ((s8[8388608]{0:T(1024)(128)(4,1)}), s8[4194304]{0:T(1024)(128)(4,1)S(1)}, s32[]{:S(2)}) async-start(s8[8388608]{0:T(1024)(128)(4,1)} %bitcast.9), calls=%async_computation.1 | async-start | bytes 8388608
  0.7 4.9 %copy-start = (bf16[128,4096]{1,0:T(8,128)(2,1)S(1)}, bf16[128,4096]{1,0:T(8,128)(2,1)}, u32[]{:S(2)}) copy-start(bf16[128,4096]{1,0:T(8,128)(2,1)} %head_ref.1) | copy-start | bytes 3145732
  3.4 27.5 %collective-permute-start = (bf16[2176,512]{1,0:T(8,128)(2,1)S(1)}, bf16[2176,512]{1,0:T(8,128)(2,1)S(1)}, u32[]{:S(2)}, u32[]{:S(2)}) collective-permute-start(bf16[2176,512]{1,0:T(8,128)(2,1)S(1)} %get-tuple-element.36.mine_ref), channel_id=1, source_target_pairs={{0,1},{1,2},{2,3},{3,0},{4,5},{5,6},{6,7},{7,4},{8,9},{9,10},{10,1... | collective-permute-start | bytes 6684680 | tf_op jit(solution)/shard_map/ppermute | solution.py:52
  5.0 27.4 %collective-permute-start.1 = (bf16[2176,512]{1,0:T(8,128)(2,1)S(1)}, bf16[2176,512]{1,0:T(8,128)(2,1)S(1)}, u32[]{:S(2)}, u32[]{:S(2)}) collective-permute-start(bf16[2176,512]{1,0:T(8,128)(2,1)S(1)} %get-tuple-element.37), channel_id=1, source_target_pairs={{0,3},{1,0},{2,1},{3,2},{4,7},{5,4},{6,5},{7,6},{8,11},{9,8},{10,9... | collective-permute-start | bytes 6684680 | tf_op jit(solution)/shard_map/ppermute | solution.py:52
  8.5 3.4 %collective-permute-start.2 = (bf16[128,1024]{1,0:T(8,128)(2,1)S(1)}, bf16[128,1024]{1,0:T(8,128)(2,1)S(1)}, u32[]{:S(2)}, u32[]{:S(2)}) collective-permute-start(bf16[128,1024]{1,0:T(8,128)(2,1)S(1)} %get-tuple-element.38), channel_id=1, source_target_pairs={{128,0},{129,1},{130,2},{131,3},{132,4},{133,5},{134,6},{135,7},{1... | collective-permute-start | bytes 786440 | tf_op jit(solution)/shard_map/ppermute | solution.py:236
  11.9 11.0 %collective-permute-start.3 = (bf16[128,1024]{1,0:T(8,128)(2,1)S(1)}, bf16[128,1024]{1,0:T(8,128)(2,1)S(1)}, u32[]{:S(2)}, u32[]{:S(2)}) collective-permute-start(bf16[128,1024]{1,0:T(8,128)(2,1)S(1)} %collective-permute-done.2), channel_id=1, source_target_pairs={{0,32},{32,64},{64,96},{96,0},{1,33},{33,65},{65,97},{97,1},{2,34}... | collective-permute-start | bytes 786440 | tf_op jit(solution)/shard_map/ppermute | solution.py:214
  15.7 12.8 %collective-permute-start.4 = (bf16[128,1024]{1,0:T(8,128)(2,1)S(1)}, bf16[128,1024]{1,0:T(8,128)(2,1)S(1)}, u32[]{:S(2)}, u32[]{:S(2)}) collective-permute-start(bf16[128,1024]{1,0:T(8,128)(2,1)S(1)} %collective-permute-done.2), channel_id=1, source_target_pairs={{0,64},{32,96},{64,0},{96,32},{1,65},{33,97},{65,1},{97,33},{2,66}... | collective-permute-start | bytes 786440 | tf_op jit(solution)/shard_map/ppermute | solution.py:214
  19.0 10.9 %collective-permute-start.5 = (bf16[128,1024]{1,0:T(8,128)(2,1)S(1)}, bf16[128,1024]{1,0:T(8,128)(2,1)S(1)}, u32[]{:S(2)}, u32[]{:S(2)}) collective-permute-start(bf16[128,1024]{1,0:T(8,128)(2,1)S(1)} %collective-permute-done.2), channel_id=1, source_target_pairs={{0,96},{32,0},{64,32},{96,64},{1,97},{33,1},{65,33},{97,65},{2,98}... | collective-permute-start | bytes 786440 | tf_op jit(solution)/shard_map/ppermute | solution.py:214
  32.5 21.6 %collective-permute-start.6 = (bf16[896,512]{1,0:T(8,128)(2,1)S(1)}, bf16[896,512]{1,0:T(8,128)(2,1)S(1)}, u32[]{:S(2)}, u32[]{:S(2)}) collective-permute-start(bf16[896,512]{1,0:T(8,128)(2,1)S(1)} %slice.6), channel_id=1, source_target_pairs={{0,1},{1,2},{2,3},{3,0},{4,5},{5,6},{6,7},{7,4},{8,9},{9,10},{10,1... | collective-permute-start | bytes 2752520 | tf_op jit(solution)/shard_map/ppermute | solution.py:52
  33.8 20.2 %collective-permute-start.7 = (bf16[896,512]{1,0:T(8,128)(2,1)S(1)}, bf16[896,512]{1,0:T(8,128)(2,1)S(1)}, u32[]{:S(2)}, u32[]{:S(2)}) collective-permute-start(bf16[896,512]{1,0:T(8,128)(2,1)S(1)} %slice.7), channel_id=1, source_target_pairs={{0,3},{1,0},{2,1},{3,2},{4,7},{5,4},{6,5},{7,6},{8,11},{9,8},{10,9... | collective-permute-start | bytes 2752520 | tf_op jit(solution)/shard_map/ppermute | solution.py:52
  35.5 13.3 %collective-permute-start.8 = (bf16[256,512]{1,0:T(8,128)(2,1)S(1)}, bf16[256,512]{1,0:T(8,128)(2,1)S(1)}, u32[]{:S(2)}, u32[]{:S(2)}) collective-permute-start(bf16[256,512]{1,0:T(8,128)(2,1)S(1)} %get-tuple-element.47), channel_id=1, source_target_pairs={{0,1},{1,2},{2,3},{3,0},{4,5},{5,6},{6,7},{7,4},{8,9},{9,10},{10,1... | collective-permute-start | bytes 786440 | tf_op jit(solution)/shard_map/ppermute | solution.py:52
  36.8 13.3 %collective-permute-start.9 = (bf16[256,512]{1,0:T(8,128)(2,1)S(1)}, bf16[256,512]{1,0:T(8,128)(2,1)S(1)}, u32[]{:S(2)}, u32[]{:S(2)}) collective-permute-start(bf16[256,512]{1,0:T(8,128)(2,1)S(1)} %get-tuple-element.48), channel_id=1, source_target_pairs={{0,3},{1,0},{2,1},{3,2},{4,7},{5,4},{6,5},{7,6},{8,11},{9,8},{10,9... | collective-permute-start | bytes 786440 | tf_op jit(solution)/shard_map/ppermute | solution.py:52
  37.6 16.4 %collective-permute-start.10 = (bf16[256,512]{1,0:T(8,128)(2,1)S(1)}, bf16[256,512]{1,0:T(8,128)(2,1)S(1)}, u32[]{:S(2)}, u32[]{:S(2)}) collective-permute-start(bf16[256,512]{1,0:T(8,128)(2,1)S(1)} %get-tuple-element.49), channel_id=1, source_target_pairs={{0,2},{1,3},{2,0},{3,1},{4,6},{5,7},{6,4},{7,5},{8,10},{9,11},{10,... | collective-permute-start | bytes 786440 | tf_op jit(solution)/shard_map/ppermute | solution.py:52
  55.6 10.6 %collective-permute-start.11 = (f16[1040,128]{1,0:T(8,128)(2,1)S(1)}, f16[1040,128]{1,0:T(8,128)(2,1)S(1)}, u32[]{:S(2)}, u32[]{:S(2)}) collective-permute-start(f16[1040,128]{1,0:T(8,128)(2,1)S(1)} %convert_element_type.42), channel_id=1, source_target_pairs={{0,4},{1,5},{2,6},{3,7},{4,8},{5,9},{6,10},{7,11},{8,12},{9,13},{1... | collective-permute-start | bytes 798728 | tf_op jit(solution)/shard_map/ppermute | solution.py:52
  57.4 8.8 %collective-permute-start.12 = (f16[1040,128]{1,0:T(8,128)(2,1)S(1)}, f16[1040,128]{1,0:T(8,128)(2,1)S(1)}, u32[]{:S(2)}, u32[]{:S(2)}) collective-permute-start(f16[1040,128]{1,0:T(8,128)(2,1)S(1)} %convert_element_type.43), channel_id=1, source_target_pairs={{0,8},{1,9},{2,10},{3,11},{4,12},{5,13},{6,14},{7,15},{8,0},{9,1},... | collective-permute-start | bytes 798728 | tf_op jit(solution)/shard_map/ppermute | solution.py:52
  58.5 9.3 %collective-permute-start.13 = (f16[1040,128]{1,0:T(8,128)(2,1)S(1)}, f16[1040,128]{1,0:T(8,128)(2,1)S(1)}, u32[]{:S(2)}, u32[]{:S(2)}) collective-permute-start(f16[1040,128]{1,0:T(8,128)(2,1)S(1)} %convert_element_type.44), channel_id=1, source_target_pairs={{0,12},{1,13},{2,14},{3,15},{4,0},{5,1},{6,2},{7,3},{8,4},{9,5},{1... | collective-permute-start | bytes 798728 | tf_op jit(solution)/shard_map/ppermute | solution.py:52
  62.5 12.2 %collective-permute-start.14 = (f16[1040,128]{1,0:T(8,128)(2,1)S(1)}, f16[1040,128]{1,0:T(8,128)(2,1)S(1)}, u32[]{:S(2)}, u32[]{:S(2)}) collective-permute-start(f16[1040,128]{1,0:T(8,128)(2,1)S(1)} %convert_element_type.45), channel_id=1, source_target_pairs={{0,4},{1,5},{2,6},{3,7},{4,8},{5,9},{6,10},{7,11},{8,12},{9,13},{1... | collective-permute-start | bytes 798728 | tf_op jit(solution)/shard_map/ppermute | solution.py:52
  62.6 12.1 %collective-permute-start.15 = (f16[1040,128]{1,0:T(8,128)(2,1)S(1)}, f16[1040,128]{1,0:T(8,128)(2,1)S(1)}, u32[]{:S(2)}, u32[]{:S(2)}) collective-permute-start(f16[1040,128]{1,0:T(8,128)(2,1)S(1)} %convert_element_type.47), channel_id=1, source_target_pairs={{0,8},{1,9},{2,10},{3,11},{4,12},{5,13},{6,14},{7,15},{8,0},{9,1},... | collective-permute-start | bytes 798728 | tf_op jit(solution)/shard_map/ppermute | solution.py:52
  66.2 8.6 %collective-permute-start.16 = (f16[1040,128]{1,0:T(8,128)(2,1)S(1)}, f16[1040,128]{1,0:T(8,128)(2,1)S(1)}, u32[]{:S(2)}, u32[]{:S(2)}) collective-permute-start(f16[1040,128]{1,0:T(8,128)(2,1)S(1)} %convert_element_type.49), channel_id=1, source_target_pairs={{0,12},{1,13},{2,14},{3,15},{4,0},{5,1},{6,2},{7,3},{8,4},{9,5},{1... | collective-permute-start | bytes 798728 | tf_op jit(solution)/shard_map/ppermute | solution.py:52
  68.3 15.0 %collective-permute-start.17 = (f16[1040,128]{1,0:T(8,128)(2,1)S(1)}, f16[1040,128]{1,0:T(8,128)(2,1)S(1)}, u32[]{:S(2)}, u32[]{:S(2)}) collective-permute-start(f16[1040,128]{1,0:T(8,128)(2,1)S(1)} %convert_element_type.54), channel_id=1, source_target_pairs={{0,16},{16,0},{1,17},{17,1},{2,18},{18,2},{3,19},{19,3},{4,20},{20... | collective-permute-start | bytes 798728 | tf_op jit(solution)/shard_map/ppermute | solution.py:272

commit v10 on v9

--- a/solution.py
+++ b/solution.py
@@ -75,7 +75,7 @@
 CONTRACT_LAST = (((1,), (1,)), ((), ()))
 
 
-def entry_kernel(pending_ref, x_ref, stash_ref, right_ref, left_ref, own_ref, x_in, stash_in, count_in, sems):
+def entry_kernel(pending_ref, x_ref, stash_ref, right_on, left_on, right_ref, left_ref, own_ref, x_in, stash_in, count_in, sems):
     micro, rows, width = x_ref.shape
     half, depth = width // 2, (micro - 1) * rows
     pieces = [(pending_ref, count_in), (x_ref, x_in)]
@@ -89,15 +89,14 @@
     for m in range(micro):
         turned = jnp.where(m >= micro - count, x_in[m].astype(F32), 0.0).T.astype(BF16)
         lanes = slice(m * rows, (m + 1) * rows)
-        for out, order in ((right_ref, (half, 0)), (left_ref, (0, half))):
-            for at, top in zip((0, half), order):
-                out[at:at + half, lanes] = turned[top:top + half]
+        for out, top in ((right_on, 0), (right_ref, half), (left_on, half), (left_ref, 0)):
+            out[:half, lanes] = turned[top:top + half]
     share = depth // 2
     plans = []
     for z in range(2):
-        at = width + z * share
-        plans += [(right_ref, at, z, 2, 0, share), (left_ref, at, z, 2, share, depth)]
-        at = width + (1 + z) * depth
+        at = half + z * share
+        plans += [(right_on, at, z, 2, 0, share), (left_on, at, z, 2, share, depth)]
+        at = half + z * depth
         plans += [(right_ref, at, z, 1, 0, depth), (left_ref, at, z, RING - 1, 0, depth), (own_ref, z * depth, z, 0, 0, depth)]
     for m in range(micro - 1):
         copies[2 + m].wait()
@@ -143,38 +142,33 @@
                 out[z * rows:(z + 1) * rows, b * LANES:(b + 1) * LANES] = last
 
 
-def halves(ref, half, swapped):
-    return (ref.at[half:2 * half], ref.at[0:half]) if swapped else (ref.at[0:half], ref.at[half:2 * half])
-
-
-def early_kernel(mine_ref, own_ref, left_ref, right_ref, acc_ref):
+def early_kernel(mine_on, mine_ref, own_ref, left_on, left_ref, right_on, right_ref, acc_ref):
     width, depth = acc_ref.shape[0], own_ref.shape[0] // 2
     half, lanes = width // 2, acc_ref.shape[1] // 2
-    sides = [halves(mine_ref, half, True), halves(left_ref, half, True), halves(right_ref, half, False)]
+    sides = [(mine_on, mine_ref), (left_on, left_ref), (right_ref, right_on)]
     for r in range(2):
-        lhs = jnp.concatenate([side[r][:, :depth] for side in sides], axis=1)
+        lhs = jnp.concatenate([side[r][:half, :depth] for side in sides], axis=1)
         for z in range(2):
-            at = width + (1 + z) * depth
+            at = half + z * depth
             rhs = [own_ref[z * depth:(z + 1) * depth, :], left_ref[at:at + depth, :], right_ref[at:at + depth, :]]
             rhs = jnp.concatenate(rhs, axis=0)
             acc_ref[r * half:(r + 1) * half, z * lanes:(z + 1) * lanes] = jnp.dot(lhs, rhs, preferred_element_type=F32)
 
 
-def late_kernel(z, acc_ref, mine_ref, left_ref, right_ref, upper_ref, lower_ref, own_last, left_last, right_last, two_last,
-                keep_ref, *rest):
+def late_kernel(z, acc_ref, mine_on, mine_ref, left_on, left_ref, right_on, right_ref, upper_ref, lower_ref,
+                two_last, left_last, right_last, own_last, keep_ref, *rest):
     sends, sum_ref = rest[:-1], rest[-1]
     width, rows = acc_ref.shape[0], own_last.shape[0] // 2
     half, lanes = width // 2, acc_ref.shape[1] // 2
     depth = mine_ref.shape[1] - rows
-    mine, left, right = halves(mine_ref, half, True), halves(left_ref, half, True), halves(right_ref, half, False)
-    far = (upper_ref, lower_ref)
+    mine, left, right, far = (mine_on, mine_ref), (left_on, left_ref), (right_ref, right_on), (upper_ref, lower_ref)
     rhs = [ref[z * rows:(z + 1) * rows, :] for ref in (own_last, left_last, right_last, two_last)]
     at = half + z * depth // 2
     rhs += [ref[at:at + depth // 2, :] for ref in far]
     rhs = jnp.concatenate(rhs, axis=0)
     largest = jnp.full((1, lanes), TINY, F32)
     for r in range(2):
-        lhs = [mine[r][:, depth:], left[r][:, depth:], right[r][:, depth:], far[r][:half, depth:], far[r][:half, :depth]]
+        lhs = [side[r][:half, depth:] for side in (mine, left, right, far)] + [far[r][:half, :depth]]
         total = jnp.dot(jnp.concatenate(lhs, axis=1), rhs, preferred_element_type=F32)
         total = total + acc_ref[r * half:(r + 1) * half, z * lanes:(z + 1) * lanes]
         largest = jnp.maximum(largest, jnp.max(jnp.abs(total), axis=0, keepdims=True))
@@ -221,33 +215,33 @@
     columns = head_grad.shape[1]
     matmul = dict(flops=2 * rows * width * columns, moved=2 * 2**20)
 
-    side = ((width + 3 * depth, lanes), BF16)
-    right, left, own = call(
-        entry_kernel,
-        [side, side, ((2 * depth, lanes), BF16)],
+    going, staying = ((half + depth, lanes), BF16), ((half + 2 * depth, lanes), BF16)
+    right_on, left_on, right, left, own = call(
+        entry_kernel, [going, going, staying, staying, ((2 * depth, lanes), BF16)],
         [in_hbm(v) for v in (pending, inputs, grads)], [pl.BlockSpec(memory_space=pltpu.HBM)] * 3,
         scratch=[pltpu.VMEM(inputs.shape, BF16), pltpu.VMEM(grads.shape, BF16), pltpu.SMEM(pending.shape, pending.dtype),
                  pltpu.SemaphoreType.DMA((micro + 6,))],
         flops=ENTRY_FLOPS, moved=12 * 2**20, limit=ENTRY_LIMIT,
     )
-    from_left, from_right = shifted(right, True, 1), shifted(left, True, -1)
+    from_left_on, from_right_on = shifted(right_on, True, 1), shifted(left_on, True, -1)
 
     first, small = call(first_kernel, [((rows, width), F32), ((rows, width), BF16)], (head_grad, weights[0]), whole(2), **matmul)
     shard = lax.ppermute(small, "section", [(1, 0)])
-    rel = [shard] + [on_first(shard, by) for by in range(1, RING)]
-    from_left, from_right, *rel = lax.optimization_barrier((from_left, from_right, *rel))
+    staying_right, staying_left, shard = lax.optimization_barrier((right, left, shard))
+    from_left, from_right = shifted(staying_right, True, 1), shifted(staying_left, True, -1)
+    one = on_first(shard, 1)
+    shard, one, from_left_on, from_right_on = lax.optimization_barrier((shard, one, from_left_on, from_right_on))
+    upper, lower = shifted(from_left_on, True, 1), shifted(from_right_on, True, -1)
+    rel = [shard, one, on_first(shard, 2), on_first(shard, 3)]
     rel = jnp.stack(rel, 0)
 
-    passed = half + depth
-    upper = shifted(from_left[half:half + passed], True, 1)
-    lower = shifted(from_right[half:half + passed], True, -1)
     edge = ((2 * rows, lanes), BF16)
     last_right, last_left, last_own, last_two = call(
         pack_last_kernel, [edge] * 4, (head_grad, rel), whole(2), moved=4 * 2**20
     )
-    last = [last_own, shifted(last_right, True, 1), shifted(last_left, True, -1), shifted(last_two, True, 2)]
+    last = [shifted(last_two, True, 2), shifted(last_right, True, 1), shifted(last_left, True, -1), last_own]
     (acc,) = call(
-        early_kernel, [((width, 2 * lanes), F32)], (right, own, from_left, from_right), whole(4),
+        early_kernel, [((width, 2 * lanes), F32)], (right_on, right, own, from_left_on, from_left, from_right_on, from_right), whole(7),
         flops=2 * width * 2 * lanes * 3 * depth, moved=12 * 2**20,
     )
     acc, upper, lower, *last = lax.optimization_barrier((acc, upper, lower, *last))
@@ -256,7 +250,7 @@
     def late(z):
         return call(
             functools.partial(late_kernel, z), [((width, LANES), F32)] + [send] * 3,
-            (acc, right, from_left, from_right, upper, lower, *last), whole(10),
+            (acc, right_on, right, from_left_on, from_left, from_right_on, from_right, upper, lower, *last), whole(13),
             scratch=[pltpu.VMEM((width, lanes), F32)],
             flops=2 * width * lanes * (3 * rows + micro * rows), moved=8 * 2**20,
         )
@@ -264,7 +258,7 @@
     keep_far, *far_sends = late(1)
     keep_near, *near_sends = late(0)
     sends = far_sends + near_sends
-    got = [shifted(s.astype(F16), False, by) for by, s in zip((1, 2, 3, 1, 2, 3), sends)]
+    got = [shifted(sends[i].astype(F16), False, 1 + i % 3) for i in (1, 0, 2, 4, 3, 5)]
     rel, *got[:3] = lax.optimization_barrier((rel, *got[:3]))
     got = [v.astype(F32) for v in got]
     (second,) = call(second_kernel, [((rows, width), F32)], (rel, first, weights[0]), whole(3), **matmul)

time: 84.5 us -> 94.9 us (1.12)
  the two profiles are of different devices: /device:TPU:42 before, /device:TPU:24 now
where the time goes in v10:
time: 94.9 us; the launch traced here: 94.8 us
  starting transfers between devices  39.2 us (41%)
  waiting for transfers between devices  37 us (39%)
  Pallas kernels  17 us (18%)
    ppermute x15, starting transfers between devices, shifted(): return lax.ppermute(value, ('section', 'y', 'x'), pairs_over(along, by))  21.9 us
    ppermute x3, waiting for transfers between devices, on_first(): lax.ppermute(value, ('section', 'z_lo'), [(i, (i + by) % RING) for i in r...  17.5 us
    pallas_call x9, Pallas kernels, call(): pl.pallas_call(kernel, out_shape=[jax.ShapeDtypeStruct(s, t) for s, t in...  17 us
    ppermute x15, waiting for transfers between devices, shifted(): return lax.ppermute(value, ('section', 'y', 'x'), pairs_over(along, by))  13.7 us
    ppermute x3, starting transfers between devices, on_first(): lax.ppermute(value, ('section', 'z_lo'), [(i, (i + by) % RING) for i in r...  10.3 us
    ppermute x1, starting transfers between devices, local(): other = lax.ppermute(far.astype(F16), 'z_hi', [(0, 1), (1, 0)]).astype(F32)  5.71 us
    ppermute x1, waiting for transfers between devices, local(): other = lax.ppermute(far.astype(F16), 'z_hi', [(0, 1), (1, 0)]).astype(F32)  3.7 us
    ppermute x1, waiting for transfers between devices, local(): shard = lax.ppermute(small, 'section', [(1, 0)])  2.13 us
  transfers between devices with their start and end apart: 20, of which 8 were waited for; matrix products, arithmetic and copies ran while one was open for 1% of the time, Pallas kernels for 12%

profile of v10, /device:TPU:24, one launch (start us, length us, event | category | flops | bytes accessed | tf_op | source)
XLA Modules:
  0.0 94.8 jit_solution(11725568472829472593)
XLA Ops:
  0.6 0.0 slice-start
  0.6 0.0 slice-start.1
  0.7 2.7 %shard_map.68 = (bf16[896,512]{1,0:T(8,128)(2,1)S(1)}, bf16[896,512]{1,0:T(8,128)(2,1)S(1)}, bf16[1280,512]{1,0:T(8,128)(2,1)S(1)}, bf16[1280,512]{1,0:T(8,128)(2,1)S(1)}, bf16[768,512]{1,0:T(8,128)(2,1)S(1)}) custom-call(s32[2]{0:T(128)} %pending_ref.1, bf16[4,128,1024]{2,1,0:T(8,128)(2,1)} %bitcast.20, bf16[3,128,4096]{2,1,0:T(8,128)(2,1)} %bitcast.19), custom_call_target="tpu_custom_call" | custom-call | flops 10000000000 | bytes 12582912 | tf_op jit(solution)/shard_map/pallas_call | solution.py:64
  3.4 1.6 %collective-permute-start.2 = (bf16[896,512]{1,0:T(8,128)(2,1)S(1)}, bf16[896,512]{1,0:T(8,128)(2,1)S(1)}, u32[]{:S(2)}, u32[]{:S(2)}) collective-permute-start(bf16[896,512]{1,0:T(8,128)(2,1)S(1)} %get-tuple-element.43.mine_on), channel_id=1, source_target_pairs={{0,1},{1,2},{2,3},{3,0},{4,5},{5,6},{6,7},{7,4},{8,9},{9,10},{10,1... | collective-permute-start | bytes 2752520 | tf_op jit(solution)/shard_map/ppermute | solution.py:52
  5.0 1.7 %collective-permute-start.3 = (bf16[896,512]{1,0:T(8,128)(2,1)S(1)}, bf16[896,512]{1,0:T(8,128)(2,1)S(1)}, u32[]{:S(2)}, u32[]{:S(2)}) collective-permute-start(bf16[896,512]{1,0:T(8,128)(2,1)S(1)} %get-tuple-element.44), channel_id=1, source_target_pairs={{0,3},{1,0},{2,1},{3,2},{4,7},{5,4},{6,5},{7,6},{8,11},{9,8},{10,9... | collective-permute-start | bytes 2752520 | tf_op jit(solution)/shard_map/ppermute | solution.py:52
  6.7 2.9 %shard_map.69 = (f32[128,1024]{1,0:T(8,128)S(1)}, bf16[128,1024]{1,0:T(8,128)(2,1)S(1)}) custom-call(bf16[128,4096]{1,0:T(8,128)(2,1)S(1)} %copy-done, bf16[1024,4096]{1,0:T(8,128)(2,1)S(1)} %bitcast.11), custom_call_target="tpu_custom_call" | custom-call | flops 1073741824 | bytes 2097152 | tf_op jit(solution)/shard_map/pallas_call | solution.py:64
  9.6 1.3 %collective-permute-start = (bf16[128,1024]{1,0:T(8,128)(2,1)S(1)}, bf16[128,1024]{1,0:T(8,128)(2,1)S(1)}, u32[]{:S(2)}, u32[]{:S(2)}) collective-permute-start(bf16[128,1024]{1,0:T(8,128)(2,1)S(1)} %get-tuple-element.41), channel_id=1, source_target_pairs={{128,0},{129,1},{130,2},{131,3},{132,4},{133,5},{134,6},{135,7},{1... | collective-permute-start | bytes 786440 | tf_op jit(solution)/shard_map/ppermute | solution.py:229
  10.9 2.1 %collective-permute-done = bf16[128,1024]{1,0:T(8,128)(2,1)S(1)} collective-permute-done((bf16[128,1024]{1,0:T(8,128)(2,1)S(1)}, bf16[128,1024]{1,0:T(8,128)(2,1)S(1)}, u32[]{:S(2)}, u32[]{:S(2)}) %collective-permute-start) | collective-permute-done | bytes 262176 | tf_op jit(solution)/shard_map/ppermute | solution.py:229
  13.1 0.3 collective-permute-start.6
  13.4 2.9 %collective-permute-start.7 = (bf16[1280,512]{1,0:T(8,128)(2,1)S(1)}, bf16[1280,512]{1,0:T(8,128)(2,1)S(1)}, u32[]{:S(2)}, u32[]{:S(2)}) collective-permute-start(bf16[1280,512]{1,0:T(8,128)(2,1)S(1)} %get-tuple-element.51), channel_id=1, source_target_pairs={{0,3},{1,0},{2,1},{3,2},{4,7},{5,4},{6,5},{7,6},{8,11},{9,8},{10,9... | collective-permute-start | bytes 3932168 | tf_op jit(solution)/shard_map/ppermute | solution.py:52
  16.3 3.8 %collective-permute-start.1 = (bf16[128,1024]{1,0:T(8,128)(2,1)S(1)}, bf16[128,1024]{1,0:T(8,128)(2,1)S(1)}, u32[]{:S(2)}, u32[]{:S(2)}) collective-permute-start(bf16[128,1024]{1,0:T(8,128)(2,1)S(1)} %collective-permute-done), channel_id=1, source_target_pairs={{0,32},{32,64},{64,96},{96,0},{1,33},{33,65},{65,97},{97,1},{2,34}... | collective-permute-start | bytes 786440 | tf_op jit(solution)/shard_map/ppermute | solution.py:208
  20.1 7.0 %collective-permute-done.1 = bf16[128,1024]{1,0:T(8,128)(2,1)S(1)} collective-permute-done((bf16[128,1024]{1,0:T(8,128)(2,1)S(1)}, bf16[128,1024]{1,0:T(8,128)(2,1)S(1)}, u32[]{:S(2)}, u32[]{:S(2)}) %collective-permute-start.1) | collective-permute-done | bytes 262176 | tf_op jit(solution)/shard_map/ppermute | solution.py:208
  27.2 0.0 collective-permute-done.2.left_on
  27.2 0.0 collective-permute-done.3.right_on
  27.2 3.9 %collective-permute-start.5 = (bf16[128,1024]{1,0:T(8,128)(2,1)S(1)}, bf16[128,1024]{1,0:T(8,128)(2,1)S(1)}, u32[]{:S(2)}, u32[]{:S(2)}) collective-permute-start(bf16[128,1024]{1,0:T(8,128)(2,1)S(1)} %collective-permute-done), channel_id=1, source_target_pairs={{0,96},{32,0},{64,32},{96,64},{1,97},{33,1},{65,33},{97,65},{2,98}... | collective-permute-start | bytes 786440 | tf_op jit(solution)/shard_map/ppermute | solution.py:208
  31.1 0.1 collective-permute-start.8
  31.2 3.2 %collective-permute-start.9 = (bf16[896,512]{1,0:T(8,128)(2,1)S(1)}, bf16[896,512]{1,0:T(8,128)(2,1)S(1)}, u32[]{:S(2)}, u32[]{:S(2)}) collective-permute-start(bf16[896,512]{1,0:T(8,128)(2,1)S(1)} %collective-permute-done.3.right_on), channel_id=1, source_target_pairs={{0,3},{1,0},{2,1},{3,2},{4,7},{5,4},{6,5},{7,6},{8,11},{9,8},{10,9... | collective-permute-start | bytes 2752520 | tf_op jit(solution)/shard_map/ppermute | solution.py:52
  34.4 1.0 %collective-permute-done.5 = bf16[128,1024]{1,0:T(8,128)(2,1)S(1)} collective-permute-done((bf16[128,1024]{1,0:T(8,128)(2,1)S(1)}, bf16[128,1024]{1,0:T(8,128)(2,1)S(1)}, u32[]{:S(2)}, u32[]{:S(2)}) %collective-permute-start.5) | collective-permute-done | bytes 262176 | tf_op jit(solution)/shard_map/ppermute | solution.py:208
  35.4 2.6 %collective-permute-start.4 = (bf16[128,1024]{1,0:T(8,128)(2,1)S(1)}, bf16[128,1024]{1,0:T(8,128)(2,1)S(1)}, u32[]{:S(2)}, u32[]{:S(2)}) collective-permute-start(bf16[128,1024]{1,0:T(8,128)(2,1)S(1)} %collective-permute-done), channel_id=1, source_target_pairs={{0,64},{32,96},{64,0},{96,32},{1,65},{33,97},{65,1},{97,33},{2,66}... | collective-permute-start | bytes 786440 | tf_op jit(solution)/shard_map/ppermute | solution.py:208
  38.0 9.4 %collective-permute-done.4 = bf16[128,1024]{1,0:T(8,128)(2,1)S(1)} collective-permute-done((bf16[128,1024]{1,0:T(8,128)(2,1)S(1)}, bf16[128,1024]{1,0:T(8,128)(2,1)S(1)}, u32[]{:S(2)}, u32[]{:S(2)}) %collective-permute-start.4) | collective-permute-done | bytes 262176 | tf_op jit(solution)/shard_map/ppermute | solution.py:208
  47.4 0.1 pad_maximum_fusion.rel_ref
  47.5 0.6 shard_map.71
  48.2 0.8 collective-permute-start.10
  48.9 0.0 collective-permute-done.6.left_ref
  48.9 0.6 collective-permute-start.11
  49.5 0.0 collective-permute-done.7.right_ref
  49.5 2.6 %collective-permute-start.12 = (bf16[256,512]{1,0:T(8,128)(2,1)S(1)}, bf16[256,512]{1,0:T(8,128)(2,1)S(1)}, u32[]{:S(2)}, u32[]{:S(2)}) collective-permute-start(bf16[256,512]{1,0:T(8,128)(2,1)S(1)} %get-tuple-element.54), channel_id=1, source_target_pairs={{0,3},{1,0},{2,1},{3,2},{4,7},{5,4},{6,5},{7,6},{8,11},{9,8},{10,9... | collective-permute-start | bytes 786440 | tf_op jit(solution)/shard_map/ppermute | solution.py:52
  52.2 2.9 %shard_map.70.acc_ref = f32[1024,1024]{1,0:T(8,128)S(1)} custom-call(bf16[896,512]{1,0:T(8,128)(2,1)S(1)} %get-tuple-element.43.mine_on, bf16[1280,512]{1,0:T(8,128)(2,1)S(1)} %get-tuple-element.49.mine_ref, bf16[768,512]{1,0:T(8,128)(2,1)S(1)} %get-tuple-element.47.own_ref, bf16[896,512]{1,0:T(8,128)(2,1)S(1)} %collective-permute-done.2.left_on, ...), custom_call_target="tpu_custom_call" | custom-call | flops 2415919104 | bytes 12582912 | tf_op jit(solution)/shard_map/pallas_call | solution.py:64
  55.0 3.7 %collective-permute-done.10.two_last = bf16[256,512]{1,0:T(8,128)(2,1)S(1)} collective-permute-done((bf16[256,512]{1,0:T(8,128)(2,1)S(1)}, bf16[256,512]{1,0:T(8,128)(2,1)S(1)}, u32[]{:S(2)}, u32[]{:S(2)}) %collective-permute-start.10) | collective-permute-done | bytes 262176 | tf_op jit(solution)/shard_map/ppermute | solution.py:52
  58.7 5.8 %collective-permute-done.11.left_last = bf16[256,512]{1,0:T(8,128)(2,1)S(1)} collective-permute-done((bf16[256,512]{1,0:T(8,128)(2,1)S(1)}, bf16[256,512]{1,0:T(8,128)(2,1)S(1)}, u32[]{:S(2)}, u32[]{:S(2)}) %collective-permute-start.11) | collective-permute-done | bytes 262176 | tf_op jit(solution)/shard_map/ppermute | solution.py:52
  64.5 0.0 collective-permute-done.12.right_last
  64.5 0.0 collective-permute-done.8.upper_ref
  64.5 1.5 %shard_map.72 = (f32[1024,128]{1,0:T(8,128)S(1)}, f32[1040,128]{1,0:T(8,128)S(1)}, f32[1040,128]{1,0:T(8,128)S(1)}, f32[1040,128]{1,0:T(8,128)S(1)}) custom-call(f32[1024,1024]{1,0:T(8,128)S(1)} %shard_map.70.acc_ref, bf16[896,512]{1,0:T(8,128)(2,1)S(1)} %get-tuple-element.43.mine_on, bf16[1280,512]{1,0:T(8,128)(2,1)S(1)} %get-tuple-element.49.mine_ref, ...), custom_call_target="tpu_custom_call" | custom-call | flops 939524096 | bytes 8388608 | tf_op jit(solution)/shard_map/pallas_call | solution.py:64
  66.0 1.0 %collective-permute-start.13 = (f16[1040,128]{1,0:T(8,128)(2,1)S(1)}, f16[1040,128]{1,0:T(8,128)(2,1)S(1)}, u32[]{:S(2)}, u32[]{:S(2)}) collective-permute-start(f16[1040,128]{1,0:T(8,128)(2,1)S(1)} %convert_element_type.42), channel_id=1, source_target_pairs={{0,8},{1,9},{2,10},{3,11},{4,12},{5,13},{6,14},{7,15},{8,0},{9,1},... | collective-permute-start | bytes 798728 | tf_op jit(solution)/shard_map/ppermute | solution.py:52
  67.1 2.3 %collective-permute-start.14 = (f16[1040,128]{1,0:T(8,128)(2,1)S(1)}, f16[1040,128]{1,0:T(8,128)(2,1)S(1)}, u32[]{:S(2)}, u32[]{:S(2)}) collective-permute-start(f16[1040,128]{1,0:T(8,128)(2,1)S(1)} %convert_element_type.43), channel_id=1, source_target_pairs={{0,4},{1,5},{2,6},{3,7},{4,8},{5,9},{6,10},{7,11},{8,12},{9,13},{1... | collective-permute-start | bytes 798728 | tf_op jit(solution)/shard_map/ppermute | solution.py:52
  69.5 0.1 collective-permute-start.15
  69.6 1.5 %shard_map.74 = (f32[1024,128]{1,0:T(8,128)S(1)}, f32[1040,128]{1,0:T(8,128)S(1)}, f32[1040,128]{1,0:T(8,128)S(1)}, f32[1040,128]{1,0:T(8,128)S(1)}) custom-call(f32[1024,1024]{1,0:T(8,128)S(1)} %shard_map.70.acc_ref, bf16[896,512]{1,0:T(8,128)(2,1)S(1)} %get-tuple-element.43.mine_on, bf16[1280,512]{1,0:T(8,128)(2,1)S(1)} %get-tuple-element.49.mine_ref, ...), custom_call_target="tpu_custom_call" | custom-call | flops 939524096 | bytes 8388608 | tf_op jit(solution)/shard_map/pallas_call | solution.py:64
  71.1 2.4 %collective-permute-start.16 = (f16[1040,128]{1,0:T(8,128)(2,1)S(1)}, f16[1040,128]{1,0:T(8,128)(2,1)S(1)}, u32[]{:S(2)}, u32[]{:S(2)}) collective-permute-start(f16[1040,128]{1,0:T(8,128)(2,1)S(1)} %convert_element_type.45), channel_id=1, source_target_pairs={{0,8},{1,9},{2,10},{3,11},{4,12},{5,13},{6,14},{7,15},{8,0},{9,1},... | collective-permute-start | bytes 798728 | tf_op jit(solution)/shard_map/ppermute | solution.py:52
  73.6 1.0 %collective-permute-start.17 = (f16[1040,128]{1,0:T(8,128)(2,1)S(1)}, f16[1040,128]{1,0:T(8,128)(2,1)S(1)}, u32[]{:S(2)}, u32[]{:S(2)}) collective-permute-start(f16[1040,128]{1,0:T(8,128)(2,1)S(1)} %convert_element_type.47), channel_id=1, source_target_pairs={{0,4},{1,5},{2,6},{3,7},{4,8},{5,9},{6,10},{7,11},{8,12},{9,13},{1... | collective-permute-start | bytes 798728 | tf_op jit(solution)/shard_map/ppermute | solution.py:52
  74.6 1.2 %collective-permute-start.18 = (f16[1040,128]{1,0:T(8,128)(2,1)S(1)}, f16[1040,128]{1,0:T(8,128)(2,1)S(1)}, u32[]{:S(2)}, u32[]{:S(2)}) collective-permute-start(f16[1040,128]{1,0:T(8,128)(2,1)S(1)} %convert_element_type.49), channel_id=1, source_target_pairs={{0,12},{1,13},{2,14},{3,15},{4,0},{5,1},{6,2},{7,3},{8,4},{9,5},{1... | collective-permute-start | bytes 798728 | tf_op jit(solution)/shard_map/ppermute | solution.py:52
  75.8 0.0 collective-permute-done.14
  75.8 4.2 %collective-permute-done.15 = f16[1040,128]{1,0:T(8,128)(2,1)S(1)} collective-permute-done((f16[1040,128]{1,0:T(8,128)(2,1)S(1)}, f16[1040,128]{1,0:T(8,128)(2,1)S(1)}, u32[]{:S(2)}, u32[]{:S(2)}) %collective-permute-start.15) | collective-permute-done | bytes 266272 | tf_op jit(solution)/shard_map/ppermute | solution.py:52
  80.2 0.3 shard_map.75
  80.5 5.7 %collective-permute-start.19 = (f16[1040,128]{1,0:T(8,128)(2,1)S(1)}, f16[1040,128]{1,0:T(8,128)(2,1)S(1)}, u32[]{:S(2)}, u32[]{:S(2)}) collective-permute-start(f16[1040,128]{1,0:T(8,128)(2,1)S(1)} %convert_element_type.54), channel_id=1, source_target_pairs={{0,16},{16,0},{1,17},{17,1},{2,18},{18,2},{3,19},{19,3},{4,20},{20... | collective-permute-start | bytes 798728 | tf_op jit(solution)/shard_map/ppermute | solution.py:266
  86.2 0.0 collective-permute-done.17
  86.3 3.7 %shard_map.73 = f32[128,1024]{1,0:T(8,128)} custom-call(bf16[4,128,1024]{2,1,0:T(8,128)(2,1)S(1)} %pad_maximum_fusion.rel_ref, f32[128,1024]{1,0:T(8,128)S(1)} %get-tuple-element.67.first_ref, bf16[1024,4096]{1,0:T(8,128)(2,1)S(1)} %bitcast.12), custom_call_target="tpu_custom_call" | custom-call | flops 1073741824 | bytes 2097152 | tf_op jit(solution)/shard_map/pallas_call | solution.py:64
  90.0 3.7 %collective-permute-done.19 = f16[1040,128]{1,0:T(8,128)(2,1)S(1)} collective-permute-done((f16[1040,128]{1,0:T(8,128)(2,1)S(1)}, f16[1040,128]{1,0:T(8,128)(2,1)S(1)}, u32[]{:S(2)}, u32[]{:S(2)}) %collective-permute-start.19) | collective-permute-done | bytes 266272 | tf_op jit(solution)/shard_map/ppermute | solution.py:266
  93.8 1.0 %shard_map.76 = f32[1024,128]{1,0:T(8,128)} custom-call(f32[1024,128]{1,0:T(8,128)S(1)} %get-tuple-element.68.keep_ref, f32[1040,128]{1,0:T(8,128)S(1)} %convert_element_type.46.one_ref, f32[1040,128]{1,0:T(8,128)S(1)} %convert_element_type.48.two_ref, f32[1040,128]{1,0:T(8,128)S(1)} %convert_element_type.50.three_ref, ...), custom_call_target="tpu_custom_call" | custom-call | bytes 4194304 | tf_op jit(solution)/shard_map/pallas_call | solution.py:64
  (23 shorter events, 0.5 us)
Async XLA Ops:
  0.6 6.1 %slice-start = ((s8[8388608]{0:T(1024)(128)(4,1)}), s8[4194304]{0:T(1024)(128)(4,1)S(1)}, s32[]{:S(2)}) async-start(s8[8388608]{0:T(1024)(128)(4,1)} %bitcast.9), calls=%async_computation | async-start | bytes 8388608
  0.6 6.1 %slice-start.1 = ((s8[8388608]{0:T(1024)(128)(4,1)}), s8[4194304]{0:T(1024)(128)(4,1)S(1)}, s32[]{:S(2)}) async-start(s8[8388608]{0:T(1024)(128)(4,1)} %bitcast.9), calls=%async_computation.1 | async-start | bytes 8388608
  0.7 6.1 %copy-start = (bf16[128,4096]{1,0:T(8,128)(2,1)S(1)}, bf16[128,4096]{1,0:T(8,128)(2,1)}, u32[]{:S(2)}) copy-start(bf16[128,4096]{1,0:T(8,128)(2,1)} %head_ref.1) | copy-start | bytes 3145732
  3.4 23.8 %collective-permute-start.2 = (bf16[896,512]{1,0:T(8,128)(2,1)S(1)}, bf16[896,512]{1,0:T(8,128)(2,1)S(1)}, u32[]{:S(2)}, u32[]{:S(2)}) collective-permute-start(bf16[896,512]{1,0:T(8,128)(2,1)S(1)} %get-tuple-element.43.mine_on), channel_id=1, source_target_pairs={{0,1},{1,2},{2,3},{3,0},{4,5},{5,6},{6,7},{7,4},{8,9},{9,10},{10,1... | collective-permute-start | bytes 2752520 | tf_op jit(solution)/shard_map/ppermute | solution.py:52
  5.0 22.2 %collective-permute-start.3 = (bf16[896,512]{1,0:T(8,128)(2,1)S(1)}, bf16[896,512]{1,0:T(8,128)(2,1)S(1)}, u32[]{:S(2)}, u32[]{:S(2)}) collective-permute-start(bf16[896,512]{1,0:T(8,128)(2,1)S(1)} %get-tuple-element.44), channel_id=1, source_target_pairs={{0,3},{1,0},{2,1},{3,2},{4,7},{5,4},{6,5},{7,6},{8,11},{9,8},{10,9... | collective-permute-start | bytes 2752520 | tf_op jit(solution)/shard_map/ppermute | solution.py:52
  9.6 3.4 %collective-permute-start = (bf16[128,1024]{1,0:T(8,128)(2,1)S(1)}, bf16[128,1024]{1,0:T(8,128)(2,1)S(1)}, u32[]{:S(2)}, u32[]{:S(2)}) collective-permute-start(bf16[128,1024]{1,0:T(8,128)(2,1)S(1)} %get-tuple-element.41), channel_id=1, source_target_pairs={{128,0},{129,1},{130,2},{131,3},{132,4},{133,5},{134,6},{135,7},{1... | collective-permute-start | bytes 786440 | tf_op jit(solution)/shard_map/ppermute | solution.py:229
  13.1 35.9 %collective-permute-start.6 = (bf16[1280,512]{1,0:T(8,128)(2,1)S(1)}, bf16[1280,512]{1,0:T(8,128)(2,1)S(1)}, u32[]{:S(2)}, u32[]{:S(2)}) collective-permute-start(bf16[1280,512]{1,0:T(8,128)(2,1)S(1)} %get-tuple-element.49.mine_ref), channel_id=1, source_target_pairs={{0,1},{1,2},{2,3},{3,0},{4,5},{5,6},{6,7},{7,4},{8,9},{9,10},{10,1... | collective-permute-start | bytes 3932168 | tf_op jit(solution)/shard_map/ppermute | solution.py:52
  13.4 36.1 %collective-permute-start.7 = (bf16[1280,512]{1,0:T(8,128)(2,1)S(1)}, bf16[1280,512]{1,0:T(8,128)(2,1)S(1)}, u32[]{:S(2)}, u32[]{:S(2)}) collective-permute-start(bf16[1280,512]{1,0:T(8,128)(2,1)S(1)} %get-tuple-element.51), channel_id=1, source_target_pairs={{0,3},{1,0},{2,1},{3,2},{4,7},{5,4},{6,5},{7,6},{8,11},{9,8},{10,9... | collective-permute-start | bytes 3932168 | tf_op jit(solution)/shard_map/ppermute | solution.py:52
  16.3 10.9 %collective-permute-start.1 = (bf16[128,1024]{1,0:T(8,128)(2,1)S(1)}, bf16[128,1024]{1,0:T(8,128)(2,1)S(1)}, u32[]{:S(2)}, u32[]{:S(2)}) collective-permute-start(bf16[128,1024]{1,0:T(8,128)(2,1)S(1)} %collective-permute-done), channel_id=1, source_target_pairs={{0,32},{32,64},{64,96},{96,0},{1,33},{33,65},{65,97},{97,1},{2,34}... | collective-permute-start | bytes 786440 | tf_op jit(solution)/shard_map/ppermute | solution.py:208
  27.2 8.3 %collective-permute-start.5 = (bf16[128,1024]{1,0:T(8,128)(2,1)S(1)}, bf16[128,1024]{1,0:T(8,128)(2,1)S(1)}, u32[]{:S(2)}, u32[]{:S(2)}) collective-permute-start(bf16[128,1024]{1,0:T(8,128)(2,1)S(1)} %collective-permute-done), channel_id=1, source_target_pairs={{0,96},{32,0},{64,32},{96,64},{1,97},{33,1},{65,33},{97,65},{2,98}... | collective-permute-start | bytes 786440 | tf_op jit(solution)/shard_map/ppermute | solution.py:208
  31.1 33.4 %collective-permute-start.8 = (bf16[896,512]{1,0:T(8,128)(2,1)S(1)}, bf16[896,512]{1,0:T(8,128)(2,1)S(1)}, u32[]{:S(2)}, u32[]{:S(2)}) collective-permute-start(bf16[896,512]{1,0:T(8,128)(2,1)S(1)} %collective-permute-done.2.left_on), channel_id=1, source_target_pairs={{0,1},{1,2},{2,3},{3,0},{4,5},{5,6},{6,7},{7,4},{8,9},{9,10},{10,1... | collective-permute-start | bytes 2752520 | tf_op jit(solution)/shard_map/ppermute | solution.py:52
  31.2 33.3 %collective-permute-start.9 = (bf16[896,512]{1,0:T(8,128)(2,1)S(1)}, bf16[896,512]{1,0:T(8,128)(2,1)S(1)}, u32[]{:S(2)}, u32[]{:S(2)}) collective-permute-start(bf16[896,512]{1,0:T(8,128)(2,1)S(1)} %collective-permute-done.3.right_on), channel_id=1, source_target_pairs={{0,3},{1,0},{2,1},{3,2},{4,7},{5,4},{6,5},{7,6},{8,11},{9,8},{10,9... | collective-permute-start | bytes 2752520 | tf_op jit(solution)/shard_map/ppermute | solution.py:52
  35.4 12.0 %collective-permute-start.4 = (bf16[128,1024]{1,0:T(8,128)(2,1)S(1)}, bf16[128,1024]{1,0:T(8,128)(2,1)S(1)}, u32[]{:S(2)}, u32[]{:S(2)}) collective-permute-start(bf16[128,1024]{1,0:T(8,128)(2,1)S(1)} %collective-permute-done), channel_id=1, source_target_pairs={{0,64},{32,96},{64,0},{96,32},{1,65},{33,97},{65,1},{97,33},{2,66}... | collective-permute-start | bytes 786440 | tf_op jit(solution)/shard_map/ppermute | solution.py:208
  48.2 10.6 %collective-permute-start.10 = (bf16[256,512]{1,0:T(8,128)(2,1)S(1)}, bf16[256,512]{1,0:T(8,128)(2,1)S(1)}, u32[]{:S(2)}, u32[]{:S(2)}) collective-permute-start(bf16[256,512]{1,0:T(8,128)(2,1)S(1)} %get-tuple-element.52), channel_id=1, source_target_pairs={{0,2},{1,3},{2,0},{3,1},{4,6},{5,7},{6,4},{7,5},{8,10},{9,11},{10,... | collective-permute-start | bytes 786440 | tf_op jit(solution)/shard_map/ppermute | solution.py:52
  48.9 15.6 %collective-permute-start.11 = (bf16[256,512]{1,0:T(8,128)(2,1)S(1)}, bf16[256,512]{1,0:T(8,128)(2,1)S(1)}, u32[]{:S(2)}, u32[]{:S(2)}) collective-permute-start(bf16[256,512]{1,0:T(8,128)(2,1)S(1)} %get-tuple-element.53), channel_id=1, source_target_pairs={{0,1},{1,2},{2,3},{3,0},{4,5},{5,6},{6,7},{7,4},{8,9},{9,10},{10,1... | collective-permute-start | bytes 786440 | tf_op jit(solution)/shard_map/ppermute | solution.py:52
  49.5 15.0 %collective-permute-start.12 = (bf16[256,512]{1,0:T(8,128)(2,1)S(1)}, bf16[256,512]{1,0:T(8,128)(2,1)S(1)}, u32[]{:S(2)}, u32[]{:S(2)}) collective-permute-start(bf16[256,512]{1,0:T(8,128)(2,1)S(1)} %get-tuple-element.54), channel_id=1, source_target_pairs={{0,3},{1,0},{2,1},{3,2},{4,7},{5,4},{6,5},{7,6},{8,11},{9,8},{10,9... | collective-permute-start | bytes 786440 | tf_op jit(solution)/shard_map/ppermute | solution.py:52
  66.0 8.6 %collective-permute-start.13 = (f16[1040,128]{1,0:T(8,128)(2,1)S(1)}, f16[1040,128]{1,0:T(8,128)(2,1)S(1)}, u32[]{:S(2)}, u32[]{:S(2)}) collective-permute-start(f16[1040,128]{1,0:T(8,128)(2,1)S(1)} %convert_element_type.42), channel_id=1, source_target_pairs={{0,8},{1,9},{2,10},{3,11},{4,12},{5,13},{6,14},{7,15},{8,0},{9,1},... | collective-permute-start | bytes 798728 | tf_op jit(solution)/shard_map/ppermute | solution.py:52
  67.1 8.7 %collective-permute-start.14 = (f16[1040,128]{1,0:T(8,128)(2,1)S(1)}, f16[1040,128]{1,0:T(8,128)(2,1)S(1)}, u32[]{:S(2)}, u32[]{:S(2)}) collective-permute-start(f16[1040,128]{1,0:T(8,128)(2,1)S(1)} %convert_element_type.43), channel_id=1, source_target_pairs={{0,4},{1,5},{2,6},{3,7},{4,8},{5,9},{6,10},{7,11},{8,12},{9,13},{1... | collective-permute-start | bytes 798728 | tf_op jit(solution)/shard_map/ppermute | solution.py:52
  69.5 10.6 %collective-permute-start.15 = (f16[1040,128]{1,0:T(8,128)(2,1)S(1)}, f16[1040,128]{1,0:T(8,128)(2,1)S(1)}, u32[]{:S(2)}, u32[]{:S(2)}) collective-permute-start(f16[1040,128]{1,0:T(8,128)(2,1)S(1)} %convert_element_type.44), channel_id=1, source_target_pairs={{0,12},{1,13},{2,14},{3,15},{4,0},{5,1},{6,2},{7,3},{8,4},{9,5},{1... | collective-permute-start | bytes 798728 | tf_op jit(solution)/shard_map/ppermute | solution.py:52
  71.1 15.1 %collective-permute-start.16 = (f16[1040,128]{1,0:T(8,128)(2,1)S(1)}, f16[1040,128]{1,0:T(8,128)(2,1)S(1)}, u32[]{:S(2)}, u32[]{:S(2)}) collective-permute-start(f16[1040,128]{1,0:T(8,128)(2,1)S(1)} %convert_element_type.45), channel_id=1, source_target_pairs={{0,8},{1,9},{2,10},{3,11},{4,12},{5,13},{6,14},{7,15},{8,0},{9,1},... | collective-permute-start | bytes 798728 | tf_op jit(solution)/shard_map/ppermute | solution.py:52
  73.6 12.7 %collective-permute-start.17 = (f16[1040,128]{1,0:T(8,128)(2,1)S(1)}, f16[1040,128]{1,0:T(8,128)(2,1)S(1)}, u32[]{:S(2)}, u32[]{:S(2)}) collective-permute-start(f16[1040,128]{1,0:T(8,128)(2,1)S(1)} %convert_element_type.47), channel_id=1, source_target_pairs={{0,4},{1,5},{2,6},{3,7},{4,8},{5,9},{6,10},{7,11},{8,12},{9,13},{1... | collective-permute-start | bytes 798728 | tf_op jit(solution)/shard_map/ppermute | solution.py:52
  74.6 11.7 %collective-permute-start.18 = (f16[1040,128]{1,0:T(8,128)(2,1)S(1)}, f16[1040,128]{1,0:T(8,128)(2,1)S(1)}, u32[]{:S(2)}, u32[]{:S(2)}) collective-permute-start(f16[1040,128]{1,0:T(8,128)(2,1)S(1)} %convert_element_type.49), channel_id=1, source_target_pairs={{0,12},{1,13},{2,14},{3,15},{4,0},{5,1},{6,2},{7,3},{8,4},{9,5},{1... | collective-permute-start | bytes 798728 | tf_op jit(solution)/shard_map/ppermute | solution.py:52
  80.5 13.3 %collective-permute-start.19 = (f16[1040,128]{1,0:T(8,128)(2,1)S(1)}, f16[1040,128]{1,0:T(8,128)(2,1)S(1)}, u32[]{:S(2)}, u32[]{:S(2)}) collective-permute-start(f16[1040,128]{1,0:T(8,128)(2,1)S(1)} %convert_element_type.54), channel_id=1, source_target_pairs={{0,16},{16,0},{1,17},{17,1},{2,18},{18,2},{3,19},{19,3},{4,20},{20... | collective-permute-start | bytes 798728 | tf_op jit(solution)/shard_map/ppermute | solution.py:266

commit v11 on v10

--- a/solution.py
+++ b/solution.py
@@ -204,8 +204,9 @@
     out_ref[...] = summed(keep_ref, (one_ref, two_ref, three_ref, other_ref))
 
 
-def on_first(value, by):
-    return lax.ppermute(value, ("section", "z_lo"), [(i, (i + by) % RING) for i in range(RING)])
+def on_line(value, pairs):
+    pairs = [(s * RING + i, t * RING + j % RING) for (s, i), (t, j) in pairs]
+    return lax.ppermute(value, ("section", "z_lo"), pairs)
 
 
 def local(weights, stash_in, stash_grad, head_grad, pending):
@@ -229,10 +230,16 @@
     shard = lax.ppermute(small, "section", [(1, 0)])
     staying_right, staying_left, shard = lax.optimization_barrier((right, left, shard))
     from_left, from_right = shifted(staying_right, True, 1), shifted(staying_left, True, -1)
-    one = on_first(shard, 1)
-    shard, one, from_left_on, from_right_on = lax.optimization_barrier((shard, one, from_left_on, from_right_on))
-    upper, lower = shifted(from_left_on, True, 1), shifted(from_right_on, True, -1)
-    rel = [shard, one, on_first(shard, 2), on_first(shard, 3)]
+    places = range(RING)
+    both = jnp.where(on_last(), small, shard)
+    passed = on_line(both, [((0, i), (0, i - 1)) for i in places] + [((1, i), (1, i + 1)) for i in places])
+    passed, from_left_on, from_right_on = lax.optimization_barrier((passed, from_left_on, from_right_on))
+    upper = shifted(from_left_on, True, 1)
+    behind_two = on_line(passed, [((1, i), (0, i + 1)) for i in places])
+    passed, behind_two = lax.optimization_barrier((passed, behind_two))
+    behind = on_line(passed, [((1, i), (0, i)) for i in places])
+    lower = shifted(from_right_on, True, -1)
+    rel = [shard, behind, behind_two, passed]
     rel = jnp.stack(rel, 0)
 
     edge = ((2 * rows, lanes), BF16)

time: 94.9 us -> 90.6 us (0.955)
  waiting for transfers between devices: 37 us -> 24.3 us
  Pallas kernels: 17 us -> 24.8 us
  starting transfers between devices: 39.2 us -> 36.6 us
  other arithmetic: 0.66 us -> 2.68 us
    ppermute x15, waiting for transfers between devices: 13.7 us -> 2.76 us  [shifted(): return lax.ppermute(value, ('section', 'y', 'x'), pairs_over(along, by))]
    pallas_call x9, Pallas kernels: 17 us -> 24.8 us  [call(): pl.pallas_call(kernel, out_shape=[jax.ShapeDtypeStruct(s, t) for s, t in...]
    ppermute x3, waiting for transfers between devices: 17.5 us -> 11.6 us  [on_line(): return lax.ppermute(value, ('section', 'z_lo'), pairs)]
    ppermute x1, waiting for transfers between devices: 3.7 us -> 7.51 us  [local(): other = lax.ppermute(far.astype(F16), 'z_hi', [(0, 1), (1, 0)]).astype(F32)]
    ppermute x3, starting transfers between devices: 10.3 us -> 7.26 us  [on_line(): return lax.ppermute(value, ('section', 'z_lo'), pairs)]
    select_n x0 -> x1, other arithmetic: none -> 1.07 us  [local(): both = jnp.where(on_last(), small, shard)]
    another operation x1, other arithmetic: 0.13 us -> 1.08 us  [local(): rel = jnp.stack(rel, 0)]
  transfers between devices with their start and end apart: 20 -> 20, of which waited for: 8 -> 7; matrix products, arithmetic and copies ran while one was open for 1% -> 3% of each run, Pallas kernels for 12% -> 18%
where the time goes in v11:
time: 90.6 us; the launch traced here: 90.2 us
  starting transfers between devices  36.6 us (40%)
  Pallas kernels  24.8 us (27%)
  waiting for transfers between devices  24.3 us (27%)
  other arithmetic  2.68 us (3%)
  between operations  0.94 us (1%)
    pallas_call x9, Pallas kernels, call(): pl.pallas_call(kernel, out_shape=[jax.ShapeDtypeStruct(s, t) for s, t in...  24.8 us
    ppermute x15, starting transfers between devices, shifted(): return lax.ppermute(value, ('section', 'y', 'x'), pairs_over(along, by))  21.6 us
    ppermute x3, waiting for transfers between devices, on_line(): return lax.ppermute(value, ('section', 'z_lo'), pairs)  11.6 us
    ppermute x1, waiting for transfers between devices, local(): other = lax.ppermute(far.astype(F16), 'z_hi', [(0, 1), (1, 0)]).astype(F32)  7.51 us
    ppermute x3, starting transfers between devices, on_line(): return lax.ppermute(value, ('section', 'z_lo'), pairs)  7.26 us
    ppermute x1, starting transfers between devices, local(): other = lax.ppermute(far.astype(F16), 'z_hi', [(0, 1), (1, 0)]).astype(F32)  6.41 us
    ppermute x15, waiting for transfers between devices, shifted(): return lax.ppermute(value, ('section', 'y', 'x'), pairs_over(along, by))  2.76 us
    ppermute x1, waiting for transfers between devices, local(): shard = lax.ppermute(small, 'section', [(1, 0)])  2.47 us
  transfers between devices with their start and end apart: 20, of which 7 were waited for; matrix products, arithmetic and copies ran while one was open for 3% of the time, Pallas kernels for 18%

profile of v11, /device:TPU:24, one launch (start us, length us, event | category | flops | bytes accessed | tf_op | source)
XLA Modules:
  0.0 90.2 jit_solution(12313138045417785220)
XLA Ops:
  0.6 0.0 slice-start
  0.6 0.0 slice-start.1
  0.7 0.0 copy-start
  0.7 4.1 %shard_map.68 = (bf16[896,512]{1,0:T(8,128)(2,1)S(1)}, bf16[896,512]{1,0:T(8,128)(2,1)}, bf16[1280,512]{1,0:T(8,128)(2,1)S(1)}, bf16[1280,512]{1,0:T(8,128)(2,1)}, bf16[768,512]{1,0:T(8,128)(2,1)S(1)}) custom-call(s32[2]{0:T(128)} %pending_ref.1, bf16[4,128,1024]{2,1,0:T(8,128)(2,1)} %bitcast.21, bf16[3,128,4096]{2,1,0:T(8,128)(2,1)} %bitcast.20), custom_call_target="tpu_custom_call" | custom-call | flops 10000000000 | bytes 12582912 | tf_op jit(solution)/shard_map/pallas_call | solution.py:64
  4.8 1.6 %collective-permute-start.2 = (bf16[896,512]{1,0:T(8,128)(2,1)S(1)}, bf16[896,512]{1,0:T(8,128)(2,1)}, u32[]{:S(2)}, u32[]{:S(2)}) collective-permute-start(bf16[896,512]{1,0:T(8,128)(2,1)S(1)} %get-tuple-element.44.mine_on), channel_id=1, source_target_pairs={{0,1},{1,2},{2,3},{3,0},{4,5},{5,6},{6,7},{7,4},{8,9},{9,10},{10,1... | collective-permute-start | bytes 2752520 | tf_op jit(solution)/shard_map/ppermute | solution.py:52
  6.4 1.7 %collective-permute-start.3 = (bf16[896,512]{1,0:T(8,128)(2,1)}, bf16[896,512]{1,0:T(8,128)(2,1)}, u32[]{:S(2)}, u32[]{:S(2)}) collective-permute-start(bf16[896,512]{1,0:T(8,128)(2,1)} %get-tuple-element.45), channel_id=1, source_target_pairs={{0,3},{1,0},{2,1},{3,2},{4,7},{5,4},{6,5},{7,6},{8,11},{9,8},{10,9... | collective-permute-start | bytes 2752520 | tf_op jit(solution)/shard_map/ppermute | solution.py:52
  8.1 3.6 %shard_map.69 = (f32[128,1024]{1,0:T(8,128)S(1)}, bf16[128,1024]{1,0:T(8,128)(2,1)}) custom-call(bf16[128,4096]{1,0:T(8,128)(2,1)S(1)} %copy-done, bf16[1024,4096]{1,0:T(8,128)(2,1)S(1)} %bitcast.11), custom_call_target="tpu_custom_call" | custom-call | flops 1073741824 | bytes 2097152 | tf_op jit(solution)/shard_map/pallas_call | solution.py:64
  11.7 0.8 copy-done.4
  12.5 1.3 %collective-permute-start = (bf16[128,1024]{1,0:T(8,128)(2,1)}, bf16[128,1024]{1,0:T(8,128)(2,1)}, u32[]{:S(2)}, u32[]{:S(2)}) collective-permute-start(bf16[128,1024]{1,0:T(8,128)(2,1)} %get-tuple-element.42), channel_id=1, source_target_pairs={{128,0},{129,1},{130,2},{131,3},{132,4},{133,5},{134,6},{135,7},{1... | collective-permute-start | bytes 786440 | tf_op jit(solution)/shard_map/ppermute | solution.py:230
  13.8 2.5 %collective-permute-done = bf16[128,1024]{1,0:T(8,128)(2,1)} collective-permute-done((bf16[128,1024]{1,0:T(8,128)(2,1)}, bf16[128,1024]{1,0:T(8,128)(2,1)}, u32[]{:S(2)}, u32[]{:S(2)}) %collective-permute-start) | collective-permute-done | bytes 262176 | tf_op jit(solution)/shard_map/ppermute | solution.py:230
  16.3 0.3 collective-permute-start.6
  16.6 3.0 %collective-permute-start.7 = (bf16[1280,512]{1,0:T(8,128)(2,1)}, bf16[1280,512]{1,0:T(8,128)(2,1)}, u32[]{:S(2)}, u32[]{:S(2)}) collective-permute-start(bf16[1280,512]{1,0:T(8,128)(2,1)} %get-tuple-element.53), channel_id=1, source_target_pairs={{0,3},{1,0},{2,1},{3,2},{4,7},{5,4},{6,5},{7,6},{8,11},{9,8},{10,9... | collective-permute-start | bytes 3932168 | tf_op jit(solution)/shard_map/ppermute | solution.py:52
  19.5 1.1 %broadcast_select_fusion = bf16[128,1024]{1,0:T(8,128)(2,1)S(1)} fusion(bf16[128,1024]{1,0:T(8,128)(2,1)} %get-tuple-element.42, bf16[128,1024]{1,0:T(8,128)(2,1)} %collective-permute-done, pred[]{:T(512)S(6)} %eq.3), kind=kLoop, calls=%fused_computation.1 | loop fusion | flops 131072 | bytes 786433 | tf_op jit(solution)/shard_map/jit(_where)/select_n | solution.py:234
  20.6 4.7 %collective-permute-start.1 = (bf16[128,1024]{1,0:T(8,128)(2,1)S(1)}, bf16[128,1024]{1,0:T(8,128)(2,1)S(1)}, u32[]{:S(2)}, u32[]{:S(2)}) collective-permute-start(bf16[128,1024]{1,0:T(8,128)(2,1)S(1)} %broadcast_select_fusion), channel_id=1, source_target_pairs={{0,96},{32,0},{64,32},{96,64},{128,160},{160,192},{192,224},{224,1... | collective-permute-start | bytes 786440 | tf_op jit(solution)/shard_map/ppermute | solution.py:209
  25.3 4.6 %collective-permute-done.1 = bf16[128,1024]{1,0:T(8,128)(2,1)S(1)} collective-permute-done((bf16[128,1024]{1,0:T(8,128)(2,1)S(1)}, bf16[128,1024]{1,0:T(8,128)(2,1)S(1)}, u32[]{:S(2)}, u32[]{:S(2)}) %collective-permute-start.1) | collective-permute-done | bytes 262176 | tf_op jit(solution)/shard_map/ppermute | solution.py:209
  29.9 1.3 %collective-permute-start.4 = (bf16[128,1024]{1,0:T(8,128)(2,1)S(1)}, bf16[128,1024]{1,0:T(8,128)(2,1)S(1)}, u32[]{:S(2)}, u32[]{:S(2)}) collective-permute-start(bf16[128,1024]{1,0:T(8,128)(2,1)S(1)} %collective-permute-done.1), channel_id=1, source_target_pairs={{128,32},{160,64},{192,96},{224,0},{129,33},{161,65},{193,97},{225... | collective-permute-start | bytes 786440 | tf_op jit(solution)/shard_map/ppermute | solution.py:209
  31.1 0.1 collective-permute-start.8
  31.2 3.2 %collective-permute-start.9 = (bf16[896,512]{1,0:T(8,128)(2,1)}, bf16[896,512]{1,0:T(8,128)(2,1)S(1)}, u32[]{:S(2)}, u32[]{:S(2)}) collective-permute-start(bf16[896,512]{1,0:T(8,128)(2,1)} %collective-permute-done.3.right_on), channel_id=1, source_target_pairs={{0,3},{1,0},{2,1},{3,2},{4,7},{5,4},{6,5},{7,6},{8,11},{9,8},{10,9... | collective-permute-start | bytes 2752520 | tf_op jit(solution)/shard_map/ppermute | solution.py:52
  34.5 4.9 %collective-permute-done.4 = bf16[128,1024]{1,0:T(8,128)(2,1)S(1)} collective-permute-done((bf16[128,1024]{1,0:T(8,128)(2,1)S(1)}, bf16[128,1024]{1,0:T(8,128)(2,1)S(1)}, u32[]{:S(2)}, u32[]{:S(2)}) %collective-permute-start.4) | collective-permute-done | bytes 262176 | tf_op jit(solution)/shard_map/ppermute | solution.py:209
  39.3 1.3 %collective-permute-start.5 = (bf16[128,1024]{1,0:T(8,128)(2,1)S(1)}, bf16[128,1024]{1,0:T(8,128)(2,1)S(1)}, u32[]{:S(2)}, u32[]{:S(2)}) collective-permute-start(bf16[128,1024]{1,0:T(8,128)(2,1)S(1)} %collective-permute-done.1), channel_id=1, source_target_pairs={{128,0},{160,32},{192,64},{224,96},{129,1},{161,33},{193,65},{225,... | collective-permute-start | bytes 786440 | tf_op jit(solution)/shard_map/ppermute | solution.py:209
  40.6 2.1 %collective-permute-done.5 = bf16[128,1024]{1,0:T(8,128)(2,1)S(1)} collective-permute-done((bf16[128,1024]{1,0:T(8,128)(2,1)S(1)}, bf16[128,1024]{1,0:T(8,128)(2,1)S(1)}, u32[]{:S(2)}, u32[]{:S(2)}) %collective-permute-start.5) | collective-permute-done | bytes 262176 | tf_op jit(solution)/shard_map/ppermute | solution.py:209
  42.8 1.1 %pad_maximum_fusion.rel_ref = bf16[4,128,1024]{2,1,0:T(8,128)(2,1)S(1)} fusion(bf16[1,128,1024]{2,1,0:T(8,128)(2,1)S(1)} %bitcast.17, bf16[1,128,1024]{2,1,0:T(8,128)(2,1)S(1)} %bitcast.18, bf16[1,128,1024]{2,1,0:T(8,128)(2,1)S(1)} %bitcast.19, bf16[1,128,1024]{2,1,0:T(8,128)(2,1)} %bitcast.3), kind=kLoop, calls=%fused_computation | loop fusion | flops 1572864 | bytes 2097152 | tf_op jit(solution)/shard_map/stack | solution.py:243
  43.9 0.6 shard_map.71
  44.5 0.3 collective-permute-start.10
  44.8 0.0 collective-permute-done.6.left_ref
  44.8 0.6 collective-permute-start.11
  45.4 0.0 collective-permute-done.7.right_ref
  45.4 2.7 %collective-permute-start.12 = (bf16[256,512]{1,0:T(8,128)(2,1)S(1)}, bf16[256,512]{1,0:T(8,128)(2,1)S(1)}, u32[]{:S(2)}, u32[]{:S(2)}) collective-permute-start(bf16[256,512]{1,0:T(8,128)(2,1)S(1)} %get-tuple-element.56), channel_id=1, source_target_pairs={{0,3},{1,0},{2,1},{3,2},{4,7},{5,4},{6,5},{7,6},{8,11},{9,8},{10,9... | collective-permute-start | bytes 786440 | tf_op jit(solution)/shard_map/ppermute | solution.py:52
  48.1 4.7 %shard_map.70.acc_ref = f32[1024,1024]{1,0:T(8,128)S(1)} custom-call(bf16[896,512]{1,0:T(8,128)(2,1)S(1)} %get-tuple-element.44.mine_on, bf16[1280,512]{1,0:T(8,128)(2,1)S(1)} %get-tuple-element.51.mine_ref, bf16[768,512]{1,0:T(8,128)(2,1)S(1)} %copy-done.3, bf16[896,512]{1,0:T(8,128)(2,1)} %collective-permute-done.2.left_on, ...), custom_call_target="tpu_custom_call" | custom-call | flops 2415919104 | bytes 12582912 | tf_op jit(solution)/shard_map/pallas_call | solution.py:64
  52.8 0.0 collective-permute-done.10.two_last
  52.8 2.4 %collective-permute-done.11.left_last = bf16[256,512]{1,0:T(8,128)(2,1)S(1)} collective-permute-done((bf16[256,512]{1,0:T(8,128)(2,1)S(1)}, bf16[256,512]{1,0:T(8,128)(2,1)S(1)}, u32[]{:S(2)}, u32[]{:S(2)}) %collective-permute-start.11) | collective-permute-done | bytes 262176 | tf_op jit(solution)/shard_map/ppermute | solution.py:52
  55.2 0.0 collective-permute-done.12.right_last
  55.3 3.3 %shard_map.72 = (f32[1024,128]{1,0:T(8,128)S(1)}, f32[1040,128]{1,0:T(8,128)S(1)}, f32[1040,128]{1,0:T(8,128)S(1)}, f32[1040,128]{1,0:T(8,128)S(1)}) custom-call(f32[1024,1024]{1,0:T(8,128)S(1)} %shard_map.70.acc_ref, bf16[896,512]{1,0:T(8,128)(2,1)S(1)} %get-tuple-element.44.mine_on, bf16[1280,512]{1,0:T(8,128)(2,1)S(1)} %get-tuple-element.51.mine_ref, ...), custom_call_target="tpu_custom_call" | custom-call | flops 939524096 | bytes 8388608 | tf_op jit(solution)/shard_map/pallas_call | solution.py:64
  58.6 1.3 %collective-permute-start.13 = (f16[1040,128]{1,0:T(8,128)(2,1)S(1)}, f16[1040,128]{1,0:T(8,128)(2,1)S(1)}, u32[]{:S(2)}, u32[]{:S(2)}) collective-permute-start(f16[1040,128]{1,0:T(8,128)(2,1)S(1)} %convert_element_type.42), channel_id=1, source_target_pairs={{0,8},{1,9},{2,10},{3,11},{4,12},{5,13},{6,14},{7,15},{8,0},{9,1},... | collective-permute-start | bytes 798728 | tf_op jit(solution)/shard_map/ppermute | solution.py:52
  60.0 2.3 %collective-permute-start.14 = (f16[1040,128]{1,0:T(8,128)(2,1)S(1)}, f16[1040,128]{1,0:T(8,128)(2,1)S(1)}, u32[]{:S(2)}, u32[]{:S(2)}) collective-permute-start(f16[1040,128]{1,0:T(8,128)(2,1)S(1)} %convert_element_type.43), channel_id=1, source_target_pairs={{0,4},{1,5},{2,6},{3,7},{4,8},{5,9},{6,10},{7,11},{8,12},{9,13},{1... | collective-permute-start | bytes 798728 | tf_op jit(solution)/shard_map/ppermute | solution.py:52
  62.3 0.0 slice-start.3
  62.3 0.1 collective-permute-start.15
  62.4 3.5 %shard_map.74 = (f32[1024,128]{1,0:T(8,128)S(1)}, f32[1040,128]{1,0:T(8,128)S(1)}, f32[1040,128]{1,0:T(8,128)S(1)}, f32[1040,128]{1,0:T(8,128)S(1)}) custom-call(f32[1024,1024]{1,0:T(8,128)S(1)} %shard_map.70.acc_ref, bf16[896,512]{1,0:T(8,128)(2,1)S(1)} %get-tuple-element.44.mine_on, bf16[1280,512]{1,0:T(8,128)(2,1)S(1)} %get-tuple-element.51.mine_ref, ...), custom_call_target="tpu_custom_call" | custom-call | flops 939524096 | bytes 8388608 | tf_op jit(solution)/shard_map/pallas_call | solution.py:64
  65.9 2.3 %collective-permute-start.16 = (f16[1040,128]{1,0:T(8,128)(2,1)S(1)}, f16[1040,128]{1,0:T(8,128)(2,1)S(1)}, u32[]{:S(2)}, u32[]{:S(2)}) collective-permute-start(f16[1040,128]{1,0:T(8,128)(2,1)S(1)} %convert_element_type.45), channel_id=1, source_target_pairs={{0,8},{1,9},{2,10},{3,11},{4,12},{5,13},{6,14},{7,15},{8,0},{9,1},... | collective-permute-start | bytes 798728 | tf_op jit(solution)/shard_map/ppermute | solution.py:52
  68.3 1.8 %collective-permute-start.17 = (f16[1040,128]{1,0:T(8,128)(2,1)S(1)}, f16[1040,128]{1,0:T(8,128)(2,1)S(1)}, u32[]{:S(2)}, u32[]{:S(2)}) collective-permute-start(f16[1040,128]{1,0:T(8,128)(2,1)S(1)} %convert_element_type.47), channel_id=1, source_target_pairs={{0,4},{1,5},{2,6},{3,7},{4,8},{5,9},{6,10},{7,11},{8,12},{9,13},{1... | collective-permute-start | bytes 798728 | tf_op jit(solution)/shard_map/ppermute | solution.py:52
  70.1 0.4 collective-permute-start.18
  70.7 0.3 shard_map.75
  71.0 0.0 copy-start.5
  71.0 6.4 %collective-permute-start.19 = (f16[1040,128]{1,0:T(8,128)(2,1)S(1)}, f16[1040,128]{1,0:T(8,128)(2,1)S(1)}, u32[]{:S(2)}, u32[]{:S(2)}) collective-permute-start(f16[1040,128]{1,0:T(8,128)(2,1)S(1)} %convert_element_type.54), channel_id=1, source_target_pairs={{0,16},{16,0},{1,17},{17,1},{2,18},{18,2},{3,19},{19,3},{4,20},{20... | collective-permute-start | bytes 798728 | tf_op jit(solution)/shard_map/ppermute | solution.py:273
  77.5 0.3 collective-permute-done.18
  77.9 3.7 %shard_map.73 = f32[128,1024]{1,0:T(8,128)} custom-call(bf16[4,128,1024]{2,1,0:T(8,128)(2,1)S(1)} %pad_maximum_fusion.rel_ref, f32[128,1024]{1,0:T(8,128)S(1)} %copy-done.5, bf16[1024,4096]{1,0:T(8,128)(2,1)S(1)} %bitcast.14), custom_call_target="tpu_custom_call" | custom-call | flops 1073741824 | bytes 2097152 | tf_op jit(solution)/shard_map/pallas_call | solution.py:64
  81.6 7.5 %collective-permute-done.19 = f16[1040,128]{1,0:T(8,128)(2,1)S(1)} collective-permute-done((f16[1040,128]{1,0:T(8,128)(2,1)S(1)}, f16[1040,128]{1,0:T(8,128)(2,1)S(1)}, u32[]{:S(2)}, u32[]{:S(2)}) %collective-permute-start.19) | collective-permute-done | bytes 266272 | tf_op jit(solution)/shard_map/ppermute | solution.py:273
  89.2 1.0 %shard_map.76 = f32[1024,128]{1,0:T(8,128)} custom-call(f32[1024,128]{1,0:T(8,128)S(1)} %get-tuple-element.70.keep_ref, f32[1040,128]{1,0:T(8,128)S(1)} %convert_element_type.46.one_ref, f32[1040,128]{1,0:T(8,128)S(1)} %convert_element_type.48.two_ref, f32[1040,128]{1,0:T(8,128)S(1)} %convert_element_type.50.three_ref, ...), custom_call_target="tpu_custom_call" | custom-call | bytes 4194304 | tf_op jit(solution)/shard_map/pallas_call | solution.py:64
  (39 shorter events, 0.6 us)
Async XLA Ops:
  0.6 7.5 %slice-start = ((s8[8388608]{0:T(1024)(128)(4,1)}), s8[4194304]{0:T(1024)(128)(4,1)S(1)}, s32[]{:S(2)}) async-start(s8[8388608]{0:T(1024)(128)(4,1)} %bitcast.9), calls=%async_computation | async-start | bytes 8388608
  0.6 7.5 %slice-start.1 = ((s8[8388608]{0:T(1024)(128)(4,1)}), s8[4194304]{0:T(1024)(128)(4,1)S(1)}, s32[]{:S(2)}) async-start(s8[8388608]{0:T(1024)(128)(4,1)} %bitcast.9), calls=%async_computation.1 | async-start | bytes 8388608
  0.7 7.5 %copy-start = (bf16[128,4096]{1,0:T(8,128)(2,1)S(1)}, bf16[128,4096]{1,0:T(8,128)(2,1)}, u32[]{:S(2)}) copy-start(bf16[128,4096]{1,0:T(8,128)(2,1)} %head_ref.1) | copy-start | bytes 3145732
  4.8 6.9 %copy-start.2 = (bf16[768,512]{1,0:T(8,128)(2,1)}, bf16[768,512]{1,0:T(8,128)(2,1)S(1)}, u32[]{:S(2)}) copy-start(bf16[768,512]{1,0:T(8,128)(2,1)S(1)} %get-tuple-element.49.own_ref) | copy-start | bytes 2359300
  4.8 25.1 %collective-permute-start.2 = (bf16[896,512]{1,0:T(8,128)(2,1)S(1)}, bf16[896,512]{1,0:T(8,128)(2,1)}, u32[]{:S(2)}, u32[]{:S(2)}) collective-permute-start(bf16[896,512]{1,0:T(8,128)(2,1)S(1)} %get-tuple-element.44.mine_on), channel_id=1, source_target_pairs={{0,1},{1,2},{2,3},{3,0},{4,5},{5,6},{6,7},{7,4},{8,9},{9,10},{10,1... | collective-permute-start | bytes 2752520 | tf_op jit(solution)/shard_map/ppermute | solution.py:52
  6.4 23.5 %collective-permute-start.3 = (bf16[896,512]{1,0:T(8,128)(2,1)}, bf16[896,512]{1,0:T(8,128)(2,1)}, u32[]{:S(2)}, u32[]{:S(2)}) collective-permute-start(bf16[896,512]{1,0:T(8,128)(2,1)} %get-tuple-element.45), channel_id=1, source_target_pairs={{0,3},{1,0},{2,1},{3,2},{4,7},{5,4},{6,5},{7,6},{8,11},{9,8},{10,9... | collective-permute-start | bytes 2752520 | tf_op jit(solution)/shard_map/ppermute | solution.py:52
  11.7 0.8 copy-start.4
  12.5 3.8 %collective-permute-start = (bf16[128,1024]{1,0:T(8,128)(2,1)}, bf16[128,1024]{1,0:T(8,128)(2,1)}, u32[]{:S(2)}, u32[]{:S(2)}) collective-permute-start(bf16[128,1024]{1,0:T(8,128)(2,1)} %get-tuple-element.42), channel_id=1, source_target_pairs={{128,0},{129,1},{130,2},{131,3},{132,4},{133,5},{134,6},{135,7},{1... | collective-permute-start | bytes 786440 | tf_op jit(solution)/shard_map/ppermute | solution.py:230
  16.3 28.6 %collective-permute-start.6 = (bf16[1280,512]{1,0:T(8,128)(2,1)S(1)}, bf16[1280,512]{1,0:T(8,128)(2,1)S(1)}, u32[]{:S(2)}, u32[]{:S(2)}) collective-permute-start(bf16[1280,512]{1,0:T(8,128)(2,1)S(1)} %get-tuple-element.51.mine_ref), channel_id=1, source_target_pairs={{0,1},{1,2},{2,3},{3,0},{4,5},{5,6},{6,7},{7,4},{8,9},{9,10},{10,1... | collective-permute-start | bytes 3932168 | tf_op jit(solution)/shard_map/ppermute | solution.py:52
  16.6 28.9 %collective-permute-start.7 = (bf16[1280,512]{1,0:T(8,128)(2,1)}, bf16[1280,512]{1,0:T(8,128)(2,1)}, u32[]{:S(2)}, u32[]{:S(2)}) collective-permute-start(bf16[1280,512]{1,0:T(8,128)(2,1)} %get-tuple-element.53), channel_id=1, source_target_pairs={{0,3},{1,0},{2,1},{3,2},{4,7},{5,4},{6,5},{7,6},{8,11},{9,8},{10,9... | collective-permute-start | bytes 3932168 | tf_op jit(solution)/shard_map/ppermute | solution.py:52
  19.5 24.3 %copy-start.1 = (bf16[128,4096]{1,0:T(8,128)(2,1)S(1)}, bf16[128,4096]{1,0:T(8,128)(2,1)}, u32[]{:S(2)}) copy-start(bf16[128,4096]{1,0:T(8,128)(2,1)} %head_ref.1) | copy-start | bytes 3145732
  20.6 9.3 %collective-permute-start.1 = (bf16[128,1024]{1,0:T(8,128)(2,1)S(1)}, bf16[128,1024]{1,0:T(8,128)(2,1)S(1)}, u32[]{:S(2)}, u32[]{:S(2)}) collective-permute-start(bf16[128,1024]{1,0:T(8,128)(2,1)S(1)} %broadcast_select_fusion), channel_id=1, source_target_pairs={{0,96},{32,0},{64,32},{96,64},{128,160},{160,192},{192,224},{224,1... | collective-permute-start | bytes 786440 | tf_op jit(solution)/shard_map/ppermute | solution.py:209
  29.9 9.5 %collective-permute-start.4 = (bf16[128,1024]{1,0:T(8,128)(2,1)S(1)}, bf16[128,1024]{1,0:T(8,128)(2,1)S(1)}, u32[]{:S(2)}, u32[]{:S(2)}) collective-permute-start(bf16[128,1024]{1,0:T(8,128)(2,1)S(1)} %collective-permute-done.1), channel_id=1, source_target_pairs={{128,32},{160,64},{192,96},{224,0},{129,33},{161,65},{193,97},{225... | collective-permute-start | bytes 786440 | tf_op jit(solution)/shard_map/ppermute | solution.py:209
  31.1 24.1 %collective-permute-start.8 = (bf16[896,512]{1,0:T(8,128)(2,1)}, bf16[896,512]{1,0:T(8,128)(2,1)S(1)}, u32[]{:S(2)}, u32[]{:S(2)}) collective-permute-start(bf16[896,512]{1,0:T(8,128)(2,1)} %collective-permute-done.2.left_on), channel_id=1, source_target_pairs={{0,1},{1,2},{2,3},{3,0},{4,5},{5,6},{6,7},{7,4},{8,9},{9,10},{10,1... | collective-permute-start | bytes 2752520 | tf_op jit(solution)/shard_map/ppermute | solution.py:52
  31.2 24.0 %collective-permute-start.9 = (bf16[896,512]{1,0:T(8,128)(2,1)}, bf16[896,512]{1,0:T(8,128)(2,1)S(1)}, u32[]{:S(2)}, u32[]{:S(2)}) collective-permute-start(bf16[896,512]{1,0:T(8,128)(2,1)} %collective-permute-done.3.right_on), channel_id=1, source_target_pairs={{0,3},{1,0},{2,1},{3,2},{4,7},{5,4},{6,5},{7,6},{8,11},{9,8},{10,9... | collective-permute-start | bytes 2752520 | tf_op jit(solution)/shard_map/ppermute | solution.py:52
  39.3 3.4 %collective-permute-start.5 = (bf16[128,1024]{1,0:T(8,128)(2,1)S(1)}, bf16[128,1024]{1,0:T(8,128)(2,1)S(1)}, u32[]{:S(2)}, u32[]{:S(2)}) collective-permute-start(bf16[128,1024]{1,0:T(8,128)(2,1)S(1)} %collective-permute-done.1), channel_id=1, source_target_pairs={{128,0},{160,32},{192,64},{224,96},{129,1},{161,33},{193,65},{225,... | collective-permute-start | bytes 786440 | tf_op jit(solution)/shard_map/ppermute | solution.py:209
  43.8 4.2 %copy-start.3 = (bf16[768,512]{1,0:T(8,128)(2,1)S(1)}, bf16[768,512]{1,0:T(8,128)(2,1)}, u32[]{:S(2)}) copy-start(bf16[768,512]{1,0:T(8,128)(2,1)} %copy-done.2) | copy-start | bytes 2359300
  44.5 8.3 %collective-permute-start.10 = (bf16[256,512]{1,0:T(8,128)(2,1)S(1)}, bf16[256,512]{1,0:T(8,128)(2,1)S(1)}, u32[]{:S(2)}, u32[]{:S(2)}) collective-permute-start(bf16[256,512]{1,0:T(8,128)(2,1)S(1)} %get-tuple-element.54), channel_id=1, source_target_pairs={{0,2},{1,3},{2,0},{3,1},{4,6},{5,7},{6,4},{7,5},{8,10},{9,11},{10,... | collective-permute-start | bytes 786440 | tf_op jit(solution)/shard_map/ppermute | solution.py:52
  44.8 10.4 %collective-permute-start.11 = (bf16[256,512]{1,0:T(8,128)(2,1)S(1)}, bf16[256,512]{1,0:T(8,128)(2,1)S(1)}, u32[]{:S(2)}, u32[]{:S(2)}) collective-permute-start(bf16[256,512]{1,0:T(8,128)(2,1)S(1)} %get-tuple-element.55), channel_id=1, source_target_pairs={{0,1},{1,2},{2,3},{3,0},{4,5},{5,6},{6,7},{7,4},{8,9},{9,10},{10,1... | collective-permute-start | bytes 786440 | tf_op jit(solution)/shard_map/ppermute | solution.py:52
  45.4 9.8 %collective-permute-start.12 = (bf16[256,512]{1,0:T(8,128)(2,1)S(1)}, bf16[256,512]{1,0:T(8,128)(2,1)S(1)}, u32[]{:S(2)}, u32[]{:S(2)}) collective-permute-start(bf16[256,512]{1,0:T(8,128)(2,1)S(1)} %get-tuple-element.56), channel_id=1, source_target_pairs={{0,3},{1,0},{2,1},{3,2},{4,7},{5,4},{6,5},{7,6},{8,11},{9,8},{10,9... | collective-permute-start | bytes 786440 | tf_op jit(solution)/shard_map/ppermute | solution.py:52
  58.6 11.5 %collective-permute-start.13 = (f16[1040,128]{1,0:T(8,128)(2,1)S(1)}, f16[1040,128]{1,0:T(8,128)(2,1)S(1)}, u32[]{:S(2)}, u32[]{:S(2)}) collective-permute-start(f16[1040,128]{1,0:T(8,128)(2,1)S(1)} %convert_element_type.42), channel_id=1, source_target_pairs={{0,8},{1,9},{2,10},{3,11},{4,12},{5,13},{6,14},{7,15},{8,0},{9,1},... | collective-permute-start | bytes 798728 | tf_op jit(solution)/shard_map/ppermute | solution.py:52
  60.0 17.9 %slice-start.2 = ((s8[8388608]{0:T(1024)(128)(4,1)}), s8[4194304]{0:T(1024)(128)(4,1)S(1)}, s32[]{:S(2)}) async-start(s8[8388608]{0:T(1024)(128)(4,1)} %bitcast.12), calls=%async_computation.2 | async-start | bytes 8388608
  60.0 10.5 %collective-permute-start.14 = (f16[1040,128]{1,0:T(8,128)(2,1)S(1)}, f16[1040,128]{1,0:T(8,128)(2,1)S(1)}, u32[]{:S(2)}, u32[]{:S(2)}) collective-permute-start(f16[1040,128]{1,0:T(8,128)(2,1)S(1)} %convert_element_type.43), channel_id=1, source_target_pairs={{0,4},{1,5},{2,6},{3,7},{4,8},{5,9},{6,10},{7,11},{8,12},{9,13},{1... | collective-permute-start | bytes 798728 | tf_op jit(solution)/shard_map/ppermute | solution.py:52
  62.3 15.6 %slice-start.3 = ((s8[8388608]{0:T(1024)(128)(4,1)}), s8[4194304]{0:T(1024)(128)(4,1)S(1)}, s32[]{:S(2)}) async-start(s8[8388608]{0:T(1024)(128)(4,1)} %bitcast.12), calls=%async_computation.3 | async-start | bytes 8388608
  62.3 8.2 %collective-permute-start.15 = (f16[1040,128]{1,0:T(8,128)(2,1)S(1)}, f16[1040,128]{1,0:T(8,128)(2,1)S(1)}, u32[]{:S(2)}, u32[]{:S(2)}) collective-permute-start(f16[1040,128]{1,0:T(8,128)(2,1)S(1)} %convert_element_type.44), channel_id=1, source_target_pairs={{0,12},{1,13},{2,14},{3,15},{4,0},{5,1},{6,2},{7,3},{8,4},{9,5},{1... | collective-permute-start | bytes 798728 | tf_op jit(solution)/shard_map/ppermute | solution.py:52
  65.9 11.5 %collective-permute-start.16 = (f16[1040,128]{1,0:T(8,128)(2,1)S(1)}, f16[1040,128]{1,0:T(8,128)(2,1)S(1)}, u32[]{:S(2)}, u32[]{:S(2)}) collective-permute-start(f16[1040,128]{1,0:T(8,128)(2,1)S(1)} %convert_element_type.45), channel_id=1, source_target_pairs={{0,8},{1,9},{2,10},{3,11},{4,12},{5,13},{6,14},{7,15},{8,0},{9,1},... | collective-permute-start | bytes 798728 | tf_op jit(solution)/shard_map/ppermute | solution.py:52
  68.3 9.1 %collective-permute-start.17 = (f16[1040,128]{1,0:T(8,128)(2,1)S(1)}, f16[1040,128]{1,0:T(8,128)(2,1)S(1)}, u32[]{:S(2)}, u32[]{:S(2)}) collective-permute-start(f16[1040,128]{1,0:T(8,128)(2,1)S(1)} %convert_element_type.47), channel_id=1, source_target_pairs={{0,4},{1,5},{2,6},{3,7},{4,8},{5,9},{6,10},{7,11},{8,12},{9,13},{1... | collective-permute-start | bytes 798728 | tf_op jit(solution)/shard_map/ppermute | solution.py:52
  70.1 7.7 %collective-permute-start.18 = (f16[1040,128]{1,0:T(8,128)(2,1)S(1)}, f16[1040,128]{1,0:T(8,128)(2,1)S(1)}, u32[]{:S(2)}, u32[]{:S(2)}) collective-permute-start(f16[1040,128]{1,0:T(8,128)(2,1)S(1)} %convert_element_type.49), channel_id=1, source_target_pairs={{0,12},{1,13},{2,14},{3,15},{4,0},{5,1},{6,2},{7,3},{8,4},{9,5},{1... | collective-permute-start | bytes 798728 | tf_op jit(solution)/shard_map/ppermute | solution.py:52
  71.0 6.9 %copy-start.5 = (f32[128,1024]{1,0:T(8,128)S(1)}, f32[128,1024]{1,0:T(8,128)}, u32[]{:S(2)}) copy-start(f32[128,1024]{1,0:T(8,128)} %copy-done.4) | copy-start | bytes 1572868
  71.0 18.1 %collective-permute-start.19 = (f16[1040,128]{1,0:T(8,128)(2,1)S(1)}, f16[1040,128]{1,0:T(8,128)(2,1)S(1)}, u32[]{:S(2)}, u32[]{:S(2)}) collective-permute-start(f16[1040,128]{1,0:T(8,128)(2,1)S(1)} %convert_element_type.54), channel_id=1, source_target_pairs={{0,16},{16,0},{1,17},{17,1},{2,18},{18,2},{3,19},{19,3},{4,20},{20... | collective-permute-start | bytes 798728 | tf_op jit(solution)/shard_map/ppermute | solution.py:273

commit v12 on v11

--- a/solution.py
+++ b/solution.py
@@ -114,7 +114,7 @@
     for i in range(0, weight_ref.shape[0], step):
         out = lax.dot_general(grad_ref[...], weight_ref[i:i + step, :], CONTRACT_LAST, preferred_element_type=F32)
         out_ref[:, i:i + step] = out
-        small_ref[:, i:i + step] = out.astype(BF16)
+        small_ref[:, i:i + step] = jnp.where(on_last(), out, 0.0).astype(BF16)
 
 
 def second_kernel(rel_ref, first_ref, weight_ref, out_ref):
@@ -231,7 +231,7 @@
     staying_right, staying_left, shard = lax.optimization_barrier((right, left, shard))
     from_left, from_right = shifted(staying_right, True, 1), shifted(staying_left, True, -1)
     places = range(RING)
-    both = jnp.where(on_last(), small, shard)
+    both = small + shard
     passed = on_line(both, [((0, i), (0, i - 1)) for i in places] + [((1, i), (1, i + 1)) for i in places])
     passed, from_left_on, from_right_on = lax.optimization_barrier((passed, from_left_on, from_right_on))
     upper = shifted(from_left_on, True, 1)

time: 90.6 us -> 81.5 us (0.90)
  Pallas kernels: 24.8 us -> 17 us
  other arithmetic: 2.68 us -> 0.72 us
  waiting for transfers between devices: 24.3 us -> 25.9 us
    pallas_call x9, Pallas kernels: 24.8 us -> 17 us  [call(): pl.pallas_call(kernel, out_shape=[jax.ShapeDtypeStruct(s, t) for s, t in...]
    ppermute x15, waiting for transfers between devices: 2.76 us -> 8.75 us  [shifted(): return lax.ppermute(value, ('section', 'y', 'x'), pairs_over(along, by))]
    ppermute x1, waiting for transfers between devices: 7.51 us -> 3.46 us  [local(): other = lax.ppermute(far.astype(F16), 'z_hi', [(0, 1), (1, 0)]).astype(F32)]
    select_n x1 -> x0, other arithmetic: 1.07 us -> none  [local(): both = jnp.where(on_last(), small, shard)]
    another operation x1, other arithmetic: 1.08 us -> 0.13 us  [local(): rel = jnp.stack(rel, 0)]
  transfers between devices with their start and end apart: 20 -> 20, of which waited for: 7 -> 9; matrix products, arithmetic and copies ran while one was open for 3% -> 1% of each run, Pallas kernels for 18% -> 15%
where the time goes in v12:
time: 81.5 us; the launch traced here: 81.1 us
  starting transfers between devices  36.6 us (45%)
  waiting for transfers between devices  25.9 us (32%)
  Pallas kernels  17 us (21%)
  between operations  0.88 us (1%)
    ppermute x15, starting transfers between devices, shifted(): return lax.ppermute(value, ('section', 'y', 'x'), pairs_over(along, by))  21.5 us
    pallas_call x9, Pallas kernels, call(): pl.pallas_call(kernel, out_shape=[jax.ShapeDtypeStruct(s, t) for s, t in...  17 us
    ppermute x3, waiting for transfers between devices, on_line(): return lax.ppermute(value, ('section', 'z_lo'), pairs)  11.6 us
    ppermute x15, waiting for transfers between devices, shifted(): return lax.ppermute(value, ('section', 'y', 'x'), pairs_over(along, by))  8.75 us
    ppermute x3, starting transfers between devices, on_line(): return lax.ppermute(value, ('section', 'z_lo'), pairs)  7.26 us
    ppermute x1, starting transfers between devices, local(): other = lax.ppermute(far.astype(F16), 'z_hi', [(0, 1), (1, 0)]).astype(F32)  6.47 us
    ppermute x1, waiting for transfers between devices, local(): other = lax.ppermute(far.astype(F16), 'z_hi', [(0, 1), (1, 0)]).astype(F32)  3.46 us
    ppermute x1, waiting for transfers between devices, local(): shard = lax.ppermute(small, 'section', [(1, 0)])  2.13 us
  transfers between devices with their start and end apart: 20, of which 9 were waited for; matrix products, arithmetic and copies ran while one was open for 1% of the time, Pallas kernels for 15%

profile of v12, /device:TPU:24, one launch (start us, length us, event | category | flops | bytes accessed | tf_op | source)
XLA Modules:
  0.0 81.1 jit_solution(14260317630925880831)
XLA Ops:
  0.6 0.0 slice-start
  0.6 0.0 slice-start.1
  0.7 2.7 %shard_map.68 = (bf16[896,512]{1,0:T(8,128)(2,1)S(1)}, bf16[896,512]{1,0:T(8,128)(2,1)S(1)}, bf16[1280,512]{1,0:T(8,128)(2,1)S(1)}, bf16[1280,512]{1,0:T(8,128)(2,1)S(1)}, bf16[768,512]{1,0:T(8,128)(2,1)S(1)}) custom-call(s32[2]{0:T(128)} %pending_ref.1, bf16[4,128,1024]{2,1,0:T(8,128)(2,1)} %bitcast.20, bf16[3,128,4096]{2,1,0:T(8,128)(2,1)} %bitcast.19), custom_call_target="tpu_custom_call" | custom-call | flops 10000000000 | bytes 12582912 | tf_op jit(solution)/shard_map/pallas_call | solution.py:64
  3.4 1.6 %collective-permute-start.2 = (bf16[896,512]{1,0:T(8,128)(2,1)S(1)}, bf16[896,512]{1,0:T(8,128)(2,1)S(1)}, u32[]{:S(2)}, u32[]{:S(2)}) collective-permute-start(bf16[896,512]{1,0:T(8,128)(2,1)S(1)} %get-tuple-element.44.mine_on), channel_id=1, source_target_pairs={{0,1},{1,2},{2,3},{3,0},{4,5},{5,6},{6,7},{7,4},{8,9},{9,10},{10,1... | collective-permute-start | bytes 2752520 | tf_op jit(solution)/shard_map/ppermute | solution.py:52
  5.0 1.7 %collective-permute-start.3 = (bf16[896,512]{1,0:T(8,128)(2,1)S(1)}, bf16[896,512]{1,0:T(8,128)(2,1)S(1)}, u32[]{:S(2)}, u32[]{:S(2)}) collective-permute-start(bf16[896,512]{1,0:T(8,128)(2,1)S(1)} %get-tuple-element.45), channel_id=1, source_target_pairs={{0,3},{1,0},{2,1},{3,2},{4,7},{5,4},{6,5},{7,6},{8,11},{9,8},{10,9... | collective-permute-start | bytes 2752520 | tf_op jit(solution)/shard_map/ppermute | solution.py:52
  6.7 2.9 %shard_map.69 = (f32[128,1024]{1,0:T(8,128)S(1)}, bf16[128,1024]{1,0:T(8,128)(2,1)S(1)}) custom-call(bf16[128,4096]{1,0:T(8,128)(2,1)S(1)} %copy-done, bf16[1024,4096]{1,0:T(8,128)(2,1)S(1)} %bitcast.11), custom_call_target="tpu_custom_call" | custom-call | flops 1073741824 | bytes 2097152 | tf_op jit(solution)/shard_map/pallas_call | solution.py:64
  9.6 1.3 %collective-permute-start = (bf16[128,1024]{1,0:T(8,128)(2,1)S(1)}, bf16[128,1024]{1,0:T(8,128)(2,1)S(1)}, u32[]{:S(2)}, u32[]{:S(2)}) collective-permute-start(bf16[128,1024]{1,0:T(8,128)(2,1)S(1)} %get-tuple-element.42), channel_id=1, source_target_pairs={{128,0},{129,1},{130,2},{131,3},{132,4},{133,5},{134,6},{135,7},{1... | collective-permute-start | bytes 786440 | tf_op jit(solution)/shard_map/ppermute | solution.py:230
  10.9 2.1 %collective-permute-done = bf16[128,1024]{1,0:T(8,128)(2,1)S(1)} collective-permute-done((bf16[128,1024]{1,0:T(8,128)(2,1)S(1)}, bf16[128,1024]{1,0:T(8,128)(2,1)S(1)}, u32[]{:S(2)}, u32[]{:S(2)}) %collective-permute-start) | collective-permute-done | bytes 262176 | tf_op jit(solution)/shard_map/ppermute | solution.py:230
  13.0 0.3 collective-permute-start.6
  13.4 2.9 %collective-permute-start.7 = (bf16[1280,512]{1,0:T(8,128)(2,1)S(1)}, bf16[1280,512]{1,0:T(8,128)(2,1)S(1)}, u32[]{:S(2)}, u32[]{:S(2)}) collective-permute-start(bf16[1280,512]{1,0:T(8,128)(2,1)S(1)} %get-tuple-element.53), channel_id=1, source_target_pairs={{0,3},{1,0},{2,1},{3,2},{4,7},{5,4},{6,5},{7,6},{8,11},{9,8},{10,9... | collective-permute-start | bytes 3932168 | tf_op jit(solution)/shard_map/ppermute | solution.py:52
  16.3 0.1 add.3
  16.4 4.7 %collective-permute-start.1 = (bf16[128,1024]{1,0:T(8,128)(2,1)S(1)}, bf16[128,1024]{1,0:T(8,128)(2,1)S(1)}, u32[]{:S(2)}, u32[]{:S(2)}) collective-permute-start(bf16[128,1024]{1,0:T(8,128)(2,1)S(1)} %add.3), channel_id=1, source_target_pairs={{0,96},{32,0},{64,32},{96,64},{128,160},{160,192},{192,224},{224,1... | collective-permute-start | bytes 786440 | tf_op jit(solution)/shard_map/ppermute | solution.py:209
  21.1 4.6 %collective-permute-done.1 = bf16[128,1024]{1,0:T(8,128)(2,1)S(1)} collective-permute-done((bf16[128,1024]{1,0:T(8,128)(2,1)S(1)}, bf16[128,1024]{1,0:T(8,128)(2,1)S(1)}, u32[]{:S(2)}, u32[]{:S(2)}) %collective-permute-start.1) | collective-permute-done | bytes 262176 | tf_op jit(solution)/shard_map/ppermute | solution.py:209
  25.6 0.0 collective-permute-done.2.left_on
  25.6 1.3 %collective-permute-start.4 = (bf16[128,1024]{1,0:T(8,128)(2,1)S(1)}, bf16[128,1024]{1,0:T(8,128)(2,1)S(1)}, u32[]{:S(2)}, u32[]{:S(2)}) collective-permute-start(bf16[128,1024]{1,0:T(8,128)(2,1)S(1)} %collective-permute-done.1), channel_id=1, source_target_pairs={{128,32},{160,64},{192,96},{224,0},{129,33},{161,65},{193,97},{225... | collective-permute-start | bytes 786440 | tf_op jit(solution)/shard_map/ppermute | solution.py:209
  26.9 0.1 collective-permute-start.8
  27.0 3.2 %collective-permute-start.9 = (bf16[896,512]{1,0:T(8,128)(2,1)S(1)}, bf16[896,512]{1,0:T(8,128)(2,1)S(1)}, u32[]{:S(2)}, u32[]{:S(2)}) collective-permute-start(bf16[896,512]{1,0:T(8,128)(2,1)S(1)} %collective-permute-done.3.right_on), channel_id=1, source_target_pairs={{0,3},{1,0},{2,1},{3,2},{4,7},{5,4},{6,5},{7,6},{8,11},{9,8},{10,9... | collective-permute-start | bytes 2752520 | tf_op jit(solution)/shard_map/ppermute | solution.py:52
  30.2 4.9 %collective-permute-done.4 = bf16[128,1024]{1,0:T(8,128)(2,1)S(1)} collective-permute-done((bf16[128,1024]{1,0:T(8,128)(2,1)S(1)}, bf16[128,1024]{1,0:T(8,128)(2,1)S(1)}, u32[]{:S(2)}, u32[]{:S(2)}) %collective-permute-start.4) | collective-permute-done | bytes 262176 | tf_op jit(solution)/shard_map/ppermute | solution.py:209
  35.1 1.3 %collective-permute-start.5 = (bf16[128,1024]{1,0:T(8,128)(2,1)S(1)}, bf16[128,1024]{1,0:T(8,128)(2,1)S(1)}, u32[]{:S(2)}, u32[]{:S(2)}) collective-permute-start(bf16[128,1024]{1,0:T(8,128)(2,1)S(1)} %collective-permute-done.1), channel_id=1, source_target_pairs={{128,0},{160,32},{192,64},{224,96},{129,1},{161,33},{193,65},{225,... | collective-permute-start | bytes 786440 | tf_op jit(solution)/shard_map/ppermute | solution.py:209
  36.4 2.1 %collective-permute-done.5 = bf16[128,1024]{1,0:T(8,128)(2,1)S(1)} collective-permute-done((bf16[128,1024]{1,0:T(8,128)(2,1)S(1)}, bf16[128,1024]{1,0:T(8,128)(2,1)S(1)}, u32[]{:S(2)}, u32[]{:S(2)}) %collective-permute-start.5) | collective-permute-done | bytes 262176 | tf_op jit(solution)/shard_map/ppermute | solution.py:209
  38.5 0.1 pad_maximum_fusion.rel_ref
  38.6 0.6 shard_map.71
  39.3 0.4 collective-permute-start.10
  39.7 0.6 collective-permute-start.11
  40.3 2.6 %collective-permute-start.12 = (bf16[256,512]{1,0:T(8,128)(2,1)S(1)}, bf16[256,512]{1,0:T(8,128)(2,1)S(1)}, u32[]{:S(2)}, u32[]{:S(2)}) collective-permute-start(bf16[256,512]{1,0:T(8,128)(2,1)S(1)} %get-tuple-element.56), channel_id=1, source_target_pairs={{0,3},{1,0},{2,1},{3,2},{4,7},{5,4},{6,5},{7,6},{8,11},{9,8},{10,9... | collective-permute-start | bytes 786440 | tf_op jit(solution)/shard_map/ppermute | solution.py:52
  42.9 2.9 %shard_map.70.acc_ref = f32[1024,1024]{1,0:T(8,128)S(1)} custom-call(bf16[896,512]{1,0:T(8,128)(2,1)S(1)} %get-tuple-element.44.mine_on, bf16[1280,512]{1,0:T(8,128)(2,1)S(1)} %get-tuple-element.51.mine_ref, bf16[768,512]{1,0:T(8,128)(2,1)S(1)} %get-tuple-element.49.own_ref, bf16[896,512]{1,0:T(8,128)(2,1)S(1)} %collective-permute-done.2.left_on, ...), custom_call_target="tpu_custom_call" | custom-call | flops 2415919104 | bytes 12582912 | tf_op jit(solution)/shard_map/pallas_call | solution.py:64
  45.8 1.6 %collective-permute-done.10.two_last = bf16[256,512]{1,0:T(8,128)(2,1)S(1)} collective-permute-done((bf16[256,512]{1,0:T(8,128)(2,1)S(1)}, bf16[256,512]{1,0:T(8,128)(2,1)S(1)}, u32[]{:S(2)}, u32[]{:S(2)}) %collective-permute-start.10) | collective-permute-done | bytes 262176 | tf_op jit(solution)/shard_map/ppermute | solution.py:52
  47.4 2.7 %collective-permute-done.11.left_last = bf16[256,512]{1,0:T(8,128)(2,1)S(1)} collective-permute-done((bf16[256,512]{1,0:T(8,128)(2,1)S(1)}, bf16[256,512]{1,0:T(8,128)(2,1)S(1)}, u32[]{:S(2)}, u32[]{:S(2)}) %collective-permute-start.11) | collective-permute-done | bytes 262176 | tf_op jit(solution)/shard_map/ppermute | solution.py:52
  50.1 0.0 collective-permute-done.12.right_last
  50.1 0.0 collective-permute-done.8.upper_ref
  50.1 0.0 collective-permute-done.9.lower_ref
  50.1 1.5 %shard_map.72 = (f32[1024,128]{1,0:T(8,128)S(1)}, f32[1040,128]{1,0:T(8,128)S(1)}, f32[1040,128]{1,0:T(8,128)S(1)}, f32[1040,128]{1,0:T(8,128)S(1)}) custom-call(f32[1024,1024]{1,0:T(8,128)S(1)} %shard_map.70.acc_ref, bf16[896,512]{1,0:T(8,128)(2,1)S(1)} %get-tuple-element.44.mine_on, bf16[1280,512]{1,0:T(8,128)(2,1)S(1)} %get-tuple-element.51.mine_ref, ...), custom_call_target="tpu_custom_call" | custom-call | flops 939524096 | bytes 8388608 | tf_op jit(solution)/shard_map/pallas_call | solution.py:64
  51.6 1.3 %collective-permute-start.13 = (f16[1040,128]{1,0:T(8,128)(2,1)S(1)}, f16[1040,128]{1,0:T(8,128)(2,1)S(1)}, u32[]{:S(2)}, u32[]{:S(2)}) collective-permute-start(f16[1040,128]{1,0:T(8,128)(2,1)S(1)} %convert_element_type.42), channel_id=1, source_target_pairs={{0,8},{1,9},{2,10},{3,11},{4,12},{5,13},{6,14},{7,15},{8,0},{9,1},... | collective-permute-start | bytes 798728 | tf_op jit(solution)/shard_map/ppermute | solution.py:52
  53.0 2.3 %collective-permute-start.14 = (f16[1040,128]{1,0:T(8,128)(2,1)S(1)}, f16[1040,128]{1,0:T(8,128)(2,1)S(1)}, u32[]{:S(2)}, u32[]{:S(2)}) collective-permute-start(f16[1040,128]{1,0:T(8,128)(2,1)S(1)} %convert_element_type.43), channel_id=1, source_target_pairs={{0,4},{1,5},{2,6},{3,7},{4,8},{5,9},{6,10},{7,11},{8,12},{9,13},{1... | collective-permute-start | bytes 798728 | tf_op jit(solution)/shard_map/ppermute | solution.py:52
  55.3 0.1 collective-permute-start.15
  55.3 1.5 %shard_map.74 = (f32[1024,128]{1,0:T(8,128)S(1)}, f32[1040,128]{1,0:T(8,128)S(1)}, f32[1040,128]{1,0:T(8,128)S(1)}, f32[1040,128]{1,0:T(8,128)S(1)}) custom-call(f32[1024,1024]{1,0:T(8,128)S(1)} %shard_map.70.acc_ref, bf16[896,512]{1,0:T(8,128)(2,1)S(1)} %get-tuple-element.44.mine_on, bf16[1280,512]{1,0:T(8,128)(2,1)S(1)} %get-tuple-element.51.mine_ref, ...), custom_call_target="tpu_custom_call" | custom-call | flops 939524096 | bytes 8388608 | tf_op jit(solution)/shard_map/pallas_call | solution.py:64
  56.9 2.2 %collective-permute-start.16 = (f16[1040,128]{1,0:T(8,128)(2,1)S(1)}, f16[1040,128]{1,0:T(8,128)(2,1)S(1)}, u32[]{:S(2)}, u32[]{:S(2)}) collective-permute-start(f16[1040,128]{1,0:T(8,128)(2,1)S(1)} %convert_element_type.45), channel_id=1, source_target_pairs={{0,8},{1,9},{2,10},{3,11},{4,12},{5,13},{6,14},{7,15},{8,0},{9,1},... | collective-permute-start | bytes 798728 | tf_op jit(solution)/shard_map/ppermute | solution.py:52
  59.1 1.8 %collective-permute-start.17 = (f16[1040,128]{1,0:T(8,128)(2,1)S(1)}, f16[1040,128]{1,0:T(8,128)(2,1)S(1)}, u32[]{:S(2)}, u32[]{:S(2)}) collective-permute-start(f16[1040,128]{1,0:T(8,128)(2,1)S(1)} %convert_element_type.47), channel_id=1, source_target_pairs={{0,4},{1,5},{2,6},{3,7},{4,8},{5,9},{6,10},{7,11},{8,12},{9,13},{1... | collective-permute-start | bytes 798728 | tf_op jit(solution)/shard_map/ppermute | solution.py:52
  61.0 0.3 collective-permute-start.18
  61.3 0.2 collective-permute-done.14
  61.5 4.3 %collective-permute-done.15 = f16[1040,128]{1,0:T(8,128)(2,1)S(1)} collective-permute-done((f16[1040,128]{1,0:T(8,128)(2,1)S(1)}, f16[1040,128]{1,0:T(8,128)(2,1)S(1)}, u32[]{:S(2)}, u32[]{:S(2)}) %collective-permute-start.15) | collective-permute-done | bytes 266272 | tf_op jit(solution)/shard_map/ppermute | solution.py:52
  65.9 0.3 shard_map.75
  66.3 6.5 %collective-permute-start.19 = (f16[1040,128]{1,0:T(8,128)(2,1)S(1)}, f16[1040,128]{1,0:T(8,128)(2,1)S(1)}, u32[]{:S(2)}, u32[]{:S(2)}) collective-permute-start(f16[1040,128]{1,0:T(8,128)(2,1)S(1)} %convert_element_type.54), channel_id=1, source_target_pairs={{0,16},{16,0},{1,17},{17,1},{2,18},{18,2},{3,19},{19,3},{4,20},{20... | collective-permute-start | bytes 798728 | tf_op jit(solution)/shard_map/ppermute | solution.py:273
  72.8 0.0 collective-permute-done.17
  72.8 0.0 collective-permute-done.18
  72.9 3.7 %shard_map.73 = f32[128,1024]{1,0:T(8,128)} custom-call(bf16[4,128,1024]{2,1,0:T(8,128)(2,1)S(1)} %pad_maximum_fusion.rel_ref, f32[128,1024]{1,0:T(8,128)S(1)} %get-tuple-element.69.first_ref, bf16[1024,4096]{1,0:T(8,128)(2,1)S(1)} %bitcast.12), custom_call_target="tpu_custom_call" | custom-call | flops 1073741824 | bytes 2097152 | tf_op jit(solution)/shard_map/pallas_call | solution.py:64
  76.6 3.5 %collective-permute-done.19 = f16[1040,128]{1,0:T(8,128)(2,1)S(1)} collective-permute-done((f16[1040,128]{1,0:T(8,128)(2,1)S(1)}, f16[1040,128]{1,0:T(8,128)(2,1)S(1)}, u32[]{:S(2)}, u32[]{:S(2)}) %collective-permute-start.19) | collective-permute-done | bytes 266272 | tf_op jit(solution)/shard_map/ppermute | solution.py:273
  80.1 1.0 %shard_map.76 = f32[1024,128]{1,0:T(8,128)} custom-call(f32[1024,128]{1,0:T(8,128)S(1)} %get-tuple-element.70.keep_ref, f32[1040,128]{1,0:T(8,128)S(1)} %convert_element_type.46.one_ref, f32[1040,128]{1,0:T(8,128)S(1)} %convert_element_type.48.two_ref, f32[1040,128]{1,0:T(8,128)S(1)} %convert_element_type.50.three_ref, ...), custom_call_target="tpu_custom_call" | custom-call | bytes 4194304 | tf_op jit(solution)/shard_map/pallas_call | solution.py:64
  (24 shorter events, 0.5 us)
Async XLA Ops:
  0.6 6.1 %slice-start = ((s8[8388608]{0:T(1024)(128)(4,1)}), s8[4194304]{0:T(1024)(128)(4,1)S(1)}, s32[]{:S(2)}) async-start(s8[8388608]{0:T(1024)(128)(4,1)} %bitcast.9), calls=%async_computation | async-start | bytes 8388608
  0.6 6.1 %slice-start.1 = ((s8[8388608]{0:T(1024)(128)(4,1)}), s8[4194304]{0:T(1024)(128)(4,1)S(1)}, s32[]{:S(2)}) async-start(s8[8388608]{0:T(1024)(128)(4,1)} %bitcast.9), calls=%async_computation.1 | async-start | bytes 8388608
  0.7 6.1 %copy-start = (bf16[128,4096]{1,0:T(8,128)(2,1)S(1)}, bf16[128,4096]{1,0:T(8,128)(2,1)}, u32[]{:S(2)}) copy-start(bf16[128,4096]{1,0:T(8,128)(2,1)} %head_ref.1) | copy-start | bytes 3145732
  3.4 22.2 %collective-permute-start.2 = (bf16[896,512]{1,0:T(8,128)(2,1)S(1)}, bf16[896,512]{1,0:T(8,128)(2,1)S(1)}, u32[]{:S(2)}, u32[]{:S(2)}) collective-permute-start(bf16[896,512]{1,0:T(8,128)(2,1)S(1)} %get-tuple-element.44.mine_on), channel_id=1, source_target_pairs={{0,1},{1,2},{2,3},{3,0},{4,5},{5,6},{6,7},{7,4},{8,9},{9,10},{10,1... | collective-permute-start | bytes 2752520 | tf_op jit(solution)/shard_map/ppermute | solution.py:52
  5.0 20.6 %collective-permute-start.3 = (bf16[896,512]{1,0:T(8,128)(2,1)S(1)}, bf16[896,512]{1,0:T(8,128)(2,1)S(1)}, u32[]{:S(2)}, u32[]{:S(2)}) collective-permute-start(bf16[896,512]{1,0:T(8,128)(2,1)S(1)} %get-tuple-element.45), channel_id=1, source_target_pairs={{0,3},{1,0},{2,1},{3,2},{4,7},{5,4},{6,5},{7,6},{8,11},{9,8},{10,9... | collective-permute-start | bytes 2752520 | tf_op jit(solution)/shard_map/ppermute | solution.py:52
  9.6 3.4 %collective-permute-start = (bf16[128,1024]{1,0:T(8,128)(2,1)S(1)}, bf16[128,1024]{1,0:T(8,128)(2,1)S(1)}, u32[]{:S(2)}, u32[]{:S(2)}) collective-permute-start(bf16[128,1024]{1,0:T(8,128)(2,1)S(1)} %get-tuple-element.42), channel_id=1, source_target_pairs={{128,0},{129,1},{130,2},{131,3},{132,4},{133,5},{134,6},{135,7},{1... | collective-permute-start | bytes 786440 | tf_op jit(solution)/shard_map/ppermute | solution.py:230
  13.0 26.7 %collective-permute-start.6 = (bf16[1280,512]{1,0:T(8,128)(2,1)S(1)}, bf16[1280,512]{1,0:T(8,128)(2,1)S(1)}, u32[]{:S(2)}, u32[]{:S(2)}) collective-permute-start(bf16[1280,512]{1,0:T(8,128)(2,1)S(1)} %get-tuple-element.51.mine_ref), channel_id=1, source_target_pairs={{0,1},{1,2},{2,3},{3,0},{4,5},{5,6},{6,7},{7,4},{8,9},{9,10},{10,1... | collective-permute-start | bytes 3932168 | tf_op jit(solution)/shard_map/ppermute | solution.py:52
  13.4 26.9 %collective-permute-start.7 = (bf16[1280,512]{1,0:T(8,128)(2,1)S(1)}, bf16[1280,512]{1,0:T(8,128)(2,1)S(1)}, u32[]{:S(2)}, u32[]{:S(2)}) collective-permute-start(bf16[1280,512]{1,0:T(8,128)(2,1)S(1)} %get-tuple-element.53), channel_id=1, source_target_pairs={{0,3},{1,0},{2,1},{3,2},{4,7},{5,4},{6,5},{7,6},{8,11},{9,8},{10,9... | collective-permute-start | bytes 3932168 | tf_op jit(solution)/shard_map/ppermute | solution.py:52
  16.4 9.3 %collective-permute-start.1 = (bf16[128,1024]{1,0:T(8,128)(2,1)S(1)}, bf16[128,1024]{1,0:T(8,128)(2,1)S(1)}, u32[]{:S(2)}, u32[]{:S(2)}) collective-permute-start(bf16[128,1024]{1,0:T(8,128)(2,1)S(1)} %add.3), channel_id=1, source_target_pairs={{0,96},{32,0},{64,32},{96,64},{128,160},{160,192},{192,224},{224,1... | collective-permute-start | bytes 786440 | tf_op jit(solution)/shard_map/ppermute | solution.py:209
  25.6 9.5 %collective-permute-start.4 = (bf16[128,1024]{1,0:T(8,128)(2,1)S(1)}, bf16[128,1024]{1,0:T(8,128)(2,1)S(1)}, u32[]{:S(2)}, u32[]{:S(2)}) collective-permute-start(bf16[128,1024]{1,0:T(8,128)(2,1)S(1)} %collective-permute-done.1), channel_id=1, source_target_pairs={{128,32},{160,64},{192,96},{224,0},{129,33},{161,65},{193,97},{225... | collective-permute-start | bytes 786440 | tf_op jit(solution)/shard_map/ppermute | solution.py:209
  26.9 23.2 %collective-permute-start.8 = (bf16[896,512]{1,0:T(8,128)(2,1)S(1)}, bf16[896,512]{1,0:T(8,128)(2,1)S(1)}, u32[]{:S(2)}, u32[]{:S(2)}) collective-permute-start(bf16[896,512]{1,0:T(8,128)(2,1)S(1)} %collective-permute-done.2.left_on), channel_id=1, source_target_pairs={{0,1},{1,2},{2,3},{3,0},{4,5},{5,6},{6,7},{7,4},{8,9},{9,10},{10,1... | collective-permute-start | bytes 2752520 | tf_op jit(solution)/shard_map/ppermute | solution.py:52
  27.0 23.1 %collective-permute-start.9 = (bf16[896,512]{1,0:T(8,128)(2,1)S(1)}, bf16[896,512]{1,0:T(8,128)(2,1)S(1)}, u32[]{:S(2)}, u32[]{:S(2)}) collective-permute-start(bf16[896,512]{1,0:T(8,128)(2,1)S(1)} %collective-permute-done.3.right_on), channel_id=1, source_target_pairs={{0,3},{1,0},{2,1},{3,2},{4,7},{5,4},{6,5},{7,6},{8,11},{9,8},{10,9... | collective-permute-start | bytes 2752520 | tf_op jit(solution)/shard_map/ppermute | solution.py:52
  35.1 3.4 %collective-permute-start.5 = (bf16[128,1024]{1,0:T(8,128)(2,1)S(1)}, bf16[128,1024]{1,0:T(8,128)(2,1)S(1)}, u32[]{:S(2)}, u32[]{:S(2)}) collective-permute-start(bf16[128,1024]{1,0:T(8,128)(2,1)S(1)} %collective-permute-done.1), channel_id=1, source_target_pairs={{128,0},{160,32},{192,64},{224,96},{129,1},{161,33},{193,65},{225,... | collective-permute-start | bytes 786440 | tf_op jit(solution)/shard_map/ppermute | solution.py:209
  39.3 8.1 %collective-permute-start.10 = (bf16[256,512]{1,0:T(8,128)(2,1)S(1)}, bf16[256,512]{1,0:T(8,128)(2,1)S(1)}, u32[]{:S(2)}, u32[]{:S(2)}) collective-permute-start(bf16[256,512]{1,0:T(8,128)(2,1)S(1)} %get-tuple-element.54), channel_id=1, source_target_pairs={{0,2},{1,3},{2,0},{3,1},{4,6},{5,7},{6,4},{7,5},{8,10},{9,11},{10,... | collective-permute-start | bytes 786440 | tf_op jit(solution)/shard_map/ppermute | solution.py:52
  39.7 10.4 %collective-permute-start.11 = (bf16[256,512]{1,0:T(8,128)(2,1)S(1)}, bf16[256,512]{1,0:T(8,128)(2,1)S(1)}, u32[]{:S(2)}, u32[]{:S(2)}) collective-permute-start(bf16[256,512]{1,0:T(8,128)(2,1)S(1)} %get-tuple-element.55), channel_id=1, source_target_pairs={{0,1},{1,2},{2,3},{3,0},{4,5},{5,6},{6,7},{7,4},{8,9},{9,10},{10,1... | collective-permute-start | bytes 786440 | tf_op jit(solution)/shard_map/ppermute | solution.py:52
  40.3 9.8 %collective-permute-start.12 = (bf16[256,512]{1,0:T(8,128)(2,1)S(1)}, bf16[256,512]{1,0:T(8,128)(2,1)S(1)}, u32[]{:S(2)}, u32[]{:S(2)}) collective-permute-start(bf16[256,512]{1,0:T(8,128)(2,1)S(1)} %get-tuple-element.56), channel_id=1, source_target_pairs={{0,3},{1,0},{2,1},{3,2},{4,7},{5,4},{6,5},{7,6},{8,11},{9,8},{10,9... | collective-permute-start | bytes 786440 | tf_op jit(solution)/shard_map/ppermute | solution.py:52
  51.6 9.4 %collective-permute-start.13 = (f16[1040,128]{1,0:T(8,128)(2,1)S(1)}, f16[1040,128]{1,0:T(8,128)(2,1)S(1)}, u32[]{:S(2)}, u32[]{:S(2)}) collective-permute-start(f16[1040,128]{1,0:T(8,128)(2,1)S(1)} %convert_element_type.42), channel_id=1, source_target_pairs={{0,8},{1,9},{2,10},{3,11},{4,12},{5,13},{6,14},{7,15},{8,0},{9,1},... | collective-permute-start | bytes 798728 | tf_op jit(solution)/shard_map/ppermute | solution.py:52
  53.0 8.6 %collective-permute-start.14 = (f16[1040,128]{1,0:T(8,128)(2,1)S(1)}, f16[1040,128]{1,0:T(8,128)(2,1)S(1)}, u32[]{:S(2)}, u32[]{:S(2)}) collective-permute-start(f16[1040,128]{1,0:T(8,128)(2,1)S(1)} %convert_element_type.43), channel_id=1, source_target_pairs={{0,4},{1,5},{2,6},{3,7},{4,8},{5,9},{6,10},{7,11},{8,12},{9,13},{1... | collective-permute-start | bytes 798728 | tf_op jit(solution)/shard_map/ppermute | solution.py:52
  55.3 10.6 %collective-permute-start.15 = (f16[1040,128]{1,0:T(8,128)(2,1)S(1)}, f16[1040,128]{1,0:T(8,128)(2,1)S(1)}, u32[]{:S(2)}, u32[]{:S(2)}) collective-permute-start(f16[1040,128]{1,0:T(8,128)(2,1)S(1)} %convert_element_type.44), channel_id=1, source_target_pairs={{0,12},{1,13},{2,14},{3,15},{4,0},{5,1},{6,2},{7,3},{8,4},{9,5},{1... | collective-permute-start | bytes 798728 | tf_op jit(solution)/shard_map/ppermute | solution.py:52
  56.9 15.9 %collective-permute-start.16 = (f16[1040,128]{1,0:T(8,128)(2,1)S(1)}, f16[1040,128]{1,0:T(8,128)(2,1)S(1)}, u32[]{:S(2)}, u32[]{:S(2)}) collective-permute-start(f16[1040,128]{1,0:T(8,128)(2,1)S(1)} %convert_element_type.45), channel_id=1, source_target_pairs={{0,8},{1,9},{2,10},{3,11},{4,12},{5,13},{6,14},{7,15},{8,0},{9,1},... | collective-permute-start | bytes 798728 | tf_op jit(solution)/shard_map/ppermute | solution.py:52
  59.1 13.7 %collective-permute-start.17 = (f16[1040,128]{1,0:T(8,128)(2,1)S(1)}, f16[1040,128]{1,0:T(8,128)(2,1)S(1)}, u32[]{:S(2)}, u32[]{:S(2)}) collective-permute-start(f16[1040,128]{1,0:T(8,128)(2,1)S(1)} %convert_element_type.47), channel_id=1, source_target_pairs={{0,4},{1,5},{2,6},{3,7},{4,8},{5,9},{6,10},{7,11},{8,12},{9,13},{1... | collective-permute-start | bytes 798728 | tf_op jit(solution)/shard_map/ppermute | solution.py:52
  61.0 11.8 %collective-permute-start.18 = (f16[1040,128]{1,0:T(8,128)(2,1)S(1)}, f16[1040,128]{1,0:T(8,128)(2,1)S(1)}, u32[]{:S(2)}, u32[]{:S(2)}) collective-permute-start(f16[1040,128]{1,0:T(8,128)(2,1)S(1)} %convert_element_type.49), channel_id=1, source_target_pairs={{0,12},{1,13},{2,14},{3,15},{4,0},{5,1},{6,2},{7,3},{8,4},{9,5},{1... | collective-permute-start | bytes 798728 | tf_op jit(solution)/shard_map/ppermute | solution.py:52
  66.3 13.8 %collective-permute-start.19 = (f16[1040,128]{1,0:T(8,128)(2,1)S(1)}, f16[1040,128]{1,0:T(8,128)(2,1)S(1)}, u32[]{:S(2)}, u32[]{:S(2)}) collective-permute-start(f16[1040,128]{1,0:T(8,128)(2,1)S(1)} %convert_element_type.54), channel_id=1, source_target_pairs={{0,16},{16,0},{1,17},{17,1},{2,18},{18,2},{3,19},{19,3},{4,20},{20... | collective-permute-start | bytes 798728 | tf_op jit(solution)/shard_map/ppermute | solution.py:273

commit v13 on v12

--- a/solution.py
+++ b/solution.py
@@ -200,8 +200,8 @@
     out_ref[rows:, :] = jnp.broadcast_to(power, (TAIL, LANES))
 
 
-def near_kernel(keep_ref, one_ref, two_ref, three_ref, other_ref, out_ref):
-    out_ref[...] = summed(keep_ref, (one_ref, two_ref, three_ref, other_ref))
+def near_kernel(keep_ref, *rest):
+    rest[-1][...] = summed(keep_ref, rest[:-1])
 
 
 def on_line(value, pairs):
@@ -265,13 +265,14 @@
     keep_far, *far_sends = late(1)
     keep_near, *near_sends = late(0)
     sends = far_sends + near_sends
-    got = [shifted(sends[i].astype(F16), False, 1 + i % 3) for i in (1, 0, 2, 4, 3, 5)]
+    got = [shifted(sends[i].astype(F16), False, 1 + i % 3) for i in (1, 0, 2, 4, 3)]
     rel, *got[:3] = lax.optimization_barrier((rel, *got[:3]))
-    got = [v.astype(F32) for v in got]
+    (far,) = call(far_kernel, [send], (keep_far, *[v.astype(F32) for v in got[:3]]), whole(4), moved=4 * 2**20)
+    far, final = lax.optimization_barrier((far.astype(F16), sends[5].astype(F16)))
+    other = lax.ppermute(far, "z_hi", [(0, 1), (1, 0)])
     (second,) = call(second_kernel, [((rows, width), F32)], (rel, first, weights[0]), whole(3), **matmul)
-    (far,) = call(far_kernel, [send], (keep_far, *got[:3]), whole(4), moved=4 * 2**20)
-    other = lax.ppermute(far.astype(F16), "z_hi", [(0, 1), (1, 0)]).astype(F32)
-    (block,) = call(near_kernel, [((width, LANES), F32)], (keep_near, *got[3:], other), whole(5), moved=4 * 2**20)
+    got = [v.astype(F32) for v in (*got[3:], shifted(final, False, 3))]
+    (block,) = call(near_kernel, [((width, LANES), F32)], (keep_near, other.astype(F32), *got), whole(5), moved=4 * 2**20)
     return (second[None], block[None])
 
 

time: 81.5 us -> 81.6 us (level)
  transfers between devices with their start and end apart: 20 -> 20, of which waited for: 9 -> 10; matrix products, arithmetic and copies ran while one was open for 1% -> 1% of each run, Pallas kernels for 15% -> 14%
where the time goes in v13:
time: 81.6 us; the launch traced here: 81.4 us
  starting transfers between devices  36.2 us (44%)
  waiting for transfers between devices  26.6 us (33%)
  Pallas kernels  17 us (21%)
  between operations  0.87 us (1%)
    ppermute x15, starting transfers between devices, shifted(): return lax.ppermute(value, ('section', 'y', 'x'), pairs_over(along, by))  21.2 us
    pallas_call x9, Pallas kernels, call(): pl.pallas_call(kernel, out_shape=[jax.ShapeDtypeStruct(s, t) for s, t in...  17 us
    ppermute x3, waiting for transfers between devices, on_line(): return lax.ppermute(value, ('section', 'z_lo'), pairs)  11.6 us
    ppermute x15, waiting for transfers between devices, shifted(): return lax.ppermute(value, ('section', 'y', 'x'), pairs_over(along, by))  9.37 us
    ppermute x3, starting transfers between devices, on_line(): return lax.ppermute(value, ('section', 'z_lo'), pairs)  7.26 us
    ppermute x1, starting transfers between devices, local(): other = lax.ppermute(far, 'z_hi', [(0, 1), (1, 0)])  6.47 us
    ppermute x1, waiting for transfers between devices, local(): other = lax.ppermute(far, 'z_hi', [(0, 1), (1, 0)])  3.5 us
    ppermute x1, waiting for transfers between devices, local(): shard = lax.ppermute(small, 'section', [(1, 0)])  2.13 us
  transfers between devices with their start and end apart: 20, of which 10 were waited for; matrix products, arithmetic and copies ran while one was open for 1% of the time, Pallas kernels for 14%

profile of v13, /device:TPU:24, one launch (start us, length us, event | category | flops | bytes accessed | tf_op | source)
XLA Modules:
  0.0 81.4 jit_solution(18120779415049233774)
XLA Ops:
  0.6 0.0 slice-start
  0.6 0.0 slice-start.1
  0.7 2.7 %shard_map.68 = (bf16[896,512]{1,0:T(8,128)(2,1)S(1)}, bf16[896,512]{1,0:T(8,128)(2,1)S(1)}, bf16[1280,512]{1,0:T(8,128)(2,1)S(1)}, bf16[1280,512]{1,0:T(8,128)(2,1)S(1)}, bf16[768,512]{1,0:T(8,128)(2,1)S(1)}) custom-call(s32[2]{0:T(128)} %pending_ref.1, bf16[4,128,1024]{2,1,0:T(8,128)(2,1)} %bitcast.20, bf16[3,128,4096]{2,1,0:T(8,128)(2,1)} %bitcast.19), custom_call_target="tpu_custom_call" | custom-call | flops 10000000000 | bytes 12582912 | tf_op jit(solution)/shard_map/pallas_call | solution.py:64
  3.4 1.6 %collective-permute-start.2 = (bf16[896,512]{1,0:T(8,128)(2,1)S(1)}, bf16[896,512]{1,0:T(8,128)(2,1)S(1)}, u32[]{:S(2)}, u32[]{:S(2)}) collective-permute-start(bf16[896,512]{1,0:T(8,128)(2,1)S(1)} %get-tuple-element.46.mine_on), channel_id=1, source_target_pairs={{0,1},{1,2},{2,3},{3,0},{4,5},{5,6},{6,7},{7,4},{8,9},{9,10},{10,1... | collective-permute-start | bytes 2752520 | tf_op jit(solution)/shard_map/ppermute | solution.py:52
  5.0 1.7 %collective-permute-start.3 = (bf16[896,512]{1,0:T(8,128)(2,1)S(1)}, bf16[896,512]{1,0:T(8,128)(2,1)S(1)}, u32[]{:S(2)}, u32[]{:S(2)}) collective-permute-start(bf16[896,512]{1,0:T(8,128)(2,1)S(1)} %get-tuple-element.47), channel_id=1, source_target_pairs={{0,3},{1,0},{2,1},{3,2},{4,7},{5,4},{6,5},{7,6},{8,11},{9,8},{10,9... | collective-permute-start | bytes 2752520 | tf_op jit(solution)/shard_map/ppermute | solution.py:52
  6.7 2.9 %shard_map.69 = (f32[128,1024]{1,0:T(8,128)S(1)}, bf16[128,1024]{1,0:T(8,128)(2,1)S(1)}) custom-call(bf16[128,4096]{1,0:T(8,128)(2,1)S(1)} %copy-done, bf16[1024,4096]{1,0:T(8,128)(2,1)S(1)} %bitcast.11), custom_call_target="tpu_custom_call" | custom-call | flops 1073741824 | bytes 2097152 | tf_op jit(solution)/shard_map/pallas_call | solution.py:64
  9.6 1.3 %collective-permute-start = (bf16[128,1024]{1,0:T(8,128)(2,1)S(1)}, bf16[128,1024]{1,0:T(8,128)(2,1)S(1)}, u32[]{:S(2)}, u32[]{:S(2)}) collective-permute-start(bf16[128,1024]{1,0:T(8,128)(2,1)S(1)} %get-tuple-element.44), channel_id=1, source_target_pairs={{128,0},{129,1},{130,2},{131,3},{132,4},{133,5},{134,6},{135,7},{1... | collective-permute-start | bytes 786440 | tf_op jit(solution)/shard_map/ppermute | solution.py:230
  10.9 2.1 %collective-permute-done = bf16[128,1024]{1,0:T(8,128)(2,1)S(1)} collective-permute-done((bf16[128,1024]{1,0:T(8,128)(2,1)S(1)}, bf16[128,1024]{1,0:T(8,128)(2,1)S(1)}, u32[]{:S(2)}, u32[]{:S(2)}) %collective-permute-start) | collective-permute-done | bytes 262176 | tf_op jit(solution)/shard_map/ppermute | solution.py:230
  13.0 0.3 collective-permute-start.6
  13.4 2.9 %collective-permute-start.7 = (bf16[1280,512]{1,0:T(8,128)(2,1)S(1)}, bf16[1280,512]{1,0:T(8,128)(2,1)S(1)}, u32[]{:S(2)}, u32[]{:S(2)}) collective-permute-start(bf16[1280,512]{1,0:T(8,128)(2,1)S(1)} %get-tuple-element.55), channel_id=1, source_target_pairs={{0,3},{1,0},{2,1},{3,2},{4,7},{5,4},{6,5},{7,6},{8,11},{9,8},{10,9... | collective-permute-start | bytes 3932168 | tf_op jit(solution)/shard_map/ppermute | solution.py:52
  16.3 0.1 add.3
  16.4 4.7 %collective-permute-start.1 = (bf16[128,1024]{1,0:T(8,128)(2,1)S(1)}, bf16[128,1024]{1,0:T(8,128)(2,1)S(1)}, u32[]{:S(2)}, u32[]{:S(2)}) collective-permute-start(bf16[128,1024]{1,0:T(8,128)(2,1)S(1)} %add.3), channel_id=1, source_target_pairs={{0,96},{32,0},{64,32},{96,64},{128,160},{160,192},{192,224},{224,1... | collective-permute-start | bytes 786440 | tf_op jit(solution)/shard_map/ppermute | solution.py:209
  21.1 4.6 %collective-permute-done.1 = bf16[128,1024]{1,0:T(8,128)(2,1)S(1)} collective-permute-done((bf16[128,1024]{1,0:T(8,128)(2,1)S(1)}, bf16[128,1024]{1,0:T(8,128)(2,1)S(1)}, u32[]{:S(2)}, u32[]{:S(2)}) %collective-permute-start.1) | collective-permute-done | bytes 262176 | tf_op jit(solution)/shard_map/ppermute | solution.py:209
  25.6 0.0 collective-permute-done.2.left_on
  25.6 0.0 collective-permute-done.3.right_on
  25.6 1.3 %collective-permute-start.4 = (bf16[128,1024]{1,0:T(8,128)(2,1)S(1)}, bf16[128,1024]{1,0:T(8,128)(2,1)S(1)}, u32[]{:S(2)}, u32[]{:S(2)}) collective-permute-start(bf16[128,1024]{1,0:T(8,128)(2,1)S(1)} %collective-permute-done.1), channel_id=1, source_target_pairs={{128,32},{160,64},{192,96},{224,0},{129,33},{161,65},{193,97},{225... | collective-permute-start | bytes 786440 | tf_op jit(solution)/shard_map/ppermute | solution.py:209
  26.9 0.1 collective-permute-start.8
  27.0 3.2 %collective-permute-start.9 = (bf16[896,512]{1,0:T(8,128)(2,1)S(1)}, bf16[896,512]{1,0:T(8,128)(2,1)S(1)}, u32[]{:S(2)}, u32[]{:S(2)}) collective-permute-start(bf16[896,512]{1,0:T(8,128)(2,1)S(1)} %collective-permute-done.3.right_on), channel_id=1, source_target_pairs={{0,3},{1,0},{2,1},{3,2},{4,7},{5,4},{6,5},{7,6},{8,11},{9,8},{10,9... | collective-permute-start | bytes 2752520 | tf_op jit(solution)/shard_map/ppermute | solution.py:52
  30.2 4.9 %collective-permute-done.4 = bf16[128,1024]{1,0:T(8,128)(2,1)S(1)} collective-permute-done((bf16[128,1024]{1,0:T(8,128)(2,1)S(1)}, bf16[128,1024]{1,0:T(8,128)(2,1)S(1)}, u32[]{:S(2)}, u32[]{:S(2)}) %collective-permute-start.4) | collective-permute-done | bytes 262176 | tf_op jit(solution)/shard_map/ppermute | solution.py:209
  35.1 1.3 %collective-permute-start.5 = (bf16[128,1024]{1,0:T(8,128)(2,1)S(1)}, bf16[128,1024]{1,0:T(8,128)(2,1)S(1)}, u32[]{:S(2)}, u32[]{:S(2)}) collective-permute-start(bf16[128,1024]{1,0:T(8,128)(2,1)S(1)} %collective-permute-done.1), channel_id=1, source_target_pairs={{128,0},{160,32},{192,64},{224,96},{129,1},{161,33},{193,65},{225,... | collective-permute-start | bytes 786440 | tf_op jit(solution)/shard_map/ppermute | solution.py:209
  36.4 2.1 %collective-permute-done.5 = bf16[128,1024]{1,0:T(8,128)(2,1)S(1)} collective-permute-done((bf16[128,1024]{1,0:T(8,128)(2,1)S(1)}, bf16[128,1024]{1,0:T(8,128)(2,1)S(1)}, u32[]{:S(2)}, u32[]{:S(2)}) %collective-permute-start.5) | collective-permute-done | bytes 262176 | tf_op jit(solution)/shard_map/ppermute | solution.py:209
  38.5 0.1 pad_maximum_fusion.rel_ref
  38.6 0.6 shard_map.71
  39.3 0.4 collective-permute-start.10
  39.7 0.0 collective-permute-done.6.left_ref
  39.7 0.6 collective-permute-start.11
  40.3 2.6 %collective-permute-start.12 = (bf16[256,512]{1,0:T(8,128)(2,1)S(1)}, bf16[256,512]{1,0:T(8,128)(2,1)S(1)}, u32[]{:S(2)}, u32[]{:S(2)}) collective-permute-start(bf16[256,512]{1,0:T(8,128)(2,1)S(1)} %get-tuple-element.58), channel_id=1, source_target_pairs={{0,3},{1,0},{2,1},{3,2},{4,7},{5,4},{6,5},{7,6},{8,11},{9,8},{10,9... | collective-permute-start | bytes 786440 | tf_op jit(solution)/shard_map/ppermute | solution.py:52
  42.9 2.9 %shard_map.70.acc_ref = f32[1024,1024]{1,0:T(8,128)S(1)} custom-call(bf16[896,512]{1,0:T(8,128)(2,1)S(1)} %get-tuple-element.46.mine_on, bf16[1280,512]{1,0:T(8,128)(2,1)S(1)} %get-tuple-element.53.mine_ref, bf16[768,512]{1,0:T(8,128)(2,1)S(1)} %get-tuple-element.51.own_ref, bf16[896,512]{1,0:T(8,128)(2,1)S(1)} %collective-permute-done.2.left_on, ...), custom_call_target="tpu_custom_call" | custom-call | flops 2415919104 | bytes 12582912 | tf_op jit(solution)/shard_map/pallas_call | solution.py:64
  45.8 1.5 %collective-permute-done.10.two_last = bf16[256,512]{1,0:T(8,128)(2,1)S(1)} collective-permute-done((bf16[256,512]{1,0:T(8,128)(2,1)S(1)}, bf16[256,512]{1,0:T(8,128)(2,1)S(1)}, u32[]{:S(2)}, u32[]{:S(2)}) %collective-permute-start.10) | collective-permute-done | bytes 262176 | tf_op jit(solution)/shard_map/ppermute | solution.py:52
  47.4 2.7 %collective-permute-done.11.left_last = bf16[256,512]{1,0:T(8,128)(2,1)S(1)} collective-permute-done((bf16[256,512]{1,0:T(8,128)(2,1)S(1)}, bf16[256,512]{1,0:T(8,128)(2,1)S(1)}, u32[]{:S(2)}, u32[]{:S(2)}) %collective-permute-start.11) | collective-permute-done | bytes 262176 | tf_op jit(solution)/shard_map/ppermute | solution.py:52
  50.1 1.5 %shard_map.72 = (f32[1024,128]{1,0:T(8,128)S(1)}, f32[1040,128]{1,0:T(8,128)S(1)}, f32[1040,128]{1,0:T(8,128)S(1)}, f32[1040,128]{1,0:T(8,128)S(1)}) custom-call(f32[1024,1024]{1,0:T(8,128)S(1)} %shard_map.70.acc_ref, bf16[896,512]{1,0:T(8,128)(2,1)S(1)} %get-tuple-element.46.mine_on, bf16[1280,512]{1,0:T(8,128)(2,1)S(1)} %get-tuple-element.53.mine_ref, ...), custom_call_target="tpu_custom_call" | custom-call | flops 939524096 | bytes 8388608 | tf_op jit(solution)/shard_map/pallas_call | solution.py:64
  51.6 1.3 %collective-permute-start.13 = (f16[1040,128]{1,0:T(8,128)(2,1)S(1)}, f16[1040,128]{1,0:T(8,128)(2,1)S(1)}, u32[]{:S(2)}, u32[]{:S(2)}) collective-permute-start(f16[1040,128]{1,0:T(8,128)(2,1)S(1)} %convert_element_type.42), channel_id=1, source_target_pairs={{0,8},{1,9},{2,10},{3,11},{4,12},{5,13},{6,14},{7,15},{8,0},{9,1},... | collective-permute-start | bytes 798728 | tf_op jit(solution)/shard_map/ppermute | solution.py:52
  53.0 2.3 %collective-permute-start.14 = (f16[1040,128]{1,0:T(8,128)(2,1)S(1)}, f16[1040,128]{1,0:T(8,128)(2,1)S(1)}, u32[]{:S(2)}, u32[]{:S(2)}) collective-permute-start(f16[1040,128]{1,0:T(8,128)(2,1)S(1)} %convert_element_type.43), channel_id=1, source_target_pairs={{0,4},{1,5},{2,6},{3,7},{4,8},{5,9},{6,10},{7,11},{8,12},{9,13},{1... | collective-permute-start | bytes 798728 | tf_op jit(solution)/shard_map/ppermute | solution.py:52
  55.3 0.1 collective-permute-start.15
  55.3 1.5 %shard_map.74 = (f32[1024,128]{1,0:T(8,128)S(1)}, f32[1040,128]{1,0:T(8,128)S(1)}, f32[1040,128]{1,0:T(8,128)S(1)}, f32[1040,128]{1,0:T(8,128)S(1)}) custom-call(f32[1024,1024]{1,0:T(8,128)S(1)} %shard_map.70.acc_ref, bf16[896,512]{1,0:T(8,128)(2,1)S(1)} %get-tuple-element.46.mine_on, bf16[1280,512]{1,0:T(8,128)(2,1)S(1)} %get-tuple-element.53.mine_ref, ...), custom_call_target="tpu_custom_call" | custom-call | flops 939524096 | bytes 8388608 | tf_op jit(solution)/shard_map/pallas_call | solution.py:64
  56.9 2.2 %collective-permute-start.17 = (f16[1040,128]{1,0:T(8,128)(2,1)S(1)}, f16[1040,128]{1,0:T(8,128)(2,1)S(1)}, u32[]{:S(2)}, u32[]{:S(2)}) collective-permute-start(f16[1040,128]{1,0:T(8,128)(2,1)S(1)} %convert_element_type.51), channel_id=1, source_target_pairs={{0,8},{1,9},{2,10},{3,11},{4,12},{5,13},{6,14},{7,15},{8,0},{9,1},... | collective-permute-start | bytes 798728 | tf_op jit(solution)/shard_map/ppermute | solution.py:52
  59.1 1.8 %collective-permute-start.18 = (f16[1040,128]{1,0:T(8,128)(2,1)S(1)}, f16[1040,128]{1,0:T(8,128)(2,1)S(1)}, u32[]{:S(2)}, u32[]{:S(2)}) collective-permute-start(f16[1040,128]{1,0:T(8,128)(2,1)S(1)} %convert_element_type.53), channel_id=1, source_target_pairs={{0,4},{1,5},{2,6},{3,7},{4,8},{5,9},{6,10},{7,11},{8,12},{9,13},{1... | collective-permute-start | bytes 798728 | tf_op jit(solution)/shard_map/ppermute | solution.py:52
  61.0 0.0 collective-permute-done.13
  61.0 0.5 collective-permute-done.14
  61.5 4.3 %collective-permute-done.15 = f16[1040,128]{1,0:T(8,128)(2,1)S(1)} collective-permute-done((f16[1040,128]{1,0:T(8,128)(2,1)S(1)}, f16[1040,128]{1,0:T(8,128)(2,1)S(1)}, u32[]{:S(2)}, u32[]{:S(2)}) %collective-permute-start.15) | collective-permute-done | bytes 266272 | tf_op jit(solution)/shard_map/ppermute | solution.py:52
  65.9 0.3 shard_map.75
  66.3 6.5 %collective-permute-start.16 = (f16[1040,128]{1,0:T(8,128)(2,1)S(1)}, f16[1040,128]{1,0:T(8,128)(2,1)S(1)}, u32[]{:S(2)}, u32[]{:S(2)}) collective-permute-start(f16[1040,128]{1,0:T(8,128)(2,1)S(1)} %convert_element_type.48), channel_id=1, source_target_pairs={{0,16},{16,0},{1,17},{17,1},{2,18},{18,2},{3,19},{19,3},{4,20},{20... | collective-permute-start | bytes 798728 | tf_op jit(solution)/shard_map/ppermute | solution.py:272
  72.7 0.0 collective-permute-start.19
  72.7 0.0 collective-permute-done.17
  72.8 3.7 %shard_map.73 = f32[128,1024]{1,0:T(8,128)} custom-call(bf16[4,128,1024]{2,1,0:T(8,128)(2,1)S(1)} %pad_maximum_fusion.rel_ref, f32[128,1024]{1,0:T(8,128)S(1)} %get-tuple-element.71.first_ref, bf16[1024,4096]{1,0:T(8,128)(2,1)S(1)} %bitcast.12), custom_call_target="tpu_custom_call" | custom-call | flops 1073741824 | bytes 2097152 | tf_op jit(solution)/shard_map/pallas_call | solution.py:64
  76.5 3.5 %collective-permute-done.16 = f16[1040,128]{1,0:T(8,128)(2,1)S(1)} collective-permute-done((f16[1040,128]{1,0:T(8,128)(2,1)S(1)}, f16[1040,128]{1,0:T(8,128)(2,1)S(1)}, u32[]{:S(2)}, u32[]{:S(2)}) %collective-permute-start.16) | collective-permute-done | bytes 266272 | tf_op jit(solution)/shard_map/ppermute | solution.py:272
  80.1 0.3 collective-permute-done.19
  80.4 1.0 %shard_map.76 = f32[1024,128]{1,0:T(8,128)} custom-call(f32[1024,128]{1,0:T(8,128)S(1)} %get-tuple-element.72.keep_ref, f32[1040,128]{1,0:T(8,128)S(1)} %convert_element_type.50.rest_0_, f32[1040,128]{1,0:T(8,128)S(1)} %convert_element_type.52.rest_1_, f32[1040,128]{1,0:T(8,128)S(1)} %convert_element_type.54.rest_2_, ...), custom_call_target="tpu_custom_call" | custom-call | bytes 4194304 | tf_op jit(solution)/shard_map/pallas_call | solution.py:64
  (24 shorter events, 0.5 us)
Async XLA Ops:
  0.6 6.1 %slice-start = ((s8[8388608]{0:T(1024)(128)(4,1)}), s8[4194304]{0:T(1024)(128)(4,1)S(1)}, s32[]{:S(2)}) async-start(s8[8388608]{0:T(1024)(128)(4,1)} %bitcast.9), calls=%async_computation | async-start | bytes 8388608
  0.6 6.1 %slice-start.1 = ((s8[8388608]{0:T(1024)(128)(4,1)}), s8[4194304]{0:T(1024)(128)(4,1)S(1)}, s32[]{:S(2)}) async-start(s8[8388608]{0:T(1024)(128)(4,1)} %bitcast.9), calls=%async_computation.1 | async-start | bytes 8388608
  0.7 6.1 %copy-start = (bf16[128,4096]{1,0:T(8,128)(2,1)S(1)}, bf16[128,4096]{1,0:T(8,128)(2,1)}, u32[]{:S(2)}) copy-start(bf16[128,4096]{1,0:T(8,128)(2,1)} %head_ref.1) | copy-start | bytes 3145732
  3.4 22.2 %collective-permute-start.2 = (bf16[896,512]{1,0:T(8,128)(2,1)S(1)}, bf16[896,512]{1,0:T(8,128)(2,1)S(1)}, u32[]{:S(2)}, u32[]{:S(2)}) collective-permute-start(bf16[896,512]{1,0:T(8,128)(2,1)S(1)} %get-tuple-element.46.mine_on), channel_id=1, source_target_pairs={{0,1},{1,2},{2,3},{3,0},{4,5},{5,6},{6,7},{7,4},{8,9},{9,10},{10,1... | collective-permute-start | bytes 2752520 | tf_op jit(solution)/shard_map/ppermute | solution.py:52
  5.0 20.6 %collective-permute-start.3 = (bf16[896,512]{1,0:T(8,128)(2,1)S(1)}, bf16[896,512]{1,0:T(8,128)(2,1)S(1)}, u32[]{:S(2)}, u32[]{:S(2)}) collective-permute-start(bf16[896,512]{1,0:T(8,128)(2,1)S(1)} %get-tuple-element.47), channel_id=1, source_target_pairs={{0,3},{1,0},{2,1},{3,2},{4,7},{5,4},{6,5},{7,6},{8,11},{9,8},{10,9... | collective-permute-start | bytes 2752520 | tf_op jit(solution)/shard_map/ppermute | solution.py:52
  9.6 3.4 %collective-permute-start = (bf16[128,1024]{1,0:T(8,128)(2,1)S(1)}, bf16[128,1024]{1,0:T(8,128)(2,1)S(1)}, u32[]{:S(2)}, u32[]{:S(2)}) collective-permute-start(bf16[128,1024]{1,0:T(8,128)(2,1)S(1)} %get-tuple-element.44), channel_id=1, source_target_pairs={{128,0},{129,1},{130,2},{131,3},{132,4},{133,5},{134,6},{135,7},{1... | collective-permute-start | bytes 786440 | tf_op jit(solution)/shard_map/ppermute | solution.py:230
  13.0 26.7 %collective-permute-start.6 = (bf16[1280,512]{1,0:T(8,128)(2,1)S(1)}, bf16[1280,512]{1,0:T(8,128)(2,1)S(1)}, u32[]{:S(2)}, u32[]{:S(2)}) collective-permute-start(bf16[1280,512]{1,0:T(8,128)(2,1)S(1)} %get-tuple-element.53.mine_ref), channel_id=1, source_target_pairs={{0,1},{1,2},{2,3},{3,0},{4,5},{5,6},{6,7},{7,4},{8,9},{9,10},{10,1... | collective-permute-start | bytes 3932168 | tf_op jit(solution)/shard_map/ppermute | solution.py:52
  13.4 26.9 %collective-permute-start.7 = (bf16[1280,512]{1,0:T(8,128)(2,1)S(1)}, bf16[1280,512]{1,0:T(8,128)(2,1)S(1)}, u32[]{:S(2)}, u32[]{:S(2)}) collective-permute-start(bf16[1280,512]{1,0:T(8,128)(2,1)S(1)} %get-tuple-element.55), channel_id=1, source_target_pairs={{0,3},{1,0},{2,1},{3,2},{4,7},{5,4},{6,5},{7,6},{8,11},{9,8},{10,9... | collective-permute-start | bytes 3932168 | tf_op jit(solution)/shard_map/ppermute | solution.py:52
  16.4 9.3 %collective-permute-start.1 = (bf16[128,1024]{1,0:T(8,128)(2,1)S(1)}, bf16[128,1024]{1,0:T(8,128)(2,1)S(1)}, u32[]{:S(2)}, u32[]{:S(2)}) collective-permute-start(bf16[128,1024]{1,0:T(8,128)(2,1)S(1)} %add.3), channel_id=1, source_target_pairs={{0,96},{32,0},{64,32},{96,64},{128,160},{160,192},{192,224},{224,1... | collective-permute-start | bytes 786440 | tf_op jit(solution)/shard_map/ppermute | solution.py:209
  25.6 9.5 %collective-permute-start.4 = (bf16[128,1024]{1,0:T(8,128)(2,1)S(1)}, bf16[128,1024]{1,0:T(8,128)(2,1)S(1)}, u32[]{:S(2)}, u32[]{:S(2)}) collective-permute-start(bf16[128,1024]{1,0:T(8,128)(2,1)S(1)} %collective-permute-done.1), channel_id=1, source_target_pairs={{128,32},{160,64},{192,96},{224,0},{129,33},{161,65},{193,97},{225... | collective-permute-start | bytes 786440 | tf_op jit(solution)/shard_map/ppermute | solution.py:209
  26.9 23.2 %collective-permute-start.8 = (bf16[896,512]{1,0:T(8,128)(2,1)S(1)}, bf16[896,512]{1,0:T(8,128)(2,1)S(1)}, u32[]{:S(2)}, u32[]{:S(2)}) collective-permute-start(bf16[896,512]{1,0:T(8,128)(2,1)S(1)} %collective-permute-done.2.left_on), channel_id=1, source_target_pairs={{0,1},{1,2},{2,3},{3,0},{4,5},{5,6},{6,7},{7,4},{8,9},{9,10},{10,1... | collective-permute-start | bytes 2752520 | tf_op jit(solution)/shard_map/ppermute | solution.py:52
  27.0 23.1 %collective-permute-start.9 = (bf16[896,512]{1,0:T(8,128)(2,1)S(1)}, bf16[896,512]{1,0:T(8,128)(2,1)S(1)}, u32[]{:S(2)}, u32[]{:S(2)}) collective-permute-start(bf16[896,512]{1,0:T(8,128)(2,1)S(1)} %collective-permute-done.3.right_on), channel_id=1, source_target_pairs={{0,3},{1,0},{2,1},{3,2},{4,7},{5,4},{6,5},{7,6},{8,11},{9,8},{10,9... | collective-permute-start | bytes 2752520 | tf_op jit(solution)/shard_map/ppermute | solution.py:52
  35.1 3.4 %collective-permute-start.5 = (bf16[128,1024]{1,0:T(8,128)(2,1)S(1)}, bf16[128,1024]{1,0:T(8,128)(2,1)S(1)}, u32[]{:S(2)}, u32[]{:S(2)}) collective-permute-start(bf16[128,1024]{1,0:T(8,128)(2,1)S(1)} %collective-permute-done.1), channel_id=1, source_target_pairs={{128,0},{160,32},{192,64},{224,96},{129,1},{161,33},{193,65},{225,... | collective-permute-start | bytes 786440 | tf_op jit(solution)/shard_map/ppermute | solution.py:209
  39.3 8.1 %collective-permute-start.10 = (bf16[256,512]{1,0:T(8,128)(2,1)S(1)}, bf16[256,512]{1,0:T(8,128)(2,1)S(1)}, u32[]{:S(2)}, u32[]{:S(2)}) collective-permute-start(bf16[256,512]{1,0:T(8,128)(2,1)S(1)} %get-tuple-element.56), channel_id=1, source_target_pairs={{0,2},{1,3},{2,0},{3,1},{4,6},{5,7},{6,4},{7,5},{8,10},{9,11},{10,... | collective-permute-start | bytes 786440 | tf_op jit(solution)/shard_map/ppermute | solution.py:52
  39.7 10.4 %collective-permute-start.11 = (bf16[256,512]{1,0:T(8,128)(2,1)S(1)}, bf16[256,512]{1,0:T(8,128)(2,1)S(1)}, u32[]{:S(2)}, u32[]{:S(2)}) collective-permute-start(bf16[256,512]{1,0:T(8,128)(2,1)S(1)} %get-tuple-element.57), channel_id=1, source_target_pairs={{0,1},{1,2},{2,3},{3,0},{4,5},{5,6},{6,7},{7,4},{8,9},{9,10},{10,1... | collective-permute-start | bytes 786440 | tf_op jit(solution)/shard_map/ppermute | solution.py:52
  40.3 9.8 %collective-permute-start.12 = (bf16[256,512]{1,0:T(8,128)(2,1)S(1)}, bf16[256,512]{1,0:T(8,128)(2,1)S(1)}, u32[]{:S(2)}, u32[]{:S(2)}) collective-permute-start(bf16[256,512]{1,0:T(8,128)(2,1)S(1)} %get-tuple-element.58), channel_id=1, source_target_pairs={{0,3},{1,0},{2,1},{3,2},{4,7},{5,4},{6,5},{7,6},{8,11},{9,8},{10,9... | collective-permute-start | bytes 786440 | tf_op jit(solution)/shard_map/ppermute | solution.py:52
  51.6 9.4 %collective-permute-start.13 = (f16[1040,128]{1,0:T(8,128)(2,1)S(1)}, f16[1040,128]{1,0:T(8,128)(2,1)S(1)}, u32[]{:S(2)}, u32[]{:S(2)}) collective-permute-start(f16[1040,128]{1,0:T(8,128)(2,1)S(1)} %convert_element_type.42), channel_id=1, source_target_pairs={{0,8},{1,9},{2,10},{3,11},{4,12},{5,13},{6,14},{7,15},{8,0},{9,1},... | collective-permute-start | bytes 798728 | tf_op jit(solution)/shard_map/ppermute | solution.py:52
  53.0 8.6 %collective-permute-start.14 = (f16[1040,128]{1,0:T(8,128)(2,1)S(1)}, f16[1040,128]{1,0:T(8,128)(2,1)S(1)}, u32[]{:S(2)}, u32[]{:S(2)}) collective-permute-start(f16[1040,128]{1,0:T(8,128)(2,1)S(1)} %convert_element_type.43), channel_id=1, source_target_pairs={{0,4},{1,5},{2,6},{3,7},{4,8},{5,9},{6,10},{7,11},{8,12},{9,13},{1... | collective-permute-start | bytes 798728 | tf_op jit(solution)/shard_map/ppermute | solution.py:52
  55.3 10.6 %collective-permute-start.15 = (f16[1040,128]{1,0:T(8,128)(2,1)S(1)}, f16[1040,128]{1,0:T(8,128)(2,1)S(1)}, u32[]{:S(2)}, u32[]{:S(2)}) collective-permute-start(f16[1040,128]{1,0:T(8,128)(2,1)S(1)} %convert_element_type.44), channel_id=1, source_target_pairs={{0,12},{1,13},{2,14},{3,15},{4,0},{5,1},{6,2},{7,3},{8,4},{9,5},{1... | collective-permute-start | bytes 798728 | tf_op jit(solution)/shard_map/ppermute | solution.py:52
  56.9 15.9 %collective-permute-start.17 = (f16[1040,128]{1,0:T(8,128)(2,1)S(1)}, f16[1040,128]{1,0:T(8,128)(2,1)S(1)}, u32[]{:S(2)}, u32[]{:S(2)}) collective-permute-start(f16[1040,128]{1,0:T(8,128)(2,1)S(1)} %convert_element_type.51), channel_id=1, source_target_pairs={{0,8},{1,9},{2,10},{3,11},{4,12},{5,13},{6,14},{7,15},{8,0},{9,1},... | collective-permute-start | bytes 798728 | tf_op jit(solution)/shard_map/ppermute | solution.py:52
  59.1 13.7 %collective-permute-start.18 = (f16[1040,128]{1,0:T(8,128)(2,1)S(1)}, f16[1040,128]{1,0:T(8,128)(2,1)S(1)}, u32[]{:S(2)}, u32[]{:S(2)}) collective-permute-start(f16[1040,128]{1,0:T(8,128)(2,1)S(1)} %convert_element_type.53), channel_id=1, source_target_pairs={{0,4},{1,5},{2,6},{3,7},{4,8},{5,9},{6,10},{7,11},{8,12},{9,13},{1... | collective-permute-start | bytes 798728 | tf_op jit(solution)/shard_map/ppermute | solution.py:52
  66.3 13.8 %collective-permute-start.16 = (f16[1040,128]{1,0:T(8,128)(2,1)S(1)}, f16[1040,128]{1,0:T(8,128)(2,1)S(1)}, u32[]{:S(2)}, u32[]{:S(2)}) collective-permute-start(f16[1040,128]{1,0:T(8,128)(2,1)S(1)} %convert_element_type.48), channel_id=1, source_target_pairs={{0,16},{16,0},{1,17},{17,1},{2,18},{18,2},{3,19},{19,3},{4,20},{20... | collective-permute-start | bytes 798728 | tf_op jit(solution)/shard_map/ppermute | solution.py:272
  72.7 7.6 %collective-permute-start.19 = (f16[1040,128]{1,0:T(8,128)(2,1)S(1)}, f16[1040,128]{1,0:T(8,128)(2,1)S(1)}, u32[]{:S(2)}, u32[]{:S(2)}) collective-permute-start(f16[1040,128]{1,0:T(8,128)(2,1)S(1)} %convert_element_type.49), channel_id=1, source_target_pairs={{0,12},{1,13},{2,14},{3,15},{4,0},{5,1},{6,2},{7,3},{8,4},{9,5},{1... | collective-permute-start | bytes 798728 | tf_op jit(solution)/shard_map/ppermute | solution.py:52

commit v14 on v13

--- a/solution.py
+++ b/solution.py
@@ -264,14 +264,13 @@
 
     keep_far, *far_sends = late(1)
     keep_near, *near_sends = late(0)
-    sends = far_sends + near_sends
-    got = [shifted(sends[i].astype(F16), False, 1 + i % 3) for i in (1, 0, 2, 4, 3)]
-    rel, *got[:3] = lax.optimization_barrier((rel, *got[:3]))
-    (far,) = call(far_kernel, [send], (keep_far, *[v.astype(F32) for v in got[:3]]), whole(4), moved=4 * 2**20)
-    far, final = lax.optimization_barrier((far.astype(F16), sends[5].astype(F16)))
+    got = [shifted(far_sends[b - 1].astype(F16), False, b) for b in (2, 1, 3)]
+    rel, *got = lax.optimization_barrier((rel, *got))
+    (far,) = call(far_kernel, [send], (keep_far, *[v.astype(F32) for v in got]), whole(4), moved=4 * 2**20)
+    far, *near_sends = lax.optimization_barrier((far.astype(F16), *[v.astype(F16) for v in near_sends]))
     other = lax.ppermute(far, "z_hi", [(0, 1), (1, 0)])
     (second,) = call(second_kernel, [((rows, width), F32)], (rel, first, weights[0]), whole(3), **matmul)
-    got = [v.astype(F32) for v in (*got[3:], shifted(final, False, 3))]
+    got = [shifted(near_sends[b - 1], False, b).astype(F32) for b in (2, 1, 3)]
     (block,) = call(near_kernel, [((width, LANES), F32)], (keep_near, other.astype(F32), *got), whole(5), moved=4 * 2**20)
     return (second[None], block[None])
 

time: 81.6 us -> 81.9 us (level)
  waiting for transfers between devices: 26.6 us -> 28 us
  starting transfers between devices: 36.2 us -> 35.1 us
    ppermute x15, waiting for transfers between devices: 9.37 us -> 12.7 us  [shifted(): return lax.ppermute(value, ('section', 'y', 'x'), pairs_over(along, by))]
    ppermute x1, waiting for transfers between devices: 3.5 us -> 1.6 us  [local(): other = lax.ppermute(far, 'z_hi', [(0, 1), (1, 0)])]
    ppermute x15, starting transfers between devices: 21.2 us -> 20.1 us  [shifted(): return lax.ppermute(value, ('section', 'y', 'x'), pairs_over(along, by))]
  transfers between devices with their start and end apart: 20 -> 20, of which waited for: 10 -> 11; matrix products, arithmetic and copies ran while one was open for 1% -> 1% of each run, Pallas kernels for 14% -> 14%
where the time goes in v14:
time: 81.9 us; the launch traced here: 81.7 us
  starting transfers between devices  35.1 us (43%)
  waiting for transfers between devices  28 us (34%)
  Pallas kernels  17 us (21%)
  between operations  0.87 us (1%)
    ppermute x15, starting transfers between devices, shifted(): return lax.ppermute(value, ('section', 'y', 'x'), pairs_over(along, by))  20.1 us
    pallas_call x9, Pallas kernels, call(): pl.pallas_call(kernel, out_shape=[jax.ShapeDtypeStruct(s, t) for s, t in...  17 us
    ppermute x15, waiting for transfers between devices, shifted(): return lax.ppermute(value, ('section', 'y', 'x'), pairs_over(along, by))  12.7 us
    ppermute x3, waiting for transfers between devices, on_line(): return lax.ppermute(value, ('section', 'z_lo'), pairs)  11.6 us
    ppermute x3, starting transfers between devices, on_line(): return lax.ppermute(value, ('section', 'z_lo'), pairs)  7.26 us
    ppermute x1, starting transfers between devices, local(): other = lax.ppermute(far, 'z_hi', [(0, 1), (1, 0)])  6.47 us
    ppermute x1, waiting for transfers between devices, local(): shard = lax.ppermute(small, 'section', [(1, 0)])  2.13 us
  transfers between devices with their start and end apart: 20, of which 11 were waited for; matrix products, arithmetic and copies ran while one was open for 1% of the time, Pallas kernels for 14%

profile of v14, /device:TPU:24, one launch (start us, length us, event | category | flops | bytes accessed | tf_op | source)
XLA Modules:
  0.0 81.7 jit_solution(14727582743058911632)
XLA Ops:
  0.6 0.0 slice-start
  0.6 0.0 slice-start.1
  0.7 2.7 %shard_map.68 = (bf16[896,512]{1,0:T(8,128)(2,1)S(1)}, bf16[896,512]{1,0:T(8,128)(2,1)S(1)}, bf16[1280,512]{1,0:T(8,128)(2,1)S(1)}, bf16[1280,512]{1,0:T(8,128)(2,1)S(1)}, bf16[768,512]{1,0:T(8,128)(2,1)S(1)}) custom-call(s32[2]{0:T(128)} %pending_ref.1, bf16[4,128,1024]{2,1,0:T(8,128)(2,1)} %bitcast.20, bf16[3,128,4096]{2,1,0:T(8,128)(2,1)} %bitcast.19), custom_call_target="tpu_custom_call" | custom-call | flops 10000000000 | bytes 12582912 | tf_op jit(solution)/shard_map/pallas_call | solution.py:64
  3.4 1.6 %collective-permute-start.2 = (bf16[896,512]{1,0:T(8,128)(2,1)S(1)}, bf16[896,512]{1,0:T(8,128)(2,1)S(1)}, u32[]{:S(2)}, u32[]{:S(2)}) collective-permute-start(bf16[896,512]{1,0:T(8,128)(2,1)S(1)} %get-tuple-element.48.mine_on), channel_id=1, source_target_pairs={{0,1},{1,2},{2,3},{3,0},{4,5},{5,6},{6,7},{7,4},{8,9},{9,10},{10,1... | collective-permute-start | bytes 2752520 | tf_op jit(solution)/shard_map/ppermute | solution.py:52
  5.0 1.7 %collective-permute-start.3 = (bf16[896,512]{1,0:T(8,128)(2,1)S(1)}, bf16[896,512]{1,0:T(8,128)(2,1)S(1)}, u32[]{:S(2)}, u32[]{:S(2)}) collective-permute-start(bf16[896,512]{1,0:T(8,128)(2,1)S(1)} %get-tuple-element.49), channel_id=1, source_target_pairs={{0,3},{1,0},{2,1},{3,2},{4,7},{5,4},{6,5},{7,6},{8,11},{9,8},{10,9... | collective-permute-start | bytes 2752520 | tf_op jit(solution)/shard_map/ppermute | solution.py:52
  6.7 2.9 %shard_map.69 = (f32[128,1024]{1,0:T(8,128)S(1)}, bf16[128,1024]{1,0:T(8,128)(2,1)S(1)}) custom-call(bf16[128,4096]{1,0:T(8,128)(2,1)S(1)} %copy-done, bf16[1024,4096]{1,0:T(8,128)(2,1)S(1)} %bitcast.11), custom_call_target="tpu_custom_call" | custom-call | flops 1073741824 | bytes 2097152 | tf_op jit(solution)/shard_map/pallas_call | solution.py:64
  9.6 1.3 %collective-permute-start = (bf16[128,1024]{1,0:T(8,128)(2,1)S(1)}, bf16[128,1024]{1,0:T(8,128)(2,1)S(1)}, u32[]{:S(2)}, u32[]{:S(2)}) collective-permute-start(bf16[128,1024]{1,0:T(8,128)(2,1)S(1)} %get-tuple-element.46), channel_id=1, source_target_pairs={{128,0},{129,1},{130,2},{131,3},{132,4},{133,5},{134,6},{135,7},{1... | collective-permute-start | bytes 786440 | tf_op jit(solution)/shard_map/ppermute | solution.py:230
  10.9 2.1 %collective-permute-done = bf16[128,1024]{1,0:T(8,128)(2,1)S(1)} collective-permute-done((bf16[128,1024]{1,0:T(8,128)(2,1)S(1)}, bf16[128,1024]{1,0:T(8,128)(2,1)S(1)}, u32[]{:S(2)}, u32[]{:S(2)}) %collective-permute-start) | collective-permute-done | bytes 262176 | tf_op jit(solution)/shard_map/ppermute | solution.py:230
  13.0 0.3 collective-permute-start.6
  13.4 2.9 %collective-permute-start.7 = (bf16[1280,512]{1,0:T(8,128)(2,1)S(1)}, bf16[1280,512]{1,0:T(8,128)(2,1)S(1)}, u32[]{:S(2)}, u32[]{:S(2)}) collective-permute-start(bf16[1280,512]{1,0:T(8,128)(2,1)S(1)} %get-tuple-element.57), channel_id=1, source_target_pairs={{0,3},{1,0},{2,1},{3,2},{4,7},{5,4},{6,5},{7,6},{8,11},{9,8},{10,9... | collective-permute-start | bytes 3932168 | tf_op jit(solution)/shard_map/ppermute | solution.py:52
  16.3 0.1 add.3
  16.4 4.7 %collective-permute-start.1 = (bf16[128,1024]{1,0:T(8,128)(2,1)S(1)}, bf16[128,1024]{1,0:T(8,128)(2,1)S(1)}, u32[]{:S(2)}, u32[]{:S(2)}) collective-permute-start(bf16[128,1024]{1,0:T(8,128)(2,1)S(1)} %add.3), channel_id=1, source_target_pairs={{0,96},{32,0},{64,32},{96,64},{128,160},{160,192},{192,224},{224,1... | collective-permute-start | bytes 786440 | tf_op jit(solution)/shard_map/ppermute | solution.py:209
  21.1 4.6 %collective-permute-done.1 = bf16[128,1024]{1,0:T(8,128)(2,1)S(1)} collective-permute-done((bf16[128,1024]{1,0:T(8,128)(2,1)S(1)}, bf16[128,1024]{1,0:T(8,128)(2,1)S(1)}, u32[]{:S(2)}, u32[]{:S(2)}) %collective-permute-start.1) | collective-permute-done | bytes 262176 | tf_op jit(solution)/shard_map/ppermute | solution.py:209
  25.6 0.0 collective-permute-done.2.left_on
  25.6 1.3 %collective-permute-start.4 = (bf16[128,1024]{1,0:T(8,128)(2,1)S(1)}, bf16[128,1024]{1,0:T(8,128)(2,1)S(1)}, u32[]{:S(2)}, u32[]{:S(2)}) collective-permute-start(bf16[128,1024]{1,0:T(8,128)(2,1)S(1)} %collective-permute-done.1), channel_id=1, source_target_pairs={{128,32},{160,64},{192,96},{224,0},{129,33},{161,65},{193,97},{225... | collective-permute-start | bytes 786440 | tf_op jit(solution)/shard_map/ppermute | solution.py:209
  26.9 0.1 collective-permute-start.8
  27.0 3.2 %collective-permute-start.9 = (bf16[896,512]{1,0:T(8,128)(2,1)S(1)}, bf16[896,512]{1,0:T(8,128)(2,1)S(1)}, u32[]{:S(2)}, u32[]{:S(2)}) collective-permute-start(bf16[896,512]{1,0:T(8,128)(2,1)S(1)} %collective-permute-done.3.right_on), channel_id=1, source_target_pairs={{0,3},{1,0},{2,1},{3,2},{4,7},{5,4},{6,5},{7,6},{8,11},{9,8},{10,9... | collective-permute-start | bytes 2752520 | tf_op jit(solution)/shard_map/ppermute | solution.py:52
  30.2 4.9 %collective-permute-done.4 = bf16[128,1024]{1,0:T(8,128)(2,1)S(1)} collective-permute-done((bf16[128,1024]{1,0:T(8,128)(2,1)S(1)}, bf16[128,1024]{1,0:T(8,128)(2,1)S(1)}, u32[]{:S(2)}, u32[]{:S(2)}) %collective-permute-start.4) | collective-permute-done | bytes 262176 | tf_op jit(solution)/shard_map/ppermute | solution.py:209
  35.1 1.3 %collective-permute-start.5 = (bf16[128,1024]{1,0:T(8,128)(2,1)S(1)}, bf16[128,1024]{1,0:T(8,128)(2,1)S(1)}, u32[]{:S(2)}, u32[]{:S(2)}) collective-permute-start(bf16[128,1024]{1,0:T(8,128)(2,1)S(1)} %collective-permute-done.1), channel_id=1, source_target_pairs={{128,0},{160,32},{192,64},{224,96},{129,1},{161,33},{193,65},{225,... | collective-permute-start | bytes 786440 | tf_op jit(solution)/shard_map/ppermute | solution.py:209
  36.4 2.1 %collective-permute-done.5 = bf16[128,1024]{1,0:T(8,128)(2,1)S(1)} collective-permute-done((bf16[128,1024]{1,0:T(8,128)(2,1)S(1)}, bf16[128,1024]{1,0:T(8,128)(2,1)S(1)}, u32[]{:S(2)}, u32[]{:S(2)}) %collective-permute-start.5) | collective-permute-done | bytes 262176 | tf_op jit(solution)/shard_map/ppermute | solution.py:209
  38.5 0.1 pad_maximum_fusion.rel_ref
  38.6 0.6 shard_map.71
  39.3 0.4 collective-permute-start.10
  39.7 0.0 collective-permute-done.6.left_ref
  39.7 0.6 collective-permute-start.11
  40.3 2.6 %collective-permute-start.12 = (bf16[256,512]{1,0:T(8,128)(2,1)S(1)}, bf16[256,512]{1,0:T(8,128)(2,1)S(1)}, u32[]{:S(2)}, u32[]{:S(2)}) collective-permute-start(bf16[256,512]{1,0:T(8,128)(2,1)S(1)} %get-tuple-element.60), channel_id=1, source_target_pairs={{0,3},{1,0},{2,1},{3,2},{4,7},{5,4},{6,5},{7,6},{8,11},{9,8},{10,9... | collective-permute-start | bytes 786440 | tf_op jit(solution)/shard_map/ppermute | solution.py:52
  42.9 2.9 %shard_map.70.acc_ref = f32[1024,1024]{1,0:T(8,128)S(1)} custom-call(bf16[896,512]{1,0:T(8,128)(2,1)S(1)} %get-tuple-element.48.mine_on, bf16[1280,512]{1,0:T(8,128)(2,1)S(1)} %get-tuple-element.55.mine_ref, bf16[768,512]{1,0:T(8,128)(2,1)S(1)} %get-tuple-element.53.own_ref, bf16[896,512]{1,0:T(8,128)(2,1)S(1)} %collective-permute-done.2.left_on, ...), custom_call_target="tpu_custom_call" | custom-call | flops 2415919104 | bytes 12582912 | tf_op jit(solution)/shard_map/pallas_call | solution.py:64
  45.8 1.5 %collective-permute-done.10.two_last = bf16[256,512]{1,0:T(8,128)(2,1)S(1)} collective-permute-done((bf16[256,512]{1,0:T(8,128)(2,1)S(1)}, bf16[256,512]{1,0:T(8,128)(2,1)S(1)}, u32[]{:S(2)}, u32[]{:S(2)}) %collective-permute-start.10) | collective-permute-done | bytes 262176 | tf_op jit(solution)/shard_map/ppermute | solution.py:52
  47.4 2.7 %collective-permute-done.11.left_last = bf16[256,512]{1,0:T(8,128)(2,1)S(1)} collective-permute-done((bf16[256,512]{1,0:T(8,128)(2,1)S(1)}, bf16[256,512]{1,0:T(8,128)(2,1)S(1)}, u32[]{:S(2)}, u32[]{:S(2)}) %collective-permute-start.11) | collective-permute-done | bytes 262176 | tf_op jit(solution)/shard_map/ppermute | solution.py:52
  50.1 1.5 %shard_map.72 = (f32[1024,128]{1,0:T(8,128)S(1)}, f32[1040,128]{1,0:T(8,128)S(1)}, f32[1040,128]{1,0:T(8,128)S(1)}, f32[1040,128]{1,0:T(8,128)S(1)}) custom-call(f32[1024,1024]{1,0:T(8,128)S(1)} %shard_map.70.acc_ref, bf16[896,512]{1,0:T(8,128)(2,1)S(1)} %get-tuple-element.48.mine_on, bf16[1280,512]{1,0:T(8,128)(2,1)S(1)} %get-tuple-element.55.mine_ref, ...), custom_call_target="tpu_custom_call" | custom-call | flops 939524096 | bytes 8388608 | tf_op jit(solution)/shard_map/pallas_call | solution.py:64
  51.6 1.3 %collective-permute-start.13 = (f16[1040,128]{1,0:T(8,128)(2,1)S(1)}, f16[1040,128]{1,0:T(8,128)(2,1)S(1)}, u32[]{:S(2)}, u32[]{:S(2)}) collective-permute-start(f16[1040,128]{1,0:T(8,128)(2,1)S(1)} %convert_element_type.42), channel_id=1, source_target_pairs={{0,8},{1,9},{2,10},{3,11},{4,12},{5,13},{6,14},{7,15},{8,0},{9,1},... | collective-permute-start | bytes 798728 | tf_op jit(solution)/shard_map/ppermute | solution.py:52
  53.0 2.3 %collective-permute-start.14 = (f16[1040,128]{1,0:T(8,128)(2,1)S(1)}, f16[1040,128]{1,0:T(8,128)(2,1)S(1)}, u32[]{:S(2)}, u32[]{:S(2)}) collective-permute-start(f16[1040,128]{1,0:T(8,128)(2,1)S(1)} %convert_element_type.43), channel_id=1, source_target_pairs={{0,4},{1,5},{2,6},{3,7},{4,8},{5,9},{6,10},{7,11},{8,12},{9,13},{1... | collective-permute-start | bytes 798728 | tf_op jit(solution)/shard_map/ppermute | solution.py:52
  55.3 0.1 collective-permute-start.15
  55.3 1.5 %shard_map.74 = (f32[1024,128]{1,0:T(8,128)S(1)}, f32[1040,128]{1,0:T(8,128)S(1)}, f32[1040,128]{1,0:T(8,128)S(1)}, f32[1040,128]{1,0:T(8,128)S(1)}) custom-call(f32[1024,1024]{1,0:T(8,128)S(1)} %shard_map.70.acc_ref, bf16[896,512]{1,0:T(8,128)(2,1)S(1)} %get-tuple-element.48.mine_on, bf16[1280,512]{1,0:T(8,128)(2,1)S(1)} %get-tuple-element.55.mine_ref, ...), custom_call_target="tpu_custom_call" | custom-call | flops 939524096 | bytes 8388608 | tf_op jit(solution)/shard_map/pallas_call | solution.py:64
  57.0 2.6 %collective-permute-done.13 = f16[1040,128]{1,0:T(8,128)(2,1)S(1)} collective-permute-done((f16[1040,128]{1,0:T(8,128)(2,1)S(1)}, f16[1040,128]{1,0:T(8,128)(2,1)S(1)}, u32[]{:S(2)}, u32[]{:S(2)}) %collective-permute-start.13) | collective-permute-done | bytes 266272 | tf_op jit(solution)/shard_map/ppermute | solution.py:52
  59.6 1.9 %collective-permute-done.14 = f16[1040,128]{1,0:T(8,128)(2,1)S(1)} collective-permute-done((f16[1040,128]{1,0:T(8,128)(2,1)S(1)}, f16[1040,128]{1,0:T(8,128)(2,1)S(1)}, u32[]{:S(2)}, u32[]{:S(2)}) %collective-permute-start.14) | collective-permute-done | bytes 266272 | tf_op jit(solution)/shard_map/ppermute | solution.py:52
  61.5 1.4 %collective-permute-done.15 = f16[1040,128]{1,0:T(8,128)(2,1)S(1)} collective-permute-done((f16[1040,128]{1,0:T(8,128)(2,1)S(1)}, f16[1040,128]{1,0:T(8,128)(2,1)S(1)}, u32[]{:S(2)}, u32[]{:S(2)}) %collective-permute-start.15) | collective-permute-done | bytes 266272 | tf_op jit(solution)/shard_map/ppermute | solution.py:52
  63.1 0.3 shard_map.75
  63.4 6.5 %collective-permute-start.16 = (f16[1040,128]{1,0:T(8,128)(2,1)S(1)}, f16[1040,128]{1,0:T(8,128)(2,1)S(1)}, u32[]{:S(2)}, u32[]{:S(2)}) collective-permute-start(f16[1040,128]{1,0:T(8,128)(2,1)S(1)} %convert_element_type.48), channel_id=1, source_target_pairs={{0,16},{16,0},{1,17},{17,1},{2,18},{18,2},{3,19},{19,3},{4,20},{20... | collective-permute-start | bytes 798728 | tf_op jit(solution)/shard_map/ppermute | solution.py:271
  69.9 0.9 %collective-permute-start.17 = (f16[1040,128]{1,0:T(8,128)(2,1)S(1)}, f16[1040,128]{1,0:T(8,128)(2,1)S(1)}, u32[]{:S(2)}, u32[]{:S(2)}) collective-permute-start(f16[1040,128]{1,0:T(8,128)(2,1)S(1)} %convert_element_type.50), channel_id=1, source_target_pairs={{0,8},{1,9},{2,10},{3,11},{4,12},{5,13},{6,14},{7,15},{8,0},{9,1},... | collective-permute-start | bytes 798728 | tf_op jit(solution)/shard_map/ppermute | solution.py:52
  70.8 1.5 %collective-permute-start.18 = (f16[1040,128]{1,0:T(8,128)(2,1)S(1)}, f16[1040,128]{1,0:T(8,128)(2,1)S(1)}, u32[]{:S(2)}, u32[]{:S(2)}) collective-permute-start(f16[1040,128]{1,0:T(8,128)(2,1)S(1)} %convert_element_type.49), channel_id=1, source_target_pairs={{0,4},{1,5},{2,6},{3,7},{4,8},{5,9},{6,10},{7,11},{8,12},{9,13},{1... | collective-permute-start | bytes 798728 | tf_op jit(solution)/shard_map/ppermute | solution.py:52
  72.3 0.5 collective-permute-start.19
  72.8 3.7 %shard_map.73 = f32[128,1024]{1,0:T(8,128)} custom-call(bf16[4,128,1024]{2,1,0:T(8,128)(2,1)S(1)} %pad_maximum_fusion.rel_ref, f32[128,1024]{1,0:T(8,128)S(1)} %get-tuple-element.73.first_ref, bf16[1024,4096]{1,0:T(8,128)(2,1)S(1)} %bitcast.12), custom_call_target="tpu_custom_call" | custom-call | flops 1073741824 | bytes 2097152 | tf_op jit(solution)/shard_map/pallas_call | solution.py:64
  76.5 1.6 %collective-permute-done.16 = f16[1040,128]{1,0:T(8,128)(2,1)S(1)} collective-permute-done((f16[1040,128]{1,0:T(8,128)(2,1)S(1)}, f16[1040,128]{1,0:T(8,128)(2,1)S(1)}, u32[]{:S(2)}, u32[]{:S(2)}) %collective-permute-start.16) | collective-permute-done | bytes 266272 | tf_op jit(solution)/shard_map/ppermute | solution.py:271
  78.1 0.0 collective-permute-done.17
  78.2 0.0 collective-permute-done.18
  78.2 2.4 %collective-permute-done.19 = f16[1040,128]{1,0:T(8,128)(2,1)S(1)} collective-permute-done((f16[1040,128]{1,0:T(8,128)(2,1)S(1)}, f16[1040,128]{1,0:T(8,128)(2,1)S(1)}, u32[]{:S(2)}, u32[]{:S(2)}) %collective-permute-start.19) | collective-permute-done | bytes 266272 | tf_op jit(solution)/shard_map/ppermute | solution.py:52
  80.7 1.0 %shard_map.76 = f32[1024,128]{1,0:T(8,128)} custom-call(f32[1024,128]{1,0:T(8,128)S(1)} %get-tuple-element.74.keep_ref, f32[1040,128]{1,0:T(8,128)S(1)} %convert_element_type.52.rest_0_, f32[1040,128]{1,0:T(8,128)S(1)} %convert_element_type.53.rest_1_, f32[1040,128]{1,0:T(8,128)S(1)} %convert_element_type.54.rest_2_, ...), custom_call_target="tpu_custom_call" | custom-call | bytes 4194304 | tf_op jit(solution)/shard_map/pallas_call | solution.py:64
  (24 shorter events, 0.5 us)
Async XLA Ops:
  0.6 6.1 %slice-start = ((s8[8388608]{0:T(1024)(128)(4,1)}), s8[4194304]{0:T(1024)(128)(4,1)S(1)}, s32[]{:S(2)}) async-start(s8[8388608]{0:T(1024)(128)(4,1)} %bitcast.9), calls=%async_computation | async-start | bytes 8388608
  0.6 6.1 %slice-start.1 = ((s8[8388608]{0:T(1024)(128)(4,1)}), s8[4194304]{0:T(1024)(128)(4,1)S(1)}, s32[]{:S(2)}) async-start(s8[8388608]{0:T(1024)(128)(4,1)} %bitcast.9), calls=%async_computation.1 | async-start | bytes 8388608
  0.7 6.1 %copy-start = (bf16[128,4096]{1,0:T(8,128)(2,1)S(1)}, bf16[128,4096]{1,0:T(8,128)(2,1)}, u32[]{:S(2)}) copy-start(bf16[128,4096]{1,0:T(8,128)(2,1)} %head_ref.1) | copy-start | bytes 3145732
  3.4 22.2 %collective-permute-start.2 = (bf16[896,512]{1,0:T(8,128)(2,1)S(1)}, bf16[896,512]{1,0:T(8,128)(2,1)S(1)}, u32[]{:S(2)}, u32[]{:S(2)}) collective-permute-start(bf16[896,512]{1,0:T(8,128)(2,1)S(1)} %get-tuple-element.48.mine_on), channel_id=1, source_target_pairs={{0,1},{1,2},{2,3},{3,0},{4,5},{5,6},{6,7},{7,4},{8,9},{9,10},{10,1... | collective-permute-start | bytes 2752520 | tf_op jit(solution)/shard_map/ppermute | solution.py:52
  5.0 20.6 %collective-permute-start.3 = (bf16[896,512]{1,0:T(8,128)(2,1)S(1)}, bf16[896,512]{1,0:T(8,128)(2,1)S(1)}, u32[]{:S(2)}, u32[]{:S(2)}) collective-permute-start(bf16[896,512]{1,0:T(8,128)(2,1)S(1)} %get-tuple-element.49), channel_id=1, source_target_pairs={{0,3},{1,0},{2,1},{3,2},{4,7},{5,4},{6,5},{7,6},{8,11},{9,8},{10,9... | collective-permute-start | bytes 2752520 | tf_op jit(solution)/shard_map/ppermute | solution.py:52
  9.6 3.4 %collective-permute-start = (bf16[128,1024]{1,0:T(8,128)(2,1)S(1)}, bf16[128,1024]{1,0:T(8,128)(2,1)S(1)}, u32[]{:S(2)}, u32[]{:S(2)}) collective-permute-start(bf16[128,1024]{1,0:T(8,128)(2,1)S(1)} %get-tuple-element.46), channel_id=1, source_target_pairs={{128,0},{129,1},{130,2},{131,3},{132,4},{133,5},{134,6},{135,7},{1... | collective-permute-start | bytes 786440 | tf_op jit(solution)/shard_map/ppermute | solution.py:230
  13.0 26.7 %collective-permute-start.6 = (bf16[1280,512]{1,0:T(8,128)(2,1)S(1)}, bf16[1280,512]{1,0:T(8,128)(2,1)S(1)}, u32[]{:S(2)}, u32[]{:S(2)}) collective-permute-start(bf16[1280,512]{1,0:T(8,128)(2,1)S(1)} %get-tuple-element.55.mine_ref), channel_id=1, source_target_pairs={{0,1},{1,2},{2,3},{3,0},{4,5},{5,6},{6,7},{7,4},{8,9},{9,10},{10,1... | collective-permute-start | bytes 3932168 | tf_op jit(solution)/shard_map/ppermute | solution.py:52
  13.4 26.9 %collective-permute-start.7 = (bf16[1280,512]{1,0:T(8,128)(2,1)S(1)}, bf16[1280,512]{1,0:T(8,128)(2,1)S(1)}, u32[]{:S(2)}, u32[]{:S(2)}) collective-permute-start(bf16[1280,512]{1,0:T(8,128)(2,1)S(1)} %get-tuple-element.57), channel_id=1, source_target_pairs={{0,3},{1,0},{2,1},{3,2},{4,7},{5,4},{6,5},{7,6},{8,11},{9,8},{10,9... | collective-permute-start | bytes 3932168 | tf_op jit(solution)/shard_map/ppermute | solution.py:52
  16.4 9.3 %collective-permute-start.1 = (bf16[128,1024]{1,0:T(8,128)(2,1)S(1)}, bf16[128,1024]{1,0:T(8,128)(2,1)S(1)}, u32[]{:S(2)}, u32[]{:S(2)}) collective-permute-start(bf16[128,1024]{1,0:T(8,128)(2,1)S(1)} %add.3), channel_id=1, source_target_pairs={{0,96},{32,0},{64,32},{96,64},{128,160},{160,192},{192,224},{224,1... | collective-permute-start | bytes 786440 | tf_op jit(solution)/shard_map/ppermute | solution.py:209
  25.6 9.5 %collective-permute-start.4 = (bf16[128,1024]{1,0:T(8,128)(2,1)S(1)}, bf16[128,1024]{1,0:T(8,128)(2,1)S(1)}, u32[]{:S(2)}, u32[]{:S(2)}) collective-permute-start(bf16[128,1024]{1,0:T(8,128)(2,1)S(1)} %collective-permute-done.1), channel_id=1, source_target_pairs={{128,32},{160,64},{192,96},{224,0},{129,33},{161,65},{193,97},{225... | collective-permute-start | bytes 786440 | tf_op jit(solution)/shard_map/ppermute | solution.py:209
  26.9 23.2 %collective-permute-start.8 = (bf16[896,512]{1,0:T(8,128)(2,1)S(1)}, bf16[896,512]{1,0:T(8,128)(2,1)S(1)}, u32[]{:S(2)}, u32[]{:S(2)}) collective-permute-start(bf16[896,512]{1,0:T(8,128)(2,1)S(1)} %collective-permute-done.2.left_on), channel_id=1, source_target_pairs={{0,1},{1,2},{2,3},{3,0},{4,5},{5,6},{6,7},{7,4},{8,9},{9,10},{10,1... | collective-permute-start | bytes 2752520 | tf_op jit(solution)/shard_map/ppermute | solution.py:52
  27.0 23.1 %collective-permute-start.9 = (bf16[896,512]{1,0:T(8,128)(2,1)S(1)}, bf16[896,512]{1,0:T(8,128)(2,1)S(1)}, u32[]{:S(2)}, u32[]{:S(2)}) collective-permute-start(bf16[896,512]{1,0:T(8,128)(2,1)S(1)} %collective-permute-done.3.right_on), channel_id=1, source_target_pairs={{0,3},{1,0},{2,1},{3,2},{4,7},{5,4},{6,5},{7,6},{8,11},{9,8},{10,9... | collective-permute-start | bytes 2752520 | tf_op jit(solution)/shard_map/ppermute | solution.py:52
  35.1 3.4 %collective-permute-start.5 = (bf16[128,1024]{1,0:T(8,128)(2,1)S(1)}, bf16[128,1024]{1,0:T(8,128)(2,1)S(1)}, u32[]{:S(2)}, u32[]{:S(2)}) collective-permute-start(bf16[128,1024]{1,0:T(8,128)(2,1)S(1)} %collective-permute-done.1), channel_id=1, source_target_pairs={{128,0},{160,32},{192,64},{224,96},{129,1},{161,33},{193,65},{225,... | collective-permute-start | bytes 786440 | tf_op jit(solution)/shard_map/ppermute | solution.py:209
  39.3 8.1 %collective-permute-start.10 = (bf16[256,512]{1,0:T(8,128)(2,1)S(1)}, bf16[256,512]{1,0:T(8,128)(2,1)S(1)}, u32[]{:S(2)}, u32[]{:S(2)}) collective-permute-start(bf16[256,512]{1,0:T(8,128)(2,1)S(1)} %get-tuple-element.58), channel_id=1, source_target_pairs={{0,2},{1,3},{2,0},{3,1},{4,6},{5,7},{6,4},{7,5},{8,10},{9,11},{10,... | collective-permute-start | bytes 786440 | tf_op jit(solution)/shard_map/ppermute | solution.py:52
  39.7 10.4 %collective-permute-start.11 = (bf16[256,512]{1,0:T(8,128)(2,1)S(1)}, bf16[256,512]{1,0:T(8,128)(2,1)S(1)}, u32[]{:S(2)}, u32[]{:S(2)}) collective-permute-start(bf16[256,512]{1,0:T(8,128)(2,1)S(1)} %get-tuple-element.59), channel_id=1, source_target_pairs={{0,1},{1,2},{2,3},{3,0},{4,5},{5,6},{6,7},{7,4},{8,9},{9,10},{10,1... | collective-permute-start | bytes 786440 | tf_op jit(solution)/shard_map/ppermute | solution.py:52
  40.3 9.8 %collective-permute-start.12 = (bf16[256,512]{1,0:T(8,128)(2,1)S(1)}, bf16[256,512]{1,0:T(8,128)(2,1)S(1)}, u32[]{:S(2)}, u32[]{:S(2)}) collective-permute-start(bf16[256,512]{1,0:T(8,128)(2,1)S(1)} %get-tuple-element.60), channel_id=1, source_target_pairs={{0,3},{1,0},{2,1},{3,2},{4,7},{5,4},{6,5},{7,6},{8,11},{9,8},{10,9... | collective-permute-start | bytes 786440 | tf_op jit(solution)/shard_map/ppermute | solution.py:52
  51.6 8.0 %collective-permute-start.13 = (f16[1040,128]{1,0:T(8,128)(2,1)S(1)}, f16[1040,128]{1,0:T(8,128)(2,1)S(1)}, u32[]{:S(2)}, u32[]{:S(2)}) collective-permute-start(f16[1040,128]{1,0:T(8,128)(2,1)S(1)} %convert_element_type.42), channel_id=1, source_target_pairs={{0,8},{1,9},{2,10},{3,11},{4,12},{5,13},{6,14},{7,15},{8,0},{9,1},... | collective-permute-start | bytes 798728 | tf_op jit(solution)/shard_map/ppermute | solution.py:52
  53.0 8.6 %collective-permute-start.14 = (f16[1040,128]{1,0:T(8,128)(2,1)S(1)}, f16[1040,128]{1,0:T(8,128)(2,1)S(1)}, u32[]{:S(2)}, u32[]{:S(2)}) collective-permute-start(f16[1040,128]{1,0:T(8,128)(2,1)S(1)} %convert_element_type.43), channel_id=1, source_target_pairs={{0,4},{1,5},{2,6},{3,7},{4,8},{5,9},{6,10},{7,11},{8,12},{9,13},{1... | collective-permute-start | bytes 798728 | tf_op jit(solution)/shard_map/ppermute | solution.py:52
  55.3 7.7 %collective-permute-start.15 = (f16[1040,128]{1,0:T(8,128)(2,1)S(1)}, f16[1040,128]{1,0:T(8,128)(2,1)S(1)}, u32[]{:S(2)}, u32[]{:S(2)}) collective-permute-start(f16[1040,128]{1,0:T(8,128)(2,1)S(1)} %convert_element_type.44), channel_id=1, source_target_pairs={{0,12},{1,13},{2,14},{3,15},{4,0},{5,1},{6,2},{7,3},{8,4},{9,5},{1... | collective-permute-start | bytes 798728 | tf_op jit(solution)/shard_map/ppermute | solution.py:52
  63.4 14.7 %collective-permute-start.16 = (f16[1040,128]{1,0:T(8,128)(2,1)S(1)}, f16[1040,128]{1,0:T(8,128)(2,1)S(1)}, u32[]{:S(2)}, u32[]{:S(2)}) collective-permute-start(f16[1040,128]{1,0:T(8,128)(2,1)S(1)} %convert_element_type.48), channel_id=1, source_target_pairs={{0,16},{16,0},{1,17},{17,1},{2,18},{18,2},{3,19},{19,3},{4,20},{20... | collective-permute-start | bytes 798728 | tf_op jit(solution)/shard_map/ppermute | solution.py:271
  69.9 8.2 %collective-permute-start.17 = (f16[1040,128]{1,0:T(8,128)(2,1)S(1)}, f16[1040,128]{1,0:T(8,128)(2,1)S(1)}, u32[]{:S(2)}, u32[]{:S(2)}) collective-permute-start(f16[1040,128]{1,0:T(8,128)(2,1)S(1)} %convert_element_type.50), channel_id=1, source_target_pairs={{0,8},{1,9},{2,10},{3,11},{4,12},{5,13},{6,14},{7,15},{8,0},{9,1},... | collective-permute-start | bytes 798728 | tf_op jit(solution)/shard_map/ppermute | solution.py:52
  70.8 7.4 %collective-permute-start.18 = (f16[1040,128]{1,0:T(8,128)(2,1)S(1)}, f16[1040,128]{1,0:T(8,128)(2,1)S(1)}, u32[]{:S(2)}, u32[]{:S(2)}) collective-permute-start(f16[1040,128]{1,0:T(8,128)(2,1)S(1)} %convert_element_type.49), channel_id=1, source_target_pairs={{0,4},{1,5},{2,6},{3,7},{4,8},{5,9},{6,10},{7,11},{8,12},{9,13},{1... | collective-permute-start | bytes 798728 | tf_op jit(solution)/shard_map/ppermute | solution.py:52
  72.3 8.4 %collective-permute-start.19 = (f16[1040,128]{1,0:T(8,128)(2,1)S(1)}, f16[1040,128]{1,0:T(8,128)(2,1)S(1)}, u32[]{:S(2)}, u32[]{:S(2)}) collective-permute-start(f16[1040,128]{1,0:T(8,128)(2,1)S(1)} %convert_element_type.51), channel_id=1, source_target_pairs={{0,12},{1,13},{2,14},{3,15},{4,0},{5,1},{6,2},{7,3},{8,4},{9,5},{1... | collective-permute-start | bytes 798728 | tf_op jit(solution)/shard_map/ppermute | solution.py:52

commit v15 on v14

--- a/solution.py
+++ b/solution.py
@@ -75,7 +75,8 @@
 CONTRACT_LAST = (((1,), (1,)), ((), ()))
 
 
-def entry_kernel(pending_ref, x_ref, stash_ref, right_on, left_on, right_ref, left_ref, own_ref, x_in, stash_in, count_in, sems):
+def entry_kernel(pending_ref, x_ref, stash_ref, right_on, left_on, right_ref, left_ref, right_near, left_near, own_ref,
+                 x_in, stash_in, count_in, sems):
     micro, rows, width = x_ref.shape
     half, depth = width // 2, (micro - 1) * rows
     pieces = [(pending_ref, count_in), (x_ref, x_in)]
@@ -96,8 +97,9 @@
     for z in range(2):
         at = half + z * share
         plans += [(right_on, at, z, 2, 0, share), (left_on, at, z, 2, share, depth)]
-        at = half + z * depth
-        plans += [(right_ref, at, z, 1, 0, depth), (left_ref, at, z, RING - 1, 0, depth), (own_ref, z * depth, z, 0, 0, depth)]
+        beside, at = ((right_near, left_near), 0) if z == 0 else ((right_ref, left_ref), half)
+        plans += [(out, at, z, along, 0, depth) for out, along in zip(beside, (1, RING - 1))]
+        plans += [(own_ref, z * depth, z, 0, 0, depth)]
     for m in range(micro - 1):
         copies[2 + m].wait()
         for out, base, z, along, begin, end in plans:
@@ -129,40 +131,44 @@
         out_ref[:, i:i + step] = jnp.where(on_last(), first_ref[:, i:i + step], total)
 
 
-def pack_last_kernel(head_ref, rel_ref, right_ref, left_ref, own_ref, two_ref):
+def pack_last_kernel(head_ref, rel_ref, right_in, left_in, right_ref, left_ref, own_ref, two_ref, right_near, left_near):
     tensor = lax.axis_index("z_lo")
-    rows, share = rel_ref.shape[1], rel_ref.shape[2]
+    rows, share, depth = rel_ref.shape[1], rel_ref.shape[2], right_in.shape[0]
+    right_near[:depth, :] = right_in[...]
+    left_near[:depth, :] = left_in[...]
     for z in range(2):
+        (right, left), base = ((right_near, left_near), depth) if z == 0 else ((right_ref, left_ref), 0)
         for b in range(RING):
-            for out, along in ((right_ref, 1), (left_ref, RING - 1), (own_ref, 0), (two_ref, 2)):
+            for out, top, along in ((right, base, 1), (left, base, RING - 1), (own_ref, z * rows, 0), (two_ref, z * rows, 2)):
                 at = block_start(z, along, b)
                 inner = pl.multiple_of(lax.rem(at, share), LANES)
                 chained = rel_ref[lax.rem(tensor - lax.div(at, share) + RING, RING), :, pl.ds(inner, LANES)]
                 last = jnp.where(on_last(), head_ref[:, pl.ds(at, LANES)], chained)
-                out[z * rows:(z + 1) * rows, b * LANES:(b + 1) * LANES] = last
-
-
-def early_kernel(mine_on, mine_ref, own_ref, left_on, left_ref, right_on, right_ref, acc_ref):
+                out[top:top + rows, b * LANES:(b + 1) * LANES] = last
+
+
+def early_kernel(z, mine_on, mine_ref, own_ref, left_on, left_ref, right_on, right_ref, left_cols, right_cols, acc_ref):
     width, depth = acc_ref.shape[0], own_ref.shape[0] // 2
-    half, lanes = width // 2, acc_ref.shape[1] // 2
+    half = width // 2
     sides = [(mine_on, mine_ref), (left_on, left_ref), (right_ref, right_on)]
+    at = half if z else 0
+    rhs = [own_ref[z * depth:(z + 1) * depth, :], left_cols[at:at + depth, :], right_cols[at:at + depth, :]]
+    rhs = jnp.concatenate(rhs, axis=0)
     for r in range(2):
         lhs = jnp.concatenate([side[r][:half, :depth] for side in sides], axis=1)
-        for z in range(2):
-            at = half + z * depth
-            rhs = [own_ref[z * depth:(z + 1) * depth, :], left_ref[at:at + depth, :], right_ref[at:at + depth, :]]
-            rhs = jnp.concatenate(rhs, axis=0)
-            acc_ref[r * half:(r + 1) * half, z * lanes:(z + 1) * lanes] = jnp.dot(lhs, rhs, preferred_element_type=F32)
+        acc_ref[r * half:(r + 1) * half, :] = jnp.dot(lhs, rhs, preferred_element_type=F32)
 
 
 def late_kernel(z, acc_ref, mine_on, mine_ref, left_on, left_ref, right_on, right_ref, upper_ref, lower_ref,
-                two_last, left_last, right_last, own_last, keep_ref, *rest):
+                two_last, own_last, left_last, right_last, keep_ref, *rest):
     sends, sum_ref = rest[:-1], rest[-1]
     width, rows = acc_ref.shape[0], own_last.shape[0] // 2
-    half, lanes = width // 2, acc_ref.shape[1] // 2
+    half, lanes = width // 2, acc_ref.shape[1]
     depth = mine_ref.shape[1] - rows
     mine, left, right, far = (mine_on, mine_ref), (left_on, left_ref), (right_ref, right_on), (upper_ref, lower_ref)
-    rhs = [ref[z * rows:(z + 1) * rows, :] for ref in (own_last, left_last, right_last, two_last)]
+    rhs = [own_last[z * rows:(z + 1) * rows, :]]
+    rhs += [ref[ref.shape[0] - rows:, :] for ref in (left_last, right_last)]
+    rhs += [two_last[z * rows:(z + 1) * rows, :]]
     at = half + z * depth // 2
     rhs += [ref[at:at + depth // 2, :] for ref in far]
     rhs = jnp.concatenate(rhs, axis=0)
@@ -170,7 +176,7 @@
     for r in range(2):
         lhs = [side[r][:half, depth:] for side in (mine, left, right, far)] + [far[r][:half, :depth]]
         total = jnp.dot(jnp.concatenate(lhs, axis=1), rhs, preferred_element_type=F32)
-        total = total + acc_ref[r * half:(r + 1) * half, z * lanes:(z + 1) * lanes]
+        total = total + acc_ref[r * half:(r + 1) * half, :]
         largest = jnp.maximum(largest, jnp.max(jnp.abs(total), axis=0, keepdims=True))
         sum_ref[r * half:(r + 1) * half, :] = total
     power = jnp.ceil(jnp.log2(jnp.max(largest, axis=1, keepdims=True))) - TOP
@@ -216,9 +222,9 @@
     columns = head_grad.shape[1]
     matmul = dict(flops=2 * rows * width * columns, moved=2 * 2**20)
 
-    going, staying = ((half + depth, lanes), BF16), ((half + 2 * depth, lanes), BF16)
-    right_on, left_on, right, left, own = call(
-        entry_kernel, [going, going, staying, staying, ((2 * depth, lanes), BF16)],
+    going, cols = ((half + depth, lanes), BF16), ((depth, lanes), BF16)
+    right_on, left_on, right, left, near_right, near_left, own = call(
+        entry_kernel, [going] * 4 + [cols] * 2 + [((2 * depth, lanes), BF16)],
         [in_hbm(v) for v in (pending, inputs, grads)], [pl.BlockSpec(memory_space=pltpu.HBM)] * 3,
         scratch=[pltpu.VMEM(inputs.shape, BF16), pltpu.VMEM(grads.shape, BF16), pltpu.SMEM(pending.shape, pending.dtype),
                  pltpu.SemaphoreType.DMA((micro + 6,))],
@@ -242,32 +248,43 @@
     rel = [shard, behind, behind_two, passed]
     rel = jnp.stack(rel, 0)
 
-    edge = ((2 * rows, lanes), BF16)
-    last_right, last_left, last_own, last_two = call(
-        pack_last_kernel, [edge] * 4, (head_grad, rel), whole(2), moved=4 * 2**20
+    edge, both_halves, behind_cols = [((n, lanes), BF16) for n in (rows, 2 * rows, micro * rows)]
+    last_right, last_left, last_own, last_two, near_right, near_left = call(
+        pack_last_kernel, [edge] * 2 + [both_halves] * 2 + [behind_cols] * 2, (head_grad, rel, near_right, near_left), whole(4),
+        moved=6 * 2**20,
     )
-    last = [shifted(last_two, True, 2), shifted(last_right, True, 1), shifted(last_left, True, -1), last_own]
-    (acc,) = call(
-        early_kernel, [((width, 2 * lanes), F32)], (right_on, right, own, from_left_on, from_left, from_right_on, from_right), whole(7),
-        flops=2 * width * 2 * lanes * 3 * depth, moved=12 * 2**20,
+    last = [shifted(last_two, True, 2), shifted(last_right, True, 1), shifted(last_left, True, -1)]
+    held = (right_on, right, own, from_left_on, from_left, from_right_on, from_right)
+
+    def early(z, *columns):
+        return call(
+            functools.partial(early_kernel, z), [((width, lanes), F32)], (*held, *columns), whole(9),
+            flops=2 * width * lanes * 3 * depth, moved=8 * 2**20,
+        )[0]
+
+    acc = early(1, from_left, from_right)
+    acc, upper, lower, near_right, near_left, *last = lax.optimization_barrier(
+        (acc, upper, lower, near_right, near_left, *last)
     )
-    acc, upper, lower, *last = lax.optimization_barrier((acc, upper, lower, *last))
+    two, last_from_left, last_from_right = last
+    near_from_left, near_from_right = shifted(near_right, True, 1), shifted(near_left, True, -1)
     send = ((width + TAIL, LANES), F32)
 
-    def late(z):
+    def late(z, acc, *columns):
         return call(
             functools.partial(late_kernel, z), [((width, LANES), F32)] + [send] * 3,
-            (acc, right_on, right, from_left_on, from_left, from_right_on, from_right, upper, lower, *last), whole(13),
+            (acc, right_on, right, *held[3:], upper, lower, two, last_own, *columns), whole(13),
             scratch=[pltpu.VMEM((width, lanes), F32)],
             flops=2 * width * lanes * (3 * rows + micro * rows), moved=8 * 2**20,
         )
 
-    keep_far, *far_sends = late(1)
-    keep_near, *near_sends = late(0)
+    keep_far, *far_sends = late(1, acc, last_from_left, last_from_right)
+    keep_near, *near_sends = late(0, early(0, near_from_left, near_from_right), near_from_left, near_from_right)
     got = [shifted(far_sends[b - 1].astype(F16), False, b) for b in (2, 1, 3)]
     rel, *got = lax.optimization_barrier((rel, *got))
     (far,) = call(far_kernel, [send], (keep_far, *[v.astype(F32) for v in got]), whole(4), moved=4 * 2**20)
-    far, *near_sends = lax.optimization_barrier((far.astype(F16), *[v.astype(F16) for v in near_sends]))
+    far = far.astype(F16)
+    _, *near_sends = lax.optimization_barrier((far, *[v.astype(F16) for v in near_sends]))
     other = lax.ppermute(far, "z_hi", [(0, 1), (1, 0)])
     (second,) = call(second_kernel, [((rows, width), F32)], (rel, first, weights[0]), whole(3), **matmul)
     got = [shifted(near_sends[b - 1], False, b).astype(F32) for b in (2, 1, 3)]

time: 81.9 us -> 85.3 us (1.042); the launches traced: 81.7 us -> 83.7 us
  starting transfers between devices: 35.1 us -> 39.5 us
  waiting for transfers between devices: 28 us -> 25.4 us
    ppermute x15 -> x17, starting transfers between devices: 20.1 us -> 25.3 us  [shifted(): return lax.ppermute(value, ('section', 'y', 'x'), pairs_over(along, by))]
    ppermute x3, waiting for transfers between devices: 11.6 us -> 7.6 us  [on_line(): return lax.ppermute(value, ('section', 'z_lo'), pairs)]
    ppermute x15 -> x17, waiting for transfers between devices: 12.7 us -> 15.7 us  [shifted(): return lax.ppermute(value, ('section', 'y', 'x'), pairs_over(along, by))]
    ppermute x1, waiting for transfers between devices: 1.6 us -> 0.01 us  [local(): other = lax.ppermute(far, 'z_hi', [(0, 1), (1, 0)])]
    pallas_call x9 -> x10, Pallas kernels: 17 us -> 17.1 us  [call(): pl.pallas_call(kernel, out_shape=[jax.ShapeDtypeStruct(s, t) for s, t in...]
  transfers between devices with their start and end apart: 20 -> 22, of which waited for: 11 -> 10; matrix products, arithmetic and copies ran while one was open for 1% -> 1% of each run, Pallas kernels for 14% -> 16%
where the time goes in v15:
time: 85.3 us; the launch traced here: 83.7 us
  starting transfers between devices  39.5 us (46%)
  waiting for transfers between devices  25.4 us (30%)
  Pallas kernels  17.1 us (20%)
  between operations  0.88 us (1%)
    ppermute x17, starting transfers between devices, shifted(): return lax.ppermute(value, ('section', 'y', 'x'), pairs_over(along, by))  25.3 us
    pallas_call x10, Pallas kernels, call(): pl.pallas_call(kernel, out_shape=[jax.ShapeDtypeStruct(s, t) for s, t in...  17.1 us
    ppermute x17, waiting for transfers between devices, shifted(): return lax.ppermute(value, ('section', 'y', 'x'), pairs_over(along, by))  15.7 us
    ppermute x3, waiting for transfers between devices, on_line(): return lax.ppermute(value, ('section', 'z_lo'), pairs)  7.6 us
    ppermute x3, starting transfers between devices, on_line(): return lax.ppermute(value, ('section', 'z_lo'), pairs)  7.26 us
    ppermute x1, starting transfers between devices, local(): other = lax.ppermute(far, 'z_hi', [(0, 1), (1, 0)])  5.65 us
    ppermute x1, waiting for transfers between devices, local(): shard = lax.ppermute(small, 'section', [(1, 0)])  2.13 us
  transfers between devices with their start and end apart: 22, of which 10 were waited for; matrix products, arithmetic and copies ran while one was open for 1% of the time, Pallas kernels for 16%

profile of v15, /device:TPU:24, one launch (start us, length us, event | category | flops | bytes accessed | tf_op | source)
XLA Modules:
  0.0 83.7 jit_solution(11200942648519038064)
XLA Ops:
  0.6 0.0 slice-start.1
  0.7 2.7 %shard_map.68 = (bf16[896,512]{1,0:T(8,128)(2,1)S(1)}, bf16[896,512]{1,0:T(8,128)(2,1)S(1)}, bf16[896,512]{1,0:T(8,128)(2,1)S(1)}, bf16[896,512]{1,0:T(8,128)(2,...) custom-call(s32[2]{0:T(128)} %pending_ref.1, ...), custom_call_target="tpu_custom_call" | custom-call | flops 10000000000 | bytes 12582912 | tf_op jit(solution)/shard_map/pallas_call | solution.py:64
  3.4 2.8 %collective-permute-start.3 = (bf16[896,512]{1,0:T(8,128)(2,1)S(1)}, bf16[896,512]{1,0:T(8,128)(2,1)S(1)}, u32[]{:S(2)}, u32[]{:S(2)}) collective-permute-start(bf16[896,512]{1,0:T(8,128)(2,1)S(1)} %get-tuple-element.53), channel_id=1, source_target_pairs={{0,3},{1,0},{2,1},{3,2},{4,7},{5,4},{6,5},{7,6},{8,11},{9,8},{10,9... | collective-permute-start | bytes 2752520 | tf_op jit(solution)/shard_map/ppermute | solution.py:52
  6.2 0.0 collective-permute-start.2
  6.3 2.9 %shard_map.69 = (f32[128,1024]{1,0:T(8,128)S(1)}, bf16[128,1024]{1,0:T(8,128)(2,1)S(1)}) custom-call(bf16[128,4096]{1,0:T(8,128)(2,1)S(1)} %copy-done, bf16[1024,4096]{1,0:T(8,128)(2,1)S(1)} %bitcast.11), custom_call_target="tpu_custom_call" | custom-call | flops 1073741824 | bytes 2097152 | tf_op jit(solution)/shard_map/pallas_call | solution.py:64
  9.1 1.3 %collective-permute-start = (bf16[128,1024]{1,0:T(8,128)(2,1)S(1)}, bf16[128,1024]{1,0:T(8,128)(2,1)S(1)}, u32[]{:S(2)}, u32[]{:S(2)}) collective-permute-start(bf16[128,1024]{1,0:T(8,128)(2,1)S(1)} %get-tuple-element.50), channel_id=1, source_target_pairs={{128,0},{129,1},{130,2},{131,3},{132,4},{133,5},{134,6},{135,7},{1... | collective-permute-start | bytes 786440 | tf_op jit(solution)/shard_map/ppermute | solution.py:236
  10.4 2.1 %collective-permute-done = bf16[128,1024]{1,0:T(8,128)(2,1)S(1)} collective-permute-done((bf16[128,1024]{1,0:T(8,128)(2,1)S(1)}, bf16[128,1024]{1,0:T(8,128)(2,1)S(1)}, u32[]{:S(2)}, u32[]{:S(2)}) %collective-permute-start) | collective-permute-done | bytes 262176 | tf_op jit(solution)/shard_map/ppermute | solution.py:236
  12.6 0.1 add.3
  12.7 4.7 %collective-permute-start.1 = (bf16[128,1024]{1,0:T(8,128)(2,1)S(1)}, bf16[128,1024]{1,0:T(8,128)(2,1)S(1)}, u32[]{:S(2)}, u32[]{:S(2)}) collective-permute-start(bf16[128,1024]{1,0:T(8,128)(2,1)S(1)} %add.3), channel_id=1, source_target_pairs={{0,96},{32,0},{64,32},{96,64},{128,160},{160,192},{192,224},{224,1... | collective-permute-start | bytes 786440 | tf_op jit(solution)/shard_map/ppermute | solution.py:215
  17.4 0.8 collective-permute-start.6
  18.2 2.4 %collective-permute-start.7 = (bf16[896,512]{1,0:T(8,128)(2,1)S(1)}, bf16[896,512]{1,0:T(8,128)(2,1)S(1)}, u32[]{:S(2)}, u32[]{:S(2)}) collective-permute-start(bf16[896,512]{1,0:T(8,128)(2,1)S(1)} %get-tuple-element.61), channel_id=1, source_target_pairs={{0,3},{1,0},{2,1},{3,2},{4,7},{5,4},{6,5},{7,6},{8,11},{9,8},{10,9... | collective-permute-start | bytes 2752520 | tf_op jit(solution)/shard_map/ppermute | solution.py:52
  20.6 0.7 collective-permute-done.1
  21.2 0.0 collective-permute-done.3.right_on
  21.2 0.0 collective-permute-done.2.left_on
  21.2 1.3 %collective-permute-start.4 = (bf16[128,1024]{1,0:T(8,128)(2,1)S(1)}, bf16[128,1024]{1,0:T(8,128)(2,1)S(1)}, u32[]{:S(2)}, u32[]{:S(2)}) collective-permute-start(bf16[128,1024]{1,0:T(8,128)(2,1)S(1)} %collective-permute-done.1), channel_id=1, source_target_pairs={{128,32},{160,64},{192,96},{224,0},{129,33},{161,65},{193,97},{225... | collective-permute-start | bytes 786440 | tf_op jit(solution)/shard_map/ppermute | solution.py:215
  22.5 0.9 %collective-permute-start.8 = (bf16[896,512]{1,0:T(8,128)(2,1)S(1)}, bf16[896,512]{1,0:T(8,128)(2,1)S(1)}, u32[]{:S(2)}, u32[]{:S(2)}) collective-permute-start(bf16[896,512]{1,0:T(8,128)(2,1)S(1)} %collective-permute-done.2.left_on), channel_id=1, source_target_pairs={{0,1},{1,2},{2,3},{3,0},{4,5},{5,6},{6,7},{7,4},{8,9},{9,10},{10,1... | collective-permute-start | bytes 2752520 | tf_op jit(solution)/shard_map/ppermute | solution.py:52
  23.4 2.5 %collective-permute-start.9 = (bf16[896,512]{1,0:T(8,128)(2,1)S(1)}, bf16[896,512]{1,0:T(8,128)(2,1)S(1)}, u32[]{:S(2)}, u32[]{:S(2)}) collective-permute-start(bf16[896,512]{1,0:T(8,128)(2,1)S(1)} %collective-permute-done.3.right_on), channel_id=1, source_target_pairs={{0,3},{1,0},{2,1},{3,2},{4,7},{5,4},{6,5},{7,6},{8,11},{9,8},{10,9... | collective-permute-start | bytes 2752520 | tf_op jit(solution)/shard_map/ppermute | solution.py:52
  25.9 4.8 %collective-permute-done.4 = bf16[128,1024]{1,0:T(8,128)(2,1)S(1)} collective-permute-done((bf16[128,1024]{1,0:T(8,128)(2,1)S(1)}, bf16[128,1024]{1,0:T(8,128)(2,1)S(1)}, u32[]{:S(2)}, u32[]{:S(2)}) %collective-permute-start.4) | collective-permute-done | bytes 262176 | tf_op jit(solution)/shard_map/ppermute | solution.py:215
  30.7 1.3 %collective-permute-start.5 = (bf16[128,1024]{1,0:T(8,128)(2,1)S(1)}, bf16[128,1024]{1,0:T(8,128)(2,1)S(1)}, u32[]{:S(2)}, u32[]{:S(2)}) collective-permute-start(bf16[128,1024]{1,0:T(8,128)(2,1)S(1)} %collective-permute-done.1), channel_id=1, source_target_pairs={{128,0},{160,32},{192,64},{224,96},{129,1},{161,33},{193,65},{225,... | collective-permute-start | bytes 786440 | tf_op jit(solution)/shard_map/ppermute | solution.py:215
  32.0 2.1 %collective-permute-done.5 = bf16[128,1024]{1,0:T(8,128)(2,1)S(1)} collective-permute-done((bf16[128,1024]{1,0:T(8,128)(2,1)S(1)}, bf16[128,1024]{1,0:T(8,128)(2,1)S(1)}, u32[]{:S(2)}, u32[]{:S(2)}) %collective-permute-start.5) | collective-permute-done | bytes 262176 | tf_op jit(solution)/shard_map/ppermute | solution.py:215
  34.2 0.1 pad_maximum_fusion.rel_ref
  34.3 0.7 shard_map.71
  35.0 2.4 %collective-permute-start.10 = (bf16[256,512]{1,0:T(8,128)(2,1)S(1)}, bf16[256,512]{1,0:T(8,128)(2,1)S(1)}, u32[]{:S(2)}, u32[]{:S(2)}) collective-permute-start(bf16[256,512]{1,0:T(8,128)(2,1)S(1)} %get-tuple-element.66), channel_id=1, source_target_pairs={{0,2},{1,3},{2,0},{3,1},{4,6},{5,7},{6,4},{7,5},{8,10},{9,11},{10,... | collective-permute-start | bytes 786440 | tf_op jit(solution)/shard_map/ppermute | solution.py:52
  37.4 1.7 %collective-permute-start.11 = (bf16[128,512]{1,0:T(8,128)(2,1)S(1)}, bf16[128,512]{1,0:T(8,128)(2,1)S(1)}, u32[]{:S(2)}, u32[]{:S(2)}) collective-permute-start(bf16[128,512]{1,0:T(8,128)(2,1)S(1)} %get-tuple-element.67), channel_id=1, source_target_pairs={{0,1},{1,2},{2,3},{3,0},{4,5},{5,6},{6,7},{7,4},{8,9},{9,10},{10,1... | collective-permute-start | bytes 393224 | tf_op jit(solution)/shard_map/ppermute | solution.py:52
  39.1 1.5 %collective-permute-start.12 = (bf16[128,512]{1,0:T(8,128)(2,1)S(1)}, bf16[128,512]{1,0:T(8,128)(2,1)S(1)}, u32[]{:S(2)}, u32[]{:S(2)}) collective-permute-start(bf16[128,512]{1,0:T(8,128)(2,1)S(1)} %get-tuple-element.68), channel_id=1, source_target_pairs={{0,3},{1,0},{2,1},{3,2},{4,7},{5,4},{6,5},{7,6},{8,11},{9,8},{10,9... | collective-permute-start | bytes 393224 | tf_op jit(solution)/shard_map/ppermute | solution.py:52
  40.6 1.5 %shard_map.70.acc_ref = f32[1024,512]{1,0:T(8,128)S(1)} custom-call(bf16[896,512]{1,0:T(8,128)(2,1)S(1)} %get-tuple-element.52.mine_on, bf16[896,512]{1,0:T(8,128)(2,1)S(1)} %get-tuple-element.59.mine_ref, bf16[768,512]{1,0:T(8,128)(2,1)S(1)} %get-tuple-element.57.own_ref, bf16[896,512]{1,0:T(8,128)(2,1)S(1)} %collective-permute-done.2.left_on, ...), custom_call_target="tpu_custom_call" | custom-call | flops 1207959552 | bytes 8388608 | tf_op jit(solution)/shard_map/pallas_call | solution.py:64
  42.2 4.2 %collective-permute-done.11.left_last = bf16[128,512]{1,0:T(8,128)(2,1)S(1)} collective-permute-done((bf16[128,512]{1,0:T(8,128)(2,1)S(1)}, bf16[128,512]{1,0:T(8,128)(2,1)S(1)}, u32[]{:S(2)}, u32[]{:S(2)}) %collective-permute-start.11) | collective-permute-done | bytes 131104 | tf_op jit(solution)/shard_map/ppermute | solution.py:52
  46.4 1.1 %collective-permute-start.16 = (bf16[512,512]{1,0:T(8,128)(2,1)S(1)}, bf16[512,512]{1,0:T(8,128)(2,1)S(1)}, u32[]{:S(2)}, u32[]{:S(2)}) collective-permute-start(bf16[512,512]{1,0:T(8,128)(2,1)S(1)} %get-tuple-element.81), channel_id=1, source_target_pairs={{0,1},{1,2},{2,3},{3,0},{4,5},{5,6},{6,7},{7,4},{8,9},{9,10},{10,1... | collective-permute-start | bytes 1572872 | tf_op jit(solution)/shard_map/ppermute | solution.py:52
  47.5 2.2 %collective-permute-start.17 = (bf16[512,512]{1,0:T(8,128)(2,1)S(1)}, bf16[512,512]{1,0:T(8,128)(2,1)S(1)}, u32[]{:S(2)}, u32[]{:S(2)}) collective-permute-start(bf16[512,512]{1,0:T(8,128)(2,1)S(1)} %get-tuple-element.82), channel_id=1, source_target_pairs={{0,3},{1,0},{2,1},{3,2},{4,7},{5,4},{6,5},{7,6},{8,11},{9,8},{10,9... | collective-permute-start | bytes 1572872 | tf_op jit(solution)/shard_map/ppermute | solution.py:52
  49.7 1.5 %shard_map.72 = (f32[1024,128]{1,0:T(8,128)S(1)}, f32[1040,128]{1,0:T(8,128)S(1)}, f32[1040,128]{1,0:T(8,128)S(1)}, f32[1040,128]{1,0:T(8,128)S(1)}) custom-call(f32[1024,512]{1,0:T(8,128)S(1)} %shard_map.70.acc_ref, bf16[896,512]{1,0:T(8,128)(2,1)S(1)} %get-tuple-element.52.mine_on, bf16[896,512]{1,0:T(8,128)(2,1)S(1)} %get-tuple-element.59.mine_ref, ...), custom_call_target="tpu_custom_call" | custom-call | flops 939524096 | bytes 8388608 | tf_op jit(solution)/shard_map/pallas_call | solution.py:64
  51.3 0.9 %collective-permute-start.15 = (f16[1040,128]{1,0:T(8,128)(2,1)S(1)}, f16[1040,128]{1,0:T(8,128)(2,1)S(1)}, u32[]{:S(2)}, u32[]{:S(2)}) collective-permute-start(f16[1040,128]{1,0:T(8,128)(2,1)S(1)} %convert_element_type.44), channel_id=1, source_target_pairs={{0,12},{1,13},{2,14},{3,15},{4,0},{5,1},{6,2},{7,3},{8,4},{9,5},{1... | collective-permute-start | bytes 798728 | tf_op jit(solution)/shard_map/ppermute | solution.py:52
  52.2 2.5 %collective-permute-start.14 = (f16[1040,128]{1,0:T(8,128)(2,1)S(1)}, f16[1040,128]{1,0:T(8,128)(2,1)S(1)}, u32[]{:S(2)}, u32[]{:S(2)}) collective-permute-start(f16[1040,128]{1,0:T(8,128)(2,1)S(1)} %convert_element_type.43), channel_id=1, source_target_pairs={{0,4},{1,5},{2,6},{3,7},{4,8},{5,9},{6,10},{7,11},{8,12},{9,13},{1... | collective-permute-start | bytes 798728 | tf_op jit(solution)/shard_map/ppermute | solution.py:52
  54.6 0.0 collective-permute-start.13
  54.7 4.4 %collective-permute-done.15 = f16[1040,128]{1,0:T(8,128)(2,1)S(1)} collective-permute-done((f16[1040,128]{1,0:T(8,128)(2,1)S(1)}, f16[1040,128]{1,0:T(8,128)(2,1)S(1)}, u32[]{:S(2)}, u32[]{:S(2)}) %collective-permute-start.15) | collective-permute-done | bytes 266272 | tf_op jit(solution)/shard_map/ppermute | solution.py:52
  59.0 2.4 %collective-permute-done.14 = f16[1040,128]{1,0:T(8,128)(2,1)S(1)} collective-permute-done((f16[1040,128]{1,0:T(8,128)(2,1)S(1)}, f16[1040,128]{1,0:T(8,128)(2,1)S(1)}, u32[]{:S(2)}, u32[]{:S(2)}) %collective-permute-start.14) | collective-permute-done | bytes 266272 | tf_op jit(solution)/shard_map/ppermute | solution.py:52
  61.5 1.1 %collective-permute-done.13 = f16[1040,128]{1,0:T(8,128)(2,1)S(1)} collective-permute-done((f16[1040,128]{1,0:T(8,128)(2,1)S(1)}, f16[1040,128]{1,0:T(8,128)(2,1)S(1)}, u32[]{:S(2)}, u32[]{:S(2)}) %collective-permute-start.13) | collective-permute-done | bytes 266272 | tf_op jit(solution)/shard_map/ppermute | solution.py:52
  62.7 0.3 shard_map.76
  63.0 5.6 %collective-permute-start.18 = (f16[1040,128]{1,0:T(8,128)(2,1)S(1)}, f16[1040,128]{1,0:T(8,128)(2,1)S(1)}, u32[]{:S(2)}, u32[]{:S(2)}) collective-permute-start(f16[1040,128]{1,0:T(8,128)(2,1)S(1)} %convert_element_type.48), channel_id=1, source_target_pairs={{0,16},{16,0},{1,17},{17,1},{2,18},{18,2},{3,19},{19,3},{4,20},{20... | collective-permute-start | bytes 798728 | tf_op jit(solution)/shard_map/ppermute | solution.py:288
  68.7 1.5 %shard_map.74.acc_ref = f32[1024,512]{1,0:T(8,128)S(1)} custom-call(bf16[896,512]{1,0:T(8,128)(2,1)S(1)} %get-tuple-element.52.mine_on, bf16[896,512]{1,0:T(8,128)(2,1)S(1)} %get-tuple-element.59.mine_ref, bf16[768,512]{1,0:T(8,128)(2,1)S(1)} %get-tuple-element.57.own_ref, bf16[896,512]{1,0:T(8,128)(2,1)S(1)} %collective-permute-done.2.left_on, ...), custom_call_target="tpu_custom_call" | custom-call | flops 1207959552 | bytes 8388608 | tf_op jit(solution)/shard_map/pallas_call | solution.py:64
  70.2 1.5 %shard_map.75 = (f32[1024,128]{1,0:T(8,128)S(1)}, f32[1040,128]{1,0:T(8,128)S(1)}, f32[1040,128]{1,0:T(8,128)S(1)}, f32[1040,128]{1,0:T(8,128)S(1)}) custom-call(f32[1024,512]{1,0:T(8,128)S(1)} %shard_map.74.acc_ref, bf16[896,512]{1,0:T(8,128)(2,1)S(1)} %get-tuple-element.52.mine_on, bf16[896,512]{1,0:T(8,128)(2,1)S(1)} %get-tuple-element.59.mine_ref, ...), custom_call_target="tpu_custom_call" | custom-call | flops 939524096 | bytes 8388608 | tf_op jit(solution)/shard_map/pallas_call | solution.py:64
  71.8 0.4 collective-permute-start.19
  72.2 2.5 %collective-permute-start.20 = (f16[1040,128]{1,0:T(8,128)(2,1)S(1)}, f16[1040,128]{1,0:T(8,128)(2,1)S(1)}, u32[]{:S(2)}, u32[]{:S(2)}) collective-permute-start(f16[1040,128]{1,0:T(8,128)(2,1)S(1)} %convert_element_type.50), channel_id=1, source_target_pairs={{0,4},{1,5},{2,6},{3,7},{4,8},{5,9},{6,10},{7,11},{8,12},{9,13},{1... | collective-permute-start | bytes 798728 | tf_op jit(solution)/shard_map/ppermute | solution.py:52
  74.7 0.6 collective-permute-start.21
  75.3 3.7 %shard_map.73 = f32[128,1024]{1,0:T(8,128)} custom-call(bf16[4,128,1024]{2,1,0:T(8,128)(2,1)S(1)} %pad_maximum_fusion.rel_ref, f32[128,1024]{1,0:T(8,128)S(1)} %get-tuple-element.80.first_ref, bf16[1024,4096]{1,0:T(8,128)(2,1)S(1)} %bitcast.12), custom_call_target="tpu_custom_call" | custom-call | flops 1073741824 | bytes 2097152 | tf_op jit(solution)/shard_map/pallas_call | solution.py:64
  79.0 0.8 collective-permute-done.19
  79.9 2.7 %collective-permute-done.20 = f16[1040,128]{1,0:T(8,128)(2,1)S(1)} collective-permute-done((f16[1040,128]{1,0:T(8,128)(2,1)S(1)}, f16[1040,128]{1,0:T(8,128)(2,1)S(1)}, u32[]{:S(2)}, u32[]{:S(2)}) %collective-permute-start.20) | collective-permute-done | bytes 266272 | tf_op jit(solution)/shard_map/ppermute | solution.py:52
  82.6 0.0 collective-permute-done.21
  82.7 1.0 %shard_map.77 = f32[1024,128]{1,0:T(8,128)} custom-call(f32[1024,128]{1,0:T(8,128)S(1)} %get-tuple-element.83.keep_ref, f32[1040,128]{1,0:T(8,128)S(1)} %convert_element_type.49.rest_0_, f32[1040,128]{1,0:T(8,128)S(1)} %convert_element_type.53.rest_1_, f32[1040,128]{1,0:T(8,128)S(1)} %convert_element_type.54.rest_2_, ...), custom_call_target="tpu_custom_call" | custom-call | bytes 4194304 | tf_op jit(solution)/shard_map/pallas_call | solution.py:64
  (29 shorter events, 0.6 us)
Async XLA Ops:
  0.6 5.6 %slice-start = ((s8[8388608]{0:T(1024)(128)(4,1)}), s8[4194304]{0:T(1024)(128)(4,1)S(1)}, s32[]{:S(2)}) async-start(s8[8388608]{0:T(1024)(128)(4,1)} %bitcast.9), calls=%async_computation | async-start | bytes 8388608
  0.6 5.6 %slice-start.1 = ((s8[8388608]{0:T(1024)(128)(4,1)}), s8[4194304]{0:T(1024)(128)(4,1)S(1)}, s32[]{:S(2)}) async-start(s8[8388608]{0:T(1024)(128)(4,1)} %bitcast.9), calls=%async_computation.1 | async-start | bytes 8388608
  0.7 5.6 %copy-start = (bf16[128,4096]{1,0:T(8,128)(2,1)S(1)}, bf16[128,4096]{1,0:T(8,128)(2,1)}, u32[]{:S(2)}) copy-start(bf16[128,4096]{1,0:T(8,128)(2,1)} %head_ref.1) | copy-start | bytes 3145732
  3.4 17.8 %collective-permute-start.3 = (bf16[896,512]{1,0:T(8,128)(2,1)S(1)}, bf16[896,512]{1,0:T(8,128)(2,1)S(1)}, u32[]{:S(2)}, u32[]{:S(2)}) collective-permute-start(bf16[896,512]{1,0:T(8,128)(2,1)S(1)} %get-tuple-element.53), channel_id=1, source_target_pairs={{0,3},{1,0},{2,1},{3,2},{4,7},{5,4},{6,5},{7,6},{8,11},{9,8},{10,9... | collective-permute-start | bytes 2752520 | tf_op jit(solution)/shard_map/ppermute | solution.py:52
  6.2 15.0 %collective-permute-start.2 = (bf16[896,512]{1,0:T(8,128)(2,1)S(1)}, bf16[896,512]{1,0:T(8,128)(2,1)S(1)}, u32[]{:S(2)}, u32[]{:S(2)}) collective-permute-start(bf16[896,512]{1,0:T(8,128)(2,1)S(1)} %get-tuple-element.52.mine_on), channel_id=1, source_target_pairs={{0,1},{1,2},{2,3},{3,0},{4,5},{5,6},{6,7},{7,4},{8,9},{9,10},{10,1... | collective-permute-start | bytes 2752520 | tf_op jit(solution)/shard_map/ppermute | solution.py:52
  9.1 3.4 %collective-permute-start = (bf16[128,1024]{1,0:T(8,128)(2,1)S(1)}, bf16[128,1024]{1,0:T(8,128)(2,1)S(1)}, u32[]{:S(2)}, u32[]{:S(2)}) collective-permute-start(bf16[128,1024]{1,0:T(8,128)(2,1)S(1)} %get-tuple-element.50), channel_id=1, source_target_pairs={{128,0},{129,1},{130,2},{131,3},{132,4},{133,5},{134,6},{135,7},{1... | collective-permute-start | bytes 786440 | tf_op jit(solution)/shard_map/ppermute | solution.py:236
  12.7 8.6 %collective-permute-start.1 = (bf16[128,1024]{1,0:T(8,128)(2,1)S(1)}, bf16[128,1024]{1,0:T(8,128)(2,1)S(1)}, u32[]{:S(2)}, u32[]{:S(2)}) collective-permute-start(bf16[128,1024]{1,0:T(8,128)(2,1)S(1)} %add.3), channel_id=1, source_target_pairs={{0,96},{32,0},{64,32},{96,64},{128,160},{160,192},{192,224},{224,1... | collective-permute-start | bytes 786440 | tf_op jit(solution)/shard_map/ppermute | solution.py:215
  17.4 20.0 %collective-permute-start.6 = (bf16[896,512]{1,0:T(8,128)(2,1)S(1)}, bf16[896,512]{1,0:T(8,128)(2,1)S(1)}, u32[]{:S(2)}, u32[]{:S(2)}) collective-permute-start(bf16[896,512]{1,0:T(8,128)(2,1)S(1)} %get-tuple-element.59.mine_ref), channel_id=1, source_target_pairs={{0,1},{1,2},{2,3},{3,0},{4,5},{5,6},{6,7},{7,4},{8,9},{9,10},{10,1... | collective-permute-start | bytes 2752520 | tf_op jit(solution)/shard_map/ppermute | solution.py:52
  18.2 21.0 %collective-permute-start.7 = (bf16[896,512]{1,0:T(8,128)(2,1)S(1)}, bf16[896,512]{1,0:T(8,128)(2,1)S(1)}, u32[]{:S(2)}, u32[]{:S(2)}) collective-permute-start(bf16[896,512]{1,0:T(8,128)(2,1)S(1)} %get-tuple-element.61), channel_id=1, source_target_pairs={{0,3},{1,0},{2,1},{3,2},{4,7},{5,4},{6,5},{7,6},{8,11},{9,8},{10,9... | collective-permute-start | bytes 2752520 | tf_op jit(solution)/shard_map/ppermute | solution.py:52
  21.2 9.5 %collective-permute-start.4 = (bf16[128,1024]{1,0:T(8,128)(2,1)S(1)}, bf16[128,1024]{1,0:T(8,128)(2,1)S(1)}, u32[]{:S(2)}, u32[]{:S(2)}) collective-permute-start(bf16[128,1024]{1,0:T(8,128)(2,1)S(1)} %collective-permute-done.1), channel_id=1, source_target_pairs={{128,32},{160,64},{192,96},{224,0},{129,33},{161,65},{193,97},{225... | collective-permute-start | bytes 786440 | tf_op jit(solution)/shard_map/ppermute | solution.py:215
  22.5 23.9 %collective-permute-start.8 = (bf16[896,512]{1,0:T(8,128)(2,1)S(1)}, bf16[896,512]{1,0:T(8,128)(2,1)S(1)}, u32[]{:S(2)}, u32[]{:S(2)}) collective-permute-start(bf16[896,512]{1,0:T(8,128)(2,1)S(1)} %collective-permute-done.2.left_on), channel_id=1, source_target_pairs={{0,1},{1,2},{2,3},{3,0},{4,5},{5,6},{6,7},{7,4},{8,9},{9,10},{10,1... | collective-permute-start | bytes 2752520 | tf_op jit(solution)/shard_map/ppermute | solution.py:52
  23.4 23.0 %collective-permute-start.9 = (bf16[896,512]{1,0:T(8,128)(2,1)S(1)}, bf16[896,512]{1,0:T(8,128)(2,1)S(1)}, u32[]{:S(2)}, u32[]{:S(2)}) collective-permute-start(bf16[896,512]{1,0:T(8,128)(2,1)S(1)} %collective-permute-done.3.right_on), channel_id=1, source_target_pairs={{0,3},{1,0},{2,1},{3,2},{4,7},{5,4},{6,5},{7,6},{8,11},{9,8},{10,9... | collective-permute-start | bytes 2752520 | tf_op jit(solution)/shard_map/ppermute | solution.py:52
  30.7 3.4 %collective-permute-start.5 = (bf16[128,1024]{1,0:T(8,128)(2,1)S(1)}, bf16[128,1024]{1,0:T(8,128)(2,1)S(1)}, u32[]{:S(2)}, u32[]{:S(2)}) collective-permute-start(bf16[128,1024]{1,0:T(8,128)(2,1)S(1)} %collective-permute-done.1), channel_id=1, source_target_pairs={{128,0},{160,32},{192,64},{224,96},{129,1},{161,33},{193,65},{225,... | collective-permute-start | bytes 786440 | tf_op jit(solution)/shard_map/ppermute | solution.py:215
  35.0 11.4 %collective-permute-start.10 = (bf16[256,512]{1,0:T(8,128)(2,1)S(1)}, bf16[256,512]{1,0:T(8,128)(2,1)S(1)}, u32[]{:S(2)}, u32[]{:S(2)}) collective-permute-start(bf16[256,512]{1,0:T(8,128)(2,1)S(1)} %get-tuple-element.66), channel_id=1, source_target_pairs={{0,2},{1,3},{2,0},{3,1},{4,6},{5,7},{6,4},{7,5},{8,10},{9,11},{10,... | collective-permute-start | bytes 786440 | tf_op jit(solution)/shard_map/ppermute | solution.py:52
  37.4 9.0 %collective-permute-start.11 = (bf16[128,512]{1,0:T(8,128)(2,1)S(1)}, bf16[128,512]{1,0:T(8,128)(2,1)S(1)}, u32[]{:S(2)}, u32[]{:S(2)}) collective-permute-start(bf16[128,512]{1,0:T(8,128)(2,1)S(1)} %get-tuple-element.67), channel_id=1, source_target_pairs={{0,1},{1,2},{2,3},{3,0},{4,5},{5,6},{6,7},{7,4},{8,9},{9,10},{10,1... | collective-permute-start | bytes 393224 | tf_op jit(solution)/shard_map/ppermute | solution.py:52
  39.1 7.2 %collective-permute-start.12 = (bf16[128,512]{1,0:T(8,128)(2,1)S(1)}, bf16[128,512]{1,0:T(8,128)(2,1)S(1)}, u32[]{:S(2)}, u32[]{:S(2)}) collective-permute-start(bf16[128,512]{1,0:T(8,128)(2,1)S(1)} %get-tuple-element.68), channel_id=1, source_target_pairs={{0,3},{1,0},{2,1},{3,2},{4,7},{5,4},{6,5},{7,6},{8,11},{9,8},{10,9... | collective-permute-start | bytes 393224 | tf_op jit(solution)/shard_map/ppermute | solution.py:52
  46.4 22.2 %collective-permute-start.16 = (bf16[512,512]{1,0:T(8,128)(2,1)S(1)}, bf16[512,512]{1,0:T(8,128)(2,1)S(1)}, u32[]{:S(2)}, u32[]{:S(2)}) collective-permute-start(bf16[512,512]{1,0:T(8,128)(2,1)S(1)} %get-tuple-element.81), channel_id=1, source_target_pairs={{0,1},{1,2},{2,3},{3,0},{4,5},{5,6},{6,7},{7,4},{8,9},{9,10},{10,1... | collective-permute-start | bytes 1572872 | tf_op jit(solution)/shard_map/ppermute | solution.py:52
  47.5 21.2 %collective-permute-start.17 = (bf16[512,512]{1,0:T(8,128)(2,1)S(1)}, bf16[512,512]{1,0:T(8,128)(2,1)S(1)}, u32[]{:S(2)}, u32[]{:S(2)}) collective-permute-start(bf16[512,512]{1,0:T(8,128)(2,1)S(1)} %get-tuple-element.82), channel_id=1, source_target_pairs={{0,3},{1,0},{2,1},{3,2},{4,7},{5,4},{6,5},{7,6},{8,11},{9,8},{10,9... | collective-permute-start | bytes 1572872 | tf_op jit(solution)/shard_map/ppermute | solution.py:52
  51.3 7.7 %collective-permute-start.15 = (f16[1040,128]{1,0:T(8,128)(2,1)S(1)}, f16[1040,128]{1,0:T(8,128)(2,1)S(1)}, u32[]{:S(2)}, u32[]{:S(2)}) collective-permute-start(f16[1040,128]{1,0:T(8,128)(2,1)S(1)} %convert_element_type.44), channel_id=1, source_target_pairs={{0,12},{1,13},{2,14},{3,15},{4,0},{5,1},{6,2},{7,3},{8,4},{9,5},{1... | collective-permute-start | bytes 798728 | tf_op jit(solution)/shard_map/ppermute | solution.py:52
  52.2 9.3 %collective-permute-start.14 = (f16[1040,128]{1,0:T(8,128)(2,1)S(1)}, f16[1040,128]{1,0:T(8,128)(2,1)S(1)}, u32[]{:S(2)}, u32[]{:S(2)}) collective-permute-start(f16[1040,128]{1,0:T(8,128)(2,1)S(1)} %convert_element_type.43), channel_id=1, source_target_pairs={{0,4},{1,5},{2,6},{3,7},{4,8},{5,9},{6,10},{7,11},{8,12},{9,13},{1... | collective-permute-start | bytes 798728 | tf_op jit(solution)/shard_map/ppermute | solution.py:52
  54.6 7.9 %collective-permute-start.13 = (f16[1040,128]{1,0:T(8,128)(2,1)S(1)}, f16[1040,128]{1,0:T(8,128)(2,1)S(1)}, u32[]{:S(2)}, u32[]{:S(2)}) collective-permute-start(f16[1040,128]{1,0:T(8,128)(2,1)S(1)} %convert_element_type.42), channel_id=1, source_target_pairs={{0,8},{1,9},{2,10},{3,11},{4,12},{5,13},{6,14},{7,15},{8,0},{9,1},... | collective-permute-start | bytes 798728 | tf_op jit(solution)/shard_map/ppermute | solution.py:52
  63.0 16.0 %collective-permute-start.18 = (f16[1040,128]{1,0:T(8,128)(2,1)S(1)}, f16[1040,128]{1,0:T(8,128)(2,1)S(1)}, u32[]{:S(2)}, u32[]{:S(2)}) collective-permute-start(f16[1040,128]{1,0:T(8,128)(2,1)S(1)} %convert_element_type.48), channel_id=1, source_target_pairs={{0,16},{16,0},{1,17},{17,1},{2,18},{18,2},{3,19},{19,3},{4,20},{20... | collective-permute-start | bytes 798728 | tf_op jit(solution)/shard_map/ppermute | solution.py:288
  71.8 8.0 %collective-permute-start.19 = (f16[1040,128]{1,0:T(8,128)(2,1)S(1)}, f16[1040,128]{1,0:T(8,128)(2,1)S(1)}, u32[]{:S(2)}, u32[]{:S(2)}) collective-permute-start(f16[1040,128]{1,0:T(8,128)(2,1)S(1)} %convert_element_type.51), channel_id=1, source_target_pairs={{0,8},{1,9},{2,10},{3,11},{4,12},{5,13},{6,14},{7,15},{8,0},{9,1},... | collective-permute-start | bytes 798728 | tf_op jit(solution)/shard_map/ppermute | solution.py:52
  72.2 10.4 %collective-permute-start.20 = (f16[1040,128]{1,0:T(8,128)(2,1)S(1)}, f16[1040,128]{1,0:T(8,128)(2,1)S(1)}, u32[]{:S(2)}, u32[]{:S(2)}) collective-permute-start(f16[1040,128]{1,0:T(8,128)(2,1)S(1)} %convert_element_type.50), channel_id=1, source_target_pairs={{0,4},{1,5},{2,6},{3,7},{4,8},{5,9},{6,10},{7,11},{8,12},{9,13},{1... | collective-permute-start | bytes 798728 | tf_op jit(solution)/shard_map/ppermute | solution.py:52
  74.7 7.9 %collective-permute-start.21 = (f16[1040,128]{1,0:T(8,128)(2,1)S(1)}, f16[1040,128]{1,0:T(8,128)(2,1)S(1)}, u32[]{:S(2)}, u32[]{:S(2)}) collective-permute-start(f16[1040,128]{1,0:T(8,128)(2,1)S(1)} %convert_element_type.52), channel_id=1, source_target_pairs={{0,12},{1,13},{2,14},{3,15},{4,0},{5,1},{6,2},{7,3},{8,4},{9,5},{1... | collective-permute-start | bytes 798728 | tf_op jit(solution)/shard_map/ppermute | solution.py:52

commit v16 on v12

--- a/solution.py
+++ b/solution.py
@@ -155,9 +155,9 @@
             acc_ref[r * half:(r + 1) * half, z * lanes:(z + 1) * lanes] = jnp.dot(lhs, rhs, preferred_element_type=F32)
 
 
-def late_kernel(z, acc_ref, mine_on, mine_ref, left_on, left_ref, right_on, right_ref, upper_ref, lower_ref,
-                two_last, left_last, right_last, own_last, keep_ref, *rest):
-    sends, sum_ref = rest[:-1], rest[-1]
+def late_kernel(z, blocks, acc_ref, mine_on, mine_ref, left_on, left_ref, right_on, right_ref, upper_ref, lower_ref,
+                two_last, left_last, right_last, own_last, *rest):
+    outs, sum_ref = rest[:-1], rest[-1]
     width, rows = acc_ref.shape[0], own_last.shape[0] // 2
     half, lanes = width // 2, acc_ref.shape[1] // 2
     depth = mine_ref.shape[1] - rows
@@ -166,20 +166,25 @@
     at = half + z * depth // 2
     rhs += [ref[at:at + depth // 2, :] for ref in far]
     rhs = jnp.concatenate(rhs, axis=0)
-    largest = jnp.full((1, lanes), TINY, F32)
+    rhs = jnp.concatenate([rhs[:, b * LANES:(b + 1) * LANES] for b in blocks], axis=1)
+    largest = jnp.full((1, len(blocks) * LANES), TINY, F32)
     for r in range(2):
         lhs = [side[r][:half, depth:] for side in (mine, left, right, far)] + [far[r][:half, :depth]]
         total = jnp.dot(jnp.concatenate(lhs, axis=1), rhs, preferred_element_type=F32)
-        total = total + acc_ref[r * half:(r + 1) * half, z * lanes:(z + 1) * lanes]
+        earlier = [acc_ref[r * half:(r + 1) * half, z * lanes + b * LANES:z * lanes + (b + 1) * LANES] for b in blocks]
+        total = total + jnp.concatenate(earlier, axis=1)
         largest = jnp.maximum(largest, jnp.max(jnp.abs(total), axis=0, keepdims=True))
         sum_ref[r * half:(r + 1) * half, :] = total
     power = jnp.ceil(jnp.log2(jnp.max(largest, axis=1, keepdims=True))) - TOP
     power = jnp.broadcast_to(power, (1, LANES))
     factor = jnp.exp2(-power)
-    keep_ref[...] = sum_ref[:, :LANES]
-    for b, out in enumerate(sends, 1):
-        out[:width, :] = sum_ref[:, b * LANES:(b + 1) * LANES] * factor
-        out[width:, :] = jnp.broadcast_to(power, (TAIL, LANES))
+    for i, (b, out) in enumerate(zip(blocks, outs)):
+        tile = sum_ref[:, i * LANES:(i + 1) * LANES]
+        if b:
+            out[:width, :] = tile * factor
+            out[width:, :] = jnp.broadcast_to(power, (TAIL, LANES))
+        else:
+            out[...] = tile
 
 
 def summed(keep_ref, refs):
@@ -200,8 +205,8 @@
     out_ref[rows:, :] = jnp.broadcast_to(power, (TAIL, LANES))
 
 
-def near_kernel(keep_ref, one_ref, two_ref, three_ref, other_ref, out_ref):
-    out_ref[...] = summed(keep_ref, (one_ref, two_ref, three_ref, other_ref))
+def near_kernel(keep_ref, *rest):
+    rest[-1][...] = summed(keep_ref, rest[:-1])
 
 
 def on_line(value, pairs):
@@ -254,24 +259,26 @@
     acc, upper, lower, *last = lax.optimization_barrier((acc, upper, lower, *last))
     send = ((width + TAIL, LANES), F32)
 
-    def late(z):
+    def late(z, blocks):
         return call(
-            functools.partial(late_kernel, z), [((width, LANES), F32)] + [send] * 3,
+            functools.partial(late_kernel, z, blocks), [send if b else ((width, LANES), F32) for b in blocks],
             (acc, right_on, right, from_left_on, from_left, from_right_on, from_right, upper, lower, *last), whole(13),
-            scratch=[pltpu.VMEM((width, lanes), F32)],
-            flops=2 * width * lanes * (3 * rows + micro * rows), moved=8 * 2**20,
+            scratch=[pltpu.VMEM((width, len(blocks) * LANES), F32)],
+            flops=2 * width * len(blocks) * LANES * (3 * rows + micro * rows), moved=8 * 2**20,
         )
 
-    keep_far, *far_sends = late(1)
-    keep_near, *near_sends = late(0)
-    sends = far_sends + near_sends
+    far_two, far_one = late(1, (2, 1))
+    far_three, keep_far = late(1, (3, 0))
+    keep_near, *near_sends = late(0, (0, 1, 2, 3))
+    sends = [far_one, far_two, far_three] + near_sends
     got = [shifted(sends[i].astype(F16), False, 1 + i % 3) for i in (1, 0, 2, 4, 3, 5)]
     rel, *got[:3] = lax.optimization_barrier((rel, *got[:3]))
     got = [v.astype(F32) for v in got]
     (second,) = call(second_kernel, [((rows, width), F32)], (rel, first, weights[0]), whole(3), **matmul)
     (far,) = call(far_kernel, [send], (keep_far, *got[:3]), whole(4), moved=4 * 2**20)
     other = lax.ppermute(far.astype(F16), "z_hi", [(0, 1), (1, 0)]).astype(F32)
-    (block,) = call(near_kernel, [((width, LANES), F32)], (keep_near, *got[3:], other), whole(5), moved=4 * 2**20)
+    (near,) = call(near_kernel, [((width, LANES), F32)], (keep_near, *got[3:]), whole(4), moved=4 * 2**20)
+    (block,) = call(near_kernel, [((width, LANES), F32)], (near, other), whole(2), moved=2 * 2**20)
     return (second[None], block[None])
 
 

time: 81.5 us -> 82.2 us (level)
    pallas_call x9 -> x11, Pallas kernels: 17 us -> 17.3 us  [call(): pl.pallas_call(kernel, out_shape=[jax.ShapeDtypeStruct(s, t) for s, t in...]
  transfers between devices with their start and end apart: 20 -> 20, of which waited for: 9 -> 8; matrix products, arithmetic and copies ran while one was open for 1% -> 1% of each run, Pallas kernels for 15% -> 16%
where the time goes in v16:
time: 82.2 us; the launch traced here: 81.3 us
  starting transfers between devices  36.6 us (45%)
  waiting for transfers between devices  25.8 us (31%)
  Pallas kernels  17.3 us (21%)
  between operations  0.9 us (1%)
    ppermute x15, starting transfers between devices, shifted(): return lax.ppermute(value, ('section', 'y', 'x'), pairs_over(along, by))  21.5 us
    pallas_call x11, Pallas kernels, call(): pl.pallas_call(kernel, out_shape=[jax.ShapeDtypeStruct(s, t) for s, t in...  17.3 us
    ppermute x3, waiting for transfers between devices, on_line(): return lax.ppermute(value, ('section', 'z_lo'), pairs)  11.6 us
    ppermute x15, waiting for transfers between devices, shifted(): return lax.ppermute(value, ('section', 'y', 'x'), pairs_over(along, by))  8.77 us
    ppermute x3, starting transfers between devices, on_line(): return lax.ppermute(value, ('section', 'z_lo'), pairs)  7.26 us
    ppermute x1, starting transfers between devices, local(): other = lax.ppermute(far.astype(F16), 'z_hi', [(0, 1), (1, 0)]).astype(F32)  6.48 us
    ppermute x1, waiting for transfers between devices, local(): other = lax.ppermute(far.astype(F16), 'z_hi', [(0, 1), (1, 0)]).astype(F32)  3.32 us
    ppermute x1, waiting for transfers between devices, local(): shard = lax.ppermute(small, 'section', [(1, 0)])  2.13 us
  transfers between devices with their start and end apart: 20, of which 8 were waited for; matrix products, arithmetic and copies ran while one was open for 1% of the time, Pallas kernels for 16%

profile of v16, /device:TPU:24, one launch (start us, length us, event | category | flops | bytes accessed | tf_op | source)
XLA Modules:
  0.0 81.3 jit_solution(16601887314395221253)
XLA Ops:
  0.6 0.0 slice-start
  0.6 0.0 slice-start.1
  0.7 2.8 %shard_map.68 = (bf16[896,512]{1,0:T(8,128)(2,1)S(1)}, bf16[896,512]{1,0:T(8,128)(2,1)S(1)}, bf16[1280,512]{1,0:T(8,128)(2,1)S(1)}, bf16[1280,512]{1,0:T(8,128)(2,1)S(1)}, bf16[768,512]{1,0:T(8,128)(2,1)S(1)}) custom-call(s32[2]{0:T(128)} %pending_ref.1, bf16[4,128,1024]{2,1,0:T(8,128)(2,1)} %bitcast.20, bf16[3,128,4096]{2,1,0:T(8,128)(2,1)} %bitcast.19), custom_call_target="tpu_custom_call" | custom-call | flops 10000000000 | bytes 12582912 | tf_op jit(solution)/shard_map/pallas_call | solution.py:64
  3.4 1.6 %collective-permute-start.2 = (bf16[896,512]{1,0:T(8,128)(2,1)S(1)}, bf16[896,512]{1,0:T(8,128)(2,1)S(1)}, u32[]{:S(2)}, u32[]{:S(2)}) collective-permute-start(bf16[896,512]{1,0:T(8,128)(2,1)S(1)} %get-tuple-element.44.mine_on), channel_id=1, source_target_pairs={{0,1},{1,2},{2,3},{3,0},{4,5},{5,6},{6,7},{7,4},{8,9},{9,10},{10,1... | collective-permute-start | bytes 2752520 | tf_op jit(solution)/shard_map/ppermute | solution.py:52
  5.0 1.7 %collective-permute-start.3 = (bf16[896,512]{1,0:T(8,128)(2,1)S(1)}, bf16[896,512]{1,0:T(8,128)(2,1)S(1)}, u32[]{:S(2)}, u32[]{:S(2)}) collective-permute-start(bf16[896,512]{1,0:T(8,128)(2,1)S(1)} %get-tuple-element.45), channel_id=1, source_target_pairs={{0,3},{1,0},{2,1},{3,2},{4,7},{5,4},{6,5},{7,6},{8,11},{9,8},{10,9... | collective-permute-start | bytes 2752520 | tf_op jit(solution)/shard_map/ppermute | solution.py:52
  6.8 2.9 %shard_map.69 = (f32[128,1024]{1,0:T(8,128)S(1)}, bf16[128,1024]{1,0:T(8,128)(2,1)S(1)}) custom-call(bf16[128,4096]{1,0:T(8,128)(2,1)S(1)} %copy-done, bf16[1024,4096]{1,0:T(8,128)(2,1)S(1)} %bitcast.11), custom_call_target="tpu_custom_call" | custom-call | flops 1073741824 | bytes 2097152 | tf_op jit(solution)/shard_map/pallas_call | solution.py:64
  9.6 1.3 %collective-permute-start = (bf16[128,1024]{1,0:T(8,128)(2,1)S(1)}, bf16[128,1024]{1,0:T(8,128)(2,1)S(1)}, u32[]{:S(2)}, u32[]{:S(2)}) collective-permute-start(bf16[128,1024]{1,0:T(8,128)(2,1)S(1)} %get-tuple-element.42), channel_id=1, source_target_pairs={{128,0},{129,1},{130,2},{131,3},{132,4},{133,5},{134,6},{135,7},{1... | collective-permute-start | bytes 786440 | tf_op jit(solution)/shard_map/ppermute | solution.py:235
  10.9 2.1 %collective-permute-done = bf16[128,1024]{1,0:T(8,128)(2,1)S(1)} collective-permute-done((bf16[128,1024]{1,0:T(8,128)(2,1)S(1)}, bf16[128,1024]{1,0:T(8,128)(2,1)S(1)}, u32[]{:S(2)}, u32[]{:S(2)}) %collective-permute-start) | collective-permute-done | bytes 262176 | tf_op jit(solution)/shard_map/ppermute | solution.py:235
  13.1 0.3 collective-permute-start.6
  13.4 2.9 %collective-permute-start.7 = (bf16[1280,512]{1,0:T(8,128)(2,1)S(1)}, bf16[1280,512]{1,0:T(8,128)(2,1)S(1)}, u32[]{:S(2)}, u32[]{:S(2)}) collective-permute-start(bf16[1280,512]{1,0:T(8,128)(2,1)S(1)} %get-tuple-element.53), channel_id=1, source_target_pairs={{0,3},{1,0},{2,1},{3,2},{4,7},{5,4},{6,5},{7,6},{8,11},{9,8},{10,9... | collective-permute-start | bytes 3932168 | tf_op jit(solution)/shard_map/ppermute | solution.py:52
  16.3 0.1 add.3
  16.4 4.7 %collective-permute-start.1 = (bf16[128,1024]{1,0:T(8,128)(2,1)S(1)}, bf16[128,1024]{1,0:T(8,128)(2,1)S(1)}, u32[]{:S(2)}, u32[]{:S(2)}) collective-permute-start(bf16[128,1024]{1,0:T(8,128)(2,1)S(1)} %add.3), channel_id=1, source_target_pairs={{0,96},{32,0},{64,32},{96,64},{128,160},{160,192},{192,224},{224,1... | collective-permute-start | bytes 786440 | tf_op jit(solution)/shard_map/ppermute | solution.py:214
  21.1 4.6 %collective-permute-done.1 = bf16[128,1024]{1,0:T(8,128)(2,1)S(1)} collective-permute-done((bf16[128,1024]{1,0:T(8,128)(2,1)S(1)}, bf16[128,1024]{1,0:T(8,128)(2,1)S(1)}, u32[]{:S(2)}, u32[]{:S(2)}) %collective-permute-start.1) | collective-permute-done | bytes 262176 | tf_op jit(solution)/shard_map/ppermute | solution.py:214
  25.6 0.0 collective-permute-done.2.left_on
  25.6 1.3 %collective-permute-start.4 = (bf16[128,1024]{1,0:T(8,128)(2,1)S(1)}, bf16[128,1024]{1,0:T(8,128)(2,1)S(1)}, u32[]{:S(2)}, u32[]{:S(2)}) collective-permute-start(bf16[128,1024]{1,0:T(8,128)(2,1)S(1)} %collective-permute-done.1), channel_id=1, source_target_pairs={{128,32},{160,64},{192,96},{224,0},{129,33},{161,65},{193,97},{225... | collective-permute-start | bytes 786440 | tf_op jit(solution)/shard_map/ppermute | solution.py:214
  26.9 0.1 collective-permute-start.8
  27.0 3.2 %collective-permute-start.9 = (bf16[896,512]{1,0:T(8,128)(2,1)S(1)}, bf16[896,512]{1,0:T(8,128)(2,1)S(1)}, u32[]{:S(2)}, u32[]{:S(2)}) collective-permute-start(bf16[896,512]{1,0:T(8,128)(2,1)S(1)} %collective-permute-done.3.right_on), channel_id=1, source_target_pairs={{0,3},{1,0},{2,1},{3,2},{4,7},{5,4},{6,5},{7,6},{8,11},{9,8},{10,9... | collective-permute-start | bytes 2752520 | tf_op jit(solution)/shard_map/ppermute | solution.py:52
  30.2 4.9 %collective-permute-done.4 = bf16[128,1024]{1,0:T(8,128)(2,1)S(1)} collective-permute-done((bf16[128,1024]{1,0:T(8,128)(2,1)S(1)}, bf16[128,1024]{1,0:T(8,128)(2,1)S(1)}, u32[]{:S(2)}, u32[]{:S(2)}) %collective-permute-start.4) | collective-permute-done | bytes 262176 | tf_op jit(solution)/shard_map/ppermute | solution.py:214
  35.1 1.3 %collective-permute-start.5 = (bf16[128,1024]{1,0:T(8,128)(2,1)S(1)}, bf16[128,1024]{1,0:T(8,128)(2,1)S(1)}, u32[]{:S(2)}, u32[]{:S(2)}) collective-permute-start(bf16[128,1024]{1,0:T(8,128)(2,1)S(1)} %collective-permute-done.1), channel_id=1, source_target_pairs={{128,0},{160,32},{192,64},{224,96},{129,1},{161,33},{193,65},{225,... | collective-permute-start | bytes 786440 | tf_op jit(solution)/shard_map/ppermute | solution.py:214
  36.4 2.1 %collective-permute-done.5 = bf16[128,1024]{1,0:T(8,128)(2,1)S(1)} collective-permute-done((bf16[128,1024]{1,0:T(8,128)(2,1)S(1)}, bf16[128,1024]{1,0:T(8,128)(2,1)S(1)}, u32[]{:S(2)}, u32[]{:S(2)}) %collective-permute-start.5) | collective-permute-done | bytes 262176 | tf_op jit(solution)/shard_map/ppermute | solution.py:214
  38.5 0.1 pad_maximum_fusion.rel_ref
  38.7 0.6 shard_map.71
  39.3 0.4 collective-permute-start.10
  39.7 0.6 collective-permute-start.11
  40.3 2.6 %collective-permute-start.12 = (bf16[256,512]{1,0:T(8,128)(2,1)S(1)}, bf16[256,512]{1,0:T(8,128)(2,1)S(1)}, u32[]{:S(2)}, u32[]{:S(2)}) collective-permute-start(bf16[256,512]{1,0:T(8,128)(2,1)S(1)} %get-tuple-element.56), channel_id=1, source_target_pairs={{0,3},{1,0},{2,1},{3,2},{4,7},{5,4},{6,5},{7,6},{8,11},{9,8},{10,9... | collective-permute-start | bytes 786440 | tf_op jit(solution)/shard_map/ppermute | solution.py:52
  42.9 2.9 %shard_map.70.acc_ref = f32[1024,1024]{1,0:T(8,128)S(1)} custom-call(bf16[896,512]{1,0:T(8,128)(2,1)S(1)} %get-tuple-element.44.mine_on, bf16[1280,512]{1,0:T(8,128)(2,1)S(1)} %get-tuple-element.51.mine_ref, bf16[768,512]{1,0:T(8,128)(2,1)S(1)} %get-tuple-element.49.own_ref, bf16[896,512]{1,0:T(8,128)(2,1)S(1)} %collective-permute-done.2.left_on, ...), custom_call_target="tpu_custom_call" | custom-call | flops 2415919104 | bytes 12582912 | tf_op jit(solution)/shard_map/pallas_call | solution.py:64
  45.8 1.6 %collective-permute-done.10.two_last = bf16[256,512]{1,0:T(8,128)(2,1)S(1)} collective-permute-done((bf16[256,512]{1,0:T(8,128)(2,1)S(1)}, bf16[256,512]{1,0:T(8,128)(2,1)S(1)}, u32[]{:S(2)}, u32[]{:S(2)}) %collective-permute-start.10) | collective-permute-done | bytes 262176 | tf_op jit(solution)/shard_map/ppermute | solution.py:52
  47.4 2.7 %collective-permute-done.11.left_last = bf16[256,512]{1,0:T(8,128)(2,1)S(1)} collective-permute-done((bf16[256,512]{1,0:T(8,128)(2,1)S(1)}, bf16[256,512]{1,0:T(8,128)(2,1)S(1)}, u32[]{:S(2)}, u32[]{:S(2)}) %collective-permute-start.11) | collective-permute-done | bytes 262176 | tf_op jit(solution)/shard_map/ppermute | solution.py:52
  50.1 0.0 collective-permute-done.12.right_last
  50.1 0.0 collective-permute-done.8.upper_ref
  50.1 0.9 %shard_map.72 = (f32[1040,128]{1,0:T(8,128)S(1)}, f32[1040,128]{1,0:T(8,128)S(1)}) custom-call(f32[1024,1024]{1,0:T(8,128)S(1)} %shard_map.70.acc_ref, bf16[896,512]{1,0:T(8,128)(2,1)S(1)} %get-tuple-element.44.mine_on, bf16[1280,512]{1,0:T(8,128)(2,1)S(1)} %get-tuple-element.51.mine_ref, bf16[896,512]{1,0:T(8,128)(2,1)S(1)} %collective-permute-done.2.left_on, ...), custom_call_target="tpu_custom_call" | custom-call | flops 469762048 | bytes 8388608 | tf_op jit(solution)/shard_map/pallas_call | solution.py:64
  51.0 1.3 %collective-permute-start.13 = (f16[1040,128]{1,0:T(8,128)(2,1)S(1)}, f16[1040,128]{1,0:T(8,128)(2,1)S(1)}, u32[]{:S(2)}, u32[]{:S(2)}) collective-permute-start(f16[1040,128]{1,0:T(8,128)(2,1)S(1)} %convert_element_type.42), channel_id=1, source_target_pairs={{0,8},{1,9},{2,10},{3,11},{4,12},{5,13},{6,14},{7,15},{8,0},{9,1},... | collective-permute-start | bytes 798728 | tf_op jit(solution)/shard_map/ppermute | solution.py:52
  52.4 2.2 %collective-permute-start.14 = (f16[1040,128]{1,0:T(8,128)(2,1)S(1)}, f16[1040,128]{1,0:T(8,128)(2,1)S(1)}, u32[]{:S(2)}, u32[]{:S(2)}) collective-permute-start(f16[1040,128]{1,0:T(8,128)(2,1)S(1)} %convert_element_type.43), channel_id=1, source_target_pairs={{0,4},{1,5},{2,6},{3,7},{4,8},{5,9},{6,10},{7,11},{8,12},{9,13},{1... | collective-permute-start | bytes 798728 | tf_op jit(solution)/shard_map/ppermute | solution.py:52
  54.7 0.8 %shard_map.73 = (f32[1040,128]{1,0:T(8,128)S(1)}, f32[1024,128]{1,0:T(8,128)S(1)}) custom-call(f32[1024,1024]{1,0:T(8,128)S(1)} %shard_map.70.acc_ref, bf16[896,512]{1,0:T(8,128)(2,1)S(1)} %get-tuple-element.44.mine_on, bf16[1280,512]{1,0:T(8,128)(2,1)S(1)} %get-tuple-element.51.mine_ref, bf16[896,512]{1,0:T(8,128)(2,1)S(1)} %collective-permute-done.2.left_on, ...), custom_call_target="tpu_custom_call" | custom-call | flops 469762048 | bytes 8388608 | tf_op jit(solution)/shard_map/pallas_call | solution.py:64
  55.6 0.1 collective-permute-start.15
  55.6 1.5 %shard_map.75 = (f32[1024,128]{1,0:T(8,128)S(1)}, f32[1040,128]{1,0:T(8,128)S(1)}, f32[1040,128]{1,0:T(8,128)S(1)}, f32[1040,128]{1,0:T(8,128)S(1)}) custom-call(f32[1024,1024]{1,0:T(8,128)S(1)} %shard_map.70.acc_ref, bf16[896,512]{1,0:T(8,128)(2,1)S(1)} %get-tuple-element.44.mine_on, bf16[1280,512]{1,0:T(8,128)(2,1)S(1)} %get-tuple-element.51.mine_ref, ...), custom_call_target="tpu_custom_call" | custom-call | flops 939524096 | bytes 8388608 | tf_op jit(solution)/shard_map/pallas_call | solution.py:64
  57.2 2.2 %collective-permute-start.16 = (f16[1040,128]{1,0:T(8,128)(2,1)S(1)}, f16[1040,128]{1,0:T(8,128)(2,1)S(1)}, u32[]{:S(2)}, u32[]{:S(2)}) collective-permute-start(f16[1040,128]{1,0:T(8,128)(2,1)S(1)} %convert_element_type.45), channel_id=1, source_target_pairs={{0,8},{1,9},{2,10},{3,11},{4,12},{5,13},{6,14},{7,15},{8,0},{9,1},... | collective-permute-start | bytes 798728 | tf_op jit(solution)/shard_map/ppermute | solution.py:52
  59.4 1.9 %collective-permute-start.17 = (f16[1040,128]{1,0:T(8,128)(2,1)S(1)}, f16[1040,128]{1,0:T(8,128)(2,1)S(1)}, u32[]{:S(2)}, u32[]{:S(2)}) collective-permute-start(f16[1040,128]{1,0:T(8,128)(2,1)S(1)} %convert_element_type.47), channel_id=1, source_target_pairs={{0,4},{1,5},{2,6},{3,7},{4,8},{5,9},{6,10},{7,11},{8,12},{9,13},{1... | collective-permute-start | bytes 798728 | tf_op jit(solution)/shard_map/ppermute | solution.py:52
  61.3 0.3 collective-permute-start.18
  61.6 0.0 collective-permute-done.14
  61.6 4.5 %collective-permute-done.15 = f16[1040,128]{1,0:T(8,128)(2,1)S(1)} collective-permute-done((f16[1040,128]{1,0:T(8,128)(2,1)S(1)}, f16[1040,128]{1,0:T(8,128)(2,1)S(1)}, u32[]{:S(2)}, u32[]{:S(2)}) %collective-permute-start.15) | collective-permute-done | bytes 266272 | tf_op jit(solution)/shard_map/ppermute | solution.py:52
  66.2 0.3 shard_map.77
  66.6 6.5 %collective-permute-start.19 = (f16[1040,128]{1,0:T(8,128)(2,1)S(1)}, f16[1040,128]{1,0:T(8,128)(2,1)S(1)}, u32[]{:S(2)}, u32[]{:S(2)}) collective-permute-start(f16[1040,128]{1,0:T(8,128)(2,1)S(1)} %convert_element_type.54), channel_id=1, source_target_pairs={{0,16},{16,0},{1,17},{17,1},{2,18},{18,2},{3,19},{19,3},{4,20},{20... | collective-permute-start | bytes 798728 | tf_op jit(solution)/shard_map/ppermute | solution.py:279
  73.1 0.0 collective-permute-done.17
  73.2 0.2 shard_map.76.keep_ref
  73.4 3.7 %shard_map.74 = f32[128,1024]{1,0:T(8,128)} custom-call(bf16[4,128,1024]{2,1,0:T(8,128)(2,1)S(1)} %pad_maximum_fusion.rel_ref, f32[128,1024]{1,0:T(8,128)S(1)} %get-tuple-element.69.first_ref, bf16[1024,4096]{1,0:T(8,128)(2,1)S(1)} %bitcast.12), custom_call_target="tpu_custom_call" | custom-call | flops 1073741824 | bytes 2097152 | tf_op jit(solution)/shard_map/pallas_call | solution.py:64
  77.0 3.3 %collective-permute-done.19 = f16[1040,128]{1,0:T(8,128)(2,1)S(1)} collective-permute-done((f16[1040,128]{1,0:T(8,128)(2,1)S(1)}, f16[1040,128]{1,0:T(8,128)(2,1)S(1)}, u32[]{:S(2)}, u32[]{:S(2)}) %collective-permute-start.19) | collective-permute-done | bytes 266272 | tf_op jit(solution)/shard_map/ppermute | solution.py:279
  80.4 0.9 %shard_map.78 = f32[1024,128]{1,0:T(8,128)} custom-call(f32[1024,128]{1,0:T(8,128)S(1)} %shard_map.76.keep_ref, f32[1040,128]{1,0:T(8,128)S(1)} %convert_element_type.55.rest_0_), custom_call_target="tpu_custom_call" | custom-call | bytes 2097152 | tf_op jit(solution)/shard_map/pallas_call | solution.py:64
  (26 shorter events, 0.6 us)
Async XLA Ops:
  0.6 6.1 %slice-start = ((s8[8388608]{0:T(1024)(128)(4,1)}), s8[4194304]{0:T(1024)(128)(4,1)S(1)}, s32[]{:S(2)}) async-start(s8[8388608]{0:T(1024)(128)(4,1)} %bitcast.9), calls=%async_computation | async-start | bytes 8388608
  0.6 6.1 %slice-start.1 = ((s8[8388608]{0:T(1024)(128)(4,1)}), s8[4194304]{0:T(1024)(128)(4,1)S(1)}, s32[]{:S(2)}) async-start(s8[8388608]{0:T(1024)(128)(4,1)} %bitcast.9), calls=%async_computation.1 | async-start | bytes 8388608
  0.7 6.1 %copy-start = (bf16[128,4096]{1,0:T(8,128)(2,1)S(1)}, bf16[128,4096]{1,0:T(8,128)(2,1)}, u32[]{:S(2)}) copy-start(bf16[128,4096]{1,0:T(8,128)(2,1)} %head_ref.1) | copy-start | bytes 3145732
  3.4 22.2 %collective-permute-start.2 = (bf16[896,512]{1,0:T(8,128)(2,1)S(1)}, bf16[896,512]{1,0:T(8,128)(2,1)S(1)}, u32[]{:S(2)}, u32[]{:S(2)}) collective-permute-start(bf16[896,512]{1,0:T(8,128)(2,1)S(1)} %get-tuple-element.44.mine_on), channel_id=1, source_target_pairs={{0,1},{1,2},{2,3},{3,0},{4,5},{5,6},{6,7},{7,4},{8,9},{9,10},{10,1... | collective-permute-start | bytes 2752520 | tf_op jit(solution)/shard_map/ppermute | solution.py:52
  5.0 20.6 %collective-permute-start.3 = (bf16[896,512]{1,0:T(8,128)(2,1)S(1)}, bf16[896,512]{1,0:T(8,128)(2,1)S(1)}, u32[]{:S(2)}, u32[]{:S(2)}) collective-permute-start(bf16[896,512]{1,0:T(8,128)(2,1)S(1)} %get-tuple-element.45), channel_id=1, source_target_pairs={{0,3},{1,0},{2,1},{3,2},{4,7},{5,4},{6,5},{7,6},{8,11},{9,8},{10,9... | collective-permute-start | bytes 2752520 | tf_op jit(solution)/shard_map/ppermute | solution.py:52
  9.6 3.4 %collective-permute-start = (bf16[128,1024]{1,0:T(8,128)(2,1)S(1)}, bf16[128,1024]{1,0:T(8,128)(2,1)S(1)}, u32[]{:S(2)}, u32[]{:S(2)}) collective-permute-start(bf16[128,1024]{1,0:T(8,128)(2,1)S(1)} %get-tuple-element.42), channel_id=1, source_target_pairs={{128,0},{129,1},{130,2},{131,3},{132,4},{133,5},{134,6},{135,7},{1... | collective-permute-start | bytes 786440 | tf_op jit(solution)/shard_map/ppermute | solution.py:235
  13.1 26.6 %collective-permute-start.6 = (bf16[1280,512]{1,0:T(8,128)(2,1)S(1)}, bf16[1280,512]{1,0:T(8,128)(2,1)S(1)}, u32[]{:S(2)}, u32[]{:S(2)}) collective-permute-start(bf16[1280,512]{1,0:T(8,128)(2,1)S(1)} %get-tuple-element.51.mine_ref), channel_id=1, source_target_pairs={{0,1},{1,2},{2,3},{3,0},{4,5},{5,6},{6,7},{7,4},{8,9},{9,10},{10,1... | collective-permute-start | bytes 3932168 | tf_op jit(solution)/shard_map/ppermute | solution.py:52
  13.4 26.9 %collective-permute-start.7 = (bf16[1280,512]{1,0:T(8,128)(2,1)S(1)}, bf16[1280,512]{1,0:T(8,128)(2,1)S(1)}, u32[]{:S(2)}, u32[]{:S(2)}) collective-permute-start(bf16[1280,512]{1,0:T(8,128)(2,1)S(1)} %get-tuple-element.53), channel_id=1, source_target_pairs={{0,3},{1,0},{2,1},{3,2},{4,7},{5,4},{6,5},{7,6},{8,11},{9,8},{10,9... | collective-permute-start | bytes 3932168 | tf_op jit(solution)/shard_map/ppermute | solution.py:52
  16.4 9.3 %collective-permute-start.1 = (bf16[128,1024]{1,0:T(8,128)(2,1)S(1)}, bf16[128,1024]{1,0:T(8,128)(2,1)S(1)}, u32[]{:S(2)}, u32[]{:S(2)}) collective-permute-start(bf16[128,1024]{1,0:T(8,128)(2,1)S(1)} %add.3), channel_id=1, source_target_pairs={{0,96},{32,0},{64,32},{96,64},{128,160},{160,192},{192,224},{224,1... | collective-permute-start | bytes 786440 | tf_op jit(solution)/shard_map/ppermute | solution.py:214
  25.6 9.5 %collective-permute-start.4 = (bf16[128,1024]{1,0:T(8,128)(2,1)S(1)}, bf16[128,1024]{1,0:T(8,128)(2,1)S(1)}, u32[]{:S(2)}, u32[]{:S(2)}) collective-permute-start(bf16[128,1024]{1,0:T(8,128)(2,1)S(1)} %collective-permute-done.1), channel_id=1, source_target_pairs={{128,32},{160,64},{192,96},{224,0},{129,33},{161,65},{193,97},{225... | collective-permute-start | bytes 786440 | tf_op jit(solution)/shard_map/ppermute | solution.py:214
  26.9 23.2 %collective-permute-start.8 = (bf16[896,512]{1,0:T(8,128)(2,1)S(1)}, bf16[896,512]{1,0:T(8,128)(2,1)S(1)}, u32[]{:S(2)}, u32[]{:S(2)}) collective-permute-start(bf16[896,512]{1,0:T(8,128)(2,1)S(1)} %collective-permute-done.2.left_on), channel_id=1, source_target_pairs={{0,1},{1,2},{2,3},{3,0},{4,5},{5,6},{6,7},{7,4},{8,9},{9,10},{10,1... | collective-permute-start | bytes 2752520 | tf_op jit(solution)/shard_map/ppermute | solution.py:52
  27.0 23.1 %collective-permute-start.9 = (bf16[896,512]{1,0:T(8,128)(2,1)S(1)}, bf16[896,512]{1,0:T(8,128)(2,1)S(1)}, u32[]{:S(2)}, u32[]{:S(2)}) collective-permute-start(bf16[896,512]{1,0:T(8,128)(2,1)S(1)} %collective-permute-done.3.right_on), channel_id=1, source_target_pairs={{0,3},{1,0},{2,1},{3,2},{4,7},{5,4},{6,5},{7,6},{8,11},{9,8},{10,9... | collective-permute-start | bytes 2752520 | tf_op jit(solution)/shard_map/ppermute | solution.py:52
  35.1 3.4 %collective-permute-start.5 = (bf16[128,1024]{1,0:T(8,128)(2,1)S(1)}, bf16[128,1024]{1,0:T(8,128)(2,1)S(1)}, u32[]{:S(2)}, u32[]{:S(2)}) collective-permute-start(bf16[128,1024]{1,0:T(8,128)(2,1)S(1)} %collective-permute-done.1), channel_id=1, source_target_pairs={{128,0},{160,32},{192,64},{224,96},{129,1},{161,33},{193,65},{225,... | collective-permute-start | bytes 786440 | tf_op jit(solution)/shard_map/ppermute | solution.py:214
  39.3 8.1 %collective-permute-start.10 = (bf16[256,512]{1,0:T(8,128)(2,1)S(1)}, bf16[256,512]{1,0:T(8,128)(2,1)S(1)}, u32[]{:S(2)}, u32[]{:S(2)}) collective-permute-start(bf16[256,512]{1,0:T(8,128)(2,1)S(1)} %get-tuple-element.54), channel_id=1, source_target_pairs={{0,2},{1,3},{2,0},{3,1},{4,6},{5,7},{6,4},{7,5},{8,10},{9,11},{10,... | collective-permute-start | bytes 786440 | tf_op jit(solution)/shard_map/ppermute | solution.py:52
  39.7 10.4 %collective-permute-start.11 = (bf16[256,512]{1,0:T(8,128)(2,1)S(1)}, bf16[256,512]{1,0:T(8,128)(2,1)S(1)}, u32[]{:S(2)}, u32[]{:S(2)}) collective-permute-start(bf16[256,512]{1,0:T(8,128)(2,1)S(1)} %get-tuple-element.55), channel_id=1, source_target_pairs={{0,1},{1,2},{2,3},{3,0},{4,5},{5,6},{6,7},{7,4},{8,9},{9,10},{10,1... | collective-permute-start | bytes 786440 | tf_op jit(solution)/shard_map/ppermute | solution.py:52
  40.3 9.8 %collective-permute-start.12 = (bf16[256,512]{1,0:T(8,128)(2,1)S(1)}, bf16[256,512]{1,0:T(8,128)(2,1)S(1)}, u32[]{:S(2)}, u32[]{:S(2)}) collective-permute-start(bf16[256,512]{1,0:T(8,128)(2,1)S(1)} %get-tuple-element.56), channel_id=1, source_target_pairs={{0,3},{1,0},{2,1},{3,2},{4,7},{5,4},{6,5},{7,6},{8,11},{9,8},{10,9... | collective-permute-start | bytes 786440 | tf_op jit(solution)/shard_map/ppermute | solution.py:52
  51.0 10.3 %collective-permute-start.13 = (f16[1040,128]{1,0:T(8,128)(2,1)S(1)}, f16[1040,128]{1,0:T(8,128)(2,1)S(1)}, u32[]{:S(2)}, u32[]{:S(2)}) collective-permute-start(f16[1040,128]{1,0:T(8,128)(2,1)S(1)} %convert_element_type.42), channel_id=1, source_target_pairs={{0,8},{1,9},{2,10},{3,11},{4,12},{5,13},{6,14},{7,15},{8,0},{9,1},... | collective-permute-start | bytes 798728 | tf_op jit(solution)/shard_map/ppermute | solution.py:52
  52.4 9.2 %collective-permute-start.14 = (f16[1040,128]{1,0:T(8,128)(2,1)S(1)}, f16[1040,128]{1,0:T(8,128)(2,1)S(1)}, u32[]{:S(2)}, u32[]{:S(2)}) collective-permute-start(f16[1040,128]{1,0:T(8,128)(2,1)S(1)} %convert_element_type.43), channel_id=1, source_target_pairs={{0,4},{1,5},{2,6},{3,7},{4,8},{5,9},{6,10},{7,11},{8,12},{9,13},{1... | collective-permute-start | bytes 798728 | tf_op jit(solution)/shard_map/ppermute | solution.py:52
  55.6 10.6 %collective-permute-start.15 = (f16[1040,128]{1,0:T(8,128)(2,1)S(1)}, f16[1040,128]{1,0:T(8,128)(2,1)S(1)}, u32[]{:S(2)}, u32[]{:S(2)}) collective-permute-start(f16[1040,128]{1,0:T(8,128)(2,1)S(1)} %convert_element_type.44), channel_id=1, source_target_pairs={{0,12},{1,13},{2,14},{3,15},{4,0},{5,1},{6,2},{7,3},{8,4},{9,5},{1... | collective-permute-start | bytes 798728 | tf_op jit(solution)/shard_map/ppermute | solution.py:52
  57.2 15.9 %collective-permute-start.16 = (f16[1040,128]{1,0:T(8,128)(2,1)S(1)}, f16[1040,128]{1,0:T(8,128)(2,1)S(1)}, u32[]{:S(2)}, u32[]{:S(2)}) collective-permute-start(f16[1040,128]{1,0:T(8,128)(2,1)S(1)} %convert_element_type.45), channel_id=1, source_target_pairs={{0,8},{1,9},{2,10},{3,11},{4,12},{5,13},{6,14},{7,15},{8,0},{9,1},... | collective-permute-start | bytes 798728 | tf_op jit(solution)/shard_map/ppermute | solution.py:52
  59.4 13.7 %collective-permute-start.17 = (f16[1040,128]{1,0:T(8,128)(2,1)S(1)}, f16[1040,128]{1,0:T(8,128)(2,1)S(1)}, u32[]{:S(2)}, u32[]{:S(2)}) collective-permute-start(f16[1040,128]{1,0:T(8,128)(2,1)S(1)} %convert_element_type.47), channel_id=1, source_target_pairs={{0,4},{1,5},{2,6},{3,7},{4,8},{5,9},{6,10},{7,11},{8,12},{9,13},{1... | collective-permute-start | bytes 798728 | tf_op jit(solution)/shard_map/ppermute | solution.py:52
  61.3 11.8 %collective-permute-start.18 = (f16[1040,128]{1,0:T(8,128)(2,1)S(1)}, f16[1040,128]{1,0:T(8,128)(2,1)S(1)}, u32[]{:S(2)}, u32[]{:S(2)}) collective-permute-start(f16[1040,128]{1,0:T(8,128)(2,1)S(1)} %convert_element_type.49), channel_id=1, source_target_pairs={{0,12},{1,13},{2,14},{3,15},{4,0},{5,1},{6,2},{7,3},{8,4},{9,5},{1... | collective-permute-start | bytes 798728 | tf_op jit(solution)/shard_map/ppermute | solution.py:52
  66.6 13.8 %collective-permute-start.19 = (f16[1040,128]{1,0:T(8,128)(2,1)S(1)}, f16[1040,128]{1,0:T(8,128)(2,1)S(1)}, u32[]{:S(2)}, u32[]{:S(2)}) collective-permute-start(f16[1040,128]{1,0:T(8,128)(2,1)S(1)} %convert_element_type.54), channel_id=1, source_target_pairs={{0,16},{16,0},{1,17},{17,1},{2,18},{18,2},{3,19},{19,3},{4,20},{20... | collective-permute-start | bytes 798728 | tf_op jit(solution)/shard_map/ppermute | solution.py:279

commit v17 on v12

--- a/solution.py
+++ b/solution.py
@@ -228,8 +228,7 @@
 
     first, small = call(first_kernel, [((rows, width), F32), ((rows, width), BF16)], (head_grad, weights[0]), whole(2), **matmul)
     shard = lax.ppermute(small, "section", [(1, 0)])
-    staying_right, staying_left, shard = lax.optimization_barrier((right, left, shard))
-    from_left, from_right = shifted(staying_right, True, 1), shifted(staying_left, True, -1)
+    from_left, from_right = shifted(right, True, 1), shifted(left, True, -1)
     places = range(RING)
     both = small + shard
     passed = on_line(both, [((0, i), (0, i - 1)) for i in places] + [((1, i), (1, i + 1)) for i in places])

time: 81.5 us -> 81.1 us (level)
  transfers between devices with their start and end apart: 20 -> 20, of which waited for: 9 -> 8; matrix products, arithmetic and copies ran while one was open for 1% -> 1% of each run, Pallas kernels for 15% -> 15%
where the time goes in v17:
time: 81.1 us; the launch traced here: 81 us
  starting transfers between devices  37.3 us (46%)
  waiting for transfers between devices  25.1 us (31%)
  Pallas kernels  17 us (21%)
  between operations  0.88 us (1%)
    ppermute x15, starting transfers between devices, shifted(): return lax.ppermute(value, ('section', 'y', 'x'), pairs_over(along, by))  21.8 us
    pallas_call x9, Pallas kernels, call(): pl.pallas_call(kernel, out_shape=[jax.ShapeDtypeStruct(s, t) for s, t in...  17 us
    ppermute x3, waiting for transfers between devices, on_line(): return lax.ppermute(value, ('section', 'z_lo'), pairs)  10.9 us
    ppermute x15, waiting for transfers between devices, shifted(): return lax.ppermute(value, ('section', 'y', 'x'), pairs_over(along, by))  8.46 us
    ppermute x3, starting transfers between devices, on_line(): return lax.ppermute(value, ('section', 'z_lo'), pairs)  7.26 us
    ppermute x1, starting transfers between devices, local(): other = lax.ppermute(far.astype(F16), 'z_hi', [(0, 1), (1, 0)]).astype(F32)  6.95 us
    ppermute x1, waiting for transfers between devices, local(): other = lax.ppermute(far.astype(F16), 'z_hi', [(0, 1), (1, 0)]).astype(F32)  3.55 us
    ppermute x1, waiting for transfers between devices, local(): shard = lax.ppermute(small, 'section', [(1, 0)])  2.13 us
  transfers between devices with their start and end apart: 20, of which 8 were waited for; matrix products, arithmetic and copies ran while one was open for 1% of the time, Pallas kernels for 15%

profile of v17, /device:TPU:24, one launch (start us, length us, event | category | flops | bytes accessed | tf_op | source)
XLA Modules:
  0.0 81.0 jit_solution(7594672600084311428)
XLA Ops:
  0.6 0.0 slice-start
  0.6 0.0 slice-start.1
  0.7 2.7 %shard_map.69 = (bf16[896,512]{1,0:T(8,128)(2,1)S(1)}, bf16[896,512]{1,0:T(8,128)(2,1)S(1)}, bf16[1280,512]{1,0:T(8,128)(2,1)S(1)}, bf16[1280,512]{1,0:T(8,128)(2,1)S(1)}, bf16[768,512]{1,0:T(8,128)(2,1)S(1)}) custom-call(s32[2]{0:T(128)} %pending_ref.1, bf16[4,128,1024]{2,1,0:T(8,128)(2,1)} %bitcast.20, bf16[3,128,4096]{2,1,0:T(8,128)(2,1)} %bitcast.19), custom_call_target="tpu_custom_call" | custom-call | flops 10000000000 | bytes 12582912 | tf_op jit(solution)/shard_map/pallas_call | solution.py:64
  3.4 1.6 %collective-permute-start.2 = (bf16[896,512]{1,0:T(8,128)(2,1)S(1)}, bf16[896,512]{1,0:T(8,128)(2,1)S(1)}, u32[]{:S(2)}, u32[]{:S(2)}) collective-permute-start(bf16[896,512]{1,0:T(8,128)(2,1)S(1)} %get-tuple-element.38.mine_on), channel_id=1, source_target_pairs={{0,1},{1,2},{2,3},{3,0},{4,5},{5,6},{6,7},{7,4},{8,9},{9,10},{10,1... | collective-permute-start | bytes 2752520 | tf_op jit(solution)/shard_map/ppermute | solution.py:52
  5.0 1.7 %collective-permute-start.3 = (bf16[896,512]{1,0:T(8,128)(2,1)S(1)}, bf16[896,512]{1,0:T(8,128)(2,1)S(1)}, u32[]{:S(2)}, u32[]{:S(2)}) collective-permute-start(bf16[896,512]{1,0:T(8,128)(2,1)S(1)} %get-tuple-element.39), channel_id=1, source_target_pairs={{0,3},{1,0},{2,1},{3,2},{4,7},{5,4},{6,5},{7,6},{8,11},{9,8},{10,9... | collective-permute-start | bytes 2752520 | tf_op jit(solution)/shard_map/ppermute | solution.py:52
  6.7 0.3 collective-permute-start.6
  7.0 3.0 %collective-permute-start.7 = (bf16[1280,512]{1,0:T(8,128)(2,1)S(1)}, bf16[1280,512]{1,0:T(8,128)(2,1)S(1)}, u32[]{:S(2)}, u32[]{:S(2)}) collective-permute-start(bf16[1280,512]{1,0:T(8,128)(2,1)S(1)} %get-tuple-element.47), channel_id=1, source_target_pairs={{0,3},{1,0},{2,1},{3,2},{4,7},{5,4},{6,5},{7,6},{8,11},{9,8},{10,9... | collective-permute-start | bytes 3932168 | tf_op jit(solution)/shard_map/ppermute | solution.py:52
  10.0 2.9 %shard_map.68 = (f32[128,1024]{1,0:T(8,128)S(1)}, bf16[128,1024]{1,0:T(8,128)(2,1)S(1)}) custom-call(bf16[128,4096]{1,0:T(8,128)(2,1)S(1)} %copy-done, bf16[1024,4096]{1,0:T(8,128)(2,1)S(1)} %bitcast.11), custom_call_target="tpu_custom_call" | custom-call | flops 1073741824 | bytes 2097152 | tf_op jit(solution)/shard_map/pallas_call | solution.py:64
  12.8 1.3 %collective-permute-start = (bf16[128,1024]{1,0:T(8,128)(2,1)S(1)}, bf16[128,1024]{1,0:T(8,128)(2,1)S(1)}, u32[]{:S(2)}, u32[]{:S(2)}) collective-permute-start(bf16[128,1024]{1,0:T(8,128)(2,1)S(1)} %get-tuple-element.37), channel_id=1, source_target_pairs={{128,0},{129,1},{130,2},{131,3},{132,4},{133,5},{134,6},{135,7},{1... | collective-permute-start | bytes 786440 | tf_op jit(solution)/shard_map/ppermute | solution.py:230
  14.1 2.1 %collective-permute-done = bf16[128,1024]{1,0:T(8,128)(2,1)S(1)} collective-permute-done((bf16[128,1024]{1,0:T(8,128)(2,1)S(1)}, bf16[128,1024]{1,0:T(8,128)(2,1)S(1)}, u32[]{:S(2)}, u32[]{:S(2)}) %collective-permute-start) | collective-permute-done | bytes 262176 | tf_op jit(solution)/shard_map/ppermute | solution.py:230
  16.3 0.1 add.3
  16.3 4.7 %collective-permute-start.1 = (bf16[128,1024]{1,0:T(8,128)(2,1)S(1)}, bf16[128,1024]{1,0:T(8,128)(2,1)S(1)}, u32[]{:S(2)}, u32[]{:S(2)}) collective-permute-start(bf16[128,1024]{1,0:T(8,128)(2,1)S(1)} %add.3), channel_id=1, source_target_pairs={{0,96},{32,0},{64,32},{96,64},{128,160},{160,192},{192,224},{224,1... | collective-permute-start | bytes 786440 | tf_op jit(solution)/shard_map/ppermute | solution.py:209
  21.0 3.9 %collective-permute-done.1 = bf16[128,1024]{1,0:T(8,128)(2,1)S(1)} collective-permute-done((bf16[128,1024]{1,0:T(8,128)(2,1)S(1)}, bf16[128,1024]{1,0:T(8,128)(2,1)S(1)}, u32[]{:S(2)}, u32[]{:S(2)}) %collective-permute-start.1) | collective-permute-done | bytes 262176 | tf_op jit(solution)/shard_map/ppermute | solution.py:209
  24.9 0.0 collective-permute-done.2.left_on
  24.9 0.0 collective-permute-done.3.right_on
  24.9 1.3 %collective-permute-start.4 = (bf16[128,1024]{1,0:T(8,128)(2,1)S(1)}, bf16[128,1024]{1,0:T(8,128)(2,1)S(1)}, u32[]{:S(2)}, u32[]{:S(2)}) collective-permute-start(bf16[128,1024]{1,0:T(8,128)(2,1)S(1)} %collective-permute-done.1), channel_id=1, source_target_pairs={{128,32},{160,64},{192,96},{224,0},{129,33},{161,65},{193,97},{225... | collective-permute-start | bytes 786440 | tf_op jit(solution)/shard_map/ppermute | solution.py:209
  26.2 0.1 collective-permute-start.8
  26.3 3.2 %collective-permute-start.9 = (bf16[896,512]{1,0:T(8,128)(2,1)S(1)}, bf16[896,512]{1,0:T(8,128)(2,1)S(1)}, u32[]{:S(2)}, u32[]{:S(2)}) collective-permute-start(bf16[896,512]{1,0:T(8,128)(2,1)S(1)} %collective-permute-done.3.right_on), channel_id=1, source_target_pairs={{0,3},{1,0},{2,1},{3,2},{4,7},{5,4},{6,5},{7,6},{8,11},{9,8},{10,9... | collective-permute-start | bytes 2752520 | tf_op jit(solution)/shard_map/ppermute | solution.py:52
  29.6 4.9 %collective-permute-done.4 = bf16[128,1024]{1,0:T(8,128)(2,1)S(1)} collective-permute-done((bf16[128,1024]{1,0:T(8,128)(2,1)S(1)}, bf16[128,1024]{1,0:T(8,128)(2,1)S(1)}, u32[]{:S(2)}, u32[]{:S(2)}) %collective-permute-start.4) | collective-permute-done | bytes 262176 | tf_op jit(solution)/shard_map/ppermute | solution.py:209
  34.4 1.3 %collective-permute-start.5 = (bf16[128,1024]{1,0:T(8,128)(2,1)S(1)}, bf16[128,1024]{1,0:T(8,128)(2,1)S(1)}, u32[]{:S(2)}, u32[]{:S(2)}) collective-permute-start(bf16[128,1024]{1,0:T(8,128)(2,1)S(1)} %collective-permute-done.1), channel_id=1, source_target_pairs={{128,0},{160,32},{192,64},{224,96},{129,1},{161,33},{193,65},{225,... | collective-permute-start | bytes 786440 | tf_op jit(solution)/shard_map/ppermute | solution.py:209
  35.7 2.1 %collective-permute-done.5 = bf16[128,1024]{1,0:T(8,128)(2,1)S(1)} collective-permute-done((bf16[128,1024]{1,0:T(8,128)(2,1)S(1)}, bf16[128,1024]{1,0:T(8,128)(2,1)S(1)}, u32[]{:S(2)}, u32[]{:S(2)}) %collective-permute-start.5) | collective-permute-done | bytes 262176 | tf_op jit(solution)/shard_map/ppermute | solution.py:209
  37.9 0.1 pad_maximum_fusion.rel_ref
  38.0 0.6 shard_map.71
  38.6 0.7 collective-permute-start.10
  39.3 0.0 collective-permute-done.6.left_ref
  39.3 0.6 collective-permute-start.11
  39.9 0.0 collective-permute-done.7.right_ref
  39.9 2.6 %collective-permute-start.12 = (bf16[256,512]{1,0:T(8,128)(2,1)S(1)}, bf16[256,512]{1,0:T(8,128)(2,1)S(1)}, u32[]{:S(2)}, u32[]{:S(2)}) collective-permute-start(bf16[256,512]{1,0:T(8,128)(2,1)S(1)} %get-tuple-element.50), channel_id=1, source_target_pairs={{0,3},{1,0},{2,1},{3,2},{4,7},{5,4},{6,5},{7,6},{8,11},{9,8},{10,9... | collective-permute-start | bytes 786440 | tf_op jit(solution)/shard_map/ppermute | solution.py:52
  42.6 2.9 %shard_map.70.acc_ref = f32[1024,1024]{1,0:T(8,128)S(1)} custom-call(bf16[896,512]{1,0:T(8,128)(2,1)S(1)} %get-tuple-element.38.mine_on, bf16[1280,512]{1,0:T(8,128)(2,1)S(1)} %get-tuple-element.43.mine_ref, bf16[768,512]{1,0:T(8,128)(2,1)S(1)} %get-tuple-element.44.own_ref, bf16[896,512]{1,0:T(8,128)(2,1)S(1)} %collective-permute-done.2.left_on, ...), custom_call_target="tpu_custom_call" | custom-call | flops 2415919104 | bytes 12582912 | tf_op jit(solution)/shard_map/pallas_call | solution.py:64
  45.4 1.3 %collective-permute-done.10.two_last = bf16[256,512]{1,0:T(8,128)(2,1)S(1)} collective-permute-done((bf16[256,512]{1,0:T(8,128)(2,1)S(1)}, bf16[256,512]{1,0:T(8,128)(2,1)S(1)}, u32[]{:S(2)}, u32[]{:S(2)}) %collective-permute-start.10) | collective-permute-done | bytes 262176 | tf_op jit(solution)/shard_map/ppermute | solution.py:52
  46.7 2.7 %collective-permute-done.11.left_last = bf16[256,512]{1,0:T(8,128)(2,1)S(1)} collective-permute-done((bf16[256,512]{1,0:T(8,128)(2,1)S(1)}, bf16[256,512]{1,0:T(8,128)(2,1)S(1)}, u32[]{:S(2)}, u32[]{:S(2)}) %collective-permute-start.11) | collective-permute-done | bytes 262176 | tf_op jit(solution)/shard_map/ppermute | solution.py:52
  49.4 1.5 %shard_map.72 = (f32[1024,128]{1,0:T(8,128)S(1)}, f32[1040,128]{1,0:T(8,128)S(1)}, f32[1040,128]{1,0:T(8,128)S(1)}, f32[1040,128]{1,0:T(8,128)S(1)}) custom-call(f32[1024,1024]{1,0:T(8,128)S(1)} %shard_map.70.acc_ref, bf16[896,512]{1,0:T(8,128)(2,1)S(1)} %get-tuple-element.38.mine_on, bf16[1280,512]{1,0:T(8,128)(2,1)S(1)} %get-tuple-element.43.mine_ref, ...), custom_call_target="tpu_custom_call" | custom-call | flops 939524096 | bytes 8388608 | tf_op jit(solution)/shard_map/pallas_call | solution.py:64
  50.9 1.3 %collective-permute-start.13 = (f16[1040,128]{1,0:T(8,128)(2,1)S(1)}, f16[1040,128]{1,0:T(8,128)(2,1)S(1)}, u32[]{:S(2)}, u32[]{:S(2)}) collective-permute-start(f16[1040,128]{1,0:T(8,128)(2,1)S(1)} %convert_element_type.42), channel_id=1, source_target_pairs={{0,8},{1,9},{2,10},{3,11},{4,12},{5,13},{6,14},{7,15},{8,0},{9,1},... | collective-permute-start | bytes 798728 | tf_op jit(solution)/shard_map/ppermute | solution.py:52
  52.3 2.3 %collective-permute-start.14 = (f16[1040,128]{1,0:T(8,128)(2,1)S(1)}, f16[1040,128]{1,0:T(8,128)(2,1)S(1)}, u32[]{:S(2)}, u32[]{:S(2)}) collective-permute-start(f16[1040,128]{1,0:T(8,128)(2,1)S(1)} %convert_element_type.43), channel_id=1, source_target_pairs={{0,4},{1,5},{2,6},{3,7},{4,8},{5,9},{6,10},{7,11},{8,12},{9,13},{1... | collective-permute-start | bytes 798728 | tf_op jit(solution)/shard_map/ppermute | solution.py:52
  54.6 0.1 collective-permute-start.15
  54.7 1.5 %shard_map.74 = (f32[1024,128]{1,0:T(8,128)S(1)}, f32[1040,128]{1,0:T(8,128)S(1)}, f32[1040,128]{1,0:T(8,128)S(1)}, f32[1040,128]{1,0:T(8,128)S(1)}) custom-call(f32[1024,1024]{1,0:T(8,128)S(1)} %shard_map.70.acc_ref, bf16[896,512]{1,0:T(8,128)(2,1)S(1)} %get-tuple-element.38.mine_on, bf16[1280,512]{1,0:T(8,128)(2,1)S(1)} %get-tuple-element.43.mine_ref, ...), custom_call_target="tpu_custom_call" | custom-call | flops 939524096 | bytes 8388608 | tf_op jit(solution)/shard_map/pallas_call | solution.py:64
  56.2 2.2 %collective-permute-start.16 = (f16[1040,128]{1,0:T(8,128)(2,1)S(1)}, f16[1040,128]{1,0:T(8,128)(2,1)S(1)}, u32[]{:S(2)}, u32[]{:S(2)}) collective-permute-start(f16[1040,128]{1,0:T(8,128)(2,1)S(1)} %convert_element_type.45), channel_id=1, source_target_pairs={{0,8},{1,9},{2,10},{3,11},{4,12},{5,13},{6,14},{7,15},{8,0},{9,1},... | collective-permute-start | bytes 798728 | tf_op jit(solution)/shard_map/ppermute | solution.py:52
  58.5 1.5 %collective-permute-start.17 = (f16[1040,128]{1,0:T(8,128)(2,1)S(1)}, f16[1040,128]{1,0:T(8,128)(2,1)S(1)}, u32[]{:S(2)}, u32[]{:S(2)}) collective-permute-start(f16[1040,128]{1,0:T(8,128)(2,1)S(1)} %convert_element_type.47), channel_id=1, source_target_pairs={{0,4},{1,5},{2,6},{3,7},{4,8},{5,9},{6,10},{7,11},{8,12},{9,13},{1... | collective-permute-start | bytes 798728 | tf_op jit(solution)/shard_map/ppermute | solution.py:52
  60.0 0.7 collective-permute-start.18
  60.7 0.0 collective-permute-done.14
  60.7 4.5 %collective-permute-done.15 = f16[1040,128]{1,0:T(8,128)(2,1)S(1)} collective-permute-done((f16[1040,128]{1,0:T(8,128)(2,1)S(1)}, f16[1040,128]{1,0:T(8,128)(2,1)S(1)}, u32[]{:S(2)}, u32[]{:S(2)}) %collective-permute-start.15) | collective-permute-done | bytes 266272 | tf_op jit(solution)/shard_map/ppermute | solution.py:52
  65.3 0.3 shard_map.75
  65.6 6.9 %collective-permute-start.19 = (f16[1040,128]{1,0:T(8,128)(2,1)S(1)}, f16[1040,128]{1,0:T(8,128)(2,1)S(1)}, u32[]{:S(2)}, u32[]{:S(2)}) collective-permute-start(f16[1040,128]{1,0:T(8,128)(2,1)S(1)} %convert_element_type.54), channel_id=1, source_target_pairs={{0,16},{16,0},{1,17},{17,1},{2,18},{18,2},{3,19},{19,3},{4,20},{20... | collective-permute-start | bytes 798728 | tf_op jit(solution)/shard_map/ppermute | solution.py:272
  72.6 0.0 collective-permute-done.17
  72.7 0.0 collective-permute-done.18
  72.7 3.7 %shard_map.73 = f32[128,1024]{1,0:T(8,128)} custom-call(bf16[4,128,1024]{2,1,0:T(8,128)(2,1)S(1)} %pad_maximum_fusion.rel_ref, f32[128,1024]{1,0:T(8,128)S(1)} %get-tuple-element.63.first_ref, bf16[1024,4096]{1,0:T(8,128)(2,1)S(1)} %bitcast.12), custom_call_target="tpu_custom_call" | custom-call | flops 1073741824 | bytes 2097152 | tf_op jit(solution)/shard_map/pallas_call | solution.py:64
  76.4 3.5 %collective-permute-done.19 = f16[1040,128]{1,0:T(8,128)(2,1)S(1)} collective-permute-done((f16[1040,128]{1,0:T(8,128)(2,1)S(1)}, f16[1040,128]{1,0:T(8,128)(2,1)S(1)}, u32[]{:S(2)}, u32[]{:S(2)}) %collective-permute-start.19) | collective-permute-done | bytes 266272 | tf_op jit(solution)/shard_map/ppermute | solution.py:272
  80.0 1.0 %shard_map.76 = f32[1024,128]{1,0:T(8,128)} custom-call(f32[1024,128]{1,0:T(8,128)S(1)} %get-tuple-element.64.keep_ref, f32[1040,128]{1,0:T(8,128)S(1)} %convert_element_type.46.one_ref, f32[1040,128]{1,0:T(8,128)S(1)} %convert_element_type.48.two_ref, f32[1040,128]{1,0:T(8,128)S(1)} %convert_element_type.50.three_ref, ...), custom_call_target="tpu_custom_call" | custom-call | bytes 4194304 | tf_op jit(solution)/shard_map/pallas_call | solution.py:64
  (24 shorter events, 0.5 us)
Async XLA Ops:
  0.6 9.3 %slice-start = ((s8[8388608]{0:T(1024)(128)(4,1)}), s8[4194304]{0:T(1024)(128)(4,1)S(1)}, s32[]{:S(2)}) async-start(s8[8388608]{0:T(1024)(128)(4,1)} %bitcast.9), calls=%async_computation | async-start | bytes 8388608
  0.6 9.3 %slice-start.1 = ((s8[8388608]{0:T(1024)(128)(4,1)}), s8[4194304]{0:T(1024)(128)(4,1)S(1)}, s32[]{:S(2)}) async-start(s8[8388608]{0:T(1024)(128)(4,1)} %bitcast.9), calls=%async_computation.1 | async-start | bytes 8388608
  0.7 9.3 %copy-start = (bf16[128,4096]{1,0:T(8,128)(2,1)S(1)}, bf16[128,4096]{1,0:T(8,128)(2,1)}, u32[]{:S(2)}) copy-start(bf16[128,4096]{1,0:T(8,128)(2,1)} %head_ref.1) | copy-start | bytes 3145732
  3.4 21.5 %collective-permute-start.2 = (bf16[896,512]{1,0:T(8,128)(2,1)S(1)}, bf16[896,512]{1,0:T(8,128)(2,1)S(1)}, u32[]{:S(2)}, u32[]{:S(2)}) collective-permute-start(bf16[896,512]{1,0:T(8,128)(2,1)S(1)} %get-tuple-element.38.mine_on), channel_id=1, source_target_pairs={{0,1},{1,2},{2,3},{3,0},{4,5},{5,6},{6,7},{7,4},{8,9},{9,10},{10,1... | collective-permute-start | bytes 2752520 | tf_op jit(solution)/shard_map/ppermute | solution.py:52
  5.0 20.0 %collective-permute-start.3 = (bf16[896,512]{1,0:T(8,128)(2,1)S(1)}, bf16[896,512]{1,0:T(8,128)(2,1)S(1)}, u32[]{:S(2)}, u32[]{:S(2)}) collective-permute-start(bf16[896,512]{1,0:T(8,128)(2,1)S(1)} %get-tuple-element.39), channel_id=1, source_target_pairs={{0,3},{1,0},{2,1},{3,2},{4,7},{5,4},{6,5},{7,6},{8,11},{9,8},{10,9... | collective-permute-start | bytes 2752520 | tf_op jit(solution)/shard_map/ppermute | solution.py:52
  6.7 32.6 %collective-permute-start.6 = (bf16[1280,512]{1,0:T(8,128)(2,1)S(1)}, bf16[1280,512]{1,0:T(8,128)(2,1)S(1)}, u32[]{:S(2)}, u32[]{:S(2)}) collective-permute-start(bf16[1280,512]{1,0:T(8,128)(2,1)S(1)} %get-tuple-element.43.mine_ref), channel_id=1, source_target_pairs={{0,1},{1,2},{2,3},{3,0},{4,5},{5,6},{6,7},{7,4},{8,9},{9,10},{10,1... | collective-permute-start | bytes 3932168 | tf_op jit(solution)/shard_map/ppermute | solution.py:52
  7.0 32.9 %collective-permute-start.7 = (bf16[1280,512]{1,0:T(8,128)(2,1)S(1)}, bf16[1280,512]{1,0:T(8,128)(2,1)S(1)}, u32[]{:S(2)}, u32[]{:S(2)}) collective-permute-start(bf16[1280,512]{1,0:T(8,128)(2,1)S(1)} %get-tuple-element.47), channel_id=1, source_target_pairs={{0,3},{1,0},{2,1},{3,2},{4,7},{5,4},{6,5},{7,6},{8,11},{9,8},{10,9... | collective-permute-start | bytes 3932168 | tf_op jit(solution)/shard_map/ppermute | solution.py:52
  12.8 3.4 %collective-permute-start = (bf16[128,1024]{1,0:T(8,128)(2,1)S(1)}, bf16[128,1024]{1,0:T(8,128)(2,1)S(1)}, u32[]{:S(2)}, u32[]{:S(2)}) collective-permute-start(bf16[128,1024]{1,0:T(8,128)(2,1)S(1)} %get-tuple-element.37), channel_id=1, source_target_pairs={{128,0},{129,1},{130,2},{131,3},{132,4},{133,5},{134,6},{135,7},{1... | collective-permute-start | bytes 786440 | tf_op jit(solution)/shard_map/ppermute | solution.py:230
  16.3 8.6 %collective-permute-start.1 = (bf16[128,1024]{1,0:T(8,128)(2,1)S(1)}, bf16[128,1024]{1,0:T(8,128)(2,1)S(1)}, u32[]{:S(2)}, u32[]{:S(2)}) collective-permute-start(bf16[128,1024]{1,0:T(8,128)(2,1)S(1)} %add.3), channel_id=1, source_target_pairs={{0,96},{32,0},{64,32},{96,64},{128,160},{160,192},{192,224},{224,1... | collective-permute-start | bytes 786440 | tf_op jit(solution)/shard_map/ppermute | solution.py:209
  24.9 9.5 %collective-permute-start.4 = (bf16[128,1024]{1,0:T(8,128)(2,1)S(1)}, bf16[128,1024]{1,0:T(8,128)(2,1)S(1)}, u32[]{:S(2)}, u32[]{:S(2)}) collective-permute-start(bf16[128,1024]{1,0:T(8,128)(2,1)S(1)} %collective-permute-done.1), channel_id=1, source_target_pairs={{128,32},{160,64},{192,96},{224,0},{129,33},{161,65},{193,97},{225... | collective-permute-start | bytes 786440 | tf_op jit(solution)/shard_map/ppermute | solution.py:209
  26.2 23.2 %collective-permute-start.8 = (bf16[896,512]{1,0:T(8,128)(2,1)S(1)}, bf16[896,512]{1,0:T(8,128)(2,1)S(1)}, u32[]{:S(2)}, u32[]{:S(2)}) collective-permute-start(bf16[896,512]{1,0:T(8,128)(2,1)S(1)} %collective-permute-done.2.left_on), channel_id=1, source_target_pairs={{0,1},{1,2},{2,3},{3,0},{4,5},{5,6},{6,7},{7,4},{8,9},{9,10},{10,1... | collective-permute-start | bytes 2752520 | tf_op jit(solution)/shard_map/ppermute | solution.py:52
  26.3 23.1 %collective-permute-start.9 = (bf16[896,512]{1,0:T(8,128)(2,1)S(1)}, bf16[896,512]{1,0:T(8,128)(2,1)S(1)}, u32[]{:S(2)}, u32[]{:S(2)}) collective-permute-start(bf16[896,512]{1,0:T(8,128)(2,1)S(1)} %collective-permute-done.3.right_on), channel_id=1, source_target_pairs={{0,3},{1,0},{2,1},{3,2},{4,7},{5,4},{6,5},{7,6},{8,11},{9,8},{10,9... | collective-permute-start | bytes 2752520 | tf_op jit(solution)/shard_map/ppermute | solution.py:52
  34.4 3.4 %collective-permute-start.5 = (bf16[128,1024]{1,0:T(8,128)(2,1)S(1)}, bf16[128,1024]{1,0:T(8,128)(2,1)S(1)}, u32[]{:S(2)}, u32[]{:S(2)}) collective-permute-start(bf16[128,1024]{1,0:T(8,128)(2,1)S(1)} %collective-permute-done.1), channel_id=1, source_target_pairs={{128,0},{160,32},{192,64},{224,96},{129,1},{161,33},{193,65},{225,... | collective-permute-start | bytes 786440 | tf_op jit(solution)/shard_map/ppermute | solution.py:209
  38.6 8.1 %collective-permute-start.10 = (bf16[256,512]{1,0:T(8,128)(2,1)S(1)}, bf16[256,512]{1,0:T(8,128)(2,1)S(1)}, u32[]{:S(2)}, u32[]{:S(2)}) collective-permute-start(bf16[256,512]{1,0:T(8,128)(2,1)S(1)} %get-tuple-element.48), channel_id=1, source_target_pairs={{0,2},{1,3},{2,0},{3,1},{4,6},{5,7},{6,4},{7,5},{8,10},{9,11},{10,... | collective-permute-start | bytes 786440 | tf_op jit(solution)/shard_map/ppermute | solution.py:52
  39.3 10.1 %collective-permute-start.11 = (bf16[256,512]{1,0:T(8,128)(2,1)S(1)}, bf16[256,512]{1,0:T(8,128)(2,1)S(1)}, u32[]{:S(2)}, u32[]{:S(2)}) collective-permute-start(bf16[256,512]{1,0:T(8,128)(2,1)S(1)} %get-tuple-element.49), channel_id=1, source_target_pairs={{0,1},{1,2},{2,3},{3,0},{4,5},{5,6},{6,7},{7,4},{8,9},{9,10},{10,1... | collective-permute-start | bytes 786440 | tf_op jit(solution)/shard_map/ppermute | solution.py:52
  39.9 9.5 %collective-permute-start.12 = (bf16[256,512]{1,0:T(8,128)(2,1)S(1)}, bf16[256,512]{1,0:T(8,128)(2,1)S(1)}, u32[]{:S(2)}, u32[]{:S(2)}) collective-permute-start(bf16[256,512]{1,0:T(8,128)(2,1)S(1)} %get-tuple-element.50), channel_id=1, source_target_pairs={{0,3},{1,0},{2,1},{3,2},{4,7},{5,4},{6,5},{7,6},{8,11},{9,8},{10,9... | collective-permute-start | bytes 786440 | tf_op jit(solution)/shard_map/ppermute | solution.py:52
  50.9 9.1 %collective-permute-start.13 = (f16[1040,128]{1,0:T(8,128)(2,1)S(1)}, f16[1040,128]{1,0:T(8,128)(2,1)S(1)}, u32[]{:S(2)}, u32[]{:S(2)}) collective-permute-start(f16[1040,128]{1,0:T(8,128)(2,1)S(1)} %convert_element_type.42), channel_id=1, source_target_pairs={{0,8},{1,9},{2,10},{3,11},{4,12},{5,13},{6,14},{7,15},{8,0},{9,1},... | collective-permute-start | bytes 798728 | tf_op jit(solution)/shard_map/ppermute | solution.py:52
  52.3 8.4 %collective-permute-start.14 = (f16[1040,128]{1,0:T(8,128)(2,1)S(1)}, f16[1040,128]{1,0:T(8,128)(2,1)S(1)}, u32[]{:S(2)}, u32[]{:S(2)}) collective-permute-start(f16[1040,128]{1,0:T(8,128)(2,1)S(1)} %convert_element_type.43), channel_id=1, source_target_pairs={{0,4},{1,5},{2,6},{3,7},{4,8},{5,9},{6,10},{7,11},{8,12},{9,13},{1... | collective-permute-start | bytes 798728 | tf_op jit(solution)/shard_map/ppermute | solution.py:52
  54.6 10.6 %collective-permute-start.15 = (f16[1040,128]{1,0:T(8,128)(2,1)S(1)}, f16[1040,128]{1,0:T(8,128)(2,1)S(1)}, u32[]{:S(2)}, u32[]{:S(2)}) collective-permute-start(f16[1040,128]{1,0:T(8,128)(2,1)S(1)} %convert_element_type.44), channel_id=1, source_target_pairs={{0,12},{1,13},{2,14},{3,15},{4,0},{5,1},{6,2},{7,3},{8,4},{9,5},{1... | collective-permute-start | bytes 798728 | tf_op jit(solution)/shard_map/ppermute | solution.py:52
  56.2 16.3 %collective-permute-start.16 = (f16[1040,128]{1,0:T(8,128)(2,1)S(1)}, f16[1040,128]{1,0:T(8,128)(2,1)S(1)}, u32[]{:S(2)}, u32[]{:S(2)}) collective-permute-start(f16[1040,128]{1,0:T(8,128)(2,1)S(1)} %convert_element_type.45), channel_id=1, source_target_pairs={{0,8},{1,9},{2,10},{3,11},{4,12},{5,13},{6,14},{7,15},{8,0},{9,1},... | collective-permute-start | bytes 798728 | tf_op jit(solution)/shard_map/ppermute | solution.py:52
  58.5 14.1 %collective-permute-start.17 = (f16[1040,128]{1,0:T(8,128)(2,1)S(1)}, f16[1040,128]{1,0:T(8,128)(2,1)S(1)}, u32[]{:S(2)}, u32[]{:S(2)}) collective-permute-start(f16[1040,128]{1,0:T(8,128)(2,1)S(1)} %convert_element_type.47), channel_id=1, source_target_pairs={{0,4},{1,5},{2,6},{3,7},{4,8},{5,9},{6,10},{7,11},{8,12},{9,13},{1... | collective-permute-start | bytes 798728 | tf_op jit(solution)/shard_map/ppermute | solution.py:52
  60.0 12.6 %collective-permute-start.18 = (f16[1040,128]{1,0:T(8,128)(2,1)S(1)}, f16[1040,128]{1,0:T(8,128)(2,1)S(1)}, u32[]{:S(2)}, u32[]{:S(2)}) collective-permute-start(f16[1040,128]{1,0:T(8,128)(2,1)S(1)} %convert_element_type.49), channel_id=1, source_target_pairs={{0,12},{1,13},{2,14},{3,15},{4,0},{5,1},{6,2},{7,3},{8,4},{9,5},{1... | collective-permute-start | bytes 798728 | tf_op jit(solution)/shard_map/ppermute | solution.py:52
  65.6 14.3 %collective-permute-start.19 = (f16[1040,128]{1,0:T(8,128)(2,1)S(1)}, f16[1040,128]{1,0:T(8,128)(2,1)S(1)}, u32[]{:S(2)}, u32[]{:S(2)}) collective-permute-start(f16[1040,128]{1,0:T(8,128)(2,1)S(1)} %convert_element_type.54), channel_id=1, source_target_pairs={{0,16},{16,0},{1,17},{17,1},{2,18},{18,2},{3,19},{19,3},{4,20},{20... | collective-permute-start | bytes 798728 | tf_op jit(solution)/shard_map/ppermute | solution.py:272

commit v18 on v17

--- a/solution.py
+++ b/solution.py
@@ -264,7 +264,7 @@
     keep_far, *far_sends = late(1)
     keep_near, *near_sends = late(0)
     sends = far_sends + near_sends
-    got = [shifted(sends[i].astype(F16), False, 1 + i % 3) for i in (1, 0, 2, 4, 3, 5)]
+    got = [shifted(sends[i].astype(F16), False, 1 + i % 3) for i in (0, 2, 1, 3, 5, 4)]
     rel, *got[:3] = lax.optimization_barrier((rel, *got[:3]))
     got = [v.astype(F32) for v in got]
     (second,) = call(second_kernel, [((rows, width), F32)], (rel, first, weights[0]), whole(3), **matmul)

time: 81.1 us -> 81.1 us (level)
  the two profiles are of different devices: /device:TPU:24 before, /device:TPU:32 now
where the time goes in v18:
time: 81.1 us; the launch traced here: 81 us
  starting transfers between devices  35 us (43%)
  waiting for transfers between devices  27.4 us (34%)
  Pallas kernels  17 us (21%)
  between operations  0.86 us (1%)
    ppermute x15, starting transfers between devices, shifted(): return lax.ppermute(value, ('section', 'y', 'x'), pairs_over(along, by))  23.3 us
    pallas_call x9, Pallas kernels, call(): pl.pallas_call(kernel, out_shape=[jax.ShapeDtypeStruct(s, t) for s, t in...  17 us
    ppermute x3, waiting for transfers between devices, on_line(): return lax.ppermute(value, ('section', 'z_lo'), pairs)  12.4 us
    ppermute x1, waiting for transfers between devices, local(): other = lax.ppermute(far.astype(F16), 'z_hi', [(0, 1), (1, 0)]).astype(F32)  7.66 us
    ppermute x1, starting transfers between devices, local(): other = lax.ppermute(far.astype(F16), 'z_hi', [(0, 1), (1, 0)]).astype(F32)  5.95 us
    ppermute x15, waiting for transfers between devices, shifted(): return lax.ppermute(value, ('section', 'y', 'x'), pairs_over(along, by))  5.25 us
    ppermute x3, starting transfers between devices, on_line(): return lax.ppermute(value, ('section', 'z_lo'), pairs)  4.47 us
    ppermute x1, waiting for transfers between devices, local(): shard = lax.ppermute(small, 'section', [(1, 0)])  2.13 us
  transfers between devices with their start and end apart: 20, of which 9 were waited for; matrix products, arithmetic and copies ran while one was open for 1% of the time, Pallas kernels for 15%

profile of v18, /device:TPU:32, one launch (start us, length us, event | category | flops | bytes accessed | tf_op | source)
XLA Modules:
  0.0 81.0 jit_solution(10281782400567761498)
XLA Ops:
  0.6 0.0 slice-start
  0.6 0.0 slice-start.1
  0.7 2.7 %shard_map.69 = (bf16[896,512]{1,0:T(8,128)(2,1)S(1)}, bf16[896,512]{1,0:T(8,128)(2,1)S(1)}, bf16[1280,512]{1,0:T(8,128)(2,1)S(1)}, bf16[1280,512]{1,0:T(8,128)(2,1)S(1)}, bf16[768,512]{1,0:T(8,128)(2,1)S(1)}) custom-call(s32[2]{0:T(128)} %pending_ref.1, bf16[4,128,1024]{2,1,0:T(8,128)(2,1)} %bitcast.20, bf16[3,128,4096]{2,1,0:T(8,128)(2,1)} %bitcast.19), custom_call_target="tpu_custom_call" | custom-call | flops 10000000000 | bytes 12582912 | tf_op jit(solution)/shard_map/pallas_call | solution.py:64
  3.4 1.6 %collective-permute-start.2 = (bf16[896,512]{1,0:T(8,128)(2,1)S(1)}, bf16[896,512]{1,0:T(8,128)(2,1)S(1)}, u32[]{:S(2)}, u32[]{:S(2)}) collective-permute-start(bf16[896,512]{1,0:T(8,128)(2,1)S(1)} %get-tuple-element.38.mine_on), channel_id=1, source_target_pairs={{0,1},{1,2},{2,3},{3,0},{4,5},{5,6},{6,7},{7,4},{8,9},{9,10},{10,1... | collective-permute-start | bytes 2752520 | tf_op jit(solution)/shard_map/ppermute | solution.py:52
  5.0 1.7 %collective-permute-start.3 = (bf16[896,512]{1,0:T(8,128)(2,1)S(1)}, bf16[896,512]{1,0:T(8,128)(2,1)S(1)}, u32[]{:S(2)}, u32[]{:S(2)}) collective-permute-start(bf16[896,512]{1,0:T(8,128)(2,1)S(1)} %get-tuple-element.39), channel_id=1, source_target_pairs={{0,3},{1,0},{2,1},{3,2},{4,7},{5,4},{6,5},{7,6},{8,11},{9,8},{10,9... | collective-permute-start | bytes 2752520 | tf_op jit(solution)/shard_map/ppermute | solution.py:52
  6.7 0.3 collective-permute-start.6
  7.0 3.0 %collective-permute-start.7 = (bf16[1280,512]{1,0:T(8,128)(2,1)S(1)}, bf16[1280,512]{1,0:T(8,128)(2,1)S(1)}, u32[]{:S(2)}, u32[]{:S(2)}) collective-permute-start(bf16[1280,512]{1,0:T(8,128)(2,1)S(1)} %get-tuple-element.47), channel_id=1, source_target_pairs={{0,3},{1,0},{2,1},{3,2},{4,7},{5,4},{6,5},{7,6},{8,11},{9,8},{10,9... | collective-permute-start | bytes 3932168 | tf_op jit(solution)/shard_map/ppermute | solution.py:52
  10.0 2.9 %shard_map.68 = (f32[128,1024]{1,0:T(8,128)S(1)}, bf16[128,1024]{1,0:T(8,128)(2,1)S(1)}) custom-call(bf16[128,4096]{1,0:T(8,128)(2,1)S(1)} %copy-done, bf16[1024,4096]{1,0:T(8,128)(2,1)S(1)} %bitcast.11), custom_call_target="tpu_custom_call" | custom-call | flops 1073741824 | bytes 2097152 | tf_op jit(solution)/shard_map/pallas_call | solution.py:64
  12.9 1.3 %collective-permute-start = (bf16[128,1024]{1,0:T(8,128)(2,1)S(1)}, bf16[128,1024]{1,0:T(8,128)(2,1)S(1)}, u32[]{:S(2)}, u32[]{:S(2)}) collective-permute-start(bf16[128,1024]{1,0:T(8,128)(2,1)S(1)} %get-tuple-element.37), channel_id=1, source_target_pairs={{128,0},{129,1},{130,2},{131,3},{132,4},{133,5},{134,6},{135,7},{1... | collective-permute-start | bytes 786440 | tf_op jit(solution)/shard_map/ppermute | solution.py:230
  14.2 2.1 %collective-permute-done = bf16[128,1024]{1,0:T(8,128)(2,1)S(1)} collective-permute-done((bf16[128,1024]{1,0:T(8,128)(2,1)S(1)}, bf16[128,1024]{1,0:T(8,128)(2,1)S(1)}, u32[]{:S(2)}, u32[]{:S(2)}) %collective-permute-start) | collective-permute-done | bytes 262176 | tf_op jit(solution)/shard_map/ppermute | solution.py:230
  16.3 0.1 add.3
  16.4 1.9 %collective-permute-start.1 = (bf16[128,1024]{1,0:T(8,128)(2,1)S(1)}, bf16[128,1024]{1,0:T(8,128)(2,1)S(1)}, u32[]{:S(2)}, u32[]{:S(2)}) collective-permute-start(bf16[128,1024]{1,0:T(8,128)(2,1)S(1)} %add.3), channel_id=1, source_target_pairs={{0,96},{32,0},{64,32},{96,64},{128,160},{160,192},{192,224},{224,1... | collective-permute-start | bytes 786440 | tf_op jit(solution)/shard_map/ppermute | solution.py:209
  18.3 6.0 %collective-permute-done.1 = bf16[128,1024]{1,0:T(8,128)(2,1)S(1)} collective-permute-done((bf16[128,1024]{1,0:T(8,128)(2,1)S(1)}, bf16[128,1024]{1,0:T(8,128)(2,1)S(1)}, u32[]{:S(2)}, u32[]{:S(2)}) %collective-permute-start.1) | collective-permute-done | bytes 262176 | tf_op jit(solution)/shard_map/ppermute | solution.py:209
  24.3 0.0 collective-permute-done.2.left_on
  24.3 0.0 collective-permute-done.3.right_on
  24.3 1.3 %collective-permute-start.4 = (bf16[128,1024]{1,0:T(8,128)(2,1)S(1)}, bf16[128,1024]{1,0:T(8,128)(2,1)S(1)}, u32[]{:S(2)}, u32[]{:S(2)}) collective-permute-start(bf16[128,1024]{1,0:T(8,128)(2,1)S(1)} %collective-permute-done.1), channel_id=1, source_target_pairs={{128,32},{160,64},{192,96},{224,0},{129,33},{161,65},{193,97},{225... | collective-permute-start | bytes 786440 | tf_op jit(solution)/shard_map/ppermute | solution.py:209
  25.6 0.1 collective-permute-start.8
  25.7 3.2 %collective-permute-start.9 = (bf16[896,512]{1,0:T(8,128)(2,1)S(1)}, bf16[896,512]{1,0:T(8,128)(2,1)S(1)}, u32[]{:S(2)}, u32[]{:S(2)}) collective-permute-start(bf16[896,512]{1,0:T(8,128)(2,1)S(1)} %collective-permute-done.3.right_on), channel_id=1, source_target_pairs={{0,3},{1,0},{2,1},{3,2},{4,7},{5,4},{6,5},{7,6},{8,11},{9,8},{10,9... | collective-permute-start | bytes 2752520 | tf_op jit(solution)/shard_map/ppermute | solution.py:52
  28.9 4.3 %collective-permute-done.4 = bf16[128,1024]{1,0:T(8,128)(2,1)S(1)} collective-permute-done((bf16[128,1024]{1,0:T(8,128)(2,1)S(1)}, bf16[128,1024]{1,0:T(8,128)(2,1)S(1)}, u32[]{:S(2)}, u32[]{:S(2)}) %collective-permute-start.4) | collective-permute-done | bytes 262176 | tf_op jit(solution)/shard_map/ppermute | solution.py:209
  33.2 1.3 %collective-permute-start.5 = (bf16[128,1024]{1,0:T(8,128)(2,1)S(1)}, bf16[128,1024]{1,0:T(8,128)(2,1)S(1)}, u32[]{:S(2)}, u32[]{:S(2)}) collective-permute-start(bf16[128,1024]{1,0:T(8,128)(2,1)S(1)} %collective-permute-done.1), channel_id=1, source_target_pairs={{128,0},{160,32},{192,64},{224,96},{129,1},{161,33},{193,65},{225,... | collective-permute-start | bytes 786440 | tf_op jit(solution)/shard_map/ppermute | solution.py:209
  34.4 2.1 %collective-permute-done.5 = bf16[128,1024]{1,0:T(8,128)(2,1)S(1)} collective-permute-done((bf16[128,1024]{1,0:T(8,128)(2,1)S(1)}, bf16[128,1024]{1,0:T(8,128)(2,1)S(1)}, u32[]{:S(2)}, u32[]{:S(2)}) %collective-permute-start.5) | collective-permute-done | bytes 262176 | tf_op jit(solution)/shard_map/ppermute | solution.py:209
  36.6 0.1 pad_maximum_fusion.rel_ref
  36.7 0.6 shard_map.71
  37.4 0.9 %collective-permute-start.10 = (bf16[256,512]{1,0:T(8,128)(2,1)S(1)}, bf16[256,512]{1,0:T(8,128)(2,1)S(1)}, u32[]{:S(2)}, u32[]{:S(2)}) collective-permute-start(bf16[256,512]{1,0:T(8,128)(2,1)S(1)} %get-tuple-element.48), channel_id=1, source_target_pairs={{0,2},{1,3},{2,0},{3,1},{4,6},{5,7},{6,4},{7,5},{8,10},{9,11},{10,... | collective-permute-start | bytes 786440 | tf_op jit(solution)/shard_map/ppermute | solution.py:52
  38.2 0.2 collective-permute-start.11
  38.5 3.0 %collective-permute-start.12 = (bf16[256,512]{1,0:T(8,128)(2,1)S(1)}, bf16[256,512]{1,0:T(8,128)(2,1)S(1)}, u32[]{:S(2)}, u32[]{:S(2)}) collective-permute-start(bf16[256,512]{1,0:T(8,128)(2,1)S(1)} %get-tuple-element.50), channel_id=1, source_target_pairs={{0,3},{1,0},{2,1},{3,2},{4,7},{5,4},{6,5},{7,6},{8,11},{9,8},{10,9... | collective-permute-start | bytes 786440 | tf_op jit(solution)/shard_map/ppermute | solution.py:52
  41.5 2.9 %shard_map.70.acc_ref = f32[1024,1024]{1,0:T(8,128)S(1)} custom-call(bf16[896,512]{1,0:T(8,128)(2,1)S(1)} %get-tuple-element.38.mine_on, bf16[1280,512]{1,0:T(8,128)(2,1)S(1)} %get-tuple-element.43.mine_ref, bf16[768,512]{1,0:T(8,128)(2,1)S(1)} %get-tuple-element.44.own_ref, bf16[896,512]{1,0:T(8,128)(2,1)S(1)} %collective-permute-done.2.left_on, ...), custom_call_target="tpu_custom_call" | custom-call | flops 2415919104 | bytes 12582912 | tf_op jit(solution)/shard_map/pallas_call | solution.py:64
  44.4 1.5 %collective-permute-done.10.two_last = bf16[256,512]{1,0:T(8,128)(2,1)S(1)} collective-permute-done((bf16[256,512]{1,0:T(8,128)(2,1)S(1)}, bf16[256,512]{1,0:T(8,128)(2,1)S(1)}, u32[]{:S(2)}, u32[]{:S(2)}) %collective-permute-start.10) | collective-permute-done | bytes 262176 | tf_op jit(solution)/shard_map/ppermute | solution.py:52
  45.9 2.7 %collective-permute-done.11.left_last = bf16[256,512]{1,0:T(8,128)(2,1)S(1)} collective-permute-done((bf16[256,512]{1,0:T(8,128)(2,1)S(1)}, bf16[256,512]{1,0:T(8,128)(2,1)S(1)}, u32[]{:S(2)}, u32[]{:S(2)}) %collective-permute-start.11) | collective-permute-done | bytes 262176 | tf_op jit(solution)/shard_map/ppermute | solution.py:52
  48.6 0.0 collective-permute-done.8.upper_ref
  48.6 0.0 collective-permute-done.9.lower_ref
  48.6 1.5 %shard_map.72 = (f32[1024,128]{1,0:T(8,128)S(1)}, f32[1040,128]{1,0:T(8,128)S(1)}, f32[1040,128]{1,0:T(8,128)S(1)}, f32[1040,128]{1,0:T(8,128)S(1)}) custom-call(f32[1024,1024]{1,0:T(8,128)S(1)} %shard_map.70.acc_ref, bf16[896,512]{1,0:T(8,128)(2,1)S(1)} %get-tuple-element.38.mine_on, bf16[1280,512]{1,0:T(8,128)(2,1)S(1)} %get-tuple-element.43.mine_ref, ...), custom_call_target="tpu_custom_call" | custom-call | flops 939524096 | bytes 8388608 | tf_op jit(solution)/shard_map/pallas_call | solution.py:64
  50.1 1.6 %collective-permute-start.13 = (f16[1040,128]{1,0:T(8,128)(2,1)S(1)}, f16[1040,128]{1,0:T(8,128)(2,1)S(1)}, u32[]{:S(2)}, u32[]{:S(2)}) collective-permute-start(f16[1040,128]{1,0:T(8,128)(2,1)S(1)} %convert_element_type.42), channel_id=1, source_target_pairs={{0,4},{1,5},{2,6},{3,7},{4,8},{5,9},{6,10},{7,11},{8,12},{9,13},{1... | collective-permute-start | bytes 798728 | tf_op jit(solution)/shard_map/ppermute | solution.py:52
  51.7 1.8 %collective-permute-start.14 = (f16[1040,128]{1,0:T(8,128)(2,1)S(1)}, f16[1040,128]{1,0:T(8,128)(2,1)S(1)}, u32[]{:S(2)}, u32[]{:S(2)}) collective-permute-start(f16[1040,128]{1,0:T(8,128)(2,1)S(1)} %convert_element_type.43), channel_id=1, source_target_pairs={{0,12},{1,13},{2,14},{3,15},{4,0},{5,1},{6,2},{7,3},{8,4},{9,5},{1... | collective-permute-start | bytes 798728 | tf_op jit(solution)/shard_map/ppermute | solution.py:52
  53.6 2.0 %collective-permute-start.15 = (f16[1040,128]{1,0:T(8,128)(2,1)S(1)}, f16[1040,128]{1,0:T(8,128)(2,1)S(1)}, u32[]{:S(2)}, u32[]{:S(2)}) collective-permute-start(f16[1040,128]{1,0:T(8,128)(2,1)S(1)} %convert_element_type.44), channel_id=1, source_target_pairs={{0,8},{1,9},{2,10},{3,11},{4,12},{5,13},{6,14},{7,15},{8,0},{9,1},... | collective-permute-start | bytes 798728 | tf_op jit(solution)/shard_map/ppermute | solution.py:52
  55.6 1.5 %shard_map.74 = (f32[1024,128]{1,0:T(8,128)S(1)}, f32[1040,128]{1,0:T(8,128)S(1)}, f32[1040,128]{1,0:T(8,128)S(1)}, f32[1040,128]{1,0:T(8,128)S(1)}) custom-call(f32[1024,1024]{1,0:T(8,128)S(1)} %shard_map.70.acc_ref, bf16[896,512]{1,0:T(8,128)(2,1)S(1)} %get-tuple-element.38.mine_on, bf16[1280,512]{1,0:T(8,128)(2,1)S(1)} %get-tuple-element.43.mine_ref, ...), custom_call_target="tpu_custom_call" | custom-call | flops 939524096 | bytes 8388608 | tf_op jit(solution)/shard_map/pallas_call | solution.py:64
  57.1 0.8 collective-permute-start.16
  57.9 2.6 %collective-permute-start.17 = (f16[1040,128]{1,0:T(8,128)(2,1)S(1)}, f16[1040,128]{1,0:T(8,128)(2,1)S(1)}, u32[]{:S(2)}, u32[]{:S(2)}) collective-permute-start(f16[1040,128]{1,0:T(8,128)(2,1)S(1)} %convert_element_type.47), channel_id=1, source_target_pairs={{0,12},{1,13},{2,14},{3,15},{4,0},{5,1},{6,2},{7,3},{8,4},{9,5},{1... | collective-permute-start | bytes 798728 | tf_op jit(solution)/shard_map/ppermute | solution.py:52
  60.5 0.5 collective-permute-start.18
  61.0 0.8 collective-permute-done.15
  61.9 0.3 shard_map.75
  62.3 6.0 %collective-permute-start.19 = (f16[1040,128]{1,0:T(8,128)(2,1)S(1)}, f16[1040,128]{1,0:T(8,128)(2,1)S(1)}, u32[]{:S(2)}, u32[]{:S(2)}) collective-permute-start(f16[1040,128]{1,0:T(8,128)(2,1)S(1)} %convert_element_type.54), channel_id=1, source_target_pairs={{0,16},{16,0},{1,17},{17,1},{2,18},{18,2},{3,19},{19,3},{4,20},{20... | collective-permute-start | bytes 798728 | tf_op jit(solution)/shard_map/ppermute | solution.py:272
  68.2 0.0 collective-permute-done.16
  68.2 0.0 collective-permute-done.17
  68.3 0.3 collective-permute-done.18
  68.6 3.7 %shard_map.73 = f32[128,1024]{1,0:T(8,128)} custom-call(bf16[4,128,1024]{2,1,0:T(8,128)(2,1)S(1)} %pad_maximum_fusion.rel_ref, f32[128,1024]{1,0:T(8,128)S(1)} %get-tuple-element.63.first_ref, bf16[1024,4096]{1,0:T(8,128)(2,1)S(1)} %bitcast.12), custom_call_target="tpu_custom_call" | custom-call | flops 1073741824 | bytes 2097152 | tf_op jit(solution)/shard_map/pallas_call | solution.py:64
  72.3 7.7 %collective-permute-done.19 = f16[1040,128]{1,0:T(8,128)(2,1)S(1)} collective-permute-done((f16[1040,128]{1,0:T(8,128)(2,1)S(1)}, f16[1040,128]{1,0:T(8,128)(2,1)S(1)}, u32[]{:S(2)}, u32[]{:S(2)}) %collective-permute-start.19) | collective-permute-done | bytes 266272 | tf_op jit(solution)/shard_map/ppermute | solution.py:272
  80.0 1.0 %shard_map.76 = f32[1024,128]{1,0:T(8,128)} custom-call(f32[1024,128]{1,0:T(8,128)S(1)} %get-tuple-element.64.keep_ref, f32[1040,128]{1,0:T(8,128)S(1)} %convert_element_type.46.one_ref, f32[1040,128]{1,0:T(8,128)S(1)} %convert_element_type.48.two_ref, f32[1040,128]{1,0:T(8,128)S(1)} %convert_element_type.50.three_ref, ...), custom_call_target="tpu_custom_call" | custom-call | bytes 4194304 | tf_op jit(solution)/shard_map/pallas_call | solution.py:64
  (24 shorter events, 0.5 us)
Async XLA Ops:
  0.6 9.3 %slice-start = ((s8[8388608]{0:T(1024)(128)(4,1)}), s8[4194304]{0:T(1024)(128)(4,1)S(1)}, s32[]{:S(2)}) async-start(s8[8388608]{0:T(1024)(128)(4,1)} %bitcast.9), calls=%async_computation | async-start | bytes 8388608
  0.6 9.3 %slice-start.1 = ((s8[8388608]{0:T(1024)(128)(4,1)}), s8[4194304]{0:T(1024)(128)(4,1)S(1)}, s32[]{:S(2)}) async-start(s8[8388608]{0:T(1024)(128)(4,1)} %bitcast.9), calls=%async_computation.1 | async-start | bytes 8388608
  0.7 9.3 %copy-start = (bf16[128,4096]{1,0:T(8,128)(2,1)S(1)}, bf16[128,4096]{1,0:T(8,128)(2,1)}, u32[]{:S(2)}) copy-start(bf16[128,4096]{1,0:T(8,128)(2,1)} %head_ref.1) | copy-start | bytes 3145732
  3.4 20.9 %collective-permute-start.2 = (bf16[896,512]{1,0:T(8,128)(2,1)S(1)}, bf16[896,512]{1,0:T(8,128)(2,1)S(1)}, u32[]{:S(2)}, u32[]{:S(2)}) collective-permute-start(bf16[896,512]{1,0:T(8,128)(2,1)S(1)} %get-tuple-element.38.mine_on), channel_id=1, source_target_pairs={{0,1},{1,2},{2,3},{3,0},{4,5},{5,6},{6,7},{7,4},{8,9},{9,10},{10,1... | collective-permute-start | bytes 2752520 | tf_op jit(solution)/shard_map/ppermute | solution.py:52
  5.0 19.3 %collective-permute-start.3 = (bf16[896,512]{1,0:T(8,128)(2,1)S(1)}, bf16[896,512]{1,0:T(8,128)(2,1)S(1)}, u32[]{:S(2)}, u32[]{:S(2)}) collective-permute-start(bf16[896,512]{1,0:T(8,128)(2,1)S(1)} %get-tuple-element.39), channel_id=1, source_target_pairs={{0,3},{1,0},{2,1},{3,2},{4,7},{5,4},{6,5},{7,6},{8,11},{9,8},{10,9... | collective-permute-start | bytes 2752520 | tf_op jit(solution)/shard_map/ppermute | solution.py:52
  6.7 31.5 %collective-permute-start.6 = (bf16[1280,512]{1,0:T(8,128)(2,1)S(1)}, bf16[1280,512]{1,0:T(8,128)(2,1)S(1)}, u32[]{:S(2)}, u32[]{:S(2)}) collective-permute-start(bf16[1280,512]{1,0:T(8,128)(2,1)S(1)} %get-tuple-element.43.mine_ref), channel_id=1, source_target_pairs={{0,1},{1,2},{2,3},{3,0},{4,5},{5,6},{6,7},{7,4},{8,9},{9,10},{10,1... | collective-permute-start | bytes 3932168 | tf_op jit(solution)/shard_map/ppermute | solution.py:52
  7.0 31.5 %collective-permute-start.7 = (bf16[1280,512]{1,0:T(8,128)(2,1)S(1)}, bf16[1280,512]{1,0:T(8,128)(2,1)S(1)}, u32[]{:S(2)}, u32[]{:S(2)}) collective-permute-start(bf16[1280,512]{1,0:T(8,128)(2,1)S(1)} %get-tuple-element.47), channel_id=1, source_target_pairs={{0,3},{1,0},{2,1},{3,2},{4,7},{5,4},{6,5},{7,6},{8,11},{9,8},{10,9... | collective-permute-start | bytes 3932168 | tf_op jit(solution)/shard_map/ppermute | solution.py:52
  12.9 3.4 %collective-permute-start = (bf16[128,1024]{1,0:T(8,128)(2,1)S(1)}, bf16[128,1024]{1,0:T(8,128)(2,1)S(1)}, u32[]{:S(2)}, u32[]{:S(2)}) collective-permute-start(bf16[128,1024]{1,0:T(8,128)(2,1)S(1)} %get-tuple-element.37), channel_id=1, source_target_pairs={{128,0},{129,1},{130,2},{131,3},{132,4},{133,5},{134,6},{135,7},{1... | collective-permute-start | bytes 786440 | tf_op jit(solution)/shard_map/ppermute | solution.py:230
  16.4 7.9 %collective-permute-start.1 = (bf16[128,1024]{1,0:T(8,128)(2,1)S(1)}, bf16[128,1024]{1,0:T(8,128)(2,1)S(1)}, u32[]{:S(2)}, u32[]{:S(2)}) collective-permute-start(bf16[128,1024]{1,0:T(8,128)(2,1)S(1)} %add.3), channel_id=1, source_target_pairs={{0,96},{32,0},{64,32},{96,64},{128,160},{160,192},{192,224},{224,1... | collective-permute-start | bytes 786440 | tf_op jit(solution)/shard_map/ppermute | solution.py:209
  24.3 8.9 %collective-permute-start.4 = (bf16[128,1024]{1,0:T(8,128)(2,1)S(1)}, bf16[128,1024]{1,0:T(8,128)(2,1)S(1)}, u32[]{:S(2)}, u32[]{:S(2)}) collective-permute-start(bf16[128,1024]{1,0:T(8,128)(2,1)S(1)} %collective-permute-done.1), channel_id=1, source_target_pairs={{128,32},{160,64},{192,96},{224,0},{129,33},{161,65},{193,97},{225... | collective-permute-start | bytes 786440 | tf_op jit(solution)/shard_map/ppermute | solution.py:209
  25.6 23.0 %collective-permute-start.8 = (bf16[896,512]{1,0:T(8,128)(2,1)S(1)}, bf16[896,512]{1,0:T(8,128)(2,1)S(1)}, u32[]{:S(2)}, u32[]{:S(2)}) collective-permute-start(bf16[896,512]{1,0:T(8,128)(2,1)S(1)} %collective-permute-done.2.left_on), channel_id=1, source_target_pairs={{0,1},{1,2},{2,3},{3,0},{4,5},{5,6},{6,7},{7,4},{8,9},{9,10},{10,1... | collective-permute-start | bytes 2752520 | tf_op jit(solution)/shard_map/ppermute | solution.py:52
  25.7 22.9 %collective-permute-start.9 = (bf16[896,512]{1,0:T(8,128)(2,1)S(1)}, bf16[896,512]{1,0:T(8,128)(2,1)S(1)}, u32[]{:S(2)}, u32[]{:S(2)}) collective-permute-start(bf16[896,512]{1,0:T(8,128)(2,1)S(1)} %collective-permute-done.3.right_on), channel_id=1, source_target_pairs={{0,3},{1,0},{2,1},{3,2},{4,7},{5,4},{6,5},{7,6},{8,11},{9,8},{10,9... | collective-permute-start | bytes 2752520 | tf_op jit(solution)/shard_map/ppermute | solution.py:52
  33.2 3.4 %collective-permute-start.5 = (bf16[128,1024]{1,0:T(8,128)(2,1)S(1)}, bf16[128,1024]{1,0:T(8,128)(2,1)S(1)}, u32[]{:S(2)}, u32[]{:S(2)}) collective-permute-start(bf16[128,1024]{1,0:T(8,128)(2,1)S(1)} %collective-permute-done.1), channel_id=1, source_target_pairs={{128,0},{160,32},{192,64},{224,96},{129,1},{161,33},{193,65},{225,... | collective-permute-start | bytes 786440 | tf_op jit(solution)/shard_map/ppermute | solution.py:209
  37.4 8.5 %collective-permute-start.10 = (bf16[256,512]{1,0:T(8,128)(2,1)S(1)}, bf16[256,512]{1,0:T(8,128)(2,1)S(1)}, u32[]{:S(2)}, u32[]{:S(2)}) collective-permute-start(bf16[256,512]{1,0:T(8,128)(2,1)S(1)} %get-tuple-element.48), channel_id=1, source_target_pairs={{0,2},{1,3},{2,0},{3,1},{4,6},{5,7},{6,4},{7,5},{8,10},{9,11},{10,... | collective-permute-start | bytes 786440 | tf_op jit(solution)/shard_map/ppermute | solution.py:52
  38.2 10.3 %collective-permute-start.11 = (bf16[256,512]{1,0:T(8,128)(2,1)S(1)}, bf16[256,512]{1,0:T(8,128)(2,1)S(1)}, u32[]{:S(2)}, u32[]{:S(2)}) collective-permute-start(bf16[256,512]{1,0:T(8,128)(2,1)S(1)} %get-tuple-element.49), channel_id=1, source_target_pairs={{0,1},{1,2},{2,3},{3,0},{4,5},{5,6},{6,7},{7,4},{8,9},{9,10},{10,1... | collective-permute-start | bytes 786440 | tf_op jit(solution)/shard_map/ppermute | solution.py:52
  38.5 10.1 %collective-permute-start.12 = (bf16[256,512]{1,0:T(8,128)(2,1)S(1)}, bf16[256,512]{1,0:T(8,128)(2,1)S(1)}, u32[]{:S(2)}, u32[]{:S(2)}) collective-permute-start(bf16[256,512]{1,0:T(8,128)(2,1)S(1)} %get-tuple-element.50), channel_id=1, source_target_pairs={{0,3},{1,0},{2,1},{3,2},{4,7},{5,4},{6,5},{7,6},{8,11},{9,8},{10,9... | collective-permute-start | bytes 786440 | tf_op jit(solution)/shard_map/ppermute | solution.py:52
  50.1 10.5 %collective-permute-start.13 = (f16[1040,128]{1,0:T(8,128)(2,1)S(1)}, f16[1040,128]{1,0:T(8,128)(2,1)S(1)}, u32[]{:S(2)}, u32[]{:S(2)}) collective-permute-start(f16[1040,128]{1,0:T(8,128)(2,1)S(1)} %convert_element_type.42), channel_id=1, source_target_pairs={{0,4},{1,5},{2,6},{3,7},{4,8},{5,9},{6,10},{7,11},{8,12},{9,13},{1... | collective-permute-start | bytes 798728 | tf_op jit(solution)/shard_map/ppermute | solution.py:52
  51.7 9.3 %collective-permute-start.14 = (f16[1040,128]{1,0:T(8,128)(2,1)S(1)}, f16[1040,128]{1,0:T(8,128)(2,1)S(1)}, u32[]{:S(2)}, u32[]{:S(2)}) collective-permute-start(f16[1040,128]{1,0:T(8,128)(2,1)S(1)} %convert_element_type.43), channel_id=1, source_target_pairs={{0,12},{1,13},{2,14},{3,15},{4,0},{5,1},{6,2},{7,3},{8,4},{9,5},{1... | collective-permute-start | bytes 798728 | tf_op jit(solution)/shard_map/ppermute | solution.py:52
  53.6 8.2 %collective-permute-start.15 = (f16[1040,128]{1,0:T(8,128)(2,1)S(1)}, f16[1040,128]{1,0:T(8,128)(2,1)S(1)}, u32[]{:S(2)}, u32[]{:S(2)}) collective-permute-start(f16[1040,128]{1,0:T(8,128)(2,1)S(1)} %convert_element_type.44), channel_id=1, source_target_pairs={{0,8},{1,9},{2,10},{3,11},{4,12},{5,13},{6,14},{7,15},{8,0},{9,1},... | collective-permute-start | bytes 798728 | tf_op jit(solution)/shard_map/ppermute | solution.py:52
  57.1 11.1 %collective-permute-start.16 = (f16[1040,128]{1,0:T(8,128)(2,1)S(1)}, f16[1040,128]{1,0:T(8,128)(2,1)S(1)}, u32[]{:S(2)}, u32[]{:S(2)}) collective-permute-start(f16[1040,128]{1,0:T(8,128)(2,1)S(1)} %convert_element_type.45), channel_id=1, source_target_pairs={{0,4},{1,5},{2,6},{3,7},{4,8},{5,9},{6,10},{7,11},{8,12},{9,13},{1... | collective-permute-start | bytes 798728 | tf_op jit(solution)/shard_map/ppermute | solution.py:52
  57.9 10.4 %collective-permute-start.17 = (f16[1040,128]{1,0:T(8,128)(2,1)S(1)}, f16[1040,128]{1,0:T(8,128)(2,1)S(1)}, u32[]{:S(2)}, u32[]{:S(2)}) collective-permute-start(f16[1040,128]{1,0:T(8,128)(2,1)S(1)} %convert_element_type.47), channel_id=1, source_target_pairs={{0,12},{1,13},{2,14},{3,15},{4,0},{5,1},{6,2},{7,3},{8,4},{9,5},{1... | collective-permute-start | bytes 798728 | tf_op jit(solution)/shard_map/ppermute | solution.py:52
  60.5 8.0 %collective-permute-start.18 = (f16[1040,128]{1,0:T(8,128)(2,1)S(1)}, f16[1040,128]{1,0:T(8,128)(2,1)S(1)}, u32[]{:S(2)}, u32[]{:S(2)}) collective-permute-start(f16[1040,128]{1,0:T(8,128)(2,1)S(1)} %convert_element_type.49), channel_id=1, source_target_pairs={{0,8},{1,9},{2,10},{3,11},{4,12},{5,13},{6,14},{7,15},{8,0},{9,1},... | collective-permute-start | bytes 798728 | tf_op jit(solution)/shard_map/ppermute | solution.py:52
  62.3 17.7 %collective-permute-start.19 = (f16[1040,128]{1,0:T(8,128)(2,1)S(1)}, f16[1040,128]{1,0:T(8,128)(2,1)S(1)}, u32[]{:S(2)}, u32[]{:S(2)}) collective-permute-start(f16[1040,128]{1,0:T(8,128)(2,1)S(1)} %convert_element_type.54), channel_id=1, source_target_pairs={{0,16},{16,0},{1,17},{17,1},{2,18},{18,2},{3,19},{19,3},{4,20},{20... | collective-permute-start | bytes 798728 | tf_op jit(solution)/shard_map/ppermute | solution.py:272
